TPU v7x, 32 devices: a whole 2x2x4 slice. The times are simulated.
32 devices in a mesh: section: 8 (over y, x, core), tensor: 4 (over z).
Axes of the slice: x: 2, y: 2, z: 4, core: 2. Of those that a mesh axis runs over, the one named last changes fastest.
Arguments:
- weights: bfloat16 [8, 4096, 4096], P('section', 'tensor'), may hold values from -0.09375 to 0.09375
- filters: float32 [8, 32, 128], P('section'), may hold values from -0.5 to 0.5
- down_input: bfloat16 [8, 512, 4096], P('section', 'tensor'), may hold values from -6 to 6
- down_cot: bfloat16 [8, 512, 4096], P('section', 'tensor'), may hold values from -6 to 6
- up_input: bfloat16 [8, 512, 4096], P('section', 'tensor'), may hold values from -6 to 6
- up_cot: bfloat16 [8, 512, 4096], P('section', 'tensor'), may hold values from -6 to 6
Outputs:
- weight_grad: bfloat16 [8, 4096, 4096], P('section', 'tensor')
- filter_grad: float32 [8, 32, 128], P('section')
- down_passed: bfloat16 [8, 512, 4096], P('section', 'tensor')
- up_passed: bfloat16 [8, 512, 4096], P('section', 'tensor')
All inputs are finite; a program needn't handle non-finite values.
Results may differ from a plain program's by a relative error of at most 0.014.
Values may be sent and summed in bfloat16 or wider, within the bound.
No kernel may reach another device: no remote copies, remote signals or barrier semaphores. Data moves between devices by JAX's collectives and lax.ppermute only.
A program may use at most 192 MiB of HBM per device.

v0:
```python
import functools

import jax
import jax.numpy as jnp
from jax import lax
from jax.experimental import pallas as pl
from jax.experimental.pallas import tpu as pltpu
from jax.sharding import PartitionSpec as P

epsilon = 1e-06
params = functools.partial(pltpu.CompilerParams, vmem_limit_bytes=63 * 1024 * 1024)
f32, bf16 = jnp.float32, jnp.bfloat16


def dot(a, b, dims=((1,), (0,))):
    return lax.dot_general(a, b, (dims, ((), ())), preferred_element_type=f32)


def shape(dims, dtype):
    return jax.ShapeDtypeStruct(dims, dtype)


def call(kernel, args, after, in_specs, **options):
    count = len(args)

    def body(*refs):
        kernel(*refs[:count], *refs[count + len(after) :])

    unread = [pl.BlockSpec(memory_space=pl.ANY)] * len(after)
    return pl.pallas_call(
        body, in_specs=list(in_specs) + unread, compiler_params=params(), **options
    )(*args, *after)


def toeplitz_kernel(filters_ref, causal_ref, ahead_ref):
    taps = filters_ref.shape[1]
    row = lax.broadcasted_iota(jnp.int32, (taps, taps), 0)
    col = lax.broadcasted_iota(jnp.int32, (taps, taps), 1)
    for g in range(filters_ref.shape[0]):
        line = jnp.broadcast_to(filters_ref[g : g + 1, :], (taps, taps))
        turned = pltpu.roll(line, 0, 1, stride=1, stride_axis=0)
        own = jnp.where(col >= row, turned, 0.0)
        beyond = jnp.where(col < row, turned, 0.0)
        ahead_ref[g, :, :taps] = own.astype(bf16)
        ahead_ref[g, :, taps:] = beyond.astype(bf16)
        causal_ref[g, :, :taps] = beyond.T.astype(bf16)
        causal_ref[g, :, taps:] = own.T.astype(bf16)


def toeplitz(filters):
    groups, taps = filters.shape
    step = 8
    out = shape((groups, taps, 2 * taps), bf16)
    spec = pl.BlockSpec((step, taps, 2 * taps), lambda i: (i, 0, 0))
    return call(
        toeplitz_kernel,
        (filters,),
        (),
        grid=(groups // step,),
        in_specs=[pl.BlockSpec((step, taps), lambda i: (i, 0))],
        out_specs=[spec, spec],
        out_shape=[out, out],
        name="toeplitz",
    )


def place(by):
    blocks = lax.axis_size("tensor")
    return lax.rem(lax.axis_index("tensor") + (by + blocks), blocks)


def window(index, size):
    return pl.ds(pl.multiple_of(index * size, size), size)


def normalise(wide):
    inverse = lax.rsqrt(jnp.mean(wide * wide, axis=1, keepdims=True) + epsilon)
    return wide * inverse, inverse


def normed_kernel(xin_ref, normed_ref):
    normed = normalise(xin_ref[...].astype(f32))[0].astype(bf16)
    width = normed_ref.shape[2]
    for i in range(normed_ref.shape[0]):
        normed_ref[i] = normed[:, i * width : (i + 1) * width]


def normed_blocks(xin, after=()):
    rows, width = xin.shape
    blocks = lax.axis_size("tensor")
    step = 32
    return call(
        normed_kernel,
        (xin,),
        after,
        grid=(rows // step,),
        in_specs=[pl.BlockSpec((step, width), lambda i: (i, 0))],
        out_specs=pl.BlockSpec((blocks, step, width // blocks), lambda i: (0, i, 0)),
        out_shape=shape((blocks, rows, width // blocks), bf16),
        name="normed_blocks",
    )


def mix_kernel(xin_ref, cot_ref, mix_ref):
    normed, _ = normalise(xin_ref[...].astype(f32))
    mix_ref[...] = (cot_ref[...].astype(f32) * normed).astype(bf16)


def grad_mix(xin, cot, after=()):
    rows, width = xin.shape
    step = 32
    spec = pl.BlockSpec((step, width), lambda i: (i, 0))
    return call(
        mix_kernel,
        (xin, cot),
        after,
        grid=(rows // step,),
        in_specs=[spec, spec],
        out_specs=spec,
        out_shape=shape((rows, width), bf16),
        name="grad_mix",
    )


def project_kernel(features_ref, weight_ref, causal_ref, part_ref, *rest):
    *mixed_refs, mixed_ref = rest
    groups, taps, _ = causal_ref.shape
    part = dot(features_ref[...], weight_ref[...]).astype(bf16)
    part_ref[...] = part
    width = part.shape[1] // groups
    for g in range(groups):
        cols = slice(g * width, (g + 1) * width)
        for start in range(0, part.shape[0], taps):
            if start == 0:
                out = dot(causal_ref[g, :, taps:], part[:taps, cols])
            else:
                out = dot(causal_ref[g], part[start - taps : start + taps, cols])
            mixed_ref[start : start + taps, cols] = out.astype(bf16)
    for s, out_ref in enumerate(mixed_refs):
        out_ref[...] = mixed_ref[window(place(s), out_ref.shape[0]), :]


def project(features, weight, causal, after=()):
    blocks = lax.axis_size("tensor")
    tokens, depth = features.shape
    rows = tokens // blocks
    width = weight.shape[1]
    groups, taps, _ = causal.shape
    step = 4
    tile = width // groups * step
    part, *mixed = call(
        project_kernel,
        (features, weight, causal),
        after,
        grid=(groups // step,),
        in_specs=[
            pl.BlockSpec((tokens, depth), lambda i: (0, 0)),
            pl.BlockSpec((depth, tile), lambda i: (0, i)),
            pl.BlockSpec((step, taps, 2 * taps), lambda i: (i, 0, 0)),
        ],
        out_specs=[pl.BlockSpec((tokens, tile), lambda i: (0, i))]
        + [pl.BlockSpec((rows, tile), lambda i: (0, i))] * blocks,
        out_shape=[shape((tokens, width), bf16)] + [shape((rows, width), bf16)] * blocks,
        scratch_shapes=[pltpu.VMEM((tokens, tile), bf16)],
        name="project",
    )
    return part, mixed


def back_kernel(blocks, *refs):
    count = 2 * blocks - 1
    mix_refs = refs[:count]
    part_ref, weight_ref, ahead_ref, grad_ref, taps_ref, back_ref, mix_ref, total = refs[count:]
    groups, taps, _ = ahead_ref.shape
    tokens = mix_ref.shape[0]
    rows = tokens // blocks
    width = mix_ref.shape[1] // groups
    mine = lax.axis_index("tensor")
    mix_ref[window(mine, rows), :] = mix_refs[0][...]
    for s in range(1, blocks):

        @pl.when(mine >= s)
        def _():
            mix_ref[window(mine - s, rows), :] = mix_refs[s][...]

        @pl.when(mine < s)
        def _():
            mix_ref[window(mine + (blocks - s), rows), :] = mix_refs[2 * blocks - 1 - s][...]

    row = lax.broadcasted_iota(jnp.int32, (taps, taps), 0)
    col = lax.broadcasted_iota(jnp.int32, (taps, taps), 1)
    starts = range(0, tokens, taps)
    for g in range(groups):
        cols = slice(g * width, (g + 1) * width)
        mix = mix_ref[:, cols]
        part = part_ref[:, cols]
        for start in starts:
            if start + taps == tokens:
                out = dot(ahead_ref[g, :, :taps], mix[start:])
            else:
                out = dot(ahead_ref[g], mix[start : start + 2 * taps])
            grad_ref[start : start + taps, cols] = out.astype(bf16)
        mixes = jnp.concatenate([mix[s : s + taps] for s in starts], axis=1)
        parts = jnp.concatenate([part[s : s + taps] for s in starts], axis=1)
        same = dot(parts, mixes, ((1,), (1,)))
        later = dot(parts[:, :-width], mixes[:, width:], ((1,), (1,)))
        pairs = jnp.where(col >= row, same, later)
        folded = pairs[0:8]
        for a in range(8, taps, 8):
            folded = folded + pltpu.roll(pairs[a : a + 8], taps - a, 1)
        line = folded[0:1]
        for b in range(1, 8):
            line = line + pltpu.roll(folded[b : b + 1], taps - b, 1)
        taps_ref[0, g : g + 1, :] = line
    product = dot(grad_ref[...], weight_ref[...], ((1,), (1,)))
    step = pl.program_id(0)

    @pl.when(step == 0)
    def _():
        total[...] = product

    @pl.when(step > 0)
    def _():
        total[...] += product

    @pl.when(step == pl.num_programs(0) - 1)
    def _():
        back_ref[...] = total[...].astype(bf16)


def back(mixes, part, weight, ahead, after=()):
    blocks = (len(mixes) + 1) // 2
    rows = mixes[0].shape[0]
    tokens, width = part.shape
    depth = weight.shape[0]
    groups, taps, _ = ahead.shape
    step = 4
    tile = width // groups * step
    spec = pl.BlockSpec((tokens, tile), lambda i: (0, i))
    return call(
        functools.partial(back_kernel, blocks),
        (*mixes, part, weight, ahead),
        after,
        grid=(groups // step,),
        in_specs=[pl.BlockSpec((rows, tile), lambda i: (0, i))] * len(mixes)
        + [
            spec,
            pl.BlockSpec((depth, tile), lambda i: (0, i)),
            pl.BlockSpec((step, taps, 2 * taps), lambda i: (i, 0, 0)),
        ],
        out_specs=[
            spec,
            pl.BlockSpec((1, step, taps), lambda i: (i, 0, 0)),
            pl.BlockSpec((tokens, depth), lambda i: (0, 0)),
        ],
        out_shape=[
            shape((tokens, width), bf16),
            shape((groups // step, step, taps), f32),
            shape((tokens, depth), bf16),
        ],
        scratch_shapes=[pltpu.VMEM((tokens, tile), bf16), pltpu.VMEM((tokens, depth), f32)],
        name="back",
    )


def weight_kernel(down_x, up_x, down_g, up_g, out_ref, down_t, up_t):
    @pl.when(pl.program_id(0) == 0)
    def _():
        down_t[...] = down_x[...].T
        up_t[...] = up_x[...].T

    out_ref[...] = (dot(down_t[...], down_g[...]) + dot(up_t[...], up_g[...])).astype(bf16)


def weight_gradient(down_x, up_x, down_g, up_g, after=()):
    tokens, depth = down_x.shape
    width = down_g.shape[1]
    tile = width // 8
    whole = pl.BlockSpec((tokens, depth), lambda i: (0, 0))
    part = pl.BlockSpec((tokens, tile), lambda i: (0, i))
    return call(
        weight_kernel,
        (down_x, up_x, down_g, up_g),
        after,
        grid=(width // tile,),
        in_specs=[whole, whole, part, part],
        out_specs=pl.BlockSpec((depth, tile), lambda i: (0, i)),
        out_shape=shape((depth, width), bf16),
        scratch_shapes=[pltpu.VMEM((depth, tokens), bf16)] * 2,
        name="weight_gradient",
    )


def finish_kernel(xin_ref, cot_ref, back_ref, *rest):
    *mixed_refs, out_ref = rest
    normed, inverse = normalise(xin_ref[...].astype(f32))
    cot = cot_ref[...].astype(f32)
    returned = jnp.concatenate([back_ref[i] for i in range(back_ref.shape[0])], axis=1)
    mixed = sum(ref[...].astype(f32) for ref in mixed_refs)
    total = cot * mixed + returned.astype(f32)
    mean = jnp.mean(total * normed, axis=1, keepdims=True)
    out_ref[0] = (cot + inverse * (total - normed * mean)).astype(bf16)


def finish(xin, cot, mixed, returned, after=()):
    rows, width = xin.shape
    blocks, _, depth = returned.shape
    step = 32
    spec = pl.BlockSpec((step, width), lambda i: (i, 0))
    return call(
        finish_kernel,
        (xin, cot, returned, *mixed),
        after,
        grid=(rows // step,),
        in_specs=[spec, spec, pl.BlockSpec((blocks, step, depth), lambda i: (0, i, 0))]
        + [spec] * len(mixed),
        out_specs=pl.BlockSpec((1, step, width), lambda i: (0, i, 0)),
        out_shape=shape((1, rows, width), bf16),
        name="finish",
    )


def exchange(x):
    blocks = lax.axis_size("tensor")
    x = x.reshape(blocks, -1, x.shape[-1])
    return lax.all_to_all(x, "tensor", split_axis=0, concat_axis=0, tiled=True)


def both_ways(right, left):
    blocks = lax.axis_size("tensor")
    onward = [(i, i + 1) for i in range(blocks - 1)]
    return (
        lax.ppermute(right, "tensor", onward),
        lax.ppermute(left, "tensor", [(j, i) for i, j in onward]),
    )


def payload_kernel(s, right_ref, left_ref, right_piece, left_piece, right_out, left_out):
    mine = lax.axis_index("tensor")
    blocks = lax.axis_size("tensor")

    def put(came, piece, out, adds):
        @pl.when(adds)
        def _():
            out[...] = (came[...].astype(f32) + piece[...].astype(f32)).astype(bf16)

        @pl.when(jnp.logical_not(adds))
        def _():
            out[...] = came[...]

    put(right_ref, right_piece, right_out, mine < s - 1)
    put(left_ref, left_piece, left_out, mine > blocks - s)


def payload(s, arrived, pieces, after=()):
    blocks = len(pieces)
    rows, width = pieces[0].shape
    step = 32
    spec = pl.BlockSpec((step, width), lambda i: (i, 0))
    return call(
        functools.partial(payload_kernel, s),
        (*arrived, pieces[blocks + 1 - s], pieces[s - 1]),
        after,
        grid=(rows // step,),
        in_specs=[spec] * 4,
        out_specs=[spec] * 2,
        out_shape=[shape((rows, width), bf16)] * 2,
        name="payload",
    )


def sort_arrivals(mix, pieces, arrivals):
    rights, lefts = zip(*arrivals)
    return [mix, *rights[:-1], *lefts[:-1]], [pieces[0], rights[-1], lefts[-1]]


def per_device(weights, filters, down_input, down_cot, up_input, up_cot):
    sections = lax.axis_size("section")
    mirror = [(s, sections - 1 - s) for s in range(sections)]
    down_pairs = [(s + 1, s) for s in range(sections - 1)]
    up_pairs = [(sections - s, s) for s in range(1, sections)]
    weight = weights[0]
    down_xin, down_cot = down_input[0], down_cot[0]
    up_xin = lax.ppermute(up_input[0], "section", mirror)
    up_cot = lax.ppermute(up_cot[0], "section", mirror)
    blocks = lax.axis_size("tensor")
    depth = weight.shape[0]
    down_x = exchange(normed_blocks(down_xin)).reshape(-1, depth)
    down_mix = grad_mix(down_xin, down_cot)
    down_arrivals = [both_ways(down_mix, down_mix)]
    causal, ahead = toeplitz(filters[0])
    up_normed = normed_blocks(up_xin)
    up_x = exchange(up_normed).reshape(-1, depth)
    up_mix = grad_mix(up_xin, up_cot, after=down_arrivals[0])
    up_arrivals = [both_ways(up_mix, up_mix)]
    down_part, down_pieces = project(down_x, weight, causal, after=(up_normed, up_mix))
    last = down_part
    for s in range(2, blocks + 1):
        sent = payload(s, down_arrivals[-1], down_pieces, after=(last,))
        down_arrivals.append(both_ways(*sent))
        if s == 2:
            up_part, up_pieces = project(up_x, weight, causal, after=sent)
        if s == blocks:
            down_mixes, down_conv = sort_arrivals(down_mix, down_pieces, down_arrivals)
            down_g, down_taps, down_back = back(down_mixes, down_part, weight, ahead, after=sent)
            sent = (down_g,)
            down_back = exchange(down_back)
        sent = payload(s, up_arrivals[-1], up_pieces, after=sent[:1])
        up_arrivals.append(both_ways(*sent))
        last = sent[0]
    up_mixes, up_conv = sort_arrivals(up_mix, up_pieces, up_arrivals)
    up_g, up_taps, up_back = back(up_mixes, up_part, weight, ahead, after=(last,))
    up_back = exchange(up_back)
    weight_grad = weight_gradient(down_x, up_x, down_g, up_g)
    taps = (down_taps + up_taps).reshape(filters.shape)
    taps = jnp.sum(lax.all_gather(taps, "tensor", axis=0, tiled=True), axis=0, keepdims=True)
    down_grad = finish(down_xin, down_cot, down_conv, down_back, after=(up_g,))
    down_passed = lax.ppermute(down_grad, "section", down_pairs)
    up_grad = finish(up_xin, up_cot, up_conv, up_back, after=(weight_grad, taps))
    up_passed = lax.ppermute(up_grad, "section", up_pairs)
    return weight_grad[None], taps, down_passed, up_passed


def solution(mesh):
    rows = P("section", "tensor", None)
    whole = P("section", None, None)
    return jax.shard_map(
        per_device,
        mesh=mesh,
        in_specs=(rows, whole, rows, rows, rows, rows),
        out_specs=(rows, whole, rows, rows),
        check_vma=False,
    )
```

profile of v0, /device:TPU:10, one launch (start us, length us, event | category | flops | bytes accessed | tf_op | source)
XLA Modules:
  0.0 387.7 jit_solution(6221829764702751843)
XLA Ops:
  4.3 5.3 %all-to-all-start = ((bf16[4,128,1024]{2,1,0:T(8,128)(2,1)}), bf16[4,128,1024]{2,1,0:T(8,128)(2,1)}, u32[]{:S(2)}, u32[]{:S(2)}) async-start(bf16[4,128,1024]{2,1,0:T(8,128)(2,1)} %normed_blocks.2), calls=%async_computation | async-start | bytes 2097152 | tf_op jit(solution)/shard_map/all_to_all | solution.py:326
  10.0 3.9 %grad_mix.2.refs_0_ = bf16[128,4096]{1,0:T(8,128)(2,1)} custom-call(bf16[128,4096]{1,0:T(8,128)(2,1)} %bitcast.19, bf16[128,4096]{1,0:T(8,128)(2,1)} %bitcast.21), custom_call_target="tpu_custom_call" | custom-call | tf_op jit(solution)/shard_map/grad_mix/pallas_call | solution.py:30
  21.5 14.7 %collective-permute-done.refs_0_ = bf16[128,4096]{1,0:T(8,128)(2,1)} collective-permute-done((bf16[128,4096]{1,0:T(8,128)(2,1)}, bf16[128,4096]{1,0:T(8,128)(2,1)}, u32[]{:S(2)}, u32[]{:S(2)}) %collective-permute-start) | collective-permute-done | bytes 1048608 | tf_op jit(solution)/shard_map/ppermute | solution.py:384
  39.9 5.1 %all-to-all-start.1 = ((bf16[4,128,1024]{2,1,0:T(8,128)(2,1)}), bf16[4,128,1024]{2,1,0:T(8,128)(2,1)}, u32[]{:S(2)}, u32[]{:S(2)}) async-start(bf16[4,128,1024]{2,1,0:T(8,128)(2,1)} %normed_blocks.3.refs_3_), calls=%async_computation.1 | async-start | bytes 2097152 | tf_op jit(solution)/shard_map/all_to_all | solution.py:326
  48.7 15.9 %collective-permute-done.2.refs_3_.refs_1_.refs_4_ = bf16[128,4096]{1,0:T(8,128)(2,1)} collective-permute-done((bf16[128,4096]{1,0:T(8,128)(2,1)}, bf16[128,4096]{1,0:T(8,128)(2,1)}, u32[]{:S(2)}, u32[]{:S(2)}) %collective-permute-start.2) | collective-permute-done | bytes 1048608 | tf_op jit(solution)/shard_map/ppermute | solution.py:334
  73.1 4.4 %collective-permute-start.6 = (bf16[128,4096]{1,0:T(8,128)(2,1)}, bf16[128,4096]{1,0:T(8,128)(2,1)}, u32[]{:S(2)}, u32[]{:S(2)}) collective-permute-start(bf16[128,4096]{1,0:T(8,128)(2,1)} %grad_mix.3.refs_4_.refs_0_), channel_id=1, source_target_pairs={{0,1},{1,2},{2,3},{4,5},{5,6},{6,7},{8,9},{9,10},{10,11},{12,13},{... | collective-permute-start | bytes 3145736 | tf_op jit(solution)/shard_map/ppermute | solution.py:333
  77.5 12.6 %project.2 = (bf16[512,4096]{1,0:T(8,128)(2,1)}, bf16[128,4096]{1,0:T(8,128)(2,1)}, bf16[128,4096]{1,0:T(8,128)(2,1)}, bf16[128,4096]{1,0:T(8,128)(2,1)}, bf16[128,4096]{1,0:T(8,128)(2,1)}) custom-call(bf16[512,1024]{1,0:T(8,128)(2,1)} %bitcast.1.refs_0_, bf16[1024,4096]{1,0:T(8,128)(2,1)} %bitcast.13, bf16[32,128,256]{2,1,0:T(8,128)(2,1)} %get-tuple-element.34.refs_2_, ...), custom_call_target="tpu_custom_call" | custom-call | tf_op jit(solution)/shard_map/project/pallas_call | solution.py:30
  90.0 4.1 %payload.6 = (bf16[128,4096]{1,0:T(8,128)(2,1)}, bf16[128,4096]{1,0:T(8,128)(2,1)}) custom-call(bf16[128,4096]{1,0:T(8,128)(2,1)} %collective-permute-done.1.refs_2_.refs_0_.refs_1_, bf16[128,4096]{1,0:T(8,128)(2,1)} %collective-permute-done.2.refs_3_.refs_1_.refs_4_, bf16[128,4096]{1,0:T(8,128)(2,1)} %get-tuple-element.35.refs_2_.refs_3_, ...), custom_call_target="tpu_custom_call" | custom-call | tf_op jit(solution)/shard_map/payload/pallas_call | solution.py:30
  96.6 4.4 %collective-permute-start.4 = (bf16[128,4096]{1,0:T(8,128)(2,1)}, bf16[128,4096]{1,0:T(8,128)(2,1)}, u32[]{:S(2)}, u32[]{:S(2)}) collective-permute-start(bf16[128,4096]{1,0:T(8,128)(2,1)} %get-tuple-element.38.refs_3_.refs_4_), channel_id=1, source_target_pairs={{0,1},{1,2},{2,3},{4,5},{5,6},{6,7},{8,9},{9,10},{10,11},{12,13},{... | collective-permute-start | bytes 3145736 | tf_op jit(solution)/shard_map/ppermute | solution.py:333
  101.0 12.5 %project.3 = (bf16[512,4096]{1,0:T(8,128)(2,1)}, bf16[128,4096]{1,0:T(8,128)(2,1)}, bf16[128,4096]{1,0:T(8,128)(2,1)}, bf16[128,4096]{1,0:T(8,128)(2,1)}, bf16[128,4096]{1,0:T(8,128)(2,1)}) custom-call(bf16[512,1024]{1,0:T(8,128)(2,1)} %bitcast.3.refs_0_.refs_1_, bf16[1024,4096]{1,0:T(8,128)(2,1)} %bitcast.14, ...), custom_call_target="tpu_custom_call" | custom-call | tf_op jit(solution)/shard_map/project/pallas_call | solution.py:30
  113.6 4.2 %payload.7 = (bf16[128,4096]{1,0:T(8,128)(2,1)}, bf16[128,4096]{1,0:T(8,128)(2,1)}) custom-call(bf16[128,4096]{1,0:T(8,128)(2,1)} %collective-permute-done.6.refs_0_.refs_1_, bf16[128,4096]{1,0:T(8,128)(2,1)} %collective-permute-done.7.refs_1_.refs_4_, bf16[128,4096]{1,0:T(8,128)(2,1)} %get-tuple-element.41.refs_2_.refs_3_, ...), custom_call_target="tpu_custom_call" | custom-call | tf_op jit(solution)/shard_map/payload/pallas_call | solution.py:30
  120.3 4.3 %collective-permute-start.10 = (bf16[128,4096]{1,0:T(8,128)(2,1)}, bf16[128,4096]{1,0:T(8,128)(2,1)}, u32[]{:S(2)}, u32[]{:S(2)}) collective-permute-start(bf16[128,4096]{1,0:T(8,128)(2,1)} %get-tuple-element.43.refs_4_), channel_id=1, source_target_pairs={{0,1},{1,2},{2,3},{4,5},{5,6},{6,7},{8,9},{9,10},{10,11},{12,13},{... | collective-permute-start | bytes 3145736 | tf_op jit(solution)/shard_map/ppermute | solution.py:333
  125.0 4.4 %payload.8 = (bf16[128,4096]{1,0:T(8,128)(2,1)}, bf16[128,4096]{1,0:T(8,128)(2,1)}) custom-call(bf16[128,4096]{1,0:T(8,128)(2,1)} %collective-permute-done.4.refs_0_.refs_2_, bf16[128,4096]{1,0:T(8,128)(2,1)} %collective-permute-done.5.refs_1_.refs_5_, bf16[128,4096]{1,0:T(8,128)(2,1)} %get-tuple-element.40.refs_2_.refs_3_, ...), custom_call_target="tpu_custom_call" | custom-call | tf_op jit(solution)/shard_map/payload/pallas_call | solution.py:30
  131.5 4.3 %collective-permute-start.8 = (bf16[128,4096]{1,0:T(8,128)(2,1)}, bf16[128,4096]{1,0:T(8,128)(2,1)}, u32[]{:S(2)}, u32[]{:S(2)}) collective-permute-start(bf16[128,4096]{1,0:T(8,128)(2,1)} %get-tuple-element.44.refs_4_), channel_id=1, source_target_pairs={{0,1},{1,2},{2,3},{4,5},{5,6},{6,7},{8,9},{9,10},{10,11},{12,13},{... | collective-permute-start | bytes 3145736 | tf_op jit(solution)/shard_map/ppermute | solution.py:333
  135.8 11.6 %collective-permute-done.11.refs_1_.refs_5_ = bf16[128,4096]{1,0:T(8,128)(2,1)} collective-permute-done((bf16[128,4096]{1,0:T(8,128)(2,1)}, bf16[128,4096]{1,0:T(8,128)(2,1)}, u32[]{:S(2)}, u32[]{:S(2)}) %collective-permute-start.11) | collective-permute-done | bytes 1048608 | tf_op jit(solution)/shard_map/ppermute | solution.py:334
  148.5 4.5 %payload.9 = (bf16[128,4096]{1,0:T(8,128)(2,1)}, bf16[128,4096]{1,0:T(8,128)(2,1)}) custom-call(bf16[128,4096]{1,0:T(8,128)(2,1)} %collective-permute-done.10.refs_0_.refs_2_, bf16[128,4096]{1,0:T(8,128)(2,1)} %collective-permute-done.11.refs_1_.refs_5_, bf16[128,4096]{1,0:T(8,128)(2,1)} %get-tuple-element.48.refs_2_.refs_3_, ...), custom_call_target="tpu_custom_call" | custom-call | tf_op jit(solution)/shard_map/payload/pallas_call | solution.py:30
  153.1 15.8 %collective-permute-done.9.refs_1_.refs_6_ = bf16[128,4096]{1,0:T(8,128)(2,1)} collective-permute-done((bf16[128,4096]{1,0:T(8,128)(2,1)}, bf16[128,4096]{1,0:T(8,128)(2,1)}, u32[]{:S(2)}, u32[]{:S(2)}) %collective-permute-start.9) | collective-permute-done | bytes 1048608 | tf_op jit(solution)/shard_map/ppermute | solution.py:334
  168.9 4.3 %payload.10 = (bf16[128,4096]{1,0:T(8,128)(2,1)}, bf16[128,4096]{1,0:T(8,128)(2,1)}) custom-call(bf16[128,4096]{1,0:T(8,128)(2,1)} %collective-permute-done.8.refs_0_.refs_3_, bf16[128,4096]{1,0:T(8,128)(2,1)} %collective-permute-done.9.refs_1_.refs_6_, bf16[128,4096]{1,0:T(8,128)(2,1)} %get-tuple-element.36.refs_3_.refs_2_, ...), custom_call_target="tpu_custom_call" | custom-call | tf_op jit(solution)/shard_map/payload/pallas_call | solution.py:30
  173.2 16.8 %back.2 = (bf16[512,4096]{1,0:T(8,128)(2,1)}, f32[8,4,128]{2,1,0:T(4,128)}, bf16[512,1024]{1,0:T(8,128)(2,1)}) custom-call(bf16[128,4096]{1,0:T(8,128)(2,1)} %grad_mix.2.refs_0_, bf16[128,4096]{1,0:T(8,128)(2,1)} %collective-permute-done.1.refs_2_.refs_0_.refs_1_, bf16[128,4096]{1,0:T(8,128)(2,1)} %collective-permute-done.4.refs_0_.refs_2_, ...), custom_call_target="tpu_custom_call" | custom-call | tf_op jit(solution)/shard_map/back/pallas_call | solution.py:30
  190.1 4.2 %all-to-all-start.2 = ((bf16[4,128,1024]{2,1,0:T(8,128)(2,1)}), bf16[4,128,1024]{2,1,0:T(8,128)(2,1)}, u32[]{:S(2)}, u32[]{:S(2)}) async-start(bf16[4,128,1024]{2,1,0:T(8,128)(2,1)} %bitcast.24), calls=%async_computation.2 | async-start | bytes 2097152 | tf_op jit(solution)/shard_map/all_to_all | solution.py:326
  196.2 3.9 %collective-permute-start.12 = (bf16[128,4096]{1,0:T(8,128)(2,1)}, bf16[128,4096]{1,0:T(8,128)(2,1)}, u32[]{:S(2)}, u32[]{:S(2)}) collective-permute-start(bf16[128,4096]{1,0:T(8,128)(2,1)} %get-tuple-element.49.refs_4_), channel_id=1, source_target_pairs={{0,1},{1,2},{2,3},{4,5},{5,6},{6,7},{8,9},{9,10},{10,11},{12,13},{... | collective-permute-start | bytes 3145736 | tf_op jit(solution)/shard_map/ppermute | solution.py:333
  200.2 39.3 %collective-permute-done.13.refs_1_.refs_6_ = bf16[128,4096]{1,0:T(8,128)(2,1)} collective-permute-done((bf16[128,4096]{1,0:T(8,128)(2,1)}, bf16[128,4096]{1,0:T(8,128)(2,1)}, u32[]{:S(2)}, u32[]{:S(2)}) %collective-permute-start.13) | collective-permute-done | bytes 1048608 | tf_op jit(solution)/shard_map/ppermute | solution.py:334
  239.5 4.3 %payload.11 = (bf16[128,4096]{1,0:T(8,128)(2,1)}, bf16[128,4096]{1,0:T(8,128)(2,1)}) custom-call(bf16[128,4096]{1,0:T(8,128)(2,1)} %collective-permute-done.12.refs_0_.refs_3_, bf16[128,4096]{1,0:T(8,128)(2,1)} %collective-permute-done.13.refs_1_.refs_6_, bf16[128,4096]{1,0:T(8,128)(2,1)} %get-tuple-element.42.refs_3_.refs_2_, ...), custom_call_target="tpu_custom_call" | custom-call | tf_op jit(solution)/shard_map/payload/pallas_call | solution.py:30
  243.8 16.9 %back.3 = (bf16[512,4096]{1,0:T(8,128)(2,1)}, f32[8,4,128]{2,1,0:T(4,128)}, bf16[512,1024]{1,0:T(8,128)(2,1)}) custom-call(bf16[128,4096]{1,0:T(8,128)(2,1)} %grad_mix.3.refs_4_.refs_0_, bf16[128,4096]{1,0:T(8,128)(2,1)} %collective-permute-done.6.refs_0_.refs_1_, bf16[128,4096]{1,0:T(8,128)(2,1)} %collective-permute-done.10.refs_0_.refs_2_, ...), custom_call_target="tpu_custom_call" | custom-call | tf_op jit(solution)/shard_map/back/pallas_call | solution.py:30
  260.7 4.8 %all-to-all-start.3 = ((bf16[4,128,1024]{2,1,0:T(8,128)(2,1)}), bf16[4,128,1024]{2,1,0:T(8,128)(2,1)}, u32[]{:S(2)}, u32[]{:S(2)}) async-start(bf16[4,128,1024]{2,1,0:T(8,128)(2,1)} %bitcast.23), calls=%async_computation.3 | async-start | bytes 2097152 | tf_op jit(solution)/shard_map/all_to_all | solution.py:326
  274.2 3.9 %collective-permute-start.17 = (bf16[128,4096]{1,0:T(8,128)(2,1)}, bf16[128,4096]{1,0:T(8,128)(2,1)}, u32[]{:S(2)}, u32[]{:S(2)}) collective-permute-start(bf16[128,4096]{1,0:T(8,128)(2,1)} %get-tuple-element.55.refs_10_), channel_id=1, source_target_pairs={{0,1},{1,2},{2,3},{4,5},{5,6},{6,7},{8,9},{9,10},{10,11},{12,13},{... | collective-permute-start | bytes 3145736 | tf_op jit(solution)/shard_map/ppermute | solution.py:333
  278.2 14.7 %weight_gradient.1.refs_6_ = bf16[1024,4096]{1,0:T(8,128)(2,1)} custom-call(bf16[512,1024]{1,0:T(8,128)(2,1)} %bitcast.1.refs_0_, bf16[512,1024]{1,0:T(8,128)(2,1)} %bitcast.3.refs_0_.refs_1_, bf16[512,4096]{1,0:T(8,128)(2,1)} %get-tuple-element.52.refs_4_.refs_2_, bf16[512,4096]{1,0:T(8,128)(2,1)} %get-tuple-element.56.refs_3_.refs_6_), custom_call_target="tpu_custom_call" | custom-call | tf_op jit(solution)/shard_map/weight_gradient/pallas_call | solution.py:30
  292.9 46.9 %all_gather.3 = f32[4,32,128]{2,1,0:T(8,128)S(1)} all-gather(f32[1,32,128]{2,1,0:T(8,128)S(1)} %bitcast.27), channel_id=1, replica_groups=mesh['section'=8,'tensor'=4] {'tensor'}, dimensions={0}, use_global_device_ids=true | all-gather | bytes 81920 | tf_op jit(solution)/shard_map/all_gather | solution.py:416
  340.4 5.2 %finish.2 = bf16[1,128,4096]{2,1,0:T(8,128)(2,1)} custom-call(bf16[128,4096]{1,0:T(8,128)(2,1)} %bitcast.20, bf16[128,4096]{1,0:T(8,128)(2,1)} %bitcast.22, bf16[4,128,1024]{2,1,0:T(8,128)(2,1)} %all-to-all-done.2.refs_2_, bf16[128,4096]{1,0:T(8,128)(2,1)} %get-tuple-element.60.refs_3_, bf16[128,4096]{1,0:T(8,128)(2,1)} %collective-permute-done.14.refs_4_, ...), custom_call_target="tpu_custom_call" | custom-call | tf_op jit(solution)/shard_map/finish/pallas_call | solution.py:30
  347.5 5.2 %finish.3 = bf16[1,128,4096]{2,1,0:T(8,128)(2,1)} custom-call(bf16[128,4096]{1,0:T(8,128)(2,1)} %collective-permute-done.refs_0_, bf16[128,4096]{1,0:T(8,128)(2,1)} %collective-permute-done.3.refs_1_, bf16[4,128,1024]{2,1,0:T(8,128)(2,1)} %all-to-all-done.3.refs_2_, bf16[128,4096]{1,0:T(8,128)(2,1)} %get-tuple-element.62.refs_3_, ...), custom_call_target="tpu_custom_call" | custom-call | tf_op jit(solution)/shard_map/finish/pallas_call | solution.py:30
  356.1 7.1 %collective-permute-done.16 = bf16[1,128,4096]{2,1,0:T(8,128)(2,1)} collective-permute-done((bf16[1,128,4096]{2,1,0:T(8,128)(2,1)}, bf16[1,128,4096]{2,1,0:T(8,128)(2,1)}, u32[]{:S(2)}, u32[]{:S(2)}) %collective-permute-start.16) | collective-permute-done | bytes 1048608 | tf_op jit(solution)/shard_map/ppermute | solution.py:418
  363.2 21.2 %collective-permute-done.19 = bf16[1,128,4096]{2,1,0:T(8,128)(2,1)S(1)} collective-permute-done((bf16[1,128,4096]{2,1,0:T(8,128)(2,1)}, bf16[1,128,4096]{2,1,0:T(8,128)(2,1)S(1)}, u32[]{:S(2)}, u32[]{:S(2)}) %collective-permute-start.19) | collective-permute-done | bytes 1048608 | tf_op jit(solution)/shard_map/ppermute | solution.py:420
  (43 shorter events, 55.9 us)
Async XLA Ops:
  4.3 35.6 %all-to-all-start = ((bf16[4,128,1024]{2,1,0:T(8,128)(2,1)}), bf16[4,128,1024]{2,1,0:T(8,128)(2,1)}, u32[]{:S(2)}, u32[]{:S(2)}) async-start(bf16[4,128,1024]{2,1,0:T(8,128)(2,1)} %normed_blocks.2), calls=%async_computation | async-start | bytes 2097152 | tf_op jit(solution)/shard_map/all_to_all | solution.py:326
  9.6 26.6 %collective-permute-start = (bf16[128,4096]{1,0:T(8,128)(2,1)}, bf16[128,4096]{1,0:T(8,128)(2,1)}, u32[]{:S(2)}, u32[]{:S(2)}) collective-permute-start(bf16[128,4096]{1,0:T(8,128)(2,1)} %bitcast.29), channel_id=1, source_target_pairs={{0,28},{4,24},{8,20},{12,16},{16,12},{20,8},{24,4},{28,0},{1,29},{... | collective-permute-start | bytes 3145736 | tf_op jit(solution)/shard_map/ppermute | solution.py:384
  13.9 50.7 %collective-permute-start.2 = (bf16[128,4096]{1,0:T(8,128)(2,1)}, bf16[128,4096]{1,0:T(8,128)(2,1)}, u32[]{:S(2)}, u32[]{:S(2)}) collective-permute-start(bf16[128,4096]{1,0:T(8,128)(2,1)} %grad_mix.2.refs_0_), channel_id=1, source_target_pairs={{1,0},{2,1},{3,2},{5,4},{6,5},{7,6},{9,8},{10,9},{11,10},{13,12},{... | collective-permute-start | bytes 3145736 | tf_op jit(solution)/shard_map/ppermute | solution.py:334
  16.0 51.2 %collective-permute-start.1 = (bf16[128,4096]{1,0:T(8,128)(2,1)}, bf16[128,4096]{1,0:T(8,128)(2,1)}, u32[]{:S(2)}, u32[]{:S(2)}) collective-permute-start(bf16[128,4096]{1,0:T(8,128)(2,1)} %grad_mix.2.refs_0_), channel_id=1, source_target_pairs={{0,1},{1,2},{2,3},{4,5},{5,6},{6,7},{8,9},{9,10},{10,11},{12,13},{... | collective-permute-start | bytes 3145736 | tf_op jit(solution)/shard_map/ppermute | solution.py:333
  19.7 47.6 %collective-permute-start.3 = (bf16[128,4096]{1,0:T(8,128)(2,1)}, bf16[128,4096]{1,0:T(8,128)(2,1)}, u32[]{:S(2)}, u32[]{:S(2)}) collective-permute-start(bf16[128,4096]{1,0:T(8,128)(2,1)} %bitcast.30), channel_id=1, source_target_pairs={{0,28},{4,24},{8,20},{12,16},{16,12},{20,8},{24,4},{28,0},{1,29},{... | collective-permute-start | bytes 3145736 | tf_op jit(solution)/shard_map/ppermute | solution.py:385
  39.9 61.2 %all-to-all-start.1 = ((bf16[4,128,1024]{2,1,0:T(8,128)(2,1)}), bf16[4,128,1024]{2,1,0:T(8,128)(2,1)}, u32[]{:S(2)}, u32[]{:S(2)}) async-start(bf16[4,128,1024]{2,1,0:T(8,128)(2,1)} %normed_blocks.3.refs_3_), calls=%async_computation.1 | async-start | bytes 2097152 | tf_op jit(solution)/shard_map/all_to_all | solution.py:326
  71.1 42.4 %collective-permute-start.7 = (bf16[128,4096]{1,0:T(8,128)(2,1)}, bf16[128,4096]{1,0:T(8,128)(2,1)}, u32[]{:S(2)}, u32[]{:S(2)}) collective-permute-start(bf16[128,4096]{1,0:T(8,128)(2,1)} %grad_mix.3.refs_4_.refs_0_), channel_id=1, source_target_pairs={{1,0},{2,1},{3,2},{5,4},{6,5},{7,6},{9,8},{10,9},{11,10},{13,12},{... | collective-permute-start | bytes 3145736 | tf_op jit(solution)/shard_map/ppermute | solution.py:334
  73.1 40.5 %collective-permute-start.6 = (bf16[128,4096]{1,0:T(8,128)(2,1)}, bf16[128,4096]{1,0:T(8,128)(2,1)}, u32[]{:S(2)}, u32[]{:S(2)}) collective-permute-start(bf16[128,4096]{1,0:T(8,128)(2,1)} %grad_mix.3.refs_4_.refs_0_), channel_id=1, source_target_pairs={{0,1},{1,2},{2,3},{4,5},{5,6},{6,7},{8,9},{9,10},{10,11},{12,13},{... | collective-permute-start | bytes 3145736 | tf_op jit(solution)/shard_map/ppermute | solution.py:333
  94.2 30.8 %collective-permute-start.5 = (bf16[128,4096]{1,0:T(8,128)(2,1)}, bf16[128,4096]{1,0:T(8,128)(2,1)}, u32[]{:S(2)}, u32[]{:S(2)}) collective-permute-start(bf16[128,4096]{1,0:T(8,128)(2,1)} %get-tuple-element.39.refs_4_), channel_id=1, source_target_pairs={{1,0},{2,1},{3,2},{5,4},{6,5},{7,6},{9,8},{10,9},{11,10},{13,12},{... | collective-permute-start | bytes 3145736 | tf_op jit(solution)/shard_map/ppermute | solution.py:334
  96.6 28.3 %collective-permute-start.4 = (bf16[128,4096]{1,0:T(8,128)(2,1)}, bf16[128,4096]{1,0:T(8,128)(2,1)}, u32[]{:S(2)}, u32[]{:S(2)}) collective-permute-start(bf16[128,4096]{1,0:T(8,128)(2,1)} %get-tuple-element.38.refs_3_.refs_4_), channel_id=1, source_target_pairs={{0,1},{1,2},{2,3},{4,5},{5,6},{6,7},{8,9},{9,10},{10,11},{12,13},{... | collective-permute-start | bytes 3145736 | tf_op jit(solution)/shard_map/ppermute | solution.py:333
  117.8 29.7 %collective-permute-start.11 = (bf16[128,4096]{1,0:T(8,128)(2,1)}, bf16[128,4096]{1,0:T(8,128)(2,1)}, u32[]{:S(2)}, u32[]{:S(2)}) collective-permute-start(bf16[128,4096]{1,0:T(8,128)(2,1)} %get-tuple-element.47), channel_id=1, source_target_pairs={{1,0},{2,1},{3,2},{5,4},{6,5},{7,6},{9,8},{10,9},{11,10},{13,12},{... | collective-permute-start | bytes 3145736 | tf_op jit(solution)/shard_map/ppermute | solution.py:334
  120.3 28.3 %collective-permute-start.10 = (bf16[128,4096]{1,0:T(8,128)(2,1)}, bf16[128,4096]{1,0:T(8,128)(2,1)}, u32[]{:S(2)}, u32[]{:S(2)}) collective-permute-start(bf16[128,4096]{1,0:T(8,128)(2,1)} %get-tuple-element.43.refs_4_), channel_id=1, source_target_pairs={{0,1},{1,2},{2,3},{4,5},{5,6},{6,7},{8,9},{9,10},{10,11},{12,13},{... | collective-permute-start | bytes 3145736 | tf_op jit(solution)/shard_map/ppermute | solution.py:333
  129.4 39.5 %collective-permute-start.9 = (bf16[128,4096]{1,0:T(8,128)(2,1)}, bf16[128,4096]{1,0:T(8,128)(2,1)}, u32[]{:S(2)}, u32[]{:S(2)}) collective-permute-start(bf16[128,4096]{1,0:T(8,128)(2,1)} %get-tuple-element.45), channel_id=1, source_target_pairs={{1,0},{2,1},{3,2},{5,4},{6,5},{7,6},{9,8},{10,9},{11,10},{13,12},{... | collective-permute-start | bytes 3145736 | tf_op jit(solution)/shard_map/ppermute | solution.py:334
  131.5 37.4 %collective-permute-start.8 = (bf16[128,4096]{1,0:T(8,128)(2,1)}, bf16[128,4096]{1,0:T(8,128)(2,1)}, u32[]{:S(2)}, u32[]{:S(2)}) collective-permute-start(bf16[128,4096]{1,0:T(8,128)(2,1)} %get-tuple-element.44.refs_4_), channel_id=1, source_target_pairs={{0,1},{1,2},{2,3},{4,5},{5,6},{6,7},{8,9},{9,10},{10,11},{12,13},{... | collective-permute-start | bytes 3145736 | tf_op jit(solution)/shard_map/ppermute | solution.py:333
  190.1 70.6 %all-to-all-start.2 = ((bf16[4,128,1024]{2,1,0:T(8,128)(2,1)}), bf16[4,128,1024]{2,1,0:T(8,128)(2,1)}, u32[]{:S(2)}, u32[]{:S(2)}) async-start(bf16[4,128,1024]{2,1,0:T(8,128)(2,1)} %bitcast.24), calls=%async_computation.2 | async-start | bytes 2097152 | tf_op jit(solution)/shard_map/all_to_all | solution.py:326
  194.3 45.2 %collective-permute-start.13 = (bf16[128,4096]{1,0:T(8,128)(2,1)}, bf16[128,4096]{1,0:T(8,128)(2,1)}, u32[]{:S(2)}, u32[]{:S(2)}) collective-permute-start(bf16[128,4096]{1,0:T(8,128)(2,1)} %get-tuple-element.53), channel_id=1, source_target_pairs={{1,0},{2,1},{3,2},{5,4},{6,5},{7,6},{9,8},{10,9},{11,10},{13,12},{... | collective-permute-start | bytes 3145736 | tf_op jit(solution)/shard_map/ppermute | solution.py:334
  196.2 43.2 %collective-permute-start.12 = (bf16[128,4096]{1,0:T(8,128)(2,1)}, bf16[128,4096]{1,0:T(8,128)(2,1)}, u32[]{:S(2)}, u32[]{:S(2)}) collective-permute-start(bf16[128,4096]{1,0:T(8,128)(2,1)} %get-tuple-element.49.refs_4_), channel_id=1, source_target_pairs={{0,1},{1,2},{2,3},{4,5},{5,6},{6,7},{8,9},{9,10},{10,11},{12,13},{... | collective-permute-start | bytes 3145736 | tf_op jit(solution)/shard_map/ppermute | solution.py:333
  260.7 86.8 %all-to-all-start.3 = ((bf16[4,128,1024]{2,1,0:T(8,128)(2,1)}), bf16[4,128,1024]{2,1,0:T(8,128)(2,1)}, u32[]{:S(2)}, u32[]{:S(2)}) async-start(bf16[4,128,1024]{2,1,0:T(8,128)(2,1)} %bitcast.23), calls=%async_computation.3 | async-start | bytes 2097152 | tf_op jit(solution)/shard_map/all_to_all | solution.py:326
  265.5 74.9 %collective-permute-start.14 = (bf16[128,4096]{1,0:T(8,128)(2,1)}, bf16[128,4096]{1,0:T(8,128)(2,1)}, u32[]{:S(2)}, u32[]{:S(2)}) collective-permute-start(bf16[128,4096]{1,0:T(8,128)(2,1)} %get-tuple-element.50.refs_10_), channel_id=1, source_target_pairs={{0,1},{1,2},{2,3},{4,5},{5,6},{6,7},{8,9},{9,10},{10,11},{12,13},{... | collective-permute-start | bytes 3145736 | tf_op jit(solution)/shard_map/ppermute | solution.py:333
  268.9 71.5 %collective-permute-start.15 = (bf16[128,4096]{1,0:T(8,128)(2,1)}, bf16[128,4096]{1,0:T(8,128)(2,1)}, u32[]{:S(2)}, u32[]{:S(2)}) collective-permute-start(bf16[128,4096]{1,0:T(8,128)(2,1)} %get-tuple-element.51.refs_11_), channel_id=1, source_target_pairs={{1,0},{2,1},{3,2},{5,4},{6,5},{7,6},{9,8},{10,9},{11,10},{13,12},{... | collective-permute-start | bytes 3145736 | tf_op jit(solution)/shard_map/ppermute | solution.py:334
  272.3 75.2 %collective-permute-start.18 = (bf16[128,4096]{1,0:T(8,128)(2,1)}, bf16[128,4096]{1,0:T(8,128)(2,1)}, u32[]{:S(2)}, u32[]{:S(2)}) collective-permute-start(bf16[128,4096]{1,0:T(8,128)(2,1)} %get-tuple-element.63), channel_id=1, source_target_pairs={{1,0},{2,1},{3,2},{5,4},{6,5},{7,6},{9,8},{10,9},{11,10},{13,12},{... | collective-permute-start | bytes 3145736 | tf_op jit(solution)/shard_map/ppermute | solution.py:334
  274.2 73.3 %collective-permute-start.17 = (bf16[128,4096]{1,0:T(8,128)(2,1)}, bf16[128,4096]{1,0:T(8,128)(2,1)}, u32[]{:S(2)}, u32[]{:S(2)}) collective-permute-start(bf16[128,4096]{1,0:T(8,128)(2,1)} %get-tuple-element.55.refs_10_), channel_id=1, source_target_pairs={{0,1},{1,2},{2,3},{4,5},{5,6},{6,7},{8,9},{9,10},{10,11},{12,13},{... | collective-permute-start | bytes 3145736 | tf_op jit(solution)/shard_map/ppermute | solution.py:333
  278.2 14.7 %copy-start = (f32[8,4,128]{2,1,0:T(4,128)S(1)}, f32[8,4,128]{2,1,0:T(4,128)}, u32[]{:S(2)}) copy-start(f32[8,4,128]{2,1,0:T(4,128)} %get-tuple-element.57) | copy-start | bytes 49156
  278.2 14.7 %copy-start.1 = (f32[8,4,128]{2,1,0:T(4,128)S(1)}, f32[8,4,128]{2,1,0:T(4,128)}, u32[]{:S(2)}) copy-start(f32[8,4,128]{2,1,0:T(4,128)} %get-tuple-element.58) | copy-start | bytes 49156
  345.6 17.6 %collective-permute-start.16 = (bf16[1,128,4096]{2,1,0:T(8,128)(2,1)}, bf16[1,128,4096]{2,1,0:T(8,128)(2,1)}, u32[]{:S(2)}, u32[]{:S(2)}) collective-permute-start(bf16[1,128,4096]{2,1,0:T(8,128)(2,1)} %finish.2), channel_id=1, source_target_pairs={{4,0},{8,4},{12,8},{16,12},{20,16},{24,20},{28,24},{5,1},{9,5},{13... | collective-permute-start | bytes 3145736 | tf_op jit(solution)/shard_map/ppermute | solution.py:418
  352.7 31.7 %collective-permute-start.19 = (bf16[1,128,4096]{2,1,0:T(8,128)(2,1)}, bf16[1,128,4096]{2,1,0:T(8,128)(2,1)S(1)}, u32[]{:S(2)}, u32[]{:S(2)}) collective-permute-start(bf16[1,128,4096]{2,1,0:T(8,128)(2,1)} %finish.3), channel_id=1, source_target_pairs={{28,4},{24,8},{20,12},{16,16},{12,20},{8,24},{4,28},{29,5},{25,9},... | collective-permute-start | bytes 3145736 | tf_op jit(solution)/shard_map/ppermute | solution.py:420
where the time goes:
time: 392 us; the launch traced here: 388 us
  waiting for transfers between devices  130 us (33%)
  Pallas kernels  129 us (33%)
  starting transfers between devices  77.6 us (20%)
  blocking collectives  46.9 us (12%)
    pallas_call x18, Pallas kernels, call(): pl.pallas_call(body, in_specs=list(in_specs) + unread, compiler_params=pa...  129 us
    ppermute x8, waiting for transfers between devices, both_ways(): lax.ppermute(left, 'tensor', [(j, i) for i, j in onward])  83 us
    all_gather x1, blocking collectives, per_device(): lax.all_gather(taps, 'tensor', axis=0, tiled=True)  46.9 us
    ppermute x8, starting transfers between devices, both_ways(): lax.ppermute(right, 'tensor', onward)  32.3 us
    ppermute x1, waiting for transfers between devices, per_device(): up_passed = lax.ppermute(up_grad, 'section', up_pairs)  21.2 us
    all_to_all x4, starting transfers between devices, exchange(): return lax.all_to_all(x, 'tensor', split_axis=0, concat_axis=0, tiled=True)  19.4 us
    ppermute x8, starting transfers between devices, both_ways(): lax.ppermute(left, 'tensor', [(j, i) for i, j in onward])  18.4 us
    ppermute x1, waiting for transfers between devices, per_device(): up_xin = lax.ppermute(up_input[0], 'section', mirror)  14.7 us
  transfers between devices with their start and end apart: 24, of which 10 were waited for; matrix products, arithmetic and copies ran while one was open for 0% of the time, Pallas kernels for 27%

commit v1 on v0

--- a/solution.py
+++ b/solution.py
@@ -20,15 +20,26 @@
     return jax.ShapeDtypeStruct(dims, dtype)
 
 
-def call(kernel, args, after, in_specs, **options):
+def call(kernel, args, after, in_specs, out_shape, flops=0, **options):
     count = len(args)
+    arrays = [*args, *(out_shape if isinstance(out_shape, list) else [out_shape])]
+    cost = pl.CostEstimate(
+        flops=flops,
+        transcendentals=0,
+        bytes_accessed=sum(x.size * x.dtype.itemsize for x in arrays),
+    )
 
     def body(*refs):
         kernel(*refs[:count], *refs[count + len(after) :])
 
     unread = [pl.BlockSpec(memory_space=pl.ANY)] * len(after)
     return pl.pallas_call(
-        body, in_specs=list(in_specs) + unread, compiler_params=params(), **options
+        body,
+        in_specs=list(in_specs) + unread,
+        out_shape=out_shape,
+        cost_estimate=cost,
+        compiler_params=params(),
+        **options,
     )(*args, *after)
 
 
@@ -78,26 +89,32 @@
     return wide * inverse, inverse
 
 
-def normed_kernel(xin_ref, normed_ref):
-    normed = normalise(xin_ref[...].astype(f32))[0].astype(bf16)
+def prepare_kernel(xin_ref, *refs):
+    *cot_ref, normed_ref = refs[: len(refs) // 2 + 1]
+    normed, _ = normalise(xin_ref[...].astype(f32))
     width = normed_ref.shape[2]
     for i in range(normed_ref.shape[0]):
-        normed_ref[i] = normed[:, i * width : (i + 1) * width]
-
-
-def normed_blocks(xin, after=()):
-    rows, width = xin.shape
+        normed_ref[i] = normed[:, i * width : (i + 1) * width].astype(bf16)
+    if cot_ref:
+        refs[-1][...] = (cot_ref[0][...].astype(f32) * normed).astype(bf16)
+
+
+def prepare(*args):
+    rows, width = args[0].shape
     blocks = lax.axis_size("tensor")
     step = 32
-    return call(
-        normed_kernel,
-        (xin,),
-        after,
+    spec = pl.BlockSpec((step, width), lambda i: (i, 0))
+    normed_spec = pl.BlockSpec((blocks, step, width // blocks), lambda i: (0, i, 0))
+    extra = len(args) - 1
+    return call(
+        prepare_kernel,
+        args,
+        (),
         grid=(rows // step,),
-        in_specs=[pl.BlockSpec((step, width), lambda i: (i, 0))],
-        out_specs=pl.BlockSpec((blocks, step, width // blocks), lambda i: (0, i, 0)),
-        out_shape=shape((blocks, rows, width // blocks), bf16),
-        name="normed_blocks",
+        in_specs=[spec] * len(args),
+        out_specs=[normed_spec] + [spec] * extra,
+        out_shape=[shape((blocks, rows, width // blocks), bf16)] + [shape((rows, width), bf16)] * extra,
+        name="prepare",
     )
 
 
@@ -162,6 +179,7 @@
         + [pl.BlockSpec((rows, tile), lambda i: (0, i))] * blocks,
         out_shape=[shape((tokens, width), bf16)] + [shape((rows, width), bf16)] * blocks,
         scratch_shapes=[pltpu.VMEM((tokens, tile), bf16)],
+        flops=2 * tokens * width * (depth + 2 * taps),
         name="project",
     )
     return part, mixed
@@ -259,6 +277,7 @@
             shape((tokens, depth), bf16),
         ],
         scratch_shapes=[pltpu.VMEM((tokens, tile), bf16), pltpu.VMEM((tokens, depth), f32)],
+        flops=2 * tokens * width * (depth + 4 * taps),
         name="back",
     )
 
@@ -287,6 +306,7 @@
         out_specs=pl.BlockSpec((depth, tile), lambda i: (0, i)),
         out_shape=shape((depth, width), bf16),
         scratch_shapes=[pltpu.VMEM((depth, tokens), bf16)] * 2,
+        flops=4 * tokens * depth * width,
         name="weight_gradient",
     )
 
@@ -374,6 +394,15 @@
     return [mix, *rights[:-1], *lefts[:-1]], [pieces[0], rights[-1], lefts[-1]]
 
 
+def sum_all(x):
+    blocks = lax.axis_size("tensor")
+    apart = 1
+    while apart < blocks:
+        x = x + lax.ppermute(x, "tensor", [(i, i ^ apart) for i in range(blocks)])
+        apart *= 2
+    return x
+
+
 def per_device(weights, filters, down_input, down_cot, up_input, up_cot):
     sections = lax.axis_size("section")
     mirror = [(s, sections - 1 - s) for s in range(sections)]
@@ -385,11 +414,11 @@
     up_cot = lax.ppermute(up_cot[0], "section", mirror)
     blocks = lax.axis_size("tensor")
     depth = weight.shape[0]
-    down_x = exchange(normed_blocks(down_xin)).reshape(-1, depth)
-    down_mix = grad_mix(down_xin, down_cot)
+    down_normed, down_mix = prepare(down_xin, down_cot)
+    down_x = exchange(down_normed).reshape(-1, depth)
     down_arrivals = [both_ways(down_mix, down_mix)]
     causal, ahead = toeplitz(filters[0])
-    up_normed = normed_blocks(up_xin)
+    (up_normed,) = prepare(up_xin)
     up_x = exchange(up_normed).reshape(-1, depth)
     up_mix = grad_mix(up_xin, up_cot, after=down_arrivals[0])
     up_arrivals = [both_ways(up_mix, up_mix)]
@@ -400,24 +429,25 @@
         down_arrivals.append(both_ways(*sent))
         if s == 2:
             up_part, up_pieces = project(up_x, weight, causal, after=sent)
-        if s == blocks:
-            down_mixes, down_conv = sort_arrivals(down_mix, down_pieces, down_arrivals)
-            down_g, down_taps, down_back = back(down_mixes, down_part, weight, ahead, after=sent)
-            sent = (down_g,)
-            down_back = exchange(down_back)
-        sent = payload(s, up_arrivals[-1], up_pieces, after=sent[:1])
+        sent = payload(s, up_arrivals[-1], up_pieces, after=sent)
         up_arrivals.append(both_ways(*sent))
         last = sent[0]
+    down_mixes, down_conv = sort_arrivals(down_mix, down_pieces, down_arrivals)
     up_mixes, up_conv = sort_arrivals(up_mix, up_pieces, up_arrivals)
     up_g, up_taps, up_back = back(up_mixes, up_part, weight, ahead, after=(last,))
     up_back = exchange(up_back)
+    down_g, down_taps, down_back = back(
+        down_mixes, down_part, weight, ahead, after=(up_g, *down_arrivals[-1])
+    )
+    down_back = exchange(down_back)
+    up_grad = finish(up_xin, up_cot, up_conv, up_back, after=(down_g,))
+    up_passed = lax.ppermute(up_grad, "section", up_pairs)
     weight_grad = weight_gradient(down_x, up_x, down_g, up_g)
-    taps = (down_taps + up_taps).reshape(filters.shape)
-    taps = jnp.sum(lax.all_gather(taps, "tensor", axis=0, tiled=True), axis=0, keepdims=True)
-    down_grad = finish(down_xin, down_cot, down_conv, down_back, after=(up_g,))
+    taps = sum_all((down_taps + up_taps).reshape(filters.shape))
+    down_grad = finish(
+        down_xin, down_cot, down_conv, down_back, after=(up_grad, weight_grad, taps)
+    )
     down_passed = lax.ppermute(down_grad, "section", down_pairs)
-    up_grad = finish(up_xin, up_cot, up_conv, up_back, after=(weight_grad, taps))
-    up_passed = lax.ppermute(up_grad, "section", up_pairs)
     return weight_grad[None], taps, down_passed, up_passed
 
 

time: 392 us -> 349 us (0.89)
  blocking collectives: 46.9 us -> 0 us
  starting transfers between devices: 77.6 us -> 87.6 us
  Pallas kernels: 129 us -> 125 us
    ppermute x8, waiting for transfers between devices: 83 us -> 30.1 us  [both_ways(): lax.ppermute(left, 'tensor', [(j, i) for i, j in onward])]
    all_gather x1 -> x0, blocking collectives: 46.9 us -> none  [per_device(): lax.all_gather(taps, 'tensor', axis=0, tiled=True)]
    ppermute x0 -> x2, waiting for transfers between devices: none -> 15 us  [sum_all(): x = x + lax.ppermute(x, 'tensor', [(i, i ^ apart) for i in range(blocks)])]
    ppermute x1, waiting for transfers between devices: 0.01 us -> 13.2 us  [per_device(): up_cot = lax.ppermute(up_cot[0], 'section', mirror)]
    ppermute x8, waiting for transfers between devices: 3.77 us -> 15.2 us  [both_ways(): lax.ppermute(right, 'tensor', onward)]
    ppermute x1, waiting for transfers between devices: 7.07 us -> 17.4 us  [per_device(): down_passed = lax.ppermute(down_grad, 'section', down_pairs)]
    ppermute x1, waiting for transfers between devices: 21.2 us -> 16.1 us  [per_device(): up_passed = lax.ppermute(up_grad, 'section', up_pairs)]
    all_to_all x4, starting transfers between devices: 19.4 us -> 24.4 us  [exchange(): return lax.all_to_all(x, 'tensor', split_axis=0, concat_axis=0, tiled=True)]
  transfers between devices with their start and end apart: 24 -> 26, of which waited for: 10 -> 14; matrix products, arithmetic and copies ran while one was open for 0% -> 0% of each run, Pallas kernels for 27% -> 33%
where the time goes in v1:
time: 349 us; the launch traced here: 346 us
  waiting for transfers between devices  129 us (37%)
  Pallas kernels  125 us (36%)
  starting transfers between devices  87.6 us (25%)
    pallas_call x17, Pallas kernels, call(): pl.pallas_call(body, in_specs=list(in_specs) + unread, out_shape=out_shap...  125 us
    ppermute x8, starting transfers between devices, both_ways(): lax.ppermute(right, 'tensor', onward)  33.3 us
    ppermute x8, waiting for transfers between devices, both_ways(): lax.ppermute(left, 'tensor', [(j, i) for i, j in onward])  30.1 us
    all_to_all x4, starting transfers between devices, exchange(): return lax.all_to_all(x, 'tensor', split_axis=0, concat_axis=0, tiled=True)  24.4 us
    ppermute x1, waiting for transfers between devices, per_device(): up_xin = lax.ppermute(up_input[0], 'section', mirror)  18.1 us
    ppermute x1, waiting for transfers between devices, per_device(): down_passed = lax.ppermute(down_grad, 'section', down_pairs)  17.4 us
    ppermute x8, starting transfers between devices, both_ways(): lax.ppermute(left, 'tensor', [(j, i) for i, j in onward])  17.3 us
    ppermute x1, waiting for transfers between devices, per_device(): up_passed = lax.ppermute(up_grad, 'section', up_pairs)  16.1 us
  transfers between devices with their start and end apart: 26, of which 14 were waited for; matrix products, arithmetic and copies ran while one was open for 0% of the time, Pallas kernels for 33%

profile of v1, /device:TPU:10, one launch (start us, length us, event | category | flops | bytes accessed | tf_op | source)
XLA Modules:
  0.0 346.0 jit_solution(2611959310114018725)
XLA Ops:
  0.6 4.1 %prepare.2 = (bf16[4,128,1024]{2,1,0:T(8,128)(2,1)}, bf16[128,4096]{1,0:T(8,128)(2,1)}) custom-call(bf16[128,4096]{1,0:T(8,128)(2,1)} %bitcast.19, bf16[128,4096]{1,0:T(8,128)(2,1)} %bitcast.21), custom_call_target="tpu_custom_call" | custom-call | bytes 4194304 | tf_op jit(solution)/shard_map/prepare/pallas_call | solution.py:36
  4.7 5.3 %all-to-all-start = ((bf16[4,128,1024]{2,1,0:T(8,128)(2,1)}), bf16[4,128,1024]{2,1,0:T(8,128)(2,1)}, u32[]{:S(2)}, u32[]{:S(2)}) async-start(bf16[4,128,1024]{2,1,0:T(8,128)(2,1)} %get-tuple-element.36), calls=%async_computation | async-start | bytes 2097152 | tf_op jit(solution)/shard_map/all_to_all | solution.py:346
  18.5 18.1 %collective-permute-done.refs_0_ = bf16[128,4096]{1,0:T(8,128)(2,1)} collective-permute-done((bf16[128,4096]{1,0:T(8,128)(2,1)}, bf16[128,4096]{1,0:T(8,128)(2,1)}, u32[]{:S(2)}, u32[]{:S(2)}) %collective-permute-start) | collective-permute-done | bytes 1048608 | tf_op jit(solution)/shard_map/ppermute | solution.py:413
  40.4 5.1 %all-to-all-start.1 = ((bf16[4,128,1024]{2,1,0:T(8,128)(2,1)}), bf16[4,128,1024]{2,1,0:T(8,128)(2,1)}, u32[]{:S(2)}, u32[]{:S(2)}) async-start(bf16[4,128,1024]{2,1,0:T(8,128)(2,1)} %prepare.3.refs_3_), calls=%async_computation.1 | async-start | bytes 2097152 | tf_op jit(solution)/shard_map/all_to_all | solution.py:346
  45.5 13.2 %collective-permute-done.3.refs_1_ = bf16[128,4096]{1,0:T(8,128)(2,1)} collective-permute-done((bf16[128,4096]{1,0:T(8,128)(2,1)}, bf16[128,4096]{1,0:T(8,128)(2,1)}, u32[]{:S(2)}, u32[]{:S(2)}) %collective-permute-start.3) | collective-permute-done | bytes 1048608 | tf_op jit(solution)/shard_map/ppermute | solution.py:414
  58.6 6.4 %collective-permute-done.2.refs_3_.refs_1_.refs_4_ = bf16[128,4096]{1,0:T(8,128)(2,1)} collective-permute-done((bf16[128,4096]{1,0:T(8,128)(2,1)}, bf16[128,4096]{1,0:T(8,128)(2,1)}, u32[]{:S(2)}, u32[]{:S(2)}) %collective-permute-start.2) | collective-permute-done | bytes 1048608 | tf_op jit(solution)/shard_map/ppermute | solution.py:354
  73.5 4.4 %collective-permute-start.6 = (bf16[128,4096]{1,0:T(8,128)(2,1)}, bf16[128,4096]{1,0:T(8,128)(2,1)}, u32[]{:S(2)}, u32[]{:S(2)}) collective-permute-start(bf16[128,4096]{1,0:T(8,128)(2,1)} %grad_mix.1.refs_4_.refs_0_), channel_id=1, source_target_pairs={{0,1},{1,2},{2,3},{4,5},{5,6},{6,7},{8,9},{9,10},{10,11},{12,13},{... | collective-permute-start | bytes 3145736 | tf_op jit(solution)/shard_map/ppermute | solution.py:353
  81.8 12.6 %project.2 = (bf16[512,4096]{1,0:T(8,128)(2,1)}, bf16[128,4096]{1,0:T(8,128)(2,1)}, bf16[128,4096]{1,0:T(8,128)(2,1)}, bf16[128,4096]{1,0:T(8,128)(2,1)}, bf16[128,4096]{1,0:T(8,128)(2,1)}) custom-call(bf16[512,1024]{1,0:T(8,128)(2,1)} %bitcast.2.refs_0_, bf16[1024,4096]{1,0:T(8,128)(2,1)} %bitcast.14, bf16[32,128,256]{2,1,0:T(8,128)(2,1)} %get-tuple-element.38.refs_2_, ...), custom_call_target="tpu_custom_call" | custom-call | flops 5368709120 | bytes 19922944 | tf_op jit(solution)/shard_map/project/pallas_call | solution.py:36
  94.4 4.1 %payload.6 = (bf16[128,4096]{1,0:T(8,128)(2,1)}, bf16[128,4096]{1,0:T(8,128)(2,1)}) custom-call(bf16[128,4096]{1,0:T(8,128)(2,1)} %collective-permute-done.1.refs_2_.refs_0_.refs_1_, bf16[128,4096]{1,0:T(8,128)(2,1)} %collective-permute-done.2.refs_3_.refs_1_.refs_4_, bf16[128,4096]{1,0:T(8,128)(2,1)} %get-tuple-element.39.refs_2_.refs_3_, ...), custom_call_target="tpu_custom_call" | custom-call | bytes 6291456 | tf_op jit(solution)/shard_map/payload/pallas_call | solution.py:36
  98.5 4.9 %collective-permute-start.4 = (bf16[128,4096]{1,0:T(8,128)(2,1)}, bf16[128,4096]{1,0:T(8,128)(2,1)}, u32[]{:S(2)}, u32[]{:S(2)}) collective-permute-start(bf16[128,4096]{1,0:T(8,128)(2,1)} %get-tuple-element.42.refs_3_.refs_4_), channel_id=1, source_target_pairs={{0,1},{1,2},{2,3},{4,5},{5,6},{6,7},{8,9},{9,10},{10,11},{12,13},{... | collective-permute-start | bytes 3145736 | tf_op jit(solution)/shard_map/ppermute | solution.py:353
  105.3 12.6 %project.3 = (bf16[512,4096]{1,0:T(8,128)(2,1)}, bf16[128,4096]{1,0:T(8,128)(2,1)}, bf16[128,4096]{1,0:T(8,128)(2,1)}, bf16[128,4096]{1,0:T(8,128)(2,1)}, bf16[128,4096]{1,0:T(8,128)(2,1)}) custom-call(bf16[512,1024]{1,0:T(8,128)(2,1)} %bitcast.4.refs_0_.refs_1_, bf16[1024,4096]{1,0:T(8,128)(2,1)} %bitcast.15, ...), custom_call_target="tpu_custom_call" | custom-call | flops 5368709120 | bytes 19922944 | tf_op jit(solution)/shard_map/project/pallas_call | solution.py:36
  118.0 4.1 %payload.7 = (bf16[128,4096]{1,0:T(8,128)(2,1)}, bf16[128,4096]{1,0:T(8,128)(2,1)}) custom-call(bf16[128,4096]{1,0:T(8,128)(2,1)} %collective-permute-done.6.refs_0_.refs_1_, bf16[128,4096]{1,0:T(8,128)(2,1)} %collective-permute-done.7.refs_1_.refs_4_, bf16[128,4096]{1,0:T(8,128)(2,1)} %get-tuple-element.45.refs_2_.refs_3_, ...), custom_call_target="tpu_custom_call" | custom-call | bytes 6291456 | tf_op jit(solution)/shard_map/payload/pallas_call | solution.py:36
  129.5 4.4 %payload.8 = (bf16[128,4096]{1,0:T(8,128)(2,1)}, bf16[128,4096]{1,0:T(8,128)(2,1)}) custom-call(bf16[128,4096]{1,0:T(8,128)(2,1)} %collective-permute-done.4.refs_0_.refs_2_, bf16[128,4096]{1,0:T(8,128)(2,1)} %collective-permute-done.5.refs_1_.refs_5_, bf16[128,4096]{1,0:T(8,128)(2,1)} %get-tuple-element.44.refs_2_.refs_3_, ...), custom_call_target="tpu_custom_call" | custom-call | bytes 6291456 | tf_op jit(solution)/shard_map/payload/pallas_call | solution.py:36
  140.6 11.3 %collective-permute-done.11.refs_1_.refs_5_ = bf16[128,4096]{1,0:T(8,128)(2,1)} collective-permute-done((bf16[128,4096]{1,0:T(8,128)(2,1)}, bf16[128,4096]{1,0:T(8,128)(2,1)}, u32[]{:S(2)}, u32[]{:S(2)}) %collective-permute-start.11) | collective-permute-done | bytes 1048608 | tf_op jit(solution)/shard_map/ppermute | solution.py:354
  152.3 4.5 %payload.9 = (bf16[128,4096]{1,0:T(8,128)(2,1)}, bf16[128,4096]{1,0:T(8,128)(2,1)}) custom-call(bf16[128,4096]{1,0:T(8,128)(2,1)} %collective-permute-done.10.refs_0_.refs_2_, bf16[128,4096]{1,0:T(8,128)(2,1)} %collective-permute-done.11.refs_1_.refs_5_, bf16[128,4096]{1,0:T(8,128)(2,1)} %get-tuple-element.52.refs_2_.refs_3_, ...), custom_call_target="tpu_custom_call" | custom-call | bytes 6291456 | tf_op jit(solution)/shard_map/payload/pallas_call | solution.py:36
  158.7 4.4 %collective-permute-start.12 = (bf16[128,4096]{1,0:T(8,128)(2,1)}, bf16[128,4096]{1,0:T(8,128)(2,1)}, u32[]{:S(2)}, u32[]{:S(2)}) collective-permute-start(bf16[128,4096]{1,0:T(8,128)(2,1)} %get-tuple-element.53.refs_4_), channel_id=1, source_target_pairs={{0,1},{1,2},{2,3},{4,5},{5,6},{6,7},{8,9},{9,10},{10,11},{12,13},{... | collective-permute-start | bytes 3145736 | tf_op jit(solution)/shard_map/ppermute | solution.py:353
  163.2 11.7 %collective-permute-done.8.refs_0_.refs_3_ = bf16[128,4096]{1,0:T(8,128)(2,1)} collective-permute-done((bf16[128,4096]{1,0:T(8,128)(2,1)}, bf16[128,4096]{1,0:T(8,128)(2,1)}, u32[]{:S(2)}, u32[]{:S(2)}) %collective-permute-start.8) | collective-permute-done | bytes 1048608 | tf_op jit(solution)/shard_map/ppermute | solution.py:353
  174.8 4.3 %payload.10 = (bf16[128,4096]{1,0:T(8,128)(2,1)}, bf16[128,4096]{1,0:T(8,128)(2,1)}) custom-call(bf16[128,4096]{1,0:T(8,128)(2,1)} %collective-permute-done.8.refs_0_.refs_3_, bf16[128,4096]{1,0:T(8,128)(2,1)} %collective-permute-done.9.refs_1_.refs_6_, bf16[128,4096]{1,0:T(8,128)(2,1)} %get-tuple-element.40.refs_3_.refs_2_, ...), custom_call_target="tpu_custom_call" | custom-call | bytes 6291456 | tf_op jit(solution)/shard_map/payload/pallas_call | solution.py:36
  179.1 4.4 %collective-permute-start.14 = (bf16[128,4096]{1,0:T(8,128)(2,1)}, bf16[128,4096]{1,0:T(8,128)(2,1)}, u32[]{:S(2)}, u32[]{:S(2)}) collective-permute-start(bf16[128,4096]{1,0:T(8,128)(2,1)} %get-tuple-element.56.refs_4_), channel_id=1, source_target_pairs={{0,1},{1,2},{2,3},{4,5},{5,6},{6,7},{8,9},{9,10},{10,11},{12,13},{... | collective-permute-start | bytes 3145736 | tf_op jit(solution)/shard_map/ppermute | solution.py:353
  185.9 10.9 %collective-permute-done.13.refs_1_.refs_6_ = bf16[128,4096]{1,0:T(8,128)(2,1)} collective-permute-done((bf16[128,4096]{1,0:T(8,128)(2,1)}, bf16[128,4096]{1,0:T(8,128)(2,1)}, u32[]{:S(2)}, u32[]{:S(2)}) %collective-permute-start.13) | collective-permute-done | bytes 1048608 | tf_op jit(solution)/shard_map/ppermute | solution.py:354
  197.3 4.3 %payload.11 = (bf16[128,4096]{1,0:T(8,128)(2,1)}, bf16[128,4096]{1,0:T(8,128)(2,1)}) custom-call(bf16[128,4096]{1,0:T(8,128)(2,1)} %collective-permute-done.12.refs_0_.refs_3_, bf16[128,4096]{1,0:T(8,128)(2,1)} %collective-permute-done.13.refs_1_.refs_6_, bf16[128,4096]{1,0:T(8,128)(2,1)} %get-tuple-element.46.refs_3_.refs_2_, ...), custom_call_target="tpu_custom_call" | custom-call | bytes 6291456 | tf_op jit(solution)/shard_map/payload/pallas_call | solution.py:36
  201.6 16.8 %back.2 = (bf16[512,4096]{1,0:T(8,128)(2,1)}, f32[8,4,128]{2,1,0:T(4,128)}, bf16[512,1024]{1,0:T(8,128)(2,1)}) custom-call(bf16[128,4096]{1,0:T(8,128)(2,1)} %grad_mix.1.refs_4_.refs_0_, bf16[128,4096]{1,0:T(8,128)(2,1)} %collective-permute-done.6.refs_0_.refs_1_, bf16[128,4096]{1,0:T(8,128)(2,1)} %collective-permute-done.10.refs_0_.refs_2_, ...), custom_call_target="tpu_custom_call" | custom-call | flops 6442450944 | bytes 27279360 | tf_op jit(solution)/shard_map/back/pallas_call | solution.py:36
  218.4 7.1 %all-to-all-start.3 = ((bf16[4,128,1024]{2,1,0:T(8,128)(2,1)}), bf16[4,128,1024]{2,1,0:T(8,128)(2,1)}, u32[]{:S(2)}, u32[]{:S(2)}) async-start(bf16[4,128,1024]{2,1,0:T(8,128)(2,1)} %bitcast.24), calls=%async_computation.3 | async-start | bytes 2097152 | tf_op jit(solution)/shard_map/all_to_all | solution.py:346
  225.5 16.8 %back.3 = (bf16[512,4096]{1,0:T(8,128)(2,1)}, f32[8,4,128]{2,1,0:T(4,128)}, bf16[512,1024]{1,0:T(8,128)(2,1)}) custom-call(bf16[128,4096]{1,0:T(8,128)(2,1)} %get-tuple-element.37.refs_0_, bf16[128,4096]{1,0:T(8,128)(2,1)} %collective-permute-done.1.refs_2_.refs_0_.refs_1_, bf16[128,4096]{1,0:T(8,128)(2,1)} %collective-permute-done.4.refs_0_.refs_2_, ...), custom_call_target="tpu_custom_call" | custom-call | flops 6442450944 | bytes 27279360 | tf_op jit(solution)/shard_map/back/pallas_call | solution.py:36
  242.3 4.2 %all-to-all-done.3.refs_2_ = bf16[4,128,1024]{2,1,0:T(8,128)(2,1)} async-done(((bf16[4,128,1024]{2,1,0:T(8,128)(2,1)}), bf16[4,128,1024]{2,1,0:T(8,128)(2,1)}, u32[]{:S(2)}, u32[]{:S(2)}) %all-to-all-start.3) | async-done | bytes 1048608 | tf_op jit(solution)/shard_map/all_to_all | solution.py:346
  246.5 6.9 %all-to-all-start.2 = ((bf16[4,128,1024]{2,1,0:T(8,128)(2,1)}), bf16[4,128,1024]{2,1,0:T(8,128)(2,1)}, u32[]{:S(2)}, u32[]{:S(2)}) async-start(bf16[4,128,1024]{2,1,0:T(8,128)(2,1)} %bitcast.23), calls=%async_computation.2 | async-start | bytes 2097152 | tf_op jit(solution)/shard_map/all_to_all | solution.py:346
  261.0 15.0 %collective-permute-done.16 = f32[1,32,128]{2,1,0:T(8,128)S(1)} collective-permute-done((f32[1,32,128]{2,1,0:T(8,128)S(1)}, f32[1,32,128]{2,1,0:T(8,128)S(1)}, u32[]{:S(2)}, u32[]{:S(2)}) %collective-permute-start.16) | collective-permute-done | bytes 16416 | tf_op jit(solution)/shard_map/ppermute | solution.py:401
  279.6 14.7 %weight_gradient.1.refs_7_ = bf16[1024,4096]{1,0:T(8,128)(2,1)} custom-call(bf16[512,1024]{1,0:T(8,128)(2,1)} %bitcast.2.refs_0_, bf16[512,1024]{1,0:T(8,128)(2,1)} %bitcast.4.refs_0_.refs_1_, bf16[512,4096]{1,0:T(8,128)(2,1)} %get-tuple-element.60.refs_2_.refs_6_, bf16[512,4096]{1,0:T(8,128)(2,1)} %get-tuple-element.59.refs_10_.refs_3_), custom_call_target="tpu_custom_call" | custom-call | flops 8589934592 | bytes 18874368 | tf_op jit(solution)/shard_map/weight_gradient/pallas_call | solution.py:36
  294.9 5.2 %finish.2.refs_6_ = bf16[1,128,4096]{2,1,0:T(8,128)(2,1)} custom-call(bf16[128,4096]{1,0:T(8,128)(2,1)} %collective-permute-done.refs_0_, bf16[128,4096]{1,0:T(8,128)(2,1)} %collective-permute-done.3.refs_1_, bf16[4,128,1024]{2,1,0:T(8,128)(2,1)} %all-to-all-done.3.refs_2_, bf16[128,4096]{1,0:T(8,128)(2,1)} %get-tuple-element.66.refs_3_, ...), custom_call_target="tpu_custom_call" | custom-call | bytes 7340032 | tf_op jit(solution)/shard_map/finish/pallas_call | solution.py:36
  300.0 5.2 %finish.3 = bf16[1,128,4096]{2,1,0:T(8,128)(2,1)} custom-call(bf16[128,4096]{1,0:T(8,128)(2,1)} %bitcast.20, bf16[128,4096]{1,0:T(8,128)(2,1)} %bitcast.22, bf16[4,128,1024]{2,1,0:T(8,128)(2,1)} %all-to-all-done.2.refs_2_, bf16[128,4096]{1,0:T(8,128)(2,1)} %get-tuple-element.64.refs_3_, bf16[128,4096]{1,0:T(8,128)(2,1)} %collective-permute-done.14.refs_11_.refs_4_, ...), custom_call_target="tpu_custom_call" | custom-call | bytes 7340032 | tf_op jit(solution)/shard_map/finish/pallas_call | solution.py:36
  310.6 17.4 %collective-permute-done.20 = bf16[1,128,4096]{2,1,0:T(8,128)(2,1)S(1)} collective-permute-done((bf16[1,128,4096]{2,1,0:T(8,128)(2,1)}, bf16[1,128,4096]{2,1,0:T(8,128)(2,1)S(1)}, u32[]{:S(2)}, u32[]{:S(2)}) %collective-permute-start.20) | collective-permute-done | bytes 1048608 | tf_op jit(solution)/shard_map/ppermute | solution.py:450
  328.0 16.1 %collective-permute-done.21 = bf16[1,128,4096]{2,1,0:T(8,128)(2,1)S(1)} collective-permute-done((bf16[1,128,4096]{2,1,0:T(8,128)(2,1)}, bf16[1,128,4096]{2,1,0:T(8,128)(2,1)S(1)}, u32[]{:S(2)}, u32[]{:S(2)}) %collective-permute-start.21) | collective-permute-done | bytes 1048608 | tf_op jit(solution)/shard_map/ppermute | solution.py:444
  (44 shorter events, 64.9 us)
Async XLA Ops:
  4.7 35.6 %all-to-all-start = ((bf16[4,128,1024]{2,1,0:T(8,128)(2,1)}), bf16[4,128,1024]{2,1,0:T(8,128)(2,1)}, u32[]{:S(2)}, u32[]{:S(2)}) async-start(bf16[4,128,1024]{2,1,0:T(8,128)(2,1)} %get-tuple-element.36), calls=%async_computation | async-start | bytes 2097152 | tf_op jit(solution)/shard_map/all_to_all | solution.py:346
  10.0 26.6 %collective-permute-start = (bf16[128,4096]{1,0:T(8,128)(2,1)}, bf16[128,4096]{1,0:T(8,128)(2,1)}, u32[]{:S(2)}, u32[]{:S(2)}) collective-permute-start(bf16[128,4096]{1,0:T(8,128)(2,1)} %bitcast.28), channel_id=1, source_target_pairs={{0,28},{4,24},{8,20},{12,16},{16,12},{20,8},{24,4},{28,0},{1,29},{... | collective-permute-start | bytes 3145736 | tf_op jit(solution)/shard_map/ppermute | solution.py:413
  10.4 48.2 %collective-permute-start.3 = (bf16[128,4096]{1,0:T(8,128)(2,1)}, bf16[128,4096]{1,0:T(8,128)(2,1)}, u32[]{:S(2)}, u32[]{:S(2)}) collective-permute-start(bf16[128,4096]{1,0:T(8,128)(2,1)} %bitcast.29), channel_id=1, source_target_pairs={{0,28},{4,24},{8,20},{12,16},{16,12},{20,8},{24,4},{28,0},{1,29},{... | collective-permute-start | bytes 3145736 | tf_op jit(solution)/shard_map/ppermute | solution.py:414
  12.7 52.3 %collective-permute-start.2 = (bf16[128,4096]{1,0:T(8,128)(2,1)}, bf16[128,4096]{1,0:T(8,128)(2,1)}, u32[]{:S(2)}, u32[]{:S(2)}) collective-permute-start(bf16[128,4096]{1,0:T(8,128)(2,1)} %get-tuple-element.37.refs_0_), channel_id=1, source_target_pairs={{1,0},{2,1},{3,2},{5,4},{6,5},{7,6},{9,8},{10,9},{11,10},{13,12},{... | collective-permute-start | bytes 3145736 | tf_op jit(solution)/shard_map/ppermute | solution.py:354
  14.6 53.1 %collective-permute-start.1 = (bf16[128,4096]{1,0:T(8,128)(2,1)}, bf16[128,4096]{1,0:T(8,128)(2,1)}, u32[]{:S(2)}, u32[]{:S(2)}) collective-permute-start(bf16[128,4096]{1,0:T(8,128)(2,1)} %get-tuple-element.37.refs_0_), channel_id=1, source_target_pairs={{0,1},{1,2},{2,3},{4,5},{5,6},{6,7},{8,9},{9,10},{10,11},{12,13},{... | collective-permute-start | bytes 3145736 | tf_op jit(solution)/shard_map/ppermute | solution.py:353
  40.4 65.0 %all-to-all-start.1 = ((bf16[4,128,1024]{2,1,0:T(8,128)(2,1)}), bf16[4,128,1024]{2,1,0:T(8,128)(2,1)}, u32[]{:S(2)}, u32[]{:S(2)}) async-start(bf16[4,128,1024]{2,1,0:T(8,128)(2,1)} %prepare.3.refs_3_), calls=%async_computation.1 | async-start | bytes 2097152 | tf_op jit(solution)/shard_map/all_to_all | solution.py:346
  71.6 46.4 %collective-permute-start.7 = (bf16[128,4096]{1,0:T(8,128)(2,1)}, bf16[128,4096]{1,0:T(8,128)(2,1)}, u32[]{:S(2)}, u32[]{:S(2)}) collective-permute-start(bf16[128,4096]{1,0:T(8,128)(2,1)} %grad_mix.1.refs_4_.refs_0_), channel_id=1, source_target_pairs={{1,0},{2,1},{3,2},{5,4},{6,5},{7,6},{9,8},{10,9},{11,10},{13,12},{... | collective-permute-start | bytes 3145736 | tf_op jit(solution)/shard_map/ppermute | solution.py:354
  73.5 44.5 %collective-permute-start.6 = (bf16[128,4096]{1,0:T(8,128)(2,1)}, bf16[128,4096]{1,0:T(8,128)(2,1)}, u32[]{:S(2)}, u32[]{:S(2)}) collective-permute-start(bf16[128,4096]{1,0:T(8,128)(2,1)} %grad_mix.1.refs_4_.refs_0_), channel_id=1, source_target_pairs={{0,1},{1,2},{2,3},{4,5},{5,6},{6,7},{8,9},{9,10},{10,11},{12,13},{... | collective-permute-start | bytes 3145736 | tf_op jit(solution)/shard_map/ppermute | solution.py:353
  98.5 29.5 %collective-permute-start.4 = (bf16[128,4096]{1,0:T(8,128)(2,1)}, bf16[128,4096]{1,0:T(8,128)(2,1)}, u32[]{:S(2)}, u32[]{:S(2)}) collective-permute-start(bf16[128,4096]{1,0:T(8,128)(2,1)} %get-tuple-element.42.refs_3_.refs_4_), channel_id=1, source_target_pairs={{0,1},{1,2},{2,3},{4,5},{5,6},{6,7},{8,9},{9,10},{10,11},{12,13},{... | collective-permute-start | bytes 3145736 | tf_op jit(solution)/shard_map/ppermute | solution.py:353
  103.4 26.1 %collective-permute-start.5 = (bf16[128,4096]{1,0:T(8,128)(2,1)}, bf16[128,4096]{1,0:T(8,128)(2,1)}, u32[]{:S(2)}, u32[]{:S(2)}) collective-permute-start(bf16[128,4096]{1,0:T(8,128)(2,1)} %get-tuple-element.43.refs_4_.refs_5_), channel_id=1, source_target_pairs={{1,0},{2,1},{3,2},{5,4},{6,5},{7,6},{9,8},{10,9},{11,10},{13,12},{... | collective-permute-start | bytes 3145736 | tf_op jit(solution)/shard_map/ppermute | solution.py:354
  122.1 29.8 %collective-permute-start.11 = (bf16[128,4096]{1,0:T(8,128)(2,1)}, bf16[128,4096]{1,0:T(8,128)(2,1)}, u32[]{:S(2)}, u32[]{:S(2)}) collective-permute-start(bf16[128,4096]{1,0:T(8,128)(2,1)} %get-tuple-element.51), channel_id=1, source_target_pairs={{1,0},{2,1},{3,2},{5,4},{6,5},{7,6},{9,8},{10,9},{11,10},{13,12},{... | collective-permute-start | bytes 3145736 | tf_op jit(solution)/shard_map/ppermute | solution.py:354
  124.0 28.3 %collective-permute-start.10 = (bf16[128,4096]{1,0:T(8,128)(2,1)}, bf16[128,4096]{1,0:T(8,128)(2,1)}, u32[]{:S(2)}, u32[]{:S(2)}) collective-permute-start(bf16[128,4096]{1,0:T(8,128)(2,1)} %get-tuple-element.47.refs_4_), channel_id=1, source_target_pairs={{0,1},{1,2},{2,3},{4,5},{5,6},{6,7},{8,9},{9,10},{10,11},{12,13},{... | collective-permute-start | bytes 3145736 | tf_op jit(solution)/shard_map/ppermute | solution.py:353
  133.8 41.0 %collective-permute-start.8 = (bf16[128,4096]{1,0:T(8,128)(2,1)}, bf16[128,4096]{1,0:T(8,128)(2,1)}, u32[]{:S(2)}, u32[]{:S(2)}) collective-permute-start(bf16[128,4096]{1,0:T(8,128)(2,1)} %get-tuple-element.48.refs_4_), channel_id=1, source_target_pairs={{0,1},{1,2},{2,3},{4,5},{5,6},{6,7},{8,9},{9,10},{10,11},{12,13},{... | collective-permute-start | bytes 3145736 | tf_op jit(solution)/shard_map/ppermute | solution.py:353
  137.3 37.5 %collective-permute-start.9 = (bf16[128,4096]{1,0:T(8,128)(2,1)}, bf16[128,4096]{1,0:T(8,128)(2,1)}, u32[]{:S(2)}, u32[]{:S(2)}) collective-permute-start(bf16[128,4096]{1,0:T(8,128)(2,1)} %get-tuple-element.49.refs_5_), channel_id=1, source_target_pairs={{1,0},{2,1},{3,2},{5,4},{6,5},{7,6},{9,8},{10,9},{11,10},{13,12},{... | collective-permute-start | bytes 3145736 | tf_op jit(solution)/shard_map/ppermute | solution.py:354
  156.8 40.1 %collective-permute-start.13 = (bf16[128,4096]{1,0:T(8,128)(2,1)}, bf16[128,4096]{1,0:T(8,128)(2,1)}, u32[]{:S(2)}, u32[]{:S(2)}) collective-permute-start(bf16[128,4096]{1,0:T(8,128)(2,1)} %get-tuple-element.54), channel_id=1, source_target_pairs={{1,0},{2,1},{3,2},{5,4},{6,5},{7,6},{9,8},{10,9},{11,10},{13,12},{... | collective-permute-start | bytes 3145736 | tf_op jit(solution)/shard_map/ppermute | solution.py:354
  158.7 38.6 %collective-permute-start.12 = (bf16[128,4096]{1,0:T(8,128)(2,1)}, bf16[128,4096]{1,0:T(8,128)(2,1)}, u32[]{:S(2)}, u32[]{:S(2)}) collective-permute-start(bf16[128,4096]{1,0:T(8,128)(2,1)} %get-tuple-element.53.refs_4_), channel_id=1, source_target_pairs={{0,1},{1,2},{2,3},{4,5},{5,6},{6,7},{8,9},{9,10},{10,11},{12,13},{... | collective-permute-start | bytes 3145736 | tf_op jit(solution)/shard_map/ppermute | solution.py:353
  179.1 46.3 %collective-permute-start.14 = (bf16[128,4096]{1,0:T(8,128)(2,1)}, bf16[128,4096]{1,0:T(8,128)(2,1)}, u32[]{:S(2)}, u32[]{:S(2)}) collective-permute-start(bf16[128,4096]{1,0:T(8,128)(2,1)} %get-tuple-element.56.refs_4_), channel_id=1, source_target_pairs={{0,1},{1,2},{2,3},{4,5},{5,6},{6,7},{8,9},{9,10},{10,11},{12,13},{... | collective-permute-start | bytes 3145736 | tf_op jit(solution)/shard_map/ppermute | solution.py:353
  183.6 41.9 %collective-permute-start.15 = (bf16[128,4096]{1,0:T(8,128)(2,1)}, bf16[128,4096]{1,0:T(8,128)(2,1)}, u32[]{:S(2)}, u32[]{:S(2)}) collective-permute-start(bf16[128,4096]{1,0:T(8,128)(2,1)} %get-tuple-element.57.refs_5_), channel_id=1, source_target_pairs={{1,0},{2,1},{3,2},{5,4},{6,5},{7,6},{9,8},{10,9},{11,10},{13,12},{... | collective-permute-start | bytes 3145736 | tf_op jit(solution)/shard_map/ppermute | solution.py:354
  218.4 28.1 %all-to-all-start.3 = ((bf16[4,128,1024]{2,1,0:T(8,128)(2,1)}), bf16[4,128,1024]{2,1,0:T(8,128)(2,1)}, u32[]{:S(2)}, u32[]{:S(2)}) async-start(bf16[4,128,1024]{2,1,0:T(8,128)(2,1)} %bitcast.24), calls=%async_computation.3 | async-start | bytes 2097152 | tf_op jit(solution)/shard_map/all_to_all | solution.py:346
  225.5 33.7 %copy-start = (f32[8,4,128]{2,1,0:T(4,128)S(1)}, f32[8,4,128]{2,1,0:T(4,128)}, u32[]{:S(2)}) copy-start(f32[8,4,128]{2,1,0:T(4,128)} %get-tuple-element.62) | copy-start | bytes 49156
  246.5 53.6 %all-to-all-start.2 = ((bf16[4,128,1024]{2,1,0:T(8,128)(2,1)}), bf16[4,128,1024]{2,1,0:T(8,128)(2,1)}, u32[]{:S(2)}, u32[]{:S(2)}) async-start(bf16[4,128,1024]{2,1,0:T(8,128)(2,1)} %bitcast.23), calls=%async_computation.2 | async-start | bytes 2097152 | tf_op jit(solution)/shard_map/all_to_all | solution.py:346
  253.4 41.5 %collective-permute-start.19 = (bf16[128,4096]{1,0:T(8,128)(2,1)}, bf16[128,4096]{1,0:T(8,128)(2,1)}, u32[]{:S(2)}, u32[]{:S(2)}) collective-permute-start(bf16[128,4096]{1,0:T(8,128)(2,1)} %get-tuple-element.67), channel_id=1, source_target_pairs={{1,0},{2,1},{3,2},{5,4},{6,5},{7,6},{9,8},{10,9},{11,10},{13,12},{... | collective-permute-start | bytes 3145736 | tf_op jit(solution)/shard_map/ppermute | solution.py:354
  255.3 39.6 %collective-permute-start.18 = (bf16[128,4096]{1,0:T(8,128)(2,1)}, bf16[128,4096]{1,0:T(8,128)(2,1)}, u32[]{:S(2)}, u32[]{:S(2)}) collective-permute-start(bf16[128,4096]{1,0:T(8,128)(2,1)} %get-tuple-element.58.refs_10_), channel_id=1, source_target_pairs={{0,1},{1,2},{2,3},{4,5},{5,6},{6,7},{8,9},{9,10},{10,11},{12,13},{... | collective-permute-start | bytes 3145736 | tf_op jit(solution)/shard_map/ppermute | solution.py:353
  259.9 16.0 %collective-permute-start.16 = (f32[1,32,128]{2,1,0:T(8,128)S(1)}, f32[1,32,128]{2,1,0:T(8,128)S(1)}, u32[]{:S(2)}, u32[]{:S(2)}) collective-permute-start(f32[1,32,128]{2,1,0:T(8,128)S(1)} %bitcast.25), channel_id=1, source_target_pairs={{0,1},{1,0},{2,3},{3,2},{4,5},{5,4},{6,7},{7,6},{8,9},{9,8},{10,11... | collective-permute-start | bytes 49160 | tf_op jit(solution)/shard_map/ppermute | solution.py:401
  275.9 18.3 %collective-permute-start.17 = (f32[1,32,128]{2,1,0:T(8,128)S(1)}, f32[1,32,128]{2,1,0:T(8,128)S(1)}, u32[]{:S(2)}, u32[]{:S(2)}) collective-permute-start(f32[1,32,128]{2,1,0:T(8,128)S(1)} %bitcast_add_fusion), channel_id=1, source_target_pairs={{0,2},{1,3},{2,0},{3,1},{4,6},{5,7},{6,4},{7,5},{8,10},{9,11},{10,... | collective-permute-start | bytes 49160 | tf_op jit(solution)/shard_map/ppermute | solution.py:401
  305.2 22.8 %collective-permute-start.20 = (bf16[1,128,4096]{2,1,0:T(8,128)(2,1)}, bf16[1,128,4096]{2,1,0:T(8,128)(2,1)S(1)}, u32[]{:S(2)}, u32[]{:S(2)}) collective-permute-start(bf16[1,128,4096]{2,1,0:T(8,128)(2,1)} %finish.3), channel_id=1, source_target_pairs={{4,0},{8,4},{12,8},{16,12},{20,16},{24,20},{28,24},{5,1},{9,5},{13... | collective-permute-start | bytes 3145736 | tf_op jit(solution)/shard_map/ppermute | solution.py:450
  307.1 36.9 %collective-permute-start.21 = (bf16[1,128,4096]{2,1,0:T(8,128)(2,1)}, bf16[1,128,4096]{2,1,0:T(8,128)(2,1)S(1)}, u32[]{:S(2)}, u32[]{:S(2)}) collective-permute-start(bf16[1,128,4096]{2,1,0:T(8,128)(2,1)} %finish.2.refs_6_), channel_id=1, source_target_pairs={{28,4},{24,8},{20,12},{16,16},{12,20},{8,24},{4,28},{29,5},{25,9},... | collective-permute-start | bytes 3145736 | tf_op jit(solution)/shard_map/ppermute | solution.py:444

commit v2 on v1

--- a/solution.py
+++ b/solution.py
@@ -394,11 +394,30 @@
     return [mix, *rights[:-1], *lefts[:-1]], [pieces[0], rights[-1], lefts[-1]]
 
 
-def sum_all(x):
+def add_kernel(a_ref, b_ref, out_ref):
+    out_ref[...] = a_ref[...] + b_ref[...]
+
+
+def add(a, b, after=()):
+    spec = pl.BlockSpec(a.shape, lambda i: (0,) * a.ndim)
+    return call(
+        add_kernel,
+        (a, b),
+        after,
+        grid=(1,),
+        in_specs=[spec, spec],
+        out_specs=spec,
+        out_shape=shape(a.shape, a.dtype),
+        name="add",
+    )
+
+
+def sum_all(x, after=()):
     blocks = lax.axis_size("tensor")
     apart = 1
     while apart < blocks:
-        x = x + lax.ppermute(x, "tensor", [(i, i ^ apart) for i in range(blocks)])
+        other = lax.ppermute(x, "tensor", [(i, i ^ apart) for i in range(blocks)])
+        x = add(x, other, after)
         apart *= 2
     return x
 
@@ -437,15 +456,16 @@
     up_g, up_taps, up_back = back(up_mixes, up_part, weight, ahead, after=(last,))
     up_back = exchange(up_back)
     down_g, down_taps, down_back = back(
-        down_mixes, down_part, weight, ahead, after=(up_g, *down_arrivals[-1])
+        down_mixes, down_part, weight, ahead, after=(up_g, *down_arrivals[-1], *up_arrivals[-1])
     )
     down_back = exchange(down_back)
     up_grad = finish(up_xin, up_cot, up_conv, up_back, after=(down_g,))
     up_passed = lax.ppermute(up_grad, "section", up_pairs)
-    weight_grad = weight_gradient(down_x, up_x, down_g, up_g)
-    taps = sum_all((down_taps + up_taps).reshape(filters.shape))
+    weight_grad = weight_gradient(down_x, up_x, down_g, up_g, after=(up_grad,))
+    taps = add(down_taps, up_taps).reshape(filters.shape)
+    taps = sum_all(taps, after=(weight_grad,))
     down_grad = finish(
-        down_xin, down_cot, down_conv, down_back, after=(up_grad, weight_grad, taps)
+        down_xin, down_cot, down_conv, down_back, after=(taps,)
     )
     down_passed = lax.ppermute(down_grad, "section", down_pairs)
     return weight_grad[None], taps, down_passed, up_passed

time: 349 us -> 341 us (0.977)
  the two profiles are of different devices: /device:TPU:10 before, /device:TPU:3 now
where the time goes in v2:
time: 341 us; the launch traced here: 337 us
  Pallas kernels  129 us (38%)
  waiting for transfers between devices  105 us (31%)
  starting transfers between devices  97.1 us (28%)
  local copies, waits for them, and re-layouts  4.45 us (1%)
    pallas_call x20, Pallas kernels, call(): pl.pallas_call(body, in_specs=list(in_specs) + unread, out_shape=out_shap...  129 us
    ppermute x8, waiting for transfers between devices, both_ways(): lax.ppermute(left, 'tensor', [(j, i) for i, j in onward])  44.4 us
    ppermute x8, starting transfers between devices, both_ways(): lax.ppermute(right, 'tensor', onward)  42.6 us
    ppermute x1, waiting for transfers between devices, per_device(): down_passed = lax.ppermute(down_grad, 'section', down_pairs)  19.8 us
    ppermute x1, waiting for transfers between devices, per_device(): up_xin = lax.ppermute(up_input[0], 'section', mirror)  17.8 us
    ppermute x1, starting transfers between devices, per_device(): down_passed = lax.ppermute(down_grad, 'section', down_pairs)  17.6 us
    all_to_all x4, starting transfers between devices, exchange(): return lax.all_to_all(x, 'tensor', split_axis=0, concat_axis=0, tiled=True)  17.4 us
    ppermute x1, waiting for transfers between devices, per_device(): up_cot = lax.ppermute(up_cot[0], 'section', mirror)  14.5 us
  transfers between devices with their start and end apart: 26, of which 9 were waited for; matrix products, arithmetic and copies ran while one was open for 0% of the time, Pallas kernels for 37%

profile of v2, /device:TPU:3, one launch (start us, length us, event | category | flops | bytes accessed | tf_op | source)
XLA Modules:
  0.0 336.9 jit_solution(1724699652507856130)
XLA Ops:
  4.7 4.6 %all-to-all-start = ((bf16[4,128,1024]{2,1,0:T(8,128)(2,1)}), bf16[4,128,1024]{2,1,0:T(8,128)(2,1)}, u32[]{:S(2)}, u32[]{:S(2)}) async-start(bf16[4,128,1024]{2,1,0:T(8,128)(2,1)} %get-tuple-element.36), calls=%async_computation | async-start | bytes 2097152 | tf_op jit(solution)/shard_map/all_to_all | solution.py:346
  13.2 5.0 %collective-permute-start.1 = (bf16[128,4096]{1,0:T(8,128)(2,1)}, bf16[128,4096]{1,0:T(8,128)(2,1)}, u32[]{:S(2)}, u32[]{:S(2)}) collective-permute-start(bf16[128,4096]{1,0:T(8,128)(2,1)} %get-tuple-element.37.refs_0_), channel_id=1, source_target_pairs={{0,1},{1,2},{2,3},{4,5},{5,6},{6,7},{8,9},{9,10},{10,11},{12,13},{... | collective-permute-start | bytes 3145736 | tf_op jit(solution)/shard_map/ppermute | solution.py:353
  18.2 17.8 %collective-permute-done.refs_0_ = bf16[128,4096]{1,0:T(8,128)(2,1)} collective-permute-done((bf16[128,4096]{1,0:T(8,128)(2,1)}, bf16[128,4096]{1,0:T(8,128)(2,1)}, u32[]{:S(2)}, u32[]{:S(2)}) %collective-permute-start) | collective-permute-done | bytes 1048608 | tf_op jit(solution)/shard_map/ppermute | solution.py:432
  39.7 4.3 %all-to-all-start.1 = ((bf16[4,128,1024]{2,1,0:T(8,128)(2,1)}), bf16[4,128,1024]{2,1,0:T(8,128)(2,1)}, u32[]{:S(2)}, u32[]{:S(2)}) async-start(bf16[4,128,1024]{2,1,0:T(8,128)(2,1)} %prepare.3.refs_3_), calls=%async_computation.1 | async-start | bytes 2097152 | tf_op jit(solution)/shard_map/all_to_all | solution.py:346
  44.0 14.5 %collective-permute-done.3.refs_1_ = bf16[128,4096]{1,0:T(8,128)(2,1)} collective-permute-done((bf16[128,4096]{1,0:T(8,128)(2,1)}, bf16[128,4096]{1,0:T(8,128)(2,1)}, u32[]{:S(2)}, u32[]{:S(2)}) %collective-permute-start.3) | collective-permute-done | bytes 1048608 | tf_op jit(solution)/shard_map/ppermute | solution.py:433
  63.6 8.1 %collective-permute-start.6 = (bf16[128,4096]{1,0:T(8,128)(2,1)}, bf16[128,4096]{1,0:T(8,128)(2,1)}, u32[]{:S(2)}, u32[]{:S(2)}) collective-permute-start(bf16[128,4096]{1,0:T(8,128)(2,1)} %grad_mix.1.refs_4_.refs_0_), channel_id=1, source_target_pairs={{0,1},{1,2},{2,3},{4,5},{5,6},{6,7},{8,9},{9,10},{10,11},{12,13},{... | collective-permute-start | bytes 3145736 | tf_op jit(solution)/shard_map/ppermute | solution.py:353
  75.7 12.6 %project.2 = (bf16[512,4096]{1,0:T(8,128)(2,1)}, bf16[128,4096]{1,0:T(8,128)(2,1)}, bf16[128,4096]{1,0:T(8,128)(2,1)}, bf16[128,4096]{1,0:T(8,128)(2,1)}, bf16[128,4096]{1,0:T(8,128)(2,1)}) custom-call(bf16[512,1024]{1,0:T(8,128)(2,1)} %bitcast.2.refs_0_, bf16[1024,4096]{1,0:T(8,128)(2,1)} %bitcast.13, bf16[32,128,256]{2,1,0:T(8,128)(2,1)} %get-tuple-element.38.refs_2_, ...), custom_call_target="tpu_custom_call" | custom-call | flops 5368709120 | bytes 19922944 | tf_op jit(solution)/shard_map/project/pallas_call | solution.py:36
  88.2 4.2 %payload.6 = (bf16[128,4096]{1,0:T(8,128)(2,1)}, bf16[128,4096]{1,0:T(8,128)(2,1)}) custom-call(bf16[128,4096]{1,0:T(8,128)(2,1)} %collective-permute-done.1.refs_2_.refs_0_.refs_1_, bf16[128,4096]{1,0:T(8,128)(2,1)} %collective-permute-done.2.refs_3_.refs_1_.refs_4_, bf16[128,4096]{1,0:T(8,128)(2,1)} %get-tuple-element.39.refs_2_.refs_3_, ...), custom_call_target="tpu_custom_call" | custom-call | bytes 6291456 | tf_op jit(solution)/shard_map/payload/pallas_call | solution.py:36
  97.1 12.6 %project.3 = (bf16[512,4096]{1,0:T(8,128)(2,1)}, bf16[128,4096]{1,0:T(8,128)(2,1)}, bf16[128,4096]{1,0:T(8,128)(2,1)}, bf16[128,4096]{1,0:T(8,128)(2,1)}, bf16[128,4096]{1,0:T(8,128)(2,1)}) custom-call(bf16[512,1024]{1,0:T(8,128)(2,1)} %bitcast.4.refs_0_.refs_1_, bf16[1024,4096]{1,0:T(8,128)(2,1)} %bitcast.14, ...), custom_call_target="tpu_custom_call" | custom-call | flops 5368709120 | bytes 19922944 | tf_op jit(solution)/shard_map/project/pallas_call | solution.py:36
  109.7 4.2 %payload.7 = (bf16[128,4096]{1,0:T(8,128)(2,1)}, bf16[128,4096]{1,0:T(8,128)(2,1)}) custom-call(bf16[128,4096]{1,0:T(8,128)(2,1)} %collective-permute-done.6.refs_0_.refs_1_, bf16[128,4096]{1,0:T(8,128)(2,1)} %collective-permute-done.7.refs_1_.refs_4_, bf16[128,4096]{1,0:T(8,128)(2,1)} %get-tuple-element.45.refs_2_.refs_3_, ...), custom_call_target="tpu_custom_call" | custom-call | bytes 6291456 | tf_op jit(solution)/shard_map/payload/pallas_call | solution.py:36
  115.2 5.5 %collective-permute-start.10 = (bf16[128,4096]{1,0:T(8,128)(2,1)}, bf16[128,4096]{1,0:T(8,128)(2,1)}, u32[]{:S(2)}, u32[]{:S(2)}) collective-permute-start(bf16[128,4096]{1,0:T(8,128)(2,1)} %get-tuple-element.47.refs_4_), channel_id=1, source_target_pairs={{0,1},{1,2},{2,3},{4,5},{5,6},{6,7},{8,9},{9,10},{10,11},{12,13},{... | collective-permute-start | bytes 3145736 | tf_op jit(solution)/shard_map/ppermute | solution.py:353
  120.7 4.5 %payload.8 = (bf16[128,4096]{1,0:T(8,128)(2,1)}, bf16[128,4096]{1,0:T(8,128)(2,1)}) custom-call(bf16[128,4096]{1,0:T(8,128)(2,1)} %collective-permute-done.4.refs_0_.refs_2_, bf16[128,4096]{1,0:T(8,128)(2,1)} %collective-permute-done.5.refs_1_.refs_5_, bf16[128,4096]{1,0:T(8,128)(2,1)} %get-tuple-element.44.refs_2_.refs_3_, ...), custom_call_target="tpu_custom_call" | custom-call | bytes 6291456 | tf_op jit(solution)/shard_map/payload/pallas_call | solution.py:36
  129.8 11.1 %collective-permute-done.11.refs_1_.refs_5_ = bf16[128,4096]{1,0:T(8,128)(2,1)} collective-permute-done((bf16[128,4096]{1,0:T(8,128)(2,1)}, bf16[128,4096]{1,0:T(8,128)(2,1)}, u32[]{:S(2)}, u32[]{:S(2)}) %collective-permute-start.11) | collective-permute-done | bytes 1048608 | tf_op jit(solution)/shard_map/ppermute | solution.py:354
  140.9 4.5 %payload.9 = (bf16[128,4096]{1,0:T(8,128)(2,1)}, bf16[128,4096]{1,0:T(8,128)(2,1)}) custom-call(bf16[128,4096]{1,0:T(8,128)(2,1)} %collective-permute-done.10.refs_0_.refs_2_, bf16[128,4096]{1,0:T(8,128)(2,1)} %collective-permute-done.11.refs_1_.refs_5_, bf16[128,4096]{1,0:T(8,128)(2,1)} %get-tuple-element.52.refs_2_.refs_3_, ...), custom_call_target="tpu_custom_call" | custom-call | bytes 6291456 | tf_op jit(solution)/shard_map/payload/pallas_call | solution.py:36
  146.8 5.9 %collective-permute-start.12 = (bf16[128,4096]{1,0:T(8,128)(2,1)}, bf16[128,4096]{1,0:T(8,128)(2,1)}, u32[]{:S(2)}, u32[]{:S(2)}) collective-permute-start(bf16[128,4096]{1,0:T(8,128)(2,1)} %get-tuple-element.53.refs_4_), channel_id=1, source_target_pairs={{0,1},{1,2},{2,3},{4,5},{5,6},{6,7},{8,9},{9,10},{10,11},{12,13},{... | collective-permute-start | bytes 3145736 | tf_op jit(solution)/shard_map/ppermute | solution.py:353
  156.7 6.7 %collective-permute-done.9.refs_1_.refs_6_ = bf16[128,4096]{1,0:T(8,128)(2,1)} collective-permute-done((bf16[128,4096]{1,0:T(8,128)(2,1)}, bf16[128,4096]{1,0:T(8,128)(2,1)}, u32[]{:S(2)}, u32[]{:S(2)}) %collective-permute-start.9) | collective-permute-done | bytes 1048608 | tf_op jit(solution)/shard_map/ppermute | solution.py:354
  163.4 4.3 %payload.10 = (bf16[128,4096]{1,0:T(8,128)(2,1)}, bf16[128,4096]{1,0:T(8,128)(2,1)}) custom-call(bf16[128,4096]{1,0:T(8,128)(2,1)} %collective-permute-done.8.refs_0_.refs_3_, bf16[128,4096]{1,0:T(8,128)(2,1)} %collective-permute-done.9.refs_1_.refs_6_, bf16[128,4096]{1,0:T(8,128)(2,1)} %get-tuple-element.40.refs_3_.refs_2_, ...), custom_call_target="tpu_custom_call" | custom-call | bytes 6291456 | tf_op jit(solution)/shard_map/payload/pallas_call | solution.py:36
  167.7 5.4 %collective-permute-start.14 = (bf16[128,4096]{1,0:T(8,128)(2,1)}, bf16[128,4096]{1,0:T(8,128)(2,1)}, u32[]{:S(2)}, u32[]{:S(2)}) collective-permute-start(bf16[128,4096]{1,0:T(8,128)(2,1)} %get-tuple-element.56.refs_4_), channel_id=1, source_target_pairs={{0,1},{1,2},{2,3},{4,5},{5,6},{6,7},{8,9},{9,10},{10,11},{12,13},{... | collective-permute-start | bytes 3145736 | tf_op jit(solution)/shard_map/ppermute | solution.py:353
  174.3 11.5 %collective-permute-done.13.refs_1_.refs_6_ = bf16[128,4096]{1,0:T(8,128)(2,1)} collective-permute-done((bf16[128,4096]{1,0:T(8,128)(2,1)}, bf16[128,4096]{1,0:T(8,128)(2,1)}, u32[]{:S(2)}, u32[]{:S(2)}) %collective-permute-start.13) | collective-permute-done | bytes 1048608 | tf_op jit(solution)/shard_map/ppermute | solution.py:354
  185.9 4.3 %payload.11 = (bf16[128,4096]{1,0:T(8,128)(2,1)}, bf16[128,4096]{1,0:T(8,128)(2,1)}) custom-call(bf16[128,4096]{1,0:T(8,128)(2,1)} %collective-permute-done.12.refs_0_.refs_3_, bf16[128,4096]{1,0:T(8,128)(2,1)} %collective-permute-done.13.refs_1_.refs_6_, bf16[128,4096]{1,0:T(8,128)(2,1)} %get-tuple-element.46.refs_3_.refs_2_, ...), custom_call_target="tpu_custom_call" | custom-call | bytes 6291456 | tf_op jit(solution)/shard_map/payload/pallas_call | solution.py:36
  191.4 6.0 %collective-permute-start.16 = (bf16[128,4096]{1,0:T(8,128)(2,1)}, bf16[128,4096]{1,0:T(8,128)(2,1)}, u32[]{:S(2)}, u32[]{:S(2)}) collective-permute-start(bf16[128,4096]{1,0:T(8,128)(2,1)} %get-tuple-element.58.refs_10_), channel_id=1, source_target_pairs={{0,1},{1,2},{2,3},{4,5},{5,6},{6,7},{8,9},{9,10},{10,11},{12,13},{... | collective-permute-start | bytes 3145736 | tf_op jit(solution)/shard_map/ppermute | solution.py:353
  197.4 16.8 %back.2 = (bf16[512,4096]{1,0:T(8,128)(2,1)}, f32[8,4,128]{2,1,0:T(4,128)}, bf16[512,1024]{1,0:T(8,128)(2,1)}) custom-call(bf16[128,4096]{1,0:T(8,128)(2,1)} %grad_mix.1.refs_4_.refs_0_, bf16[128,4096]{1,0:T(8,128)(2,1)} %collective-permute-done.6.refs_0_.refs_1_, bf16[128,4096]{1,0:T(8,128)(2,1)} %collective-permute-done.10.refs_0_.refs_2_, ...), custom_call_target="tpu_custom_call" | custom-call | flops 6442450944 | bytes 27279360 | tf_op jit(solution)/shard_map/back/pallas_call | solution.py:36
  214.3 4.3 %all-to-all-start.2 = ((bf16[4,128,1024]{2,1,0:T(8,128)(2,1)}), bf16[4,128,1024]{2,1,0:T(8,128)(2,1)}, u32[]{:S(2)}, u32[]{:S(2)}) async-start(bf16[4,128,1024]{2,1,0:T(8,128)(2,1)} %bitcast.22), calls=%async_computation.2 | async-start | bytes 2097152 | tf_op jit(solution)/shard_map/all_to_all | solution.py:346
  218.6 15.1 %collective-permute-done.17.refs_14_.refs_5_ = bf16[128,4096]{1,0:T(8,128)(2,1)} collective-permute-done((bf16[128,4096]{1,0:T(8,128)(2,1)}, bf16[128,4096]{1,0:T(8,128)(2,1)}, u32[]{:S(2)}, u32[]{:S(2)}) %collective-permute-start.17) | collective-permute-done | bytes 1048608 | tf_op jit(solution)/shard_map/ppermute | solution.py:354
  233.6 16.8 %back.3 = (bf16[512,4096]{1,0:T(8,128)(2,1)}, f32[8,4,128]{2,1,0:T(4,128)}, bf16[512,1024]{1,0:T(8,128)(2,1)}) custom-call(bf16[128,4096]{1,0:T(8,128)(2,1)} %get-tuple-element.37.refs_0_, bf16[128,4096]{1,0:T(8,128)(2,1)} %collective-permute-done.1.refs_2_.refs_0_.refs_1_, bf16[128,4096]{1,0:T(8,128)(2,1)} %collective-permute-done.4.refs_0_.refs_2_, ...), custom_call_target="tpu_custom_call" | custom-call | flops 6442450944 | bytes 27279360 | tf_op jit(solution)/shard_map/back/pallas_call | solution.py:36
  250.4 4.7 %all-to-all-done.2.refs_2_ = bf16[4,128,1024]{2,1,0:T(8,128)(2,1)} async-done(((bf16[4,128,1024]{2,1,0:T(8,128)(2,1)}), bf16[4,128,1024]{2,1,0:T(8,128)(2,1)}, u32[]{:S(2)}, u32[]{:S(2)}) %all-to-all-start.2) | async-done | bytes 1048608 | tf_op jit(solution)/shard_map/all_to_all | solution.py:346
  255.1 4.2 %all-to-all-start.3 = ((bf16[4,128,1024]{2,1,0:T(8,128)(2,1)}), bf16[4,128,1024]{2,1,0:T(8,128)(2,1)}, u32[]{:S(2)}, u32[]{:S(2)}) async-start(bf16[4,128,1024]{2,1,0:T(8,128)(2,1)} %bitcast.21), calls=%async_computation.3 | async-start | bytes 2097152 | tf_op jit(solution)/shard_map/all_to_all | solution.py:346
  262.1 5.1 %finish.2.refs_4_ = bf16[1,128,4096]{2,1,0:T(8,128)(2,1)} custom-call(bf16[128,4096]{1,0:T(8,128)(2,1)} %collective-permute-done.refs_0_, bf16[128,4096]{1,0:T(8,128)(2,1)} %collective-permute-done.3.refs_1_, bf16[4,128,1024]{2,1,0:T(8,128)(2,1)} %all-to-all-done.2.refs_2_, bf16[128,4096]{1,0:T(8,128)(2,1)} %get-tuple-element.63.refs_3_, ...), custom_call_target="tpu_custom_call" | custom-call | bytes 7340032 | tf_op jit(solution)/shard_map/finish/pallas_call | solution.py:36
  267.3 14.7 %weight_gradient.1.refs_2_ = bf16[1024,4096]{1,0:T(8,128)(2,1)} custom-call(bf16[512,1024]{1,0:T(8,128)(2,1)} %bitcast.2.refs_0_, bf16[512,1024]{1,0:T(8,128)(2,1)} %bitcast.4.refs_0_.refs_1_, bf16[512,4096]{1,0:T(8,128)(2,1)} %get-tuple-element.61.refs_6_.refs_2_, bf16[512,4096]{1,0:T(8,128)(2,1)} %get-tuple-element.59.refs_10_.refs_3_, ...), custom_call_target="tpu_custom_call" | custom-call | flops 8589934592 | bytes 18874368 | tf_op jit(solution)/shard_map/weight_gradient/pallas_call | solution.py:36
  291.1 5.2 %finish.3 = bf16[1,128,4096]{2,1,0:T(8,128)(2,1)} custom-call(bf16[128,4096]{1,0:T(8,128)(2,1)} %bitcast.18, bf16[128,4096]{1,0:T(8,128)(2,1)} %bitcast.20, bf16[4,128,1024]{2,1,0:T(8,128)(2,1)} %all-to-all-done.3.refs_2_, bf16[128,4096]{1,0:T(8,128)(2,1)} %get-tuple-element.67.refs_3_, bf16[128,4096]{1,0:T(8,128)(2,1)} %collective-permute-done.14.refs_11_.refs_4_, ...), custom_call_target="tpu_custom_call" | custom-call | bytes 7340032 | tf_op jit(solution)/shard_map/finish/pallas_call | solution.py:36
  296.2 17.6 %collective-permute-start.20 = (bf16[1,128,4096]{2,1,0:T(8,128)(2,1)}, bf16[1,128,4096]{2,1,0:T(8,128)(2,1)S(1)}, u32[]{:S(2)}, u32[]{:S(2)}) collective-permute-start(bf16[1,128,4096]{2,1,0:T(8,128)(2,1)} %finish.3), channel_id=1, source_target_pairs={{4,0},{8,4},{12,8},{16,12},{20,16},{24,20},{28,24},{5,1},{9,5},{13... | collective-permute-start | bytes 3145736 | tf_op jit(solution)/shard_map/ppermute | solution.py:470
  313.9 19.8 %collective-permute-done.20 = bf16[1,128,4096]{2,1,0:T(8,128)(2,1)S(1)} collective-permute-done((bf16[1,128,4096]{2,1,0:T(8,128)(2,1)}, bf16[1,128,4096]{2,1,0:T(8,128)(2,1)S(1)}, u32[]{:S(2)}, u32[]{:S(2)}) %collective-permute-start.20) | collective-permute-done | bytes 1048608 | tf_op jit(solution)/shard_map/ppermute | solution.py:470
  (46 shorter events, 54.2 us)
Async XLA Ops:
  4.7 35.0 %all-to-all-start = ((bf16[4,128,1024]{2,1,0:T(8,128)(2,1)}), bf16[4,128,1024]{2,1,0:T(8,128)(2,1)}, u32[]{:S(2)}, u32[]{:S(2)}) async-start(bf16[4,128,1024]{2,1,0:T(8,128)(2,1)} %get-tuple-element.36), calls=%async_computation | async-start | bytes 2097152 | tf_op jit(solution)/shard_map/all_to_all | solution.py:346
  9.3 26.7 %collective-permute-start = (bf16[128,4096]{1,0:T(8,128)(2,1)}, bf16[128,4096]{1,0:T(8,128)(2,1)}, u32[]{:S(2)}, u32[]{:S(2)}) collective-permute-start(bf16[128,4096]{1,0:T(8,128)(2,1)} %bitcast.26), channel_id=1, source_target_pairs={{0,28},{4,24},{8,20},{12,16},{16,12},{20,8},{24,4},{28,0},{1,29},{... | collective-permute-start | bytes 3145736 | tf_op jit(solution)/shard_map/ppermute | solution.py:432
  11.4 47.1 %collective-permute-start.3 = (bf16[128,4096]{1,0:T(8,128)(2,1)}, bf16[128,4096]{1,0:T(8,128)(2,1)}, u32[]{:S(2)}, u32[]{:S(2)}) collective-permute-start(bf16[128,4096]{1,0:T(8,128)(2,1)} %bitcast.27), channel_id=1, source_target_pairs={{0,28},{4,24},{8,20},{12,16},{16,12},{20,8},{24,4},{28,0},{1,29},{... | collective-permute-start | bytes 3145736 | tf_op jit(solution)/shard_map/ppermute | solution.py:433
  12.0 46.5 %collective-permute-start.2 = (bf16[128,4096]{1,0:T(8,128)(2,1)}, bf16[128,4096]{1,0:T(8,128)(2,1)}, u32[]{:S(2)}, u32[]{:S(2)}) collective-permute-start(bf16[128,4096]{1,0:T(8,128)(2,1)} %get-tuple-element.37.refs_0_), channel_id=1, source_target_pairs={{1,0},{2,1},{3,2},{5,4},{6,5},{7,6},{9,8},{10,9},{11,10},{13,12},{... | collective-permute-start | bytes 3145736 | tf_op jit(solution)/shard_map/ppermute | solution.py:354
  13.2 45.2 %collective-permute-start.1 = (bf16[128,4096]{1,0:T(8,128)(2,1)}, bf16[128,4096]{1,0:T(8,128)(2,1)}, u32[]{:S(2)}, u32[]{:S(2)}) collective-permute-start(bf16[128,4096]{1,0:T(8,128)(2,1)} %get-tuple-element.37.refs_0_), channel_id=1, source_target_pairs={{0,1},{1,2},{2,3},{4,5},{5,6},{6,7},{8,9},{9,10},{10,11},{12,13},{... | collective-permute-start | bytes 3145736 | tf_op jit(solution)/shard_map/ppermute | solution.py:353
  39.7 57.4 %all-to-all-start.1 = ((bf16[4,128,1024]{2,1,0:T(8,128)(2,1)}), bf16[4,128,1024]{2,1,0:T(8,128)(2,1)}, u32[]{:S(2)}, u32[]{:S(2)}) async-start(bf16[4,128,1024]{2,1,0:T(8,128)(2,1)} %prepare.3.refs_3_), calls=%async_computation.1 | async-start | bytes 2097152 | tf_op jit(solution)/shard_map/all_to_all | solution.py:346
  62.4 47.3 %collective-permute-start.7 = (bf16[128,4096]{1,0:T(8,128)(2,1)}, bf16[128,4096]{1,0:T(8,128)(2,1)}, u32[]{:S(2)}, u32[]{:S(2)}) collective-permute-start(bf16[128,4096]{1,0:T(8,128)(2,1)} %grad_mix.1.refs_4_.refs_0_), channel_id=1, source_target_pairs={{1,0},{2,1},{3,2},{5,4},{6,5},{7,6},{9,8},{10,9},{11,10},{13,12},{... | collective-permute-start | bytes 3145736 | tf_op jit(solution)/shard_map/ppermute | solution.py:354
  63.6 46.0 %collective-permute-start.6 = (bf16[128,4096]{1,0:T(8,128)(2,1)}, bf16[128,4096]{1,0:T(8,128)(2,1)}, u32[]{:S(2)}, u32[]{:S(2)}) collective-permute-start(bf16[128,4096]{1,0:T(8,128)(2,1)} %grad_mix.1.refs_4_.refs_0_), channel_id=1, source_target_pairs={{0,1},{1,2},{2,3},{4,5},{5,6},{6,7},{8,9},{9,10},{10,11},{12,13},{... | collective-permute-start | bytes 3145736 | tf_op jit(solution)/shard_map/ppermute | solution.py:353
  92.5 28.2 %collective-permute-start.4 = (bf16[128,4096]{1,0:T(8,128)(2,1)}, bf16[128,4096]{1,0:T(8,128)(2,1)}, u32[]{:S(2)}, u32[]{:S(2)}) collective-permute-start(bf16[128,4096]{1,0:T(8,128)(2,1)} %get-tuple-element.42.refs_3_.refs_4_), channel_id=1, source_target_pairs={{0,1},{1,2},{2,3},{4,5},{5,6},{6,7},{8,9},{9,10},{10,11},{12,13},{... | collective-permute-start | bytes 3145736 | tf_op jit(solution)/shard_map/ppermute | solution.py:353
  95.8 24.9 %collective-permute-start.5 = (bf16[128,4096]{1,0:T(8,128)(2,1)}, bf16[128,4096]{1,0:T(8,128)(2,1)}, u32[]{:S(2)}, u32[]{:S(2)}) collective-permute-start(bf16[128,4096]{1,0:T(8,128)(2,1)} %get-tuple-element.43.refs_4_.refs_5_), channel_id=1, source_target_pairs={{1,0},{2,1},{3,2},{5,4},{6,5},{7,6},{9,8},{10,9},{11,10},{13,12},{... | collective-permute-start | bytes 3145736 | tf_op jit(solution)/shard_map/ppermute | solution.py:354
  113.9 27.0 %collective-permute-start.11 = (bf16[128,4096]{1,0:T(8,128)(2,1)}, bf16[128,4096]{1,0:T(8,128)(2,1)}, u32[]{:S(2)}, u32[]{:S(2)}) collective-permute-start(bf16[128,4096]{1,0:T(8,128)(2,1)} %get-tuple-element.51), channel_id=1, source_target_pairs={{1,0},{2,1},{3,2},{5,4},{6,5},{7,6},{9,8},{10,9},{11,10},{13,12},{... | collective-permute-start | bytes 3145736 | tf_op jit(solution)/shard_map/ppermute | solution.py:354
  115.2 25.7 %collective-permute-start.10 = (bf16[128,4096]{1,0:T(8,128)(2,1)}, bf16[128,4096]{1,0:T(8,128)(2,1)}, u32[]{:S(2)}, u32[]{:S(2)}) collective-permute-start(bf16[128,4096]{1,0:T(8,128)(2,1)} %get-tuple-element.47.refs_4_), channel_id=1, source_target_pairs={{0,1},{1,2},{2,3},{4,5},{5,6},{6,7},{8,9},{9,10},{10,11},{12,13},{... | collective-permute-start | bytes 3145736 | tf_op jit(solution)/shard_map/ppermute | solution.py:353
  125.2 31.6 %collective-permute-start.8 = (bf16[128,4096]{1,0:T(8,128)(2,1)}, bf16[128,4096]{1,0:T(8,128)(2,1)}, u32[]{:S(2)}, u32[]{:S(2)}) collective-permute-start(bf16[128,4096]{1,0:T(8,128)(2,1)} %get-tuple-element.48.refs_4_), channel_id=1, source_target_pairs={{0,1},{1,2},{2,3},{4,5},{5,6},{6,7},{8,9},{9,10},{10,11},{12,13},{... | collective-permute-start | bytes 3145736 | tf_op jit(solution)/shard_map/ppermute | solution.py:353
  128.6 34.8 %collective-permute-start.9 = (bf16[128,4096]{1,0:T(8,128)(2,1)}, bf16[128,4096]{1,0:T(8,128)(2,1)}, u32[]{:S(2)}, u32[]{:S(2)}) collective-permute-start(bf16[128,4096]{1,0:T(8,128)(2,1)} %get-tuple-element.49.refs_5_), channel_id=1, source_target_pairs={{1,0},{2,1},{3,2},{5,4},{6,5},{7,6},{9,8},{10,9},{11,10},{13,12},{... | collective-permute-start | bytes 3145736 | tf_op jit(solution)/shard_map/ppermute | solution.py:354
  145.5 40.4 %collective-permute-start.13 = (bf16[128,4096]{1,0:T(8,128)(2,1)}, bf16[128,4096]{1,0:T(8,128)(2,1)}, u32[]{:S(2)}, u32[]{:S(2)}) collective-permute-start(bf16[128,4096]{1,0:T(8,128)(2,1)} %get-tuple-element.54), channel_id=1, source_target_pairs={{1,0},{2,1},{3,2},{5,4},{6,5},{7,6},{9,8},{10,9},{11,10},{13,12},{... | collective-permute-start | bytes 3145736 | tf_op jit(solution)/shard_map/ppermute | solution.py:354
  146.8 39.1 %collective-permute-start.12 = (bf16[128,4096]{1,0:T(8,128)(2,1)}, bf16[128,4096]{1,0:T(8,128)(2,1)}, u32[]{:S(2)}, u32[]{:S(2)}) collective-permute-start(bf16[128,4096]{1,0:T(8,128)(2,1)} %get-tuple-element.53.refs_4_), channel_id=1, source_target_pairs={{0,1},{1,2},{2,3},{4,5},{5,6},{6,7},{8,9},{9,10},{10,11},{12,13},{... | collective-permute-start | bytes 3145736 | tf_op jit(solution)/shard_map/ppermute | solution.py:353
  167.7 50.9 %collective-permute-start.14 = (bf16[128,4096]{1,0:T(8,128)(2,1)}, bf16[128,4096]{1,0:T(8,128)(2,1)}, u32[]{:S(2)}, u32[]{:S(2)}) collective-permute-start(bf16[128,4096]{1,0:T(8,128)(2,1)} %get-tuple-element.56.refs_4_), channel_id=1, source_target_pairs={{0,1},{1,2},{2,3},{4,5},{5,6},{6,7},{8,9},{9,10},{10,11},{12,13},{... | collective-permute-start | bytes 3145736 | tf_op jit(solution)/shard_map/ppermute | solution.py:353
  173.1 45.5 %collective-permute-start.15 = (bf16[128,4096]{1,0:T(8,128)(2,1)}, bf16[128,4096]{1,0:T(8,128)(2,1)}, u32[]{:S(2)}, u32[]{:S(2)}) collective-permute-start(bf16[128,4096]{1,0:T(8,128)(2,1)} %get-tuple-element.57.refs_5_), channel_id=1, source_target_pairs={{1,0},{2,1},{3,2},{5,4},{6,5},{7,6},{9,8},{10,9},{11,10},{13,12},{... | collective-permute-start | bytes 3145736 | tf_op jit(solution)/shard_map/ppermute | solution.py:354
  190.2 43.5 %collective-permute-start.17 = (bf16[128,4096]{1,0:T(8,128)(2,1)}, bf16[128,4096]{1,0:T(8,128)(2,1)}, u32[]{:S(2)}, u32[]{:S(2)}) collective-permute-start(bf16[128,4096]{1,0:T(8,128)(2,1)} %get-tuple-element.60), channel_id=1, source_target_pairs={{1,0},{2,1},{3,2},{5,4},{6,5},{7,6},{9,8},{10,9},{11,10},{13,12},{... | collective-permute-start | bytes 3145736 | tf_op jit(solution)/shard_map/ppermute | solution.py:354
  191.4 42.2 %collective-permute-start.16 = (bf16[128,4096]{1,0:T(8,128)(2,1)}, bf16[128,4096]{1,0:T(8,128)(2,1)}, u32[]{:S(2)}, u32[]{:S(2)}) collective-permute-start(bf16[128,4096]{1,0:T(8,128)(2,1)} %get-tuple-element.58.refs_10_), channel_id=1, source_target_pairs={{0,1},{1,2},{2,3},{4,5},{5,6},{6,7},{8,9},{9,10},{10,11},{12,13},{... | collective-permute-start | bytes 3145736 | tf_op jit(solution)/shard_map/ppermute | solution.py:353
  214.3 40.8 %all-to-all-start.2 = ((bf16[4,128,1024]{2,1,0:T(8,128)(2,1)}), bf16[4,128,1024]{2,1,0:T(8,128)(2,1)}, u32[]{:S(2)}, u32[]{:S(2)}) async-start(bf16[4,128,1024]{2,1,0:T(8,128)(2,1)} %bitcast.22), calls=%async_computation.2 | async-start | bytes 2097152 | tf_op jit(solution)/shard_map/all_to_all | solution.py:346
  255.1 36.0 %all-to-all-start.3 = ((bf16[4,128,1024]{2,1,0:T(8,128)(2,1)}), bf16[4,128,1024]{2,1,0:T(8,128)(2,1)}, u32[]{:S(2)}, u32[]{:S(2)}) async-start(bf16[4,128,1024]{2,1,0:T(8,128)(2,1)} %bitcast.21), calls=%async_computation.3 | async-start | bytes 2097152 | tf_op jit(solution)/shard_map/all_to_all | solution.py:346
  260.7 21.3 %collective-permute-start.18 = (f32[1,32,128]{2,1,0:T(8,128)}, f32[1,32,128]{2,1,0:T(8,128)S(1)}, u32[]{:S(2)}, u32[]{:S(2)}) collective-permute-start(f32[1,32,128]{2,1,0:T(8,128)} %bitcast.23), channel_id=1, source_target_pairs={{0,1},{1,0},{2,3},{3,2},{4,5},{5,4},{6,7},{7,6},{8,9},{9,8},{10,11... | collective-permute-start | bytes 49160 | tf_op jit(solution)/shard_map/ppermute | solution.py:419
  282.0 0.6 copy-start
  283.9 5.2 %collective-permute-start.19 = (f32[1,32,128]{2,1,0:T(8,128)}, f32[1,32,128]{2,1,0:T(8,128)S(1)}, u32[]{:S(2)}, u32[]{:S(2)}) collective-permute-start(f32[1,32,128]{2,1,0:T(8,128)} %add.4.refs_0_), channel_id=1, source_target_pairs={{0,2},{1,3},{2,0},{3,1},{4,6},{5,7},{6,4},{7,5},{8,10},{9,11},{10,... | collective-permute-start | bytes 49160 | tf_op jit(solution)/shard_map/ppermute | solution.py:419
  286.0 27.9 %collective-permute-start.21 = (bf16[1,128,4096]{2,1,0:T(8,128)(2,1)}, bf16[1,128,4096]{2,1,0:T(8,128)(2,1)}, u32[]{:S(2)}, u32[]{:S(2)}) collective-permute-start(bf16[1,128,4096]{2,1,0:T(8,128)(2,1)} %finish.2.refs_4_), channel_id=1, source_target_pairs={{28,4},{24,8},{20,12},{16,16},{12,20},{8,24},{4,28},{29,5},{25,9},... | collective-permute-start | bytes 3145736 | tf_op jit(solution)/shard_map/ppermute | solution.py:463
  289.1 0.6 copy-start.1
  296.2 37.4 %collective-permute-start.20 = (bf16[1,128,4096]{2,1,0:T(8,128)(2,1)}, bf16[1,128,4096]{2,1,0:T(8,128)(2,1)S(1)}, u32[]{:S(2)}, u32[]{:S(2)}) collective-permute-start(bf16[1,128,4096]{2,1,0:T(8,128)(2,1)} %finish.3), channel_id=1, source_target_pairs={{4,0},{8,4},{12,8},{16,12},{20,16},{24,20},{28,24},{5,1},{9,5},{13... | collective-permute-start | bytes 3145736 | tf_op jit(solution)/shard_map/ppermute | solution.py:470

commit v3 on v2

--- a/solution.py
+++ b/solution.py
@@ -20,14 +20,8 @@
     return jax.ShapeDtypeStruct(dims, dtype)
 
 
-def call(kernel, args, after, in_specs, out_shape, flops=0, **options):
+def call(kernel, args, after, in_specs, **options):
     count = len(args)
-    arrays = [*args, *(out_shape if isinstance(out_shape, list) else [out_shape])]
-    cost = pl.CostEstimate(
-        flops=flops,
-        transcendentals=0,
-        bytes_accessed=sum(x.size * x.dtype.itemsize for x in arrays),
-    )
 
     def body(*refs):
         kernel(*refs[:count], *refs[count + len(after) :])
@@ -36,8 +30,7 @@
     return pl.pallas_call(
         body,
         in_specs=list(in_specs) + unread,
-        out_shape=out_shape,
-        cost_estimate=cost,
+        cost_estimate=pl.CostEstimate(flops=0, transcendentals=0, bytes_accessed=0),
         compiler_params=params(),
         **options,
     )(*args, *after)
@@ -179,7 +172,6 @@
         + [pl.BlockSpec((rows, tile), lambda i: (0, i))] * blocks,
         out_shape=[shape((tokens, width), bf16)] + [shape((rows, width), bf16)] * blocks,
         scratch_shapes=[pltpu.VMEM((tokens, tile), bf16)],
-        flops=2 * tokens * width * (depth + 2 * taps),
         name="project",
     )
     return part, mixed
@@ -277,7 +269,6 @@
             shape((tokens, depth), bf16),
         ],
         scratch_shapes=[pltpu.VMEM((tokens, tile), bf16), pltpu.VMEM((tokens, depth), f32)],
-        flops=2 * tokens * width * (depth + 4 * taps),
         name="back",
     )
 
@@ -306,7 +297,6 @@
         out_specs=pl.BlockSpec((depth, tile), lambda i: (0, i)),
         out_shape=shape((depth, width), bf16),
         scratch_shapes=[pltpu.VMEM((depth, tokens), bf16)] * 2,
-        flops=4 * tokens * depth * width,
         name="weight_gradient",
     )
 
@@ -456,7 +446,7 @@
     up_g, up_taps, up_back = back(up_mixes, up_part, weight, ahead, after=(last,))
     up_back = exchange(up_back)
     down_g, down_taps, down_back = back(
-        down_mixes, down_part, weight, ahead, after=(up_g, *down_arrivals[-1], *up_arrivals[-1])
+        down_mixes, down_part, weight, ahead, after=(up_g,)
     )
     down_back = exchange(down_back)
     up_grad = finish(up_xin, up_cot, up_conv, up_back, after=(down_g,))

time: 341 us -> 354 us (1.038)
  the two profiles are of different devices: /device:TPU:3 before, /device:TPU:10 now
where the time goes in v3:
time: 354 us; the launch traced here: 350 us
  waiting for transfers between devices  136 us (38%)
  Pallas kernels  129 us (36%)
  starting transfers between devices  79.7 us (23%)
  local copies, waits for them, and re-layouts  4.46 us (1%)
    pallas_call x20, Pallas kernels, call(): pl.pallas_call(body, in_specs=list(in_specs) + unread, cost_estimate=pl.C...  129 us
    ppermute x8, waiting for transfers between devices, both_ways(): lax.ppermute(left, 'tensor', [(j, i) for i, j in onward])  63.1 us
    ppermute x8, starting transfers between devices, both_ways(): lax.ppermute(right, 'tensor', onward)  33.4 us
    ppermute x1, waiting for transfers between devices, per_device(): up_passed = lax.ppermute(up_grad, 'section', up_pairs)  23.5 us
    all_to_all x4, starting transfers between devices, exchange(): return lax.all_to_all(x, 'tensor', split_axis=0, concat_axis=0, tiled=True)  21.1 us
    ppermute x1, waiting for transfers between devices, per_device(): up_xin = lax.ppermute(up_input[0], 'section', mirror)  18.1 us
    ppermute x8, starting transfers between devices, both_ways(): lax.ppermute(left, 'tensor', [(j, i) for i, j in onward])  17.2 us
    ppermute x8, waiting for transfers between devices, both_ways(): lax.ppermute(right, 'tensor', onward)  14.9 us
  transfers between devices with their start and end apart: 26, of which 13 were waited for; matrix products, arithmetic and copies ran while one was open for 0% of the time, Pallas kernels for 30%

profile of v3, /device:TPU:10, one launch (start us, length us, event | category | flops | bytes accessed | tf_op | source)
XLA Modules:
  0.0 349.9 jit_solution(1362974111517087736)
XLA Ops:
  0.6 4.1 %prepare.2 = (bf16[4,128,1024]{2,1,0:T(8,128)(2,1)}, bf16[128,4096]{1,0:T(8,128)(2,1)}) custom-call(bf16[128,4096]{1,0:T(8,128)(2,1)} %bitcast.17, bf16[128,4096]{1,0:T(8,128)(2,1)} %bitcast.19), custom_call_target="tpu_custom_call" | custom-call | tf_op jit(solution)/shard_map/prepare/pallas_call | solution.py:30
  4.7 5.3 %all-to-all-start = ((bf16[4,128,1024]{2,1,0:T(8,128)(2,1)}), bf16[4,128,1024]{2,1,0:T(8,128)(2,1)}, u32[]{:S(2)}, u32[]{:S(2)}) async-start(bf16[4,128,1024]{2,1,0:T(8,128)(2,1)} %get-tuple-element.36), calls=%async_computation | async-start | bytes 2097152 | tf_op jit(solution)/shard_map/all_to_all | solution.py:336
  14.6 3.9 %collective-permute-start.1 = (bf16[128,4096]{1,0:T(8,128)(2,1)}, bf16[128,4096]{1,0:T(8,128)(2,1)}, u32[]{:S(2)}, u32[]{:S(2)}) collective-permute-start(bf16[128,4096]{1,0:T(8,128)(2,1)} %get-tuple-element.37.refs_0_), channel_id=1, source_target_pairs={{0,1},{1,2},{2,3},{4,5},{5,6},{6,7},{8,9},{9,10},{10,11},{12,13},{... | collective-permute-start | bytes 3145736 | tf_op jit(solution)/shard_map/ppermute | solution.py:343
  18.5 18.1 %collective-permute-done.refs_0_ = bf16[128,4096]{1,0:T(8,128)(2,1)} collective-permute-done((bf16[128,4096]{1,0:T(8,128)(2,1)}, bf16[128,4096]{1,0:T(8,128)(2,1)}, u32[]{:S(2)}, u32[]{:S(2)}) %collective-permute-start) | collective-permute-done | bytes 1048608 | tf_op jit(solution)/shard_map/ppermute | solution.py:422
  40.3 5.1 %all-to-all-start.1 = ((bf16[4,128,1024]{2,1,0:T(8,128)(2,1)}), bf16[4,128,1024]{2,1,0:T(8,128)(2,1)}, u32[]{:S(2)}, u32[]{:S(2)}) async-start(bf16[4,128,1024]{2,1,0:T(8,128)(2,1)} %prepare.3.refs_3_), calls=%async_computation.1 | async-start | bytes 2097152 | tf_op jit(solution)/shard_map/all_to_all | solution.py:336
  45.4 13.2 %collective-permute-done.3.refs_1_ = bf16[128,4096]{1,0:T(8,128)(2,1)} collective-permute-done((bf16[128,4096]{1,0:T(8,128)(2,1)}, bf16[128,4096]{1,0:T(8,128)(2,1)}, u32[]{:S(2)}, u32[]{:S(2)}) %collective-permute-start.3) | collective-permute-done | bytes 1048608 | tf_op jit(solution)/shard_map/ppermute | solution.py:423
  58.6 6.4 %collective-permute-done.2.refs_3_.refs_1_.refs_4_ = bf16[128,4096]{1,0:T(8,128)(2,1)} collective-permute-done((bf16[128,4096]{1,0:T(8,128)(2,1)}, bf16[128,4096]{1,0:T(8,128)(2,1)}, u32[]{:S(2)}, u32[]{:S(2)}) %collective-permute-start.2) | collective-permute-done | bytes 1048608 | tf_op jit(solution)/shard_map/ppermute | solution.py:344
  73.5 4.4 %collective-permute-start.6 = (bf16[128,4096]{1,0:T(8,128)(2,1)}, bf16[128,4096]{1,0:T(8,128)(2,1)}, u32[]{:S(2)}, u32[]{:S(2)}) collective-permute-start(bf16[128,4096]{1,0:T(8,128)(2,1)} %grad_mix.1.refs_4_.refs_0_), channel_id=1, source_target_pairs={{0,1},{1,2},{2,3},{4,5},{5,6},{6,7},{8,9},{9,10},{10,11},{12,13},{... | collective-permute-start | bytes 3145736 | tf_op jit(solution)/shard_map/ppermute | solution.py:343
  81.8 12.6 %project.2 = (bf16[512,4096]{1,0:T(8,128)(2,1)}, bf16[128,4096]{1,0:T(8,128)(2,1)}, bf16[128,4096]{1,0:T(8,128)(2,1)}, bf16[128,4096]{1,0:T(8,128)(2,1)}, bf16[128,4096]{1,0:T(8,128)(2,1)}) custom-call(bf16[512,1024]{1,0:T(8,128)(2,1)} %bitcast.2.refs_0_, bf16[1024,4096]{1,0:T(8,128)(2,1)} %bitcast.12, bf16[32,128,256]{2,1,0:T(8,128)(2,1)} %get-tuple-element.38.refs_2_, ...), custom_call_target="tpu_custom_call" | custom-call | tf_op jit(solution)/shard_map/project/pallas_call | solution.py:30
  94.4 4.1 %payload.6 = (bf16[128,4096]{1,0:T(8,128)(2,1)}, bf16[128,4096]{1,0:T(8,128)(2,1)}) custom-call(bf16[128,4096]{1,0:T(8,128)(2,1)} %collective-permute-done.1.refs_2_.refs_0_.refs_1_, bf16[128,4096]{1,0:T(8,128)(2,1)} %collective-permute-done.2.refs_3_.refs_1_.refs_4_, bf16[128,4096]{1,0:T(8,128)(2,1)} %get-tuple-element.39.refs_2_.refs_3_, ...), custom_call_target="tpu_custom_call" | custom-call | tf_op jit(solution)/shard_map/payload/pallas_call | solution.py:30
  98.5 5.0 %collective-permute-start.4 = (bf16[128,4096]{1,0:T(8,128)(2,1)}, bf16[128,4096]{1,0:T(8,128)(2,1)}, u32[]{:S(2)}, u32[]{:S(2)}) collective-permute-start(bf16[128,4096]{1,0:T(8,128)(2,1)} %get-tuple-element.42.refs_3_.refs_4_), channel_id=1, source_target_pairs={{0,1},{1,2},{2,3},{4,5},{5,6},{6,7},{8,9},{9,10},{10,11},{12,13},{... | collective-permute-start | bytes 3145736 | tf_op jit(solution)/shard_map/ppermute | solution.py:343
  105.4 12.7 %project.3 = (bf16[512,4096]{1,0:T(8,128)(2,1)}, bf16[128,4096]{1,0:T(8,128)(2,1)}, bf16[128,4096]{1,0:T(8,128)(2,1)}, bf16[128,4096]{1,0:T(8,128)(2,1)}, bf16[128,4096]{1,0:T(8,128)(2,1)}) custom-call(bf16[512,1024]{1,0:T(8,128)(2,1)} %bitcast.4.refs_0_.refs_1_, bf16[1024,4096]{1,0:T(8,128)(2,1)} %bitcast.13, ...), custom_call_target="tpu_custom_call" | custom-call | tf_op jit(solution)/shard_map/project/pallas_call | solution.py:30
  118.1 4.1 %payload.7 = (bf16[128,4096]{1,0:T(8,128)(2,1)}, bf16[128,4096]{1,0:T(8,128)(2,1)}) custom-call(bf16[128,4096]{1,0:T(8,128)(2,1)} %collective-permute-done.6.refs_0_.refs_1_, bf16[128,4096]{1,0:T(8,128)(2,1)} %collective-permute-done.7.refs_1_.refs_4_, bf16[128,4096]{1,0:T(8,128)(2,1)} %get-tuple-element.45.refs_2_.refs_3_, ...), custom_call_target="tpu_custom_call" | custom-call | tf_op jit(solution)/shard_map/payload/pallas_call | solution.py:30
  124.1 3.9 %collective-permute-start.10 = (bf16[128,4096]{1,0:T(8,128)(2,1)}, bf16[128,4096]{1,0:T(8,128)(2,1)}, u32[]{:S(2)}, u32[]{:S(2)}) collective-permute-start(bf16[128,4096]{1,0:T(8,128)(2,1)} %get-tuple-element.47.refs_4_), channel_id=1, source_target_pairs={{0,1},{1,2},{2,3},{4,5},{5,6},{6,7},{8,9},{9,10},{10,11},{12,13},{... | collective-permute-start | bytes 3145736 | tf_op jit(solution)/shard_map/ppermute | solution.py:343
  129.4 4.4 %payload.8 = (bf16[128,4096]{1,0:T(8,128)(2,1)}, bf16[128,4096]{1,0:T(8,128)(2,1)}) custom-call(bf16[128,4096]{1,0:T(8,128)(2,1)} %collective-permute-done.4.refs_0_.refs_2_, bf16[128,4096]{1,0:T(8,128)(2,1)} %collective-permute-done.5.refs_1_.refs_5_, bf16[128,4096]{1,0:T(8,128)(2,1)} %get-tuple-element.44.refs_2_.refs_3_, ...), custom_call_target="tpu_custom_call" | custom-call | tf_op jit(solution)/shard_map/payload/pallas_call | solution.py:30
  140.7 11.2 %collective-permute-done.11.refs_1_.refs_5_ = bf16[128,4096]{1,0:T(8,128)(2,1)} collective-permute-done((bf16[128,4096]{1,0:T(8,128)(2,1)}, bf16[128,4096]{1,0:T(8,128)(2,1)}, u32[]{:S(2)}, u32[]{:S(2)}) %collective-permute-start.11) | collective-permute-done | bytes 1048608 | tf_op jit(solution)/shard_map/ppermute | solution.py:344
  152.5 4.5 %payload.9 = (bf16[128,4096]{1,0:T(8,128)(2,1)}, bf16[128,4096]{1,0:T(8,128)(2,1)}) custom-call(bf16[128,4096]{1,0:T(8,128)(2,1)} %collective-permute-done.10.refs_0_.refs_2_, bf16[128,4096]{1,0:T(8,128)(2,1)} %collective-permute-done.11.refs_1_.refs_5_, bf16[128,4096]{1,0:T(8,128)(2,1)} %get-tuple-element.52.refs_2_.refs_3_, ...), custom_call_target="tpu_custom_call" | custom-call | tf_op jit(solution)/shard_map/payload/pallas_call | solution.py:30
  158.9 4.4 %collective-permute-start.12 = (bf16[128,4096]{1,0:T(8,128)(2,1)}, bf16[128,4096]{1,0:T(8,128)(2,1)}, u32[]{:S(2)}, u32[]{:S(2)}) collective-permute-start(bf16[128,4096]{1,0:T(8,128)(2,1)} %get-tuple-element.53.refs_4_), channel_id=1, source_target_pairs={{0,1},{1,2},{2,3},{4,5},{5,6},{6,7},{8,9},{9,10},{10,11},{12,13},{... | collective-permute-start | bytes 3145736 | tf_op jit(solution)/shard_map/ppermute | solution.py:343
  163.3 11.7 %collective-permute-done.8.refs_0_.refs_3_ = bf16[128,4096]{1,0:T(8,128)(2,1)} collective-permute-done((bf16[128,4096]{1,0:T(8,128)(2,1)}, bf16[128,4096]{1,0:T(8,128)(2,1)}, u32[]{:S(2)}, u32[]{:S(2)}) %collective-permute-start.8) | collective-permute-done | bytes 1048608 | tf_op jit(solution)/shard_map/ppermute | solution.py:343
  174.9 4.3 %payload.10 = (bf16[128,4096]{1,0:T(8,128)(2,1)}, bf16[128,4096]{1,0:T(8,128)(2,1)}) custom-call(bf16[128,4096]{1,0:T(8,128)(2,1)} %collective-permute-done.8.refs_0_.refs_3_, bf16[128,4096]{1,0:T(8,128)(2,1)} %collective-permute-done.9.refs_1_.refs_6_, bf16[128,4096]{1,0:T(8,128)(2,1)} %get-tuple-element.40.refs_3_.refs_2_, ...), custom_call_target="tpu_custom_call" | custom-call | tf_op jit(solution)/shard_map/payload/pallas_call | solution.py:30
  179.2 12.5 %collective-permute-done.13.refs_1_.refs_6_ = bf16[128,4096]{1,0:T(8,128)(2,1)} collective-permute-done((bf16[128,4096]{1,0:T(8,128)(2,1)}, bf16[128,4096]{1,0:T(8,128)(2,1)}, u32[]{:S(2)}, u32[]{:S(2)}) %collective-permute-start.13) | collective-permute-done | bytes 1048608 | tf_op jit(solution)/shard_map/ppermute | solution.py:344
  191.8 4.3 %payload.11 = (bf16[128,4096]{1,0:T(8,128)(2,1)}, bf16[128,4096]{1,0:T(8,128)(2,1)}) custom-call(bf16[128,4096]{1,0:T(8,128)(2,1)} %collective-permute-done.12.refs_0_.refs_3_, bf16[128,4096]{1,0:T(8,128)(2,1)} %collective-permute-done.13.refs_1_.refs_6_, bf16[128,4096]{1,0:T(8,128)(2,1)} %get-tuple-element.46.refs_3_.refs_2_, ...), custom_call_target="tpu_custom_call" | custom-call | tf_op jit(solution)/shard_map/payload/pallas_call | solution.py:30
  196.1 16.8 %back.2 = (bf16[512,4096]{1,0:T(8,128)(2,1)}, f32[8,4,128]{2,1,0:T(4,128)}, bf16[512,1024]{1,0:T(8,128)(2,1)}) custom-call(bf16[128,4096]{1,0:T(8,128)(2,1)} %grad_mix.1.refs_4_.refs_0_, bf16[128,4096]{1,0:T(8,128)(2,1)} %collective-permute-done.6.refs_0_.refs_1_, bf16[128,4096]{1,0:T(8,128)(2,1)} %collective-permute-done.10.refs_0_.refs_2_, ...), custom_call_target="tpu_custom_call" | custom-call | tf_op jit(solution)/shard_map/back/pallas_call | solution.py:30
  212.9 4.3 %all-to-all-start.2 = ((bf16[4,128,1024]{2,1,0:T(8,128)(2,1)}), bf16[4,128,1024]{2,1,0:T(8,128)(2,1)}, u32[]{:S(2)}, u32[]{:S(2)}) async-start(bf16[4,128,1024]{2,1,0:T(8,128)(2,1)} %bitcast.22), calls=%async_computation.2 | async-start | bytes 2097152 | tf_op jit(solution)/shard_map/all_to_all | solution.py:336
  217.2 16.8 %back.3 = (bf16[512,4096]{1,0:T(8,128)(2,1)}, f32[8,4,128]{2,1,0:T(4,128)}, bf16[512,1024]{1,0:T(8,128)(2,1)}) custom-call(bf16[128,4096]{1,0:T(8,128)(2,1)} %get-tuple-element.37.refs_0_, bf16[128,4096]{1,0:T(8,128)(2,1)} %collective-permute-done.1.refs_2_.refs_0_.refs_1_, bf16[128,4096]{1,0:T(8,128)(2,1)} %collective-permute-done.4.refs_0_.refs_2_, ...), custom_call_target="tpu_custom_call" | custom-call | tf_op jit(solution)/shard_map/back/pallas_call | solution.py:30
  235.4 6.4 %all-to-all-start.3 = ((bf16[4,128,1024]{2,1,0:T(8,128)(2,1)}), bf16[4,128,1024]{2,1,0:T(8,128)(2,1)}, u32[]{:S(2)}, u32[]{:S(2)}) async-start(bf16[4,128,1024]{2,1,0:T(8,128)(2,1)} %bitcast.21), calls=%async_computation.3 | async-start | bytes 2097152 | tf_op jit(solution)/shard_map/all_to_all | solution.py:336
  247.6 4.4 %collective-permute-start.18 = (bf16[128,4096]{1,0:T(8,128)(2,1)}, bf16[128,4096]{1,0:T(8,128)(2,1)}, u32[]{:S(2)}, u32[]{:S(2)}) collective-permute-start(bf16[128,4096]{1,0:T(8,128)(2,1)} %get-tuple-element.56.refs_4_), channel_id=1, source_target_pairs={{0,1},{1,2},{2,3},{4,5},{5,6},{6,7},{8,9},{9,10},{10,11},{12,13},{... | collective-permute-start | bytes 3145736 | tf_op jit(solution)/shard_map/ppermute | solution.py:343
  255.8 31.6 %collective-permute-done.15.refs_5_ = bf16[128,4096]{1,0:T(8,128)(2,1)} collective-permute-done((bf16[128,4096]{1,0:T(8,128)(2,1)}, bf16[128,4096]{1,0:T(8,128)(2,1)}, u32[]{:S(2)}, u32[]{:S(2)}) %collective-permute-start.15) | collective-permute-done | bytes 1048608 | tf_op jit(solution)/shard_map/ppermute | solution.py:344
  287.4 5.2 %finish.2.refs_4_ = bf16[1,128,4096]{2,1,0:T(8,128)(2,1)} custom-call(bf16[128,4096]{1,0:T(8,128)(2,1)} %collective-permute-done.refs_0_, bf16[128,4096]{1,0:T(8,128)(2,1)} %collective-permute-done.3.refs_1_, bf16[4,128,1024]{2,1,0:T(8,128)(2,1)} %all-to-all-done.2.refs_2_, bf16[128,4096]{1,0:T(8,128)(2,1)} %get-tuple-element.62.refs_3_, ...), custom_call_target="tpu_custom_call" | custom-call | tf_op jit(solution)/shard_map/finish/pallas_call | solution.py:30
  292.6 14.7 %weight_gradient.1.refs_2_ = bf16[1024,4096]{1,0:T(8,128)(2,1)} custom-call(bf16[512,1024]{1,0:T(8,128)(2,1)} %bitcast.2.refs_0_, bf16[512,1024]{1,0:T(8,128)(2,1)} %bitcast.4.refs_0_.refs_1_, bf16[512,4096]{1,0:T(8,128)(2,1)} %get-tuple-element.60.refs_6_.refs_2_, bf16[512,4096]{1,0:T(8,128)(2,1)} %get-tuple-element.59.refs_10_.refs_3_, ...), custom_call_target="tpu_custom_call" | custom-call | tf_op jit(solution)/shard_map/weight_gradient/pallas_call | solution.py:30
  316.0 5.2 %finish.3 = bf16[1,128,4096]{2,1,0:T(8,128)(2,1)} custom-call(bf16[128,4096]{1,0:T(8,128)(2,1)} %bitcast.18, bf16[128,4096]{1,0:T(8,128)(2,1)} %bitcast.20, bf16[4,128,1024]{2,1,0:T(8,128)(2,1)} %all-to-all-done.3.refs_2_, bf16[128,4096]{1,0:T(8,128)(2,1)} %get-tuple-element.67.refs_3_, bf16[128,4096]{1,0:T(8,128)(2,1)} %collective-permute-done.18.refs_4_, ...), custom_call_target="tpu_custom_call" | custom-call | tf_op jit(solution)/shard_map/finish/pallas_call | solution.py:30
  323.1 23.5 %collective-permute-done.21 = bf16[1,128,4096]{2,1,0:T(8,128)(2,1)} collective-permute-done((bf16[1,128,4096]{2,1,0:T(8,128)(2,1)}, bf16[1,128,4096]{2,1,0:T(8,128)(2,1)}, u32[]{:S(2)}, u32[]{:S(2)}) %collective-permute-start.21) | collective-permute-done | bytes 1048608 | tf_op jit(solution)/shard_map/ppermute | solution.py:453
  (46 shorter events, 59.9 us)
Async XLA Ops:
  4.7 35.6 %all-to-all-start = ((bf16[4,128,1024]{2,1,0:T(8,128)(2,1)}), bf16[4,128,1024]{2,1,0:T(8,128)(2,1)}, u32[]{:S(2)}, u32[]{:S(2)}) async-start(bf16[4,128,1024]{2,1,0:T(8,128)(2,1)} %get-tuple-element.36), calls=%async_computation | async-start | bytes 2097152 | tf_op jit(solution)/shard_map/all_to_all | solution.py:336
  10.0 26.6 %collective-permute-start = (bf16[128,4096]{1,0:T(8,128)(2,1)}, bf16[128,4096]{1,0:T(8,128)(2,1)}, u32[]{:S(2)}, u32[]{:S(2)}) collective-permute-start(bf16[128,4096]{1,0:T(8,128)(2,1)} %bitcast.26), channel_id=1, source_target_pairs={{0,28},{4,24},{8,20},{12,16},{16,12},{20,8},{24,4},{28,0},{1,29},{... | collective-permute-start | bytes 3145736 | tf_op jit(solution)/shard_map/ppermute | solution.py:422
  10.4 48.2 %collective-permute-start.3 = (bf16[128,4096]{1,0:T(8,128)(2,1)}, bf16[128,4096]{1,0:T(8,128)(2,1)}, u32[]{:S(2)}, u32[]{:S(2)}) collective-permute-start(bf16[128,4096]{1,0:T(8,128)(2,1)} %bitcast.27), channel_id=1, source_target_pairs={{0,28},{4,24},{8,20},{12,16},{16,12},{20,8},{24,4},{28,0},{1,29},{... | collective-permute-start | bytes 3145736 | tf_op jit(solution)/shard_map/ppermute | solution.py:423
  12.7 52.3 %collective-permute-start.2 = (bf16[128,4096]{1,0:T(8,128)(2,1)}, bf16[128,4096]{1,0:T(8,128)(2,1)}, u32[]{:S(2)}, u32[]{:S(2)}) collective-permute-start(bf16[128,4096]{1,0:T(8,128)(2,1)} %get-tuple-element.37.refs_0_), channel_id=1, source_target_pairs={{1,0},{2,1},{3,2},{5,4},{6,5},{7,6},{9,8},{10,9},{11,10},{13,12},{... | collective-permute-start | bytes 3145736 | tf_op jit(solution)/shard_map/ppermute | solution.py:344
  14.6 53.1 %collective-permute-start.1 = (bf16[128,4096]{1,0:T(8,128)(2,1)}, bf16[128,4096]{1,0:T(8,128)(2,1)}, u32[]{:S(2)}, u32[]{:S(2)}) collective-permute-start(bf16[128,4096]{1,0:T(8,128)(2,1)} %get-tuple-element.37.refs_0_), channel_id=1, source_target_pairs={{0,1},{1,2},{2,3},{4,5},{5,6},{6,7},{8,9},{9,10},{10,11},{12,13},{... | collective-permute-start | bytes 3145736 | tf_op jit(solution)/shard_map/ppermute | solution.py:343
  40.3 65.1 %all-to-all-start.1 = ((bf16[4,128,1024]{2,1,0:T(8,128)(2,1)}), bf16[4,128,1024]{2,1,0:T(8,128)(2,1)}, u32[]{:S(2)}, u32[]{:S(2)}) async-start(bf16[4,128,1024]{2,1,0:T(8,128)(2,1)} %prepare.3.refs_3_), calls=%async_computation.1 | async-start | bytes 2097152 | tf_op jit(solution)/shard_map/all_to_all | solution.py:336
  71.6 46.5 %collective-permute-start.7 = (bf16[128,4096]{1,0:T(8,128)(2,1)}, bf16[128,4096]{1,0:T(8,128)(2,1)}, u32[]{:S(2)}, u32[]{:S(2)}) collective-permute-start(bf16[128,4096]{1,0:T(8,128)(2,1)} %grad_mix.1.refs_4_.refs_0_), channel_id=1, source_target_pairs={{1,0},{2,1},{3,2},{5,4},{6,5},{7,6},{9,8},{10,9},{11,10},{13,12},{... | collective-permute-start | bytes 3145736 | tf_op jit(solution)/shard_map/ppermute | solution.py:344
  73.5 44.6 %collective-permute-start.6 = (bf16[128,4096]{1,0:T(8,128)(2,1)}, bf16[128,4096]{1,0:T(8,128)(2,1)}, u32[]{:S(2)}, u32[]{:S(2)}) collective-permute-start(bf16[128,4096]{1,0:T(8,128)(2,1)} %grad_mix.1.refs_4_.refs_0_), channel_id=1, source_target_pairs={{0,1},{1,2},{2,3},{4,5},{5,6},{6,7},{8,9},{9,10},{10,11},{12,13},{... | collective-permute-start | bytes 3145736 | tf_op jit(solution)/shard_map/ppermute | solution.py:343
  98.5 29.6 %collective-permute-start.4 = (bf16[128,4096]{1,0:T(8,128)(2,1)}, bf16[128,4096]{1,0:T(8,128)(2,1)}, u32[]{:S(2)}, u32[]{:S(2)}) collective-permute-start(bf16[128,4096]{1,0:T(8,128)(2,1)} %get-tuple-element.42.refs_3_.refs_4_), channel_id=1, source_target_pairs={{0,1},{1,2},{2,3},{4,5},{5,6},{6,7},{8,9},{9,10},{10,11},{12,13},{... | collective-permute-start | bytes 3145736 | tf_op jit(solution)/shard_map/ppermute | solution.py:343
  103.5 25.9 %collective-permute-start.5 = (bf16[128,4096]{1,0:T(8,128)(2,1)}, bf16[128,4096]{1,0:T(8,128)(2,1)}, u32[]{:S(2)}, u32[]{:S(2)}) collective-permute-start(bf16[128,4096]{1,0:T(8,128)(2,1)} %get-tuple-element.43.refs_4_.refs_5_), channel_id=1, source_target_pairs={{1,0},{2,1},{3,2},{5,4},{6,5},{7,6},{9,8},{10,9},{11,10},{13,12},{... | collective-permute-start | bytes 3145736 | tf_op jit(solution)/shard_map/ppermute | solution.py:344
  122.2 29.7 %collective-permute-start.11 = (bf16[128,4096]{1,0:T(8,128)(2,1)}, bf16[128,4096]{1,0:T(8,128)(2,1)}, u32[]{:S(2)}, u32[]{:S(2)}) collective-permute-start(bf16[128,4096]{1,0:T(8,128)(2,1)} %get-tuple-element.51), channel_id=1, source_target_pairs={{1,0},{2,1},{3,2},{5,4},{6,5},{7,6},{9,8},{10,9},{11,10},{13,12},{... | collective-permute-start | bytes 3145736 | tf_op jit(solution)/shard_map/ppermute | solution.py:344
  124.1 28.3 %collective-permute-start.10 = (bf16[128,4096]{1,0:T(8,128)(2,1)}, bf16[128,4096]{1,0:T(8,128)(2,1)}, u32[]{:S(2)}, u32[]{:S(2)}) collective-permute-start(bf16[128,4096]{1,0:T(8,128)(2,1)} %get-tuple-element.47.refs_4_), channel_id=1, source_target_pairs={{0,1},{1,2},{2,3},{4,5},{5,6},{6,7},{8,9},{9,10},{10,11},{12,13},{... | collective-permute-start | bytes 3145736 | tf_op jit(solution)/shard_map/ppermute | solution.py:343
  133.9 41.1 %collective-permute-start.8 = (bf16[128,4096]{1,0:T(8,128)(2,1)}, bf16[128,4096]{1,0:T(8,128)(2,1)}, u32[]{:S(2)}, u32[]{:S(2)}) collective-permute-start(bf16[128,4096]{1,0:T(8,128)(2,1)} %get-tuple-element.48.refs_4_), channel_id=1, source_target_pairs={{0,1},{1,2},{2,3},{4,5},{5,6},{6,7},{8,9},{9,10},{10,11},{12,13},{... | collective-permute-start | bytes 3145736 | tf_op jit(solution)/shard_map/ppermute | solution.py:343
  137.4 37.5 %collective-permute-start.9 = (bf16[128,4096]{1,0:T(8,128)(2,1)}, bf16[128,4096]{1,0:T(8,128)(2,1)}, u32[]{:S(2)}, u32[]{:S(2)}) collective-permute-start(bf16[128,4096]{1,0:T(8,128)(2,1)} %get-tuple-element.49.refs_5_), channel_id=1, source_target_pairs={{1,0},{2,1},{3,2},{5,4},{6,5},{7,6},{9,8},{10,9},{11,10},{13,12},{... | collective-permute-start | bytes 3145736 | tf_op jit(solution)/shard_map/ppermute | solution.py:344
  156.9 34.9 %collective-permute-start.13 = (bf16[128,4096]{1,0:T(8,128)(2,1)}, bf16[128,4096]{1,0:T(8,128)(2,1)}, u32[]{:S(2)}, u32[]{:S(2)}) collective-permute-start(bf16[128,4096]{1,0:T(8,128)(2,1)} %get-tuple-element.54), channel_id=1, source_target_pairs={{1,0},{2,1},{3,2},{5,4},{6,5},{7,6},{9,8},{10,9},{11,10},{13,12},{... | collective-permute-start | bytes 3145736 | tf_op jit(solution)/shard_map/ppermute | solution.py:344
  158.9 32.9 %collective-permute-start.12 = (bf16[128,4096]{1,0:T(8,128)(2,1)}, bf16[128,4096]{1,0:T(8,128)(2,1)}, u32[]{:S(2)}, u32[]{:S(2)}) collective-permute-start(bf16[128,4096]{1,0:T(8,128)(2,1)} %get-tuple-element.53.refs_4_), channel_id=1, source_target_pairs={{0,1},{1,2},{2,3},{4,5},{5,6},{6,7},{8,9},{9,10},{10,11},{12,13},{... | collective-permute-start | bytes 3145736 | tf_op jit(solution)/shard_map/ppermute | solution.py:343
  212.9 22.4 %all-to-all-start.2 = ((bf16[4,128,1024]{2,1,0:T(8,128)(2,1)}), bf16[4,128,1024]{2,1,0:T(8,128)(2,1)}, u32[]{:S(2)}, u32[]{:S(2)}) async-start(bf16[4,128,1024]{2,1,0:T(8,128)(2,1)} %bitcast.22), calls=%async_computation.2 | async-start | bytes 2097152 | tf_op jit(solution)/shard_map/all_to_all | solution.py:336
  235.4 80.7 %all-to-all-start.3 = ((bf16[4,128,1024]{2,1,0:T(8,128)(2,1)}), bf16[4,128,1024]{2,1,0:T(8,128)(2,1)}, u32[]{:S(2)}, u32[]{:S(2)}) async-start(bf16[4,128,1024]{2,1,0:T(8,128)(2,1)} %bitcast.21), calls=%async_computation.3 | async-start | bytes 2097152 | tf_op jit(solution)/shard_map/all_to_all | solution.py:336
  241.8 45.6 %collective-permute-start.15 = (bf16[128,4096]{1,0:T(8,128)(2,1)}, bf16[128,4096]{1,0:T(8,128)(2,1)}, u32[]{:S(2)}, u32[]{:S(2)}) collective-permute-start(bf16[128,4096]{1,0:T(8,128)(2,1)} %get-tuple-element.63), channel_id=1, source_target_pairs={{1,0},{2,1},{3,2},{5,4},{6,5},{7,6},{9,8},{10,9},{11,10},{13,12},{... | collective-permute-start | bytes 3145736 | tf_op jit(solution)/shard_map/ppermute | solution.py:344
  243.8 43.7 %collective-permute-start.14 = (bf16[128,4096]{1,0:T(8,128)(2,1)}, bf16[128,4096]{1,0:T(8,128)(2,1)}, u32[]{:S(2)}, u32[]{:S(2)}) collective-permute-start(bf16[128,4096]{1,0:T(8,128)(2,1)} %get-tuple-element.58.refs_10_), channel_id=1, source_target_pairs={{0,1},{1,2},{2,3},{4,5},{5,6},{6,7},{8,9},{9,10},{10,11},{12,13},{... | collective-permute-start | bytes 3145736 | tf_op jit(solution)/shard_map/ppermute | solution.py:343
  247.6 68.4 %collective-permute-start.18 = (bf16[128,4096]{1,0:T(8,128)(2,1)}, bf16[128,4096]{1,0:T(8,128)(2,1)}, u32[]{:S(2)}, u32[]{:S(2)}) collective-permute-start(bf16[128,4096]{1,0:T(8,128)(2,1)} %get-tuple-element.56.refs_4_), channel_id=1, source_target_pairs={{0,1},{1,2},{2,3},{4,5},{5,6},{6,7},{8,9},{9,10},{10,11},{12,13},{... | collective-permute-start | bytes 3145736 | tf_op jit(solution)/shard_map/ppermute | solution.py:343
  252.0 64.0 %collective-permute-start.19 = (bf16[128,4096]{1,0:T(8,128)(2,1)}, bf16[128,4096]{1,0:T(8,128)(2,1)}, u32[]{:S(2)}, u32[]{:S(2)}) collective-permute-start(bf16[128,4096]{1,0:T(8,128)(2,1)} %get-tuple-element.57.refs_5_), channel_id=1, source_target_pairs={{1,0},{2,1},{3,2},{5,4},{6,5},{7,6},{9,8},{10,9},{11,10},{13,12},{... | collective-permute-start | bytes 3145736 | tf_op jit(solution)/shard_map/ppermute | solution.py:344
  255.8 51.5 %collective-permute-start.16 = (f32[1,32,128]{2,1,0:T(8,128)}, f32[1,32,128]{2,1,0:T(8,128)S(1)}, u32[]{:S(2)}, u32[]{:S(2)}) collective-permute-start(f32[1,32,128]{2,1,0:T(8,128)} %bitcast.23), channel_id=1, source_target_pairs={{0,1},{1,0},{2,3},{3,2},{4,5},{5,4},{6,7},{7,6},{8,9},{9,8},{10,11... | collective-permute-start | bytes 49160 | tf_op jit(solution)/shard_map/ppermute | solution.py:409
  307.3 0.6 copy-start
  309.2 4.8 %collective-permute-start.17 = (f32[1,32,128]{2,1,0:T(8,128)}, f32[1,32,128]{2,1,0:T(8,128)S(1)}, u32[]{:S(2)}, u32[]{:S(2)}) collective-permute-start(f32[1,32,128]{2,1,0:T(8,128)} %add.4.refs_0_), channel_id=1, source_target_pairs={{0,2},{1,3},{2,0},{3,1},{4,6},{5,7},{6,4},{7,5},{8,10},{9,11},{10,... | collective-permute-start | bytes 49160 | tf_op jit(solution)/shard_map/ppermute | solution.py:409
  309.2 37.4 %collective-permute-start.21 = (bf16[1,128,4096]{2,1,0:T(8,128)(2,1)}, bf16[1,128,4096]{2,1,0:T(8,128)(2,1)}, u32[]{:S(2)}, u32[]{:S(2)}) collective-permute-start(bf16[1,128,4096]{2,1,0:T(8,128)(2,1)} %finish.2.refs_4_), channel_id=1, source_target_pairs={{28,4},{24,8},{20,12},{16,16},{12,20},{8,24},{4,28},{29,5},{25,9},... | collective-permute-start | bytes 3145736 | tf_op jit(solution)/shard_map/ppermute | solution.py:453
  314.1 0.6 copy-start.1
  321.2 25.4 %collective-permute-start.20 = (bf16[1,128,4096]{2,1,0:T(8,128)(2,1)}, bf16[1,128,4096]{2,1,0:T(8,128)(2,1)S(1)}, u32[]{:S(2)}, u32[]{:S(2)}) collective-permute-start(bf16[1,128,4096]{2,1,0:T(8,128)(2,1)} %finish.3), channel_id=1, source_target_pairs={{4,0},{8,4},{12,8},{16,12},{20,16},{24,20},{28,24},{5,1},{9,5},{13... | collective-permute-start | bytes 3145736 | tf_op jit(solution)/shard_map/ppermute | solution.py:460

commit v4 on v3

--- a/solution.py
+++ b/solution.py
@@ -30,7 +30,6 @@
     return pl.pallas_call(
         body,
         in_specs=list(in_specs) + unread,
-        cost_estimate=pl.CostEstimate(flops=0, transcendentals=0, bytes_accessed=0),
         compiler_params=params(),
         **options,
     )(*args, *after)
@@ -438,26 +437,26 @@
         down_arrivals.append(both_ways(*sent))
         if s == 2:
             up_part, up_pieces = project(up_x, weight, causal, after=sent)
+        if s == blocks:
+            down_mixes, down_conv = sort_arrivals(down_mix, down_pieces, down_arrivals)
+            down_g, down_taps, down_back = back(down_mixes, down_part, weight, ahead, after=sent)
+            down_back = exchange(down_back)
+            sent = (down_g,)
         sent = payload(s, up_arrivals[-1], up_pieces, after=sent)
         up_arrivals.append(both_ways(*sent))
         last = sent[0]
-    down_mixes, down_conv = sort_arrivals(down_mix, down_pieces, down_arrivals)
     up_mixes, up_conv = sort_arrivals(up_mix, up_pieces, up_arrivals)
-    up_g, up_taps, up_back = back(up_mixes, up_part, weight, ahead, after=(last,))
+    up_g, up_taps, up_back = back(
+        up_mixes, up_part, weight, ahead, after=(last, *down_arrivals[-1])
+    )
     up_back = exchange(up_back)
-    down_g, down_taps, down_back = back(
-        down_mixes, down_part, weight, ahead, after=(up_g,)
-    )
-    down_back = exchange(down_back)
-    up_grad = finish(up_xin, up_cot, up_conv, up_back, after=(down_g,))
+    weight_grad = weight_gradient(down_x, up_x, down_g, up_g)
+    down_grad = finish(down_xin, down_cot, down_conv, down_back, after=(weight_grad,))
+    down_passed = lax.ppermute(down_grad, "section", down_pairs)
+    taps = add(down_taps, up_taps).reshape(filters.shape)
+    taps = sum_all(taps, after=(down_grad,))
+    up_grad = finish(up_xin, up_cot, up_conv, up_back, after=(taps,))
     up_passed = lax.ppermute(up_grad, "section", up_pairs)
-    weight_grad = weight_gradient(down_x, up_x, down_g, up_g, after=(up_grad,))
-    taps = add(down_taps, up_taps).reshape(filters.shape)
-    taps = sum_all(taps, after=(weight_grad,))
-    down_grad = finish(
-        down_xin, down_cot, down_conv, down_back, after=(taps,)
-    )
-    down_passed = lax.ppermute(down_grad, "section", down_pairs)
     return weight_grad[None], taps, down_passed, up_passed
 
 

time: 354 us -> 372 us (1.051)
  waiting for transfers between devices: 136 us -> 153 us
    ppermute x8, waiting for transfers between devices: 14.9 us -> 31.5 us  [both_ways(): lax.ppermute(right, 'tensor', onward)]
    ppermute x2, waiting for transfers between devices: 1.41 us -> 12.4 us  [sum_all(): other = lax.ppermute(x, 'tensor', [(i, i ^ apart) for i in range(blocks)])]
    ppermute x8, waiting for transfers between devices: 63.1 us -> 56.3 us  [both_ways(): lax.ppermute(left, 'tensor', [(j, i) for i, j in onward])]
    ppermute x1, waiting for transfers between devices: 13.2 us -> 9.42 us  [per_device(): up_cot = lax.ppermute(up_cot[0], 'section', mirror)]
  transfers between devices with their start and end apart: 26 -> 26, of which waited for: 13 -> 16; matrix products, arithmetic and copies ran while one was open for 0% -> 0% of each run, Pallas kernels for 30% -> 28%
where the time goes in v4:
time: 372 us; the launch traced here: 367 us
  waiting for transfers between devices  153 us (41%)
  Pallas kernels  129 us (35%)
  starting transfers between devices  79.9 us (21%)
  local copies, waits for them, and re-layouts  4.46 us (1%)
    pallas_call x20, Pallas kernels, call(): pl.pallas_call(body, in_specs=list(in_specs) + unread, compiler_params=pa...  129 us
    ppermute x8, waiting for transfers between devices, both_ways(): lax.ppermute(left, 'tensor', [(j, i) for i, j in onward])  56.3 us
    ppermute x8, waiting for transfers between devices, both_ways(): lax.ppermute(right, 'tensor', onward)  31.5 us
    ppermute x8, starting transfers between devices, both_ways(): lax.ppermute(right, 'tensor', onward)  30.4 us
    ppermute x1, waiting for transfers between devices, per_device(): up_passed = lax.ppermute(up_grad, 'section', up_pairs)  23.3 us
    ppermute x8, starting transfers between devices, both_ways(): lax.ppermute(left, 'tensor', [(j, i) for i, j in onward])  19.7 us
    all_to_all x4, starting transfers between devices, exchange(): return lax.all_to_all(x, 'tensor', split_axis=0, concat_axis=0, tiled=True)  18.9 us
    ppermute x1, waiting for transfers between devices, per_device(): up_xin = lax.ppermute(up_input[0], 'section', mirror)  18.1 us
  transfers between devices with their start and end apart: 26, of which 16 were waited for; matrix products, arithmetic and copies ran while one was open for 0% of the time, Pallas kernels for 28%

profile of v4, /device:TPU:10, one launch (start us, length us, event | category | flops | bytes accessed | tf_op | source)
XLA Modules:
  0.0 367.4 jit_solution(16732092511918737841)
XLA Ops:
  0.6 4.1 %prepare.2 = (bf16[4,128,1024]{2,1,0:T(8,128)(2,1)}, bf16[128,4096]{1,0:T(8,128)(2,1)}) custom-call(bf16[128,4096]{1,0:T(8,128)(2,1)} %bitcast.17, bf16[128,4096]{1,0:T(8,128)(2,1)} %bitcast.19), custom_call_target="tpu_custom_call" | custom-call | tf_op jit(solution)/shard_map/prepare/pallas_call | solution.py:30
  4.7 5.3 %all-to-all-start = ((bf16[4,128,1024]{2,1,0:T(8,128)(2,1)}), bf16[4,128,1024]{2,1,0:T(8,128)(2,1)}, u32[]{:S(2)}, u32[]{:S(2)}) async-start(bf16[4,128,1024]{2,1,0:T(8,128)(2,1)} %get-tuple-element.36), calls=%async_computation | async-start | bytes 2097152 | tf_op jit(solution)/shard_map/all_to_all | solution.py:335
  14.6 3.9 %collective-permute-start.1 = (bf16[128,4096]{1,0:T(8,128)(2,1)}, bf16[128,4096]{1,0:T(8,128)(2,1)}, u32[]{:S(2)}, u32[]{:S(2)}) collective-permute-start(bf16[128,4096]{1,0:T(8,128)(2,1)} %get-tuple-element.37.refs_0_), channel_id=1, source_target_pairs={{0,1},{1,2},{2,3},{4,5},{5,6},{6,7},{8,9},{9,10},{10,11},{12,13},{... | collective-permute-start | bytes 3145736 | tf_op jit(solution)/shard_map/ppermute | solution.py:342
  18.5 18.1 %collective-permute-done.refs_0_ = bf16[128,4096]{1,0:T(8,128)(2,1)} collective-permute-done((bf16[128,4096]{1,0:T(8,128)(2,1)}, bf16[128,4096]{1,0:T(8,128)(2,1)}, u32[]{:S(2)}, u32[]{:S(2)}) %collective-permute-start) | collective-permute-done | bytes 1048608 | tf_op jit(solution)/shard_map/ppermute | solution.py:421
  40.3 5.1 %all-to-all-start.1 = ((bf16[4,128,1024]{2,1,0:T(8,128)(2,1)}), bf16[4,128,1024]{2,1,0:T(8,128)(2,1)}, u32[]{:S(2)}, u32[]{:S(2)}) async-start(bf16[4,128,1024]{2,1,0:T(8,128)(2,1)} %prepare.3.refs_3_), calls=%async_computation.1 | async-start | bytes 2097152 | tf_op jit(solution)/shard_map/all_to_all | solution.py:335
  49.2 9.4 %collective-permute-done.3.refs_1_ = bf16[128,4096]{1,0:T(8,128)(2,1)} collective-permute-done((bf16[128,4096]{1,0:T(8,128)(2,1)}, bf16[128,4096]{1,0:T(8,128)(2,1)}, u32[]{:S(2)}, u32[]{:S(2)}) %collective-permute-start.3) | collective-permute-done | bytes 1048608 | tf_op jit(solution)/shard_map/ppermute | solution.py:422
  58.6 6.4 %collective-permute-done.2.refs_3_.refs_1_.refs_4_ = bf16[128,4096]{1,0:T(8,128)(2,1)} collective-permute-done((bf16[128,4096]{1,0:T(8,128)(2,1)}, bf16[128,4096]{1,0:T(8,128)(2,1)}, u32[]{:S(2)}, u32[]{:S(2)}) %collective-permute-start.2) | collective-permute-done | bytes 1048608 | tf_op jit(solution)/shard_map/ppermute | solution.py:343
  73.5 4.4 %collective-permute-start.6 = (bf16[128,4096]{1,0:T(8,128)(2,1)}, bf16[128,4096]{1,0:T(8,128)(2,1)}, u32[]{:S(2)}, u32[]{:S(2)}) collective-permute-start(bf16[128,4096]{1,0:T(8,128)(2,1)} %grad_mix.1.refs_4_.refs_0_), channel_id=1, source_target_pairs={{0,1},{1,2},{2,3},{4,5},{5,6},{6,7},{8,9},{9,10},{10,11},{12,13},{... | collective-permute-start | bytes 3145736 | tf_op jit(solution)/shard_map/ppermute | solution.py:342
  77.9 12.5 %project.2 = (bf16[512,4096]{1,0:T(8,128)(2,1)}, bf16[128,4096]{1,0:T(8,128)(2,1)}, bf16[128,4096]{1,0:T(8,128)(2,1)}, bf16[128,4096]{1,0:T(8,128)(2,1)}, bf16[128,4096]{1,0:T(8,128)(2,1)}) custom-call(bf16[512,1024]{1,0:T(8,128)(2,1)} %bitcast.2.refs_0_, bf16[1024,4096]{1,0:T(8,128)(2,1)} %bitcast.12, bf16[32,128,256]{2,1,0:T(8,128)(2,1)} %get-tuple-element.38.refs_2_, ...), custom_call_target="tpu_custom_call" | custom-call | tf_op jit(solution)/shard_map/project/pallas_call | solution.py:30
  90.4 4.2 %payload.6 = (bf16[128,4096]{1,0:T(8,128)(2,1)}, bf16[128,4096]{1,0:T(8,128)(2,1)}) custom-call(bf16[128,4096]{1,0:T(8,128)(2,1)} %collective-permute-done.1.refs_2_.refs_0_.refs_1_, bf16[128,4096]{1,0:T(8,128)(2,1)} %collective-permute-done.2.refs_3_.refs_1_.refs_4_, bf16[128,4096]{1,0:T(8,128)(2,1)} %get-tuple-element.39.refs_2_.refs_3_, ...), custom_call_target="tpu_custom_call" | custom-call | tf_op jit(solution)/shard_map/payload/pallas_call | solution.py:30
  94.6 4.9 %collective-permute-start.4 = (bf16[128,4096]{1,0:T(8,128)(2,1)}, bf16[128,4096]{1,0:T(8,128)(2,1)}, u32[]{:S(2)}, u32[]{:S(2)}) collective-permute-start(bf16[128,4096]{1,0:T(8,128)(2,1)} %get-tuple-element.42.refs_3_.refs_4_), channel_id=1, source_target_pairs={{0,1},{1,2},{2,3},{4,5},{5,6},{6,7},{8,9},{9,10},{10,11},{12,13},{... | collective-permute-start | bytes 3145736 | tf_op jit(solution)/shard_map/ppermute | solution.py:342
  101.4 12.6 %project.3 = (bf16[512,4096]{1,0:T(8,128)(2,1)}, bf16[128,4096]{1,0:T(8,128)(2,1)}, bf16[128,4096]{1,0:T(8,128)(2,1)}, bf16[128,4096]{1,0:T(8,128)(2,1)}, bf16[128,4096]{1,0:T(8,128)(2,1)}) custom-call(bf16[512,1024]{1,0:T(8,128)(2,1)} %bitcast.4.refs_0_.refs_1_, bf16[1024,4096]{1,0:T(8,128)(2,1)} %bitcast.13, ...), custom_call_target="tpu_custom_call" | custom-call | tf_op jit(solution)/shard_map/project/pallas_call | solution.py:30
  114.1 4.2 %payload.7 = (bf16[128,4096]{1,0:T(8,128)(2,1)}, bf16[128,4096]{1,0:T(8,128)(2,1)}) custom-call(bf16[128,4096]{1,0:T(8,128)(2,1)} %collective-permute-done.6.refs_0_.refs_1_, bf16[128,4096]{1,0:T(8,128)(2,1)} %collective-permute-done.7.refs_1_.refs_4_, bf16[128,4096]{1,0:T(8,128)(2,1)} %get-tuple-element.45.refs_2_.refs_3_, ...), custom_call_target="tpu_custom_call" | custom-call | tf_op jit(solution)/shard_map/payload/pallas_call | solution.py:30
  120.1 3.9 %collective-permute-start.10 = (bf16[128,4096]{1,0:T(8,128)(2,1)}, bf16[128,4096]{1,0:T(8,128)(2,1)}, u32[]{:S(2)}, u32[]{:S(2)}) collective-permute-start(bf16[128,4096]{1,0:T(8,128)(2,1)} %get-tuple-element.47.refs_4_), channel_id=1, source_target_pairs={{0,1},{1,2},{2,3},{4,5},{5,6},{6,7},{8,9},{9,10},{10,11},{12,13},{... | collective-permute-start | bytes 3145736 | tf_op jit(solution)/shard_map/ppermute | solution.py:342
  127.8 4.4 %payload.8 = (bf16[128,4096]{1,0:T(8,128)(2,1)}, bf16[128,4096]{1,0:T(8,128)(2,1)}) custom-call(bf16[128,4096]{1,0:T(8,128)(2,1)} %collective-permute-done.4.refs_0_.refs_2_, bf16[128,4096]{1,0:T(8,128)(2,1)} %collective-permute-done.5.refs_1_.refs_5_, bf16[128,4096]{1,0:T(8,128)(2,1)} %get-tuple-element.44.refs_2_.refs_3_, ...), custom_call_target="tpu_custom_call" | custom-call | tf_op jit(solution)/shard_map/payload/pallas_call | solution.py:30
  134.1 4.9 %collective-permute-start.9 = (bf16[128,4096]{1,0:T(8,128)(2,1)}, bf16[128,4096]{1,0:T(8,128)(2,1)}, u32[]{:S(2)}, u32[]{:S(2)}) collective-permute-start(bf16[128,4096]{1,0:T(8,128)(2,1)} %get-tuple-element.49.refs_5_), channel_id=1, source_target_pairs={{1,0},{2,1},{3,2},{5,4},{6,5},{7,6},{9,8},{10,9},{11,10},{13,12},{... | collective-permute-start | bytes 3145736 | tf_op jit(solution)/shard_map/ppermute | solution.py:343
  139.0 11.2 %collective-permute-done.11.refs_1_.refs_5_ = bf16[128,4096]{1,0:T(8,128)(2,1)} collective-permute-done((bf16[128,4096]{1,0:T(8,128)(2,1)}, bf16[128,4096]{1,0:T(8,128)(2,1)}, u32[]{:S(2)}, u32[]{:S(2)}) %collective-permute-start.11) | collective-permute-done | bytes 1048608 | tf_op jit(solution)/shard_map/ppermute | solution.py:343
  150.2 4.5 %payload.9 = (bf16[128,4096]{1,0:T(8,128)(2,1)}, bf16[128,4096]{1,0:T(8,128)(2,1)}) custom-call(bf16[128,4096]{1,0:T(8,128)(2,1)} %collective-permute-done.10.refs_0_.refs_2_, bf16[128,4096]{1,0:T(8,128)(2,1)} %collective-permute-done.11.refs_1_.refs_5_, bf16[128,4096]{1,0:T(8,128)(2,1)} %get-tuple-element.52.refs_2_.refs_3_, ...), custom_call_target="tpu_custom_call" | custom-call | tf_op jit(solution)/shard_map/payload/pallas_call | solution.py:30
  154.7 12.7 %collective-permute-done.8.refs_0_.refs_3_ = bf16[128,4096]{1,0:T(8,128)(2,1)} collective-permute-done((bf16[128,4096]{1,0:T(8,128)(2,1)}, bf16[128,4096]{1,0:T(8,128)(2,1)}, u32[]{:S(2)}, u32[]{:S(2)}) %collective-permute-start.8) | collective-permute-done | bytes 1048608 | tf_op jit(solution)/shard_map/ppermute | solution.py:342
  169.3 4.3 %payload.10 = (bf16[128,4096]{1,0:T(8,128)(2,1)}, bf16[128,4096]{1,0:T(8,128)(2,1)}) custom-call(bf16[128,4096]{1,0:T(8,128)(2,1)} %collective-permute-done.8.refs_0_.refs_3_, bf16[128,4096]{1,0:T(8,128)(2,1)} %collective-permute-done.9.refs_1_.refs_6_, bf16[128,4096]{1,0:T(8,128)(2,1)} %get-tuple-element.40.refs_3_.refs_2_, ...), custom_call_target="tpu_custom_call" | custom-call | tf_op jit(solution)/shard_map/payload/pallas_call | solution.py:30
  173.6 16.8 %back.2 = (bf16[512,4096]{1,0:T(8,128)(2,1)}, f32[8,4,128]{2,1,0:T(4,128)}, bf16[512,1024]{1,0:T(8,128)(2,1)}) custom-call(bf16[128,4096]{1,0:T(8,128)(2,1)} %get-tuple-element.37.refs_0_, bf16[128,4096]{1,0:T(8,128)(2,1)} %collective-permute-done.1.refs_2_.refs_0_.refs_1_, bf16[128,4096]{1,0:T(8,128)(2,1)} %collective-permute-done.4.refs_0_.refs_2_, ...), custom_call_target="tpu_custom_call" | custom-call | tf_op jit(solution)/shard_map/back/pallas_call | solution.py:30
  190.4 4.2 %all-to-all-start.2 = ((bf16[4,128,1024]{2,1,0:T(8,128)(2,1)}), bf16[4,128,1024]{2,1,0:T(8,128)(2,1)}, u32[]{:S(2)}, u32[]{:S(2)}) async-start(bf16[4,128,1024]{2,1,0:T(8,128)(2,1)} %bitcast.22), calls=%async_computation.2 | async-start | bytes 2097152 | tf_op jit(solution)/shard_map/all_to_all | solution.py:335
  207.3 31.9 %collective-permute-done.13.refs_1_.refs_6_ = bf16[128,4096]{1,0:T(8,128)(2,1)} collective-permute-done((bf16[128,4096]{1,0:T(8,128)(2,1)}, bf16[128,4096]{1,0:T(8,128)(2,1)}, u32[]{:S(2)}, u32[]{:S(2)}) %collective-permute-start.13) | collective-permute-done | bytes 1048608 | tf_op jit(solution)/shard_map/ppermute | solution.py:343
  239.3 4.3 %payload.11 = (bf16[128,4096]{1,0:T(8,128)(2,1)}, bf16[128,4096]{1,0:T(8,128)(2,1)}) custom-call(bf16[128,4096]{1,0:T(8,128)(2,1)} %collective-permute-done.12.refs_0_.refs_3_, bf16[128,4096]{1,0:T(8,128)(2,1)} %collective-permute-done.13.refs_1_.refs_6_, bf16[128,4096]{1,0:T(8,128)(2,1)} %get-tuple-element.46.refs_3_.refs_2_, ...), custom_call_target="tpu_custom_call" | custom-call | tf_op jit(solution)/shard_map/payload/pallas_call | solution.py:30
  243.6 15.9 %collective-permute-done.14.refs_11_.refs_4_ = bf16[128,4096]{1,0:T(8,128)(2,1)} collective-permute-done((bf16[128,4096]{1,0:T(8,128)(2,1)}, bf16[128,4096]{1,0:T(8,128)(2,1)}, u32[]{:S(2)}, u32[]{:S(2)}) %collective-permute-start.14) | collective-permute-done | bytes 1048608 | tf_op jit(solution)/shard_map/ppermute | solution.py:342
  260.9 16.9 %back.3 = (bf16[512,4096]{1,0:T(8,128)(2,1)}, f32[8,4,128]{2,1,0:T(4,128)}, bf16[512,1024]{1,0:T(8,128)(2,1)}) custom-call(bf16[128,4096]{1,0:T(8,128)(2,1)} %grad_mix.1.refs_4_.refs_0_, bf16[128,4096]{1,0:T(8,128)(2,1)} %collective-permute-done.6.refs_0_.refs_1_, bf16[128,4096]{1,0:T(8,128)(2,1)} %collective-permute-done.10.refs_0_.refs_2_, ...), custom_call_target="tpu_custom_call" | custom-call | tf_op jit(solution)/shard_map/back/pallas_call | solution.py:30
  277.7 4.2 %all-to-all-start.3 = ((bf16[4,128,1024]{2,1,0:T(8,128)(2,1)}), bf16[4,128,1024]{2,1,0:T(8,128)(2,1)}, u32[]{:S(2)}, u32[]{:S(2)}) async-start(bf16[4,128,1024]{2,1,0:T(8,128)(2,1)} %bitcast.21), calls=%async_computation.3 | async-start | bytes 2097152 | tf_op jit(solution)/shard_map/all_to_all | solution.py:335
  290.2 14.7 %weight_gradient.1.refs_6_ = bf16[1024,4096]{1,0:T(8,128)(2,1)} custom-call(bf16[512,1024]{1,0:T(8,128)(2,1)} %bitcast.2.refs_0_, bf16[512,1024]{1,0:T(8,128)(2,1)} %bitcast.4.refs_0_.refs_1_, bf16[512,4096]{1,0:T(8,128)(2,1)} %get-tuple-element.56.refs_4_.refs_2_, bf16[512,4096]{1,0:T(8,128)(2,1)} %get-tuple-element.60.refs_3_), custom_call_target="tpu_custom_call" | custom-call | tf_op jit(solution)/shard_map/weight_gradient/pallas_call | solution.py:30
  304.9 5.2 %finish.2.refs_2_ = bf16[1,128,4096]{2,1,0:T(8,128)(2,1)} custom-call(bf16[128,4096]{1,0:T(8,128)(2,1)} %bitcast.18, bf16[128,4096]{1,0:T(8,128)(2,1)} %bitcast.20, bf16[4,128,1024]{2,1,0:T(8,128)(2,1)} %all-to-all-done.2.refs_2_, bf16[128,4096]{1,0:T(8,128)(2,1)} %get-tuple-element.64.refs_3_, bf16[128,4096]{1,0:T(8,128)(2,1)} %collective-permute-done.14.refs_11_.refs_4_, ...), custom_call_target="tpu_custom_call" | custom-call | tf_op jit(solution)/shard_map/finish/pallas_call | solution.py:30
  310.0 11.4 %collective-permute-done.16.refs_1_ = f32[1,32,128]{2,1,0:T(8,128)S(1)} collective-permute-done((f32[1,32,128]{2,1,0:T(8,128)}, f32[1,32,128]{2,1,0:T(8,128)S(1)}, u32[]{:S(2)}, u32[]{:S(2)}) %collective-permute-start.16) | collective-permute-done | bytes 16416 | tf_op jit(solution)/shard_map/ppermute | solution.py:408
  330.2 5.2 %finish.3 = bf16[1,128,4096]{2,1,0:T(8,128)(2,1)} custom-call(bf16[128,4096]{1,0:T(8,128)(2,1)} %collective-permute-done.refs_0_, bf16[128,4096]{1,0:T(8,128)(2,1)} %collective-permute-done.3.refs_1_, bf16[4,128,1024]{2,1,0:T(8,128)(2,1)} %all-to-all-done.3.refs_2_, bf16[128,4096]{1,0:T(8,128)(2,1)} %get-tuple-element.66.refs_3_, ...), custom_call_target="tpu_custom_call" | custom-call | tf_op jit(solution)/shard_map/finish/pallas_call | solution.py:30
  340.9 23.3 %collective-permute-done.21 = bf16[1,128,4096]{2,1,0:T(8,128)(2,1)S(1)} collective-permute-done((bf16[1,128,4096]{2,1,0:T(8,128)(2,1)}, bf16[1,128,4096]{2,1,0:T(8,128)(2,1)S(1)}, u32[]{:S(2)}, u32[]{:S(2)}) %collective-permute-start.21) | collective-permute-done | bytes 1048608 | tf_op jit(solution)/shard_map/ppermute | solution.py:459
  (46 shorter events, 71.6 us)
Async XLA Ops:
  4.7 35.6 %all-to-all-start = ((bf16[4,128,1024]{2,1,0:T(8,128)(2,1)}), bf16[4,128,1024]{2,1,0:T(8,128)(2,1)}, u32[]{:S(2)}, u32[]{:S(2)}) async-start(bf16[4,128,1024]{2,1,0:T(8,128)(2,1)} %get-tuple-element.36), calls=%async_computation | async-start | bytes 2097152 | tf_op jit(solution)/shard_map/all_to_all | solution.py:335
  10.0 26.6 %collective-permute-start = (bf16[128,4096]{1,0:T(8,128)(2,1)}, bf16[128,4096]{1,0:T(8,128)(2,1)}, u32[]{:S(2)}, u32[]{:S(2)}) collective-permute-start(bf16[128,4096]{1,0:T(8,128)(2,1)} %bitcast.26), channel_id=1, source_target_pairs={{0,28},{4,24},{8,20},{12,16},{16,12},{20,8},{24,4},{28,0},{1,29},{... | collective-permute-start | bytes 3145736 | tf_op jit(solution)/shard_map/ppermute | solution.py:421
  10.4 48.2 %collective-permute-start.3 = (bf16[128,4096]{1,0:T(8,128)(2,1)}, bf16[128,4096]{1,0:T(8,128)(2,1)}, u32[]{:S(2)}, u32[]{:S(2)}) collective-permute-start(bf16[128,4096]{1,0:T(8,128)(2,1)} %bitcast.27), channel_id=1, source_target_pairs={{0,28},{4,24},{8,20},{12,16},{16,12},{20,8},{24,4},{28,0},{1,29},{... | collective-permute-start | bytes 3145736 | tf_op jit(solution)/shard_map/ppermute | solution.py:422
  12.7 52.3 %collective-permute-start.2 = (bf16[128,4096]{1,0:T(8,128)(2,1)}, bf16[128,4096]{1,0:T(8,128)(2,1)}, u32[]{:S(2)}, u32[]{:S(2)}) collective-permute-start(bf16[128,4096]{1,0:T(8,128)(2,1)} %get-tuple-element.37.refs_0_), channel_id=1, source_target_pairs={{1,0},{2,1},{3,2},{5,4},{6,5},{7,6},{9,8},{10,9},{11,10},{13,12},{... | collective-permute-start | bytes 3145736 | tf_op jit(solution)/shard_map/ppermute | solution.py:343
  14.6 53.1 %collective-permute-start.1 = (bf16[128,4096]{1,0:T(8,128)(2,1)}, bf16[128,4096]{1,0:T(8,128)(2,1)}, u32[]{:S(2)}, u32[]{:S(2)}) collective-permute-start(bf16[128,4096]{1,0:T(8,128)(2,1)} %get-tuple-element.37.refs_0_), channel_id=1, source_target_pairs={{0,1},{1,2},{2,3},{4,5},{5,6},{6,7},{8,9},{9,10},{10,11},{12,13},{... | collective-permute-start | bytes 3145736 | tf_op jit(solution)/shard_map/ppermute | solution.py:342
  40.3 61.1 %all-to-all-start.1 = ((bf16[4,128,1024]{2,1,0:T(8,128)(2,1)}), bf16[4,128,1024]{2,1,0:T(8,128)(2,1)}, u32[]{:S(2)}, u32[]{:S(2)}) async-start(bf16[4,128,1024]{2,1,0:T(8,128)(2,1)} %prepare.3.refs_3_), calls=%async_computation.1 | async-start | bytes 2097152 | tf_op jit(solution)/shard_map/all_to_all | solution.py:335
  71.6 42.5 %collective-permute-start.7 = (bf16[128,4096]{1,0:T(8,128)(2,1)}, bf16[128,4096]{1,0:T(8,128)(2,1)}, u32[]{:S(2)}, u32[]{:S(2)}) collective-permute-start(bf16[128,4096]{1,0:T(8,128)(2,1)} %grad_mix.1.refs_4_.refs_0_), channel_id=1, source_target_pairs={{1,0},{2,1},{3,2},{5,4},{6,5},{7,6},{9,8},{10,9},{11,10},{13,12},{... | collective-permute-start | bytes 3145736 | tf_op jit(solution)/shard_map/ppermute | solution.py:343
  73.5 40.6 %collective-permute-start.6 = (bf16[128,4096]{1,0:T(8,128)(2,1)}, bf16[128,4096]{1,0:T(8,128)(2,1)}, u32[]{:S(2)}, u32[]{:S(2)}) collective-permute-start(bf16[128,4096]{1,0:T(8,128)(2,1)} %grad_mix.1.refs_4_.refs_0_), channel_id=1, source_target_pairs={{0,1},{1,2},{2,3},{4,5},{5,6},{6,7},{8,9},{9,10},{10,11},{12,13},{... | collective-permute-start | bytes 3145736 | tf_op jit(solution)/shard_map/ppermute | solution.py:342
  94.6 29.7 %collective-permute-start.4 = (bf16[128,4096]{1,0:T(8,128)(2,1)}, bf16[128,4096]{1,0:T(8,128)(2,1)}, u32[]{:S(2)}, u32[]{:S(2)}) collective-permute-start(bf16[128,4096]{1,0:T(8,128)(2,1)} %get-tuple-element.42.refs_3_.refs_4_), channel_id=1, source_target_pairs={{0,1},{1,2},{2,3},{4,5},{5,6},{6,7},{8,9},{9,10},{10,11},{12,13},{... | collective-permute-start | bytes 3145736 | tf_op jit(solution)/shard_map/ppermute | solution.py:342
  99.5 28.3 %collective-permute-start.5 = (bf16[128,4096]{1,0:T(8,128)(2,1)}, bf16[128,4096]{1,0:T(8,128)(2,1)}, u32[]{:S(2)}, u32[]{:S(2)}) collective-permute-start(bf16[128,4096]{1,0:T(8,128)(2,1)} %get-tuple-element.43.refs_4_.refs_5_), channel_id=1, source_target_pairs={{1,0},{2,1},{3,2},{5,4},{6,5},{7,6},{9,8},{10,9},{11,10},{13,12},{... | collective-permute-start | bytes 3145736 | tf_op jit(solution)/shard_map/ppermute | solution.py:343
  118.2 32.0 %collective-permute-start.11 = (bf16[128,4096]{1,0:T(8,128)(2,1)}, bf16[128,4096]{1,0:T(8,128)(2,1)}, u32[]{:S(2)}, u32[]{:S(2)}) collective-permute-start(bf16[128,4096]{1,0:T(8,128)(2,1)} %get-tuple-element.51), channel_id=1, source_target_pairs={{1,0},{2,1},{3,2},{5,4},{6,5},{7,6},{9,8},{10,9},{11,10},{13,12},{... | collective-permute-start | bytes 3145736 | tf_op jit(solution)/shard_map/ppermute | solution.py:343
  120.1 30.1 %collective-permute-start.10 = (bf16[128,4096]{1,0:T(8,128)(2,1)}, bf16[128,4096]{1,0:T(8,128)(2,1)}, u32[]{:S(2)}, u32[]{:S(2)}) collective-permute-start(bf16[128,4096]{1,0:T(8,128)(2,1)} %get-tuple-element.47.refs_4_), channel_id=1, source_target_pairs={{0,1},{1,2},{2,3},{4,5},{5,6},{6,7},{8,9},{9,10},{10,11},{12,13},{... | collective-permute-start | bytes 3145736 | tf_op jit(solution)/shard_map/ppermute | solution.py:342
  132.2 35.2 %collective-permute-start.8 = (bf16[128,4096]{1,0:T(8,128)(2,1)}, bf16[128,4096]{1,0:T(8,128)(2,1)}, u32[]{:S(2)}, u32[]{:S(2)}) collective-permute-start(bf16[128,4096]{1,0:T(8,128)(2,1)} %get-tuple-element.48.refs_4_), channel_id=1, source_target_pairs={{0,1},{1,2},{2,3},{4,5},{5,6},{6,7},{8,9},{9,10},{10,11},{12,13},{... | collective-permute-start | bytes 3145736 | tf_op jit(solution)/shard_map/ppermute | solution.py:342
  134.1 35.2 %collective-permute-start.9 = (bf16[128,4096]{1,0:T(8,128)(2,1)}, bf16[128,4096]{1,0:T(8,128)(2,1)}, u32[]{:S(2)}, u32[]{:S(2)}) collective-permute-start(bf16[128,4096]{1,0:T(8,128)(2,1)} %get-tuple-element.49.refs_5_), channel_id=1, source_target_pairs={{1,0},{2,1},{3,2},{5,4},{6,5},{7,6},{9,8},{10,9},{11,10},{13,12},{... | collective-permute-start | bytes 3145736 | tf_op jit(solution)/shard_map/ppermute | solution.py:343
  190.4 87.3 %all-to-all-start.2 = ((bf16[4,128,1024]{2,1,0:T(8,128)(2,1)}), bf16[4,128,1024]{2,1,0:T(8,128)(2,1)}, u32[]{:S(2)}, u32[]{:S(2)}) async-start(bf16[4,128,1024]{2,1,0:T(8,128)(2,1)} %bitcast.22), calls=%async_computation.2 | async-start | bytes 2097152 | tf_op jit(solution)/shard_map/all_to_all | solution.py:335
  194.7 44.6 %collective-permute-start.13 = (bf16[128,4096]{1,0:T(8,128)(2,1)}, bf16[128,4096]{1,0:T(8,128)(2,1)}, u32[]{:S(2)}, u32[]{:S(2)}) collective-permute-start(bf16[128,4096]{1,0:T(8,128)(2,1)} %get-tuple-element.57), channel_id=1, source_target_pairs={{1,0},{2,1},{3,2},{5,4},{6,5},{7,6},{9,8},{10,9},{11,10},{13,12},{... | collective-permute-start | bytes 3145736 | tf_op jit(solution)/shard_map/ppermute | solution.py:343
  196.6 42.7 %collective-permute-start.12 = (bf16[128,4096]{1,0:T(8,128)(2,1)}, bf16[128,4096]{1,0:T(8,128)(2,1)}, u32[]{:S(2)}, u32[]{:S(2)}) collective-permute-start(bf16[128,4096]{1,0:T(8,128)(2,1)} %get-tuple-element.53.refs_4_), channel_id=1, source_target_pairs={{0,1},{1,2},{2,3},{4,5},{5,6},{6,7},{8,9},{9,10},{10,11},{12,13},{... | collective-permute-start | bytes 3145736 | tf_op jit(solution)/shard_map/ppermute | solution.py:342
  200.5 59.0 %collective-permute-start.14 = (bf16[128,4096]{1,0:T(8,128)(2,1)}, bf16[128,4096]{1,0:T(8,128)(2,1)}, u32[]{:S(2)}, u32[]{:S(2)}) collective-permute-start(bf16[128,4096]{1,0:T(8,128)(2,1)} %get-tuple-element.54.refs_10_), channel_id=1, source_target_pairs={{0,1},{1,2},{2,3},{4,5},{5,6},{6,7},{8,9},{9,10},{10,11},{12,13},{... | collective-permute-start | bytes 3145736 | tf_op jit(solution)/shard_map/ppermute | solution.py:342
  204.0 56.9 %collective-permute-start.15 = (bf16[128,4096]{1,0:T(8,128)(2,1)}, bf16[128,4096]{1,0:T(8,128)(2,1)}, u32[]{:S(2)}, u32[]{:S(2)}) collective-permute-start(bf16[128,4096]{1,0:T(8,128)(2,1)} %get-tuple-element.55.refs_11_), channel_id=1, source_target_pairs={{1,0},{2,1},{3,2},{5,4},{6,5},{7,6},{9,8},{10,9},{11,10},{13,12},{... | collective-permute-start | bytes 3145736 | tf_op jit(solution)/shard_map/ppermute | solution.py:343
  277.7 52.4 %all-to-all-start.3 = ((bf16[4,128,1024]{2,1,0:T(8,128)(2,1)}), bf16[4,128,1024]{2,1,0:T(8,128)(2,1)}, u32[]{:S(2)}, u32[]{:S(2)}) async-start(bf16[4,128,1024]{2,1,0:T(8,128)(2,1)} %bitcast.21), calls=%async_computation.3 | async-start | bytes 2097152 | tf_op jit(solution)/shard_map/all_to_all | solution.py:335
  282.0 48.2 %collective-permute-start.20 = (bf16[128,4096]{1,0:T(8,128)(2,1)}, bf16[128,4096]{1,0:T(8,128)(2,1)}, u32[]{:S(2)}, u32[]{:S(2)}) collective-permute-start(bf16[128,4096]{1,0:T(8,128)(2,1)} %get-tuple-element.67), channel_id=1, source_target_pairs={{1,0},{2,1},{3,2},{5,4},{6,5},{7,6},{9,8},{10,9},{11,10},{13,12},{... | collective-permute-start | bytes 3145736 | tf_op jit(solution)/shard_map/ppermute | solution.py:343
  283.9 46.2 %collective-permute-start.19 = (bf16[128,4096]{1,0:T(8,128)(2,1)}, bf16[128,4096]{1,0:T(8,128)(2,1)}, u32[]{:S(2)}, u32[]{:S(2)}) collective-permute-start(bf16[128,4096]{1,0:T(8,128)(2,1)} %get-tuple-element.59.refs_10_), channel_id=1, source_target_pairs={{0,1},{1,2},{2,3},{4,5},{5,6},{6,7},{8,9},{9,10},{10,11},{12,13},{... | collective-permute-start | bytes 3145736 | tf_op jit(solution)/shard_map/ppermute | solution.py:342
  289.2 32.2 %collective-permute-start.16 = (f32[1,32,128]{2,1,0:T(8,128)}, f32[1,32,128]{2,1,0:T(8,128)S(1)}, u32[]{:S(2)}, u32[]{:S(2)}) collective-permute-start(f32[1,32,128]{2,1,0:T(8,128)} %bitcast.23), channel_id=1, source_target_pairs={{0,1},{1,0},{2,3},{3,2},{4,5},{5,4},{6,7},{7,6},{8,9},{9,8},{10,11... | collective-permute-start | bytes 49160 | tf_op jit(solution)/shard_map/ppermute | solution.py:408
  321.4 0.6 copy-start
  323.4 4.8 %collective-permute-start.17 = (f32[1,32,128]{2,1,0:T(8,128)}, f32[1,32,128]{2,1,0:T(8,128)S(1)}, u32[]{:S(2)}, u32[]{:S(2)}) collective-permute-start(f32[1,32,128]{2,1,0:T(8,128)} %add.4.refs_0_), channel_id=1, source_target_pairs={{0,2},{1,3},{2,0},{3,1},{4,6},{5,7},{6,4},{7,5},{8,10},{9,11},{10,... | collective-permute-start | bytes 49160 | tf_op jit(solution)/shard_map/ppermute | solution.py:408
  325.3 15.6 %collective-permute-start.18 = (bf16[1,128,4096]{2,1,0:T(8,128)(2,1)}, bf16[1,128,4096]{2,1,0:T(8,128)(2,1)}, u32[]{:S(2)}, u32[]{:S(2)}) collective-permute-start(bf16[1,128,4096]{2,1,0:T(8,128)(2,1)} %finish.2.refs_2_), channel_id=1, source_target_pairs={{4,0},{8,4},{12,8},{16,12},{20,16},{24,20},{28,24},{5,1},{9,5},{13... | collective-permute-start | bytes 3145736 | tf_op jit(solution)/shard_map/ppermute | solution.py:455
  328.2 0.6 copy-start.1
  335.3 28.8 %collective-permute-start.21 = (bf16[1,128,4096]{2,1,0:T(8,128)(2,1)}, bf16[1,128,4096]{2,1,0:T(8,128)(2,1)S(1)}, u32[]{:S(2)}, u32[]{:S(2)}) collective-permute-start(bf16[1,128,4096]{2,1,0:T(8,128)(2,1)} %finish.3), channel_id=1, source_target_pairs={{28,4},{24,8},{20,12},{16,16},{12,20},{8,24},{4,28},{29,5},{25,9},... | collective-permute-start | bytes 3145736 | tf_op jit(solution)/shard_map/ppermute | solution.py:459

commit v5 on v1

--- a/solution.py
+++ b/solution.py
@@ -139,6 +139,10 @@
     )
 
 
+def side_by_side(x, rows):
+    return jnp.concatenate([x[s : s + rows] for s in range(0, x.shape[0], rows)], axis=1)
+
+
 def project_kernel(features_ref, weight_ref, causal_ref, part_ref, *rest):
     *mixed_refs, mixed_ref = rest
     groups, taps, _ = causal_ref.shape
@@ -147,12 +151,11 @@
     width = part.shape[1] // groups
     for g in range(groups):
         cols = slice(g * width, (g + 1) * width)
-        for start in range(0, part.shape[0], taps):
-            if start == 0:
-                out = dot(causal_ref[g, :, taps:], part[:taps, cols])
-            else:
-                out = dot(causal_ref[g], part[start - taps : start + taps, cols])
-            mixed_ref[start : start + taps, cols] = out.astype(bf16)
+        own = side_by_side(part[:, cols], taps)
+        before = jnp.concatenate([jnp.zeros((taps, width), bf16), own[:, :-width]], axis=1)
+        out = dot(causal_ref[g], jnp.concatenate([before, own], axis=0)).astype(bf16)
+        for i in range(out.shape[1] // width):
+            mixed_ref[i * taps : (i + 1) * taps, cols] = out[:, i * width : (i + 1) * width]
     for s, out_ref in enumerate(mixed_refs):
         out_ref[...] = mixed_ref[window(place(s), out_ref.shape[0]), :]
 
@@ -185,44 +188,99 @@
     return part, mixed
 
 
-def back_kernel(blocks, *refs):
-    count = 2 * blocks - 1
-    mix_refs = refs[:count]
-    part_ref, weight_ref, ahead_ref, grad_ref, taps_ref, back_ref, mix_ref, total = refs[count:]
-    groups, taps, _ = ahead_ref.shape
-    tokens = mix_ref.shape[0]
-    rows = tokens // blocks
-    width = mix_ref.shape[1] // groups
+def assemble(block_refs, mix_ref):
+    blocks = (len(block_refs) + 1) // 2
+    rows = block_refs[0].shape[0]
     mine = lax.axis_index("tensor")
-    mix_ref[window(mine, rows), :] = mix_refs[0][...]
+    mix_ref[window(mine, rows), :] = block_refs[0][...]
     for s in range(1, blocks):
 
         @pl.when(mine >= s)
         def _():
-            mix_ref[window(mine - s, rows), :] = mix_refs[s][...]
+            mix_ref[window(mine - s, rows), :] = block_refs[s][...]
 
         @pl.when(mine < s)
         def _():
-            mix_ref[window(mine + (blocks - s), rows), :] = mix_refs[2 * blocks - 1 - s][...]
-
+            mix_ref[window(mine + (blocks - s), rows), :] = block_refs[2 * blocks - 1 - s][...]
+
+
+def with_following(mix, taps):
+    own = side_by_side(mix, taps)
+    width = mix.shape[1]
+    following = jnp.concatenate([own[:, width:], jnp.zeros((taps, width), bf16)], axis=1)
+    return jnp.concatenate([own, following], axis=0)
+
+
+def back_kernel(count, *refs):
+    weight_ref, ahead_ref, grad_ref, back_ref, mix_ref, total = refs[count:]
+    groups, taps, _ = ahead_ref.shape
+    width = mix_ref.shape[1] // groups
+    assemble(refs[:count], mix_ref)
+    for g in range(groups):
+        cols = slice(g * width, (g + 1) * width)
+        out = dot(ahead_ref[g], with_following(mix_ref[:, cols], taps)).astype(bf16)
+        for i in range(out.shape[1] // width):
+            grad_ref[i * taps : (i + 1) * taps, cols] = out[:, i * width : (i + 1) * width]
+    product = dot(grad_ref[...], weight_ref[...], ((1,), (1,)))
+    step = pl.program_id(0)
+
+    @pl.when(step == 0)
+    def _():
+        total[...] = product
+
+    @pl.when(step > 0)
+    def _():
+        total[...] += product
+
+    @pl.when(step == pl.num_programs(0) - 1)
+    def _():
+        back_ref[...] = total[...].astype(bf16)
+
+
+def back(mixes, weight, ahead, after=()):
+    rows, width = mixes[0].shape
+    tokens = (len(mixes) + 1) // 2 * rows
+    depth = weight.shape[0]
+    groups, taps, _ = ahead.shape
+    step = 4
+    tile = width // groups * step
+    return call(
+        functools.partial(back_kernel, len(mixes)),
+        (*mixes, weight, ahead),
+        after,
+        grid=(groups // step,),
+        in_specs=[pl.BlockSpec((rows, tile), lambda i: (0, i))] * len(mixes)
+        + [
+            pl.BlockSpec((depth, tile), lambda i: (0, i)),
+            pl.BlockSpec((step, taps, 2 * taps), lambda i: (i, 0, 0)),
+        ],
+        out_specs=[
+            pl.BlockSpec((tokens, tile), lambda i: (0, i)),
+            pl.BlockSpec((tokens, depth), lambda i: (0, 0)),
+        ],
+        out_shape=[shape((tokens, width), bf16), shape((tokens, depth), bf16)],
+        scratch_shapes=[pltpu.VMEM((tokens, tile), bf16), pltpu.VMEM((tokens, depth), f32)],
+        flops=2 * tokens * width * (depth + 2 * taps),
+        name="back",
+    )
+
+
+def taps_kernel(count, groups, *refs):
+    taps_ref, *mix_refs = refs[-3:]
+    taps = taps_ref.shape[2]
+    width = mix_refs[0].shape[1] // groups
     row = lax.broadcasted_iota(jnp.int32, (taps, taps), 0)
     col = lax.broadcasted_iota(jnp.int32, (taps, taps), 1)
-    starts = range(0, tokens, taps)
+    total = [0] * groups
+    for first, mix_ref in zip((0, count + 1), mix_refs):
+        assemble(refs[first : first + count], mix_ref)
+        part_ref = refs[first + count]
+        for g in range(groups):
+            cols = slice(g * width, (g + 1) * width)
+            both = with_following(mix_ref[:, cols], taps)
+            total[g] += dot(side_by_side(part_ref[:, cols], taps), both, ((1,), (1,)))
     for g in range(groups):
-        cols = slice(g * width, (g + 1) * width)
-        mix = mix_ref[:, cols]
-        part = part_ref[:, cols]
-        for start in starts:
-            if start + taps == tokens:
-                out = dot(ahead_ref[g, :, :taps], mix[start:])
-            else:
-                out = dot(ahead_ref[g], mix[start : start + 2 * taps])
-            grad_ref[start : start + taps, cols] = out.astype(bf16)
-        mixes = jnp.concatenate([mix[s : s + taps] for s in starts], axis=1)
-        parts = jnp.concatenate([part[s : s + taps] for s in starts], axis=1)
-        same = dot(parts, mixes, ((1,), (1,)))
-        later = dot(parts[:, :-width], mixes[:, width:], ((1,), (1,)))
-        pairs = jnp.where(col >= row, same, later)
+        pairs = jnp.where(col >= row, total[g][:, :taps], total[g][:, taps:])
         folded = pairs[0:8]
         for a in range(8, taps, 8):
             folded = folded + pltpu.roll(pairs[a : a + 8], taps - a, 1)
@@ -230,56 +288,28 @@
         for b in range(1, 8):
             line = line + pltpu.roll(folded[b : b + 1], taps - b, 1)
         taps_ref[0, g : g + 1, :] = line
-    product = dot(grad_ref[...], weight_ref[...], ((1,), (1,)))
-    step = pl.program_id(0)
-
-    @pl.when(step == 0)
-    def _():
-        total[...] = product
-
-    @pl.when(step > 0)
-    def _():
-        total[...] += product
-
-    @pl.when(step == pl.num_programs(0) - 1)
-    def _():
-        back_ref[...] = total[...].astype(bf16)
-
-
-def back(mixes, part, weight, ahead, after=()):
-    blocks = (len(mixes) + 1) // 2
-    rows = mixes[0].shape[0]
-    tokens, width = part.shape
-    depth = weight.shape[0]
-    groups, taps, _ = ahead.shape
+
+
+def filter_gradient(down_mixes, down_part, up_mixes, up_part, groups, taps, after=()):
+    rows, width = down_mixes[0].shape
+    tokens = down_part.shape[0]
     step = 4
     tile = width // groups * step
-    spec = pl.BlockSpec((tokens, tile), lambda i: (0, i))
-    return call(
-        functools.partial(back_kernel, blocks),
-        (*mixes, part, weight, ahead),
+    count = len(down_mixes)
+    block = [pl.BlockSpec((rows, tile), lambda i: (0, i))] * count
+    part = [pl.BlockSpec((tokens, tile), lambda i: (0, i))]
+    return call(
+        functools.partial(taps_kernel, count, step),
+        (*down_mixes, down_part, *up_mixes, up_part),
         after,
         grid=(groups // step,),
-        in_specs=[pl.BlockSpec((rows, tile), lambda i: (0, i))] * len(mixes)
-        + [
-            spec,
-            pl.BlockSpec((depth, tile), lambda i: (0, i)),
-            pl.BlockSpec((step, taps, 2 * taps), lambda i: (i, 0, 0)),
-        ],
-        out_specs=[
-            spec,
-            pl.BlockSpec((1, step, taps), lambda i: (i, 0, 0)),
-            pl.BlockSpec((tokens, depth), lambda i: (0, 0)),
-        ],
-        out_shape=[
-            shape((tokens, width), bf16),
-            shape((groups // step, step, taps), f32),
-            shape((tokens, depth), bf16),
-        ],
-        scratch_shapes=[pltpu.VMEM((tokens, tile), bf16), pltpu.VMEM((tokens, depth), f32)],
-        flops=2 * tokens * width * (depth + 4 * taps),
-        name="back",
-    )
+        in_specs=(block + part) * 2,
+        out_specs=pl.BlockSpec((1, step, taps), lambda i: (i, 0, 0)),
+        out_shape=shape((groups // step, step, taps), f32),
+        scratch_shapes=[pltpu.VMEM((tokens, tile), bf16)] * 2,
+        flops=8 * tokens * width * taps,
+        name="filter_gradient",
+    ).reshape(1, groups, taps)
 
 
 def weight_kernel(down_x, up_x, down_g, up_g, out_ref, down_t, up_t):
@@ -394,13 +424,30 @@
     return [mix, *rights[:-1], *lefts[:-1]], [pieces[0], rights[-1], lefts[-1]]
 
 
-def sum_all(x):
-    blocks = lax.axis_size("tensor")
-    apart = 1
-    while apart < blocks:
-        x = x + lax.ppermute(x, "tensor", [(i, i ^ apart) for i in range(blocks)])
-        apart *= 2
-    return x
+def sum_kernel(*refs):
+    *in_refs, out_ref, sorted_ref = refs
+    for s, ref in enumerate(in_refs):
+        sorted_ref[pl.ds(place(-s), 1)] = ref[...]
+    out_ref[...] = sum(sorted_ref[i : i + 1] for i in range(len(in_refs)))
+
+
+def sum_all(x, after=()):
+    blocks = lax.axis_size("tensor")
+    terms = [x]
+    for s in range(1, blocks):
+        terms.append(lax.ppermute(x, "tensor", [(i, (i + s) % blocks) for i in range(blocks)]))
+    spec = pl.BlockSpec(x.shape, lambda i: (0,) * x.ndim)
+    return call(
+        sum_kernel,
+        terms,
+        after,
+        grid=(1,),
+        in_specs=[spec] * blocks,
+        out_specs=spec,
+        out_shape=shape(x.shape, x.dtype),
+        scratch_shapes=[pltpu.VMEM((blocks, *x.shape[1:]), x.dtype)],
+        name="sum_all",
+    )
 
 
 def per_device(weights, filters, down_input, down_cot, up_input, up_cot):
@@ -434,19 +481,20 @@
         last = sent[0]
     down_mixes, down_conv = sort_arrivals(down_mix, down_pieces, down_arrivals)
     up_mixes, up_conv = sort_arrivals(up_mix, up_pieces, up_arrivals)
-    up_g, up_taps, up_back = back(up_mixes, up_part, weight, ahead, after=(last,))
+    up_g, up_back = back(up_mixes, weight, ahead, after=(last,))
     up_back = exchange(up_back)
-    down_g, down_taps, down_back = back(
-        down_mixes, down_part, weight, ahead, after=(up_g, *down_arrivals[-1])
+    taps = filter_gradient(
+        down_mixes, down_part, up_mixes, up_part, *filters.shape[1:], after=(up_g,)
+    )
+    down_g, down_back = back(
+        down_mixes, weight, ahead, after=(taps, *down_arrivals[-1], *up_arrivals[-1])
     )
     down_back = exchange(down_back)
     up_grad = finish(up_xin, up_cot, up_conv, up_back, after=(down_g,))
     up_passed = lax.ppermute(up_grad, "section", up_pairs)
-    weight_grad = weight_gradient(down_x, up_x, down_g, up_g)
-    taps = sum_all((down_taps + up_taps).reshape(filters.shape))
-    down_grad = finish(
-        down_xin, down_cot, down_conv, down_back, after=(up_grad, weight_grad, taps)
-    )
+    weight_grad = weight_gradient(down_x, up_x, down_g, up_g, after=(up_grad,))
+    taps = sum_all(taps, after=(weight_grad,))
+    down_grad = finish(down_xin, down_cot, down_conv, down_back, after=(taps, up_passed))
     down_passed = lax.ppermute(down_grad, "section", down_pairs)
     return weight_grad[None], taps, down_passed, up_passed
 

time: 349 us -> 364 us (1.043)
  the two profiles are of different devices: /device:TPU:10 before, /device:TPU:3 now
where the time goes in v5:
time: 364 us; the launch traced here: 360 us
  Pallas kernels  135 us (37%)
  waiting for transfers between devices  127 us (35%)
  starting transfers between devices  93.6 us (26%)
  local copies, waits for them, and re-layouts  4.44 us (1%)
    pallas_call x19, Pallas kernels, call(): pl.pallas_call(body, in_specs=list(in_specs) + unread, out_shape=out_shap...  135 us
    ppermute x8, waiting for transfers between devices, both_ways(): lax.ppermute(right, 'tensor', onward)  47.8 us
    ppermute x8, starting transfers between devices, both_ways(): lax.ppermute(right, 'tensor', onward)  42.3 us
    ppermute x8, waiting for transfers between devices, both_ways(): lax.ppermute(left, 'tensor', [(j, i) for i, j in onward])  32.6 us
    all_to_all x4, starting transfers between devices, exchange(): return lax.all_to_all(x, 'tensor', split_axis=0, concat_axis=0, tiled=True)  23.4 us
    ppermute x1, waiting for transfers between devices, per_device(): down_passed = lax.ppermute(down_grad, 'section', down_pairs)  19.8 us
    ppermute x1, waiting for transfers between devices, per_device(): up_xin = lax.ppermute(up_input[0], 'section', mirror)  18.1 us
    ppermute x8, starting transfers between devices, both_ways(): lax.ppermute(left, 'tensor', [(j, i) for i, j in onward])  10.2 us
  transfers between devices with their start and end apart: 27, of which 15 were waited for; matrix products, arithmetic and copies ran while one was open for 0% of the time, Pallas kernels for 30%

profile of v5, /device:TPU:3, one launch (start us, length us, event | category | flops | bytes accessed | tf_op | source)
XLA Modules:
  0.0 360.3 jit_solution(14158157444031042169)
XLA Ops:
  4.7 4.6 %all-to-all-start = ((bf16[4,128,1024]{2,1,0:T(8,128)(2,1)}), bf16[4,128,1024]{2,1,0:T(8,128)(2,1)}, u32[]{:S(2)}, u32[]{:S(2)}) async-start(bf16[4,128,1024]{2,1,0:T(8,128)(2,1)} %get-tuple-element.34), calls=%async_computation | async-start | bytes 2097152 | tf_op jit(solution)/shard_map/all_to_all | solution.py:376
  11.4 4.6 %collective-permute-start.1 = (bf16[128,4096]{1,0:T(8,128)(2,1)}, bf16[128,4096]{1,0:T(8,128)(2,1)}, u32[]{:S(2)}, u32[]{:S(2)}) collective-permute-start(bf16[128,4096]{1,0:T(8,128)(2,1)} %get-tuple-element.35.refs_0_), channel_id=1, source_target_pairs={{0,1},{1,2},{2,3},{4,5},{5,6},{6,7},{8,9},{9,10},{10,11},{12,13},{... | collective-permute-start | bytes 3145736 | tf_op jit(solution)/shard_map/ppermute | solution.py:383
  17.9 18.1 %collective-permute-done.refs_0_ = bf16[128,4096]{1,0:T(8,128)(2,1)} collective-permute-done((bf16[128,4096]{1,0:T(8,128)(2,1)}, bf16[128,4096]{1,0:T(8,128)(2,1)}, u32[]{:S(2)}, u32[]{:S(2)}) %collective-permute-start) | collective-permute-done | bytes 1048608 | tf_op jit(solution)/shard_map/ppermute | solution.py:460
  50.2 8.3 %collective-permute-done.3.refs_1_ = bf16[128,4096]{1,0:T(8,128)(2,1)} collective-permute-done((bf16[128,4096]{1,0:T(8,128)(2,1)}, bf16[128,4096]{1,0:T(8,128)(2,1)}, u32[]{:S(2)}, u32[]{:S(2)}) %collective-permute-start.3) | collective-permute-done | bytes 1048608 | tf_op jit(solution)/shard_map/ppermute | solution.py:461
  62.4 7.5 %collective-permute-start.6 = (bf16[128,4096]{1,0:T(8,128)(2,1)}, bf16[128,4096]{1,0:T(8,128)(2,1)}, u32[]{:S(2)}, u32[]{:S(2)}) collective-permute-start(bf16[128,4096]{1,0:T(8,128)(2,1)} %grad_mix.1.refs_4_.refs_0_.refs_8_), channel_id=1, source_target_pairs={{0,1},{1,2},{2,3},{4,5},{5,6},{6,7},{8,9},{9,10},{10,11},{12,13},{... | collective-permute-start | bytes 3145736 | tf_op jit(solution)/shard_map/ppermute | solution.py:383
  75.0 12.3 %project.2 = (bf16[512,4096]{1,0:T(8,128)(2,1)}, bf16[128,4096]{1,0:T(8,128)(2,1)}, bf16[128,4096]{1,0:T(8,128)(2,1)}, bf16[128,4096]{1,0:T(8,128)(2,1)}, bf16[128,4096]{1,0:T(8,128)(2,1)}) custom-call(bf16[512,1024]{1,0:T(8,128)(2,1)} %bitcast.2.refs_0_, bf16[1024,4096]{1,0:T(8,128)(2,1)} %bitcast.12, bf16[32,128,256]{2,1,0:T(8,128)(2,1)} %get-tuple-element.36.refs_2_, ...), custom_call_target="tpu_custom_call" | custom-call | flops 5368709120 | bytes 19922944 | tf_op jit(solution)/shard_map/project/pallas_call | solution.py:36
  91.6 4.9 %collective-permute-start.4 = (bf16[128,4096]{1,0:T(8,128)(2,1)}, bf16[128,4096]{1,0:T(8,128)(2,1)}, u32[]{:S(2)}, u32[]{:S(2)}) collective-permute-start(bf16[128,4096]{1,0:T(8,128)(2,1)} %get-tuple-element.40.refs_3_.refs_4_), channel_id=1, source_target_pairs={{0,1},{1,2},{2,3},{4,5},{5,6},{6,7},{8,9},{9,10},{10,11},{12,13},{... | collective-permute-start | bytes 3145736 | tf_op jit(solution)/shard_map/ppermute | solution.py:383
  97.8 12.4 %project.3 = (bf16[512,4096]{1,0:T(8,128)(2,1)}, bf16[128,4096]{1,0:T(8,128)(2,1)}, bf16[128,4096]{1,0:T(8,128)(2,1)}, bf16[128,4096]{1,0:T(8,128)(2,1)}, bf16[128,4096]{1,0:T(8,128)(2,1)}) custom-call(bf16[512,1024]{1,0:T(8,128)(2,1)} %bitcast.4.refs_0_.refs_1_, bf16[1024,4096]{1,0:T(8,128)(2,1)} %bitcast.13, ...), custom_call_target="tpu_custom_call" | custom-call | flops 5368709120 | bytes 19922944 | tf_op jit(solution)/shard_map/project/pallas_call | solution.py:36
  114.4 4.9 %collective-permute-start.10 = (bf16[128,4096]{1,0:T(8,128)(2,1)}, bf16[128,4096]{1,0:T(8,128)(2,1)}, u32[]{:S(2)}, u32[]{:S(2)}) collective-permute-start(bf16[128,4096]{1,0:T(8,128)(2,1)} %get-tuple-element.45.refs_4_), channel_id=1, source_target_pairs={{0,1},{1,2},{2,3},{4,5},{5,6},{6,7},{8,9},{9,10},{10,11},{12,13},{... | collective-permute-start | bytes 3145736 | tf_op jit(solution)/shard_map/ppermute | solution.py:383
  120.6 4.4 %payload.8 = (bf16[128,4096]{1,0:T(8,128)(2,1)}, bf16[128,4096]{1,0:T(8,128)(2,1)}) custom-call(bf16[128,4096]{1,0:T(8,128)(2,1)} %collective-permute-done.4.refs_0_.refs_2_, bf16[128,4096]{1,0:T(8,128)(2,1)} %collective-permute-done.5.refs_1_.refs_5_, bf16[128,4096]{1,0:T(8,128)(2,1)} %get-tuple-element.42.refs_2_.refs_3_, ...), custom_call_target="tpu_custom_call" | custom-call | bytes 6291456 | tf_op jit(solution)/shard_map/payload/pallas_call | solution.py:36
  125.0 5.0 %collective-permute-start.8 = (bf16[128,4096]{1,0:T(8,128)(2,1)}, bf16[128,4096]{1,0:T(8,128)(2,1)}, u32[]{:S(2)}, u32[]{:S(2)}) collective-permute-start(bf16[128,4096]{1,0:T(8,128)(2,1)} %get-tuple-element.46.refs_4_), channel_id=1, source_target_pairs={{0,1},{1,2},{2,3},{4,5},{5,6},{6,7},{8,9},{9,10},{10,11},{12,13},{... | collective-permute-start | bytes 3145736 | tf_op jit(solution)/shard_map/ppermute | solution.py:383
  133.3 6.3 %collective-permute-done.11.refs_1_.refs_5_.refs_13_ = bf16[128,4096]{1,0:T(8,128)(2,1)} collective-permute-done((bf16[128,4096]{1,0:T(8,128)(2,1)}, bf16[128,4096]{1,0:T(8,128)(2,1)}, u32[]{:S(2)}, u32[]{:S(2)}) %collective-permute-start.11) | collective-permute-done | bytes 1048608 | tf_op jit(solution)/shard_map/ppermute | solution.py:384
  139.6 4.4 %payload.9 = (bf16[128,4096]{1,0:T(8,128)(2,1)}, bf16[128,4096]{1,0:T(8,128)(2,1)}) custom-call(bf16[128,4096]{1,0:T(8,128)(2,1)} %collective-permute-done.10.refs_0_.refs_2_.refs_10_, bf16[128,4096]{1,0:T(8,128)(2,1)} %collective-permute-done.11.refs_1_.refs_5_.refs_13_, bf16[128,4096]{1,0:T(8,128)(2,1)} %get-tuple-element.50.refs_2_.refs_3_, ...), custom_call_target="tpu_custom_call" | custom-call | bytes 6291456 | tf_op jit(solution)/shard_map/payload/pallas_call | solution.py:36
  144.0 6.2 %collective-permute-start.12 = (bf16[128,4096]{1,0:T(8,128)(2,1)}, bf16[128,4096]{1,0:T(8,128)(2,1)}, u32[]{:S(2)}, u32[]{:S(2)}) collective-permute-start(bf16[128,4096]{1,0:T(8,128)(2,1)} %get-tuple-element.51.refs_4_), channel_id=1, source_target_pairs={{0,1},{1,2},{2,3},{4,5},{5,6},{6,7},{8,9},{9,10},{10,11},{12,13},{... | collective-permute-start | bytes 3145736 | tf_op jit(solution)/shard_map/ppermute | solution.py:383
  155.8 6.3 %collective-permute-done.9.refs_1_.refs_6_ = bf16[128,4096]{1,0:T(8,128)(2,1)} collective-permute-done((bf16[128,4096]{1,0:T(8,128)(2,1)}, bf16[128,4096]{1,0:T(8,128)(2,1)}, u32[]{:S(2)}, u32[]{:S(2)}) %collective-permute-start.9) | collective-permute-done | bytes 1048608 | tf_op jit(solution)/shard_map/ppermute | solution.py:384
  166.3 12.0 %collective-permute-done.12.refs_0_.refs_3_.refs_11_ = bf16[128,4096]{1,0:T(8,128)(2,1)} collective-permute-done((bf16[128,4096]{1,0:T(8,128)(2,1)}, bf16[128,4096]{1,0:T(8,128)(2,1)}, u32[]{:S(2)}, u32[]{:S(2)}) %collective-permute-start.12) | collective-permute-done | bytes 1048608 | tf_op jit(solution)/shard_map/ppermute | solution.py:383
  178.3 6.3 %collective-permute-done.13.refs_1_.refs_6_.refs_14_ = bf16[128,4096]{1,0:T(8,128)(2,1)} collective-permute-done((bf16[128,4096]{1,0:T(8,128)(2,1)}, bf16[128,4096]{1,0:T(8,128)(2,1)}, u32[]{:S(2)}, u32[]{:S(2)}) %collective-permute-start.13) | collective-permute-done | bytes 1048608 | tf_op jit(solution)/shard_map/ppermute | solution.py:384
  188.8 14.4 %back.2 = (bf16[512,4096]{1,0:T(8,128)(2,1)}, bf16[512,1024]{1,0:T(8,128)(2,1)}) custom-call(bf16[128,4096]{1,0:T(8,128)(2,1)} %grad_mix.1.refs_4_.refs_0_.refs_8_, bf16[128,4096]{1,0:T(8,128)(2,1)} %collective-permute-done.6.refs_0_.refs_1_.refs_9_, bf16[128,4096]{1,0:T(8,128)(2,1)} %collective-permute-done.10.refs_0_.refs_2_.refs_10_, ...), custom_call_target="tpu_custom_call" | custom-call | flops 5368709120 | bytes 23068672 | tf_op jit(solution)/shard_map/back/pallas_call | solution.py:36
  203.3 6.5 %all-to-all-start.2 = ((bf16[4,128,1024]{2,1,0:T(8,128)(2,1)}), bf16[4,128,1024]{2,1,0:T(8,128)(2,1)}, u32[]{:S(2)}, u32[]{:S(2)}) async-start(bf16[4,128,1024]{2,1,0:T(8,128)(2,1)} %bitcast.22), calls=%async_computation.2 | async-start | bytes 2097152 | tf_op jit(solution)/shard_map/all_to_all | solution.py:376
  215.4 5.0 %collective-permute-start.16 = (bf16[128,4096]{1,0:T(8,128)(2,1)}, bf16[128,4096]{1,0:T(8,128)(2,1)}, u32[]{:S(2)}, u32[]{:S(2)}) collective-permute-start(bf16[128,4096]{1,0:T(8,128)(2,1)} %get-tuple-element.56.refs_9_), channel_id=1, source_target_pairs={{0,1},{1,2},{2,3},{4,5},{5,6},{6,7},{8,9},{9,10},{10,11},{12,13},{... | collective-permute-start | bytes 3145736 | tf_op jit(solution)/shard_map/ppermute | solution.py:383
  221.7 13.8 %filter_gradient.1 = f32[8,4,128]{2,1,0:T(4,128)} custom-call(bf16[128,4096]{1,0:T(8,128)(2,1)} %get-tuple-element.35.refs_0_, bf16[128,4096]{1,0:T(8,128)(2,1)} %collective-permute-done.1.refs_2_.refs_0_.refs_1_, bf16[128,4096]{1,0:T(8,128)(2,1)} %collective-permute-done.4.refs_0_.refs_2_, bf16[128,4096]{1,0:T(8,128)(2,1)} %collective-permute-done.8.refs_0_.refs_3_, ...), custom_call_target="tpu_custom_call" | custom-call | flops 2147483648 | bytes 23085056 | tf_op jit(solution)/shard_map/filter_gradient/pallas_call | solution.py:36
  235.4 8.5 %collective-permute-done.14.refs_10_.refs_4_ = bf16[128,4096]{1,0:T(8,128)(2,1)} collective-permute-done((bf16[128,4096]{1,0:T(8,128)(2,1)}, bf16[128,4096]{1,0:T(8,128)(2,1)}, u32[]{:S(2)}, u32[]{:S(2)}) %collective-permute-start.14) | collective-permute-done | bytes 1048608 | tf_op jit(solution)/shard_map/ppermute | solution.py:383
  243.9 5.9 %collective-permute-done.15.refs_11_.refs_5_ = bf16[128,4096]{1,0:T(8,128)(2,1)} collective-permute-done((bf16[128,4096]{1,0:T(8,128)(2,1)}, bf16[128,4096]{1,0:T(8,128)(2,1)}, u32[]{:S(2)}, u32[]{:S(2)}) %collective-permute-start.15) | collective-permute-done | bytes 1048608 | tf_op jit(solution)/shard_map/ppermute | solution.py:384
  249.9 16.5 %collective-permute-done.16.refs_12_.refs_4_ = bf16[128,4096]{1,0:T(8,128)(2,1)} collective-permute-done((bf16[128,4096]{1,0:T(8,128)(2,1)}, bf16[128,4096]{1,0:T(8,128)(2,1)}, u32[]{:S(2)}, u32[]{:S(2)}) %collective-permute-start.16) | collective-permute-done | bytes 1048608 | tf_op jit(solution)/shard_map/ppermute | solution.py:383
  266.4 5.9 %collective-permute-done.17.refs_13_.refs_5_ = bf16[128,4096]{1,0:T(8,128)(2,1)} collective-permute-done((bf16[128,4096]{1,0:T(8,128)(2,1)}, bf16[128,4096]{1,0:T(8,128)(2,1)}, u32[]{:S(2)}, u32[]{:S(2)}) %collective-permute-start.17) | collective-permute-done | bytes 1048608 | tf_op jit(solution)/shard_map/ppermute | solution.py:384
  272.3 14.4 %back.3 = (bf16[512,4096]{1,0:T(8,128)(2,1)}, bf16[512,1024]{1,0:T(8,128)(2,1)}) custom-call(bf16[128,4096]{1,0:T(8,128)(2,1)} %get-tuple-element.35.refs_0_, bf16[128,4096]{1,0:T(8,128)(2,1)} %collective-permute-done.1.refs_2_.refs_0_.refs_1_, bf16[128,4096]{1,0:T(8,128)(2,1)} %collective-permute-done.4.refs_0_.refs_2_, ...), custom_call_target="tpu_custom_call" | custom-call | flops 5368709120 | bytes 23068672 | tf_op jit(solution)/shard_map/back/pallas_call | solution.py:36
  286.7 8.0 %all-to-all-start.3 = ((bf16[4,128,1024]{2,1,0:T(8,128)(2,1)}), bf16[4,128,1024]{2,1,0:T(8,128)(2,1)}, u32[]{:S(2)}, u32[]{:S(2)}) async-start(bf16[4,128,1024]{2,1,0:T(8,128)(2,1)} %bitcast.21), calls=%async_computation.3 | async-start | bytes 2097152 | tf_op jit(solution)/shard_map/all_to_all | solution.py:376
  294.7 5.2 %finish.2.refs_4_ = bf16[1,128,4096]{2,1,0:T(8,128)(2,1)} custom-call(bf16[128,4096]{1,0:T(8,128)(2,1)} %collective-permute-done.refs_0_, bf16[128,4096]{1,0:T(8,128)(2,1)} %collective-permute-done.3.refs_1_, bf16[4,128,1024]{2,1,0:T(8,128)(2,1)} %all-to-all-done.2.refs_2_, bf16[128,4096]{1,0:T(8,128)(2,1)} %get-tuple-element.61.refs_3_, ...), custom_call_target="tpu_custom_call" | custom-call | bytes 7340032 | tf_op jit(solution)/shard_map/finish/pallas_call | solution.py:36
  308.2 14.7 %weight_gradient.1.refs_4_ = bf16[1024,4096]{1,0:T(8,128)(2,1)} custom-call(bf16[512,1024]{1,0:T(8,128)(2,1)} %bitcast.2.refs_0_, bf16[512,1024]{1,0:T(8,128)(2,1)} %bitcast.4.refs_0_.refs_1_, bf16[512,4096]{1,0:T(8,128)(2,1)} %get-tuple-element.59.refs_6_.refs_2_, bf16[512,4096]{1,0:T(8,128)(2,1)} %get-tuple-element.57.refs_16_.refs_3_, ...), custom_call_target="tpu_custom_call" | custom-call | flops 8589934592 | bytes 18874368 | tf_op jit(solution)/shard_map/weight_gradient/pallas_call | solution.py:36
  325.5 5.2 %finish.3 = bf16[1,128,4096]{2,1,0:T(8,128)(2,1)} custom-call(bf16[128,4096]{1,0:T(8,128)(2,1)} %bitcast.18, bf16[128,4096]{1,0:T(8,128)(2,1)} %bitcast.20, bf16[4,128,1024]{2,1,0:T(8,128)(2,1)} %all-to-all-done.3.refs_2_, bf16[128,4096]{1,0:T(8,128)(2,1)} %get-tuple-element.63.refs_3_, bf16[128,4096]{1,0:T(8,128)(2,1)} %collective-permute-done.14.refs_10_.refs_4_, ...), custom_call_target="tpu_custom_call" | custom-call | bytes 7340032 | tf_op jit(solution)/shard_map/finish/pallas_call | solution.py:36
  330.7 6.6 %collective-permute-start.22 = (bf16[1,128,4096]{2,1,0:T(8,128)(2,1)}, bf16[1,128,4096]{2,1,0:T(8,128)(2,1)S(1)}, u32[]{:S(2)}, u32[]{:S(2)}) collective-permute-start(bf16[1,128,4096]{2,1,0:T(8,128)(2,1)} %finish.3), channel_id=1, source_target_pairs={{4,0},{8,4},{12,8},{16,12},{20,16},{24,20},{28,24},{5,1},{9,5},{13... | collective-permute-start | bytes 3145736 | tf_op jit(solution)/shard_map/ppermute | solution.py:498
  337.2 19.8 %collective-permute-done.22 = bf16[1,128,4096]{2,1,0:T(8,128)(2,1)S(1)} collective-permute-done((bf16[1,128,4096]{2,1,0:T(8,128)(2,1)}, bf16[1,128,4096]{2,1,0:T(8,128)(2,1)S(1)}, u32[]{:S(2)}, u32[]{:S(2)}) %collective-permute-start.22) | collective-permute-done | bytes 1048608 | tf_op jit(solution)/shard_map/ppermute | solution.py:498
  (51 shorter events, 80.9 us)
Async XLA Ops:
  4.7 35.0 %all-to-all-start = ((bf16[4,128,1024]{2,1,0:T(8,128)(2,1)}), bf16[4,128,1024]{2,1,0:T(8,128)(2,1)}, u32[]{:S(2)}, u32[]{:S(2)}) async-start(bf16[4,128,1024]{2,1,0:T(8,128)(2,1)} %get-tuple-element.34), calls=%async_computation | async-start | bytes 2097152 | tf_op jit(solution)/shard_map/all_to_all | solution.py:376
  9.3 26.7 %collective-permute-start = (bf16[128,4096]{1,0:T(8,128)(2,1)}, bf16[128,4096]{1,0:T(8,128)(2,1)}, u32[]{:S(2)}, u32[]{:S(2)}) collective-permute-start(bf16[128,4096]{1,0:T(8,128)(2,1)} %bitcast.29), channel_id=1, source_target_pairs={{0,28},{4,24},{8,20},{12,16},{16,12},{20,8},{24,4},{28,0},{1,29},{... | collective-permute-start | bytes 3145736 | tf_op jit(solution)/shard_map/ppermute | solution.py:460
  11.4 37.0 %collective-permute-start.1 = (bf16[128,4096]{1,0:T(8,128)(2,1)}, bf16[128,4096]{1,0:T(8,128)(2,1)}, u32[]{:S(2)}, u32[]{:S(2)}) collective-permute-start(bf16[128,4096]{1,0:T(8,128)(2,1)} %get-tuple-element.35.refs_0_), channel_id=1, source_target_pairs={{0,1},{1,2},{2,3},{4,5},{5,6},{6,7},{8,9},{9,10},{10,11},{12,13},{... | collective-permute-start | bytes 3145736 | tf_op jit(solution)/shard_map/ppermute | solution.py:383
  16.0 34.2 %collective-permute-start.2 = (bf16[128,4096]{1,0:T(8,128)(2,1)}, bf16[128,4096]{1,0:T(8,128)(2,1)}, u32[]{:S(2)}, u32[]{:S(2)}) collective-permute-start(bf16[128,4096]{1,0:T(8,128)(2,1)} %get-tuple-element.35.refs_0_), channel_id=1, source_target_pairs={{1,0},{2,1},{3,2},{5,4},{6,5},{7,6},{9,8},{10,9},{11,10},{13,12},{... | collective-permute-start | bytes 3145736 | tf_op jit(solution)/shard_map/ppermute | solution.py:384
  17.3 41.2 %collective-permute-start.3 = (bf16[128,4096]{1,0:T(8,128)(2,1)}, bf16[128,4096]{1,0:T(8,128)(2,1)}, u32[]{:S(2)}, u32[]{:S(2)}) collective-permute-start(bf16[128,4096]{1,0:T(8,128)(2,1)} %bitcast.30), channel_id=1, source_target_pairs={{0,28},{4,24},{8,20},{12,16},{16,12},{20,8},{24,4},{28,0},{1,29},{... | collective-permute-start | bytes 3145736 | tf_op jit(solution)/shard_map/ppermute | solution.py:461
  39.7 58.1 %all-to-all-start.1 = ((bf16[4,128,1024]{2,1,0:T(8,128)(2,1)}), bf16[4,128,1024]{2,1,0:T(8,128)(2,1)}, u32[]{:S(2)}, u32[]{:S(2)}) async-start(bf16[4,128,1024]{2,1,0:T(8,128)(2,1)} %prepare.3.refs_3_), calls=%async_computation.1 | async-start | bytes 2097152 | tf_op jit(solution)/shard_map/all_to_all | solution.py:376
  62.4 47.8 %collective-permute-start.6 = (bf16[128,4096]{1,0:T(8,128)(2,1)}, bf16[128,4096]{1,0:T(8,128)(2,1)}, u32[]{:S(2)}, u32[]{:S(2)}) collective-permute-start(bf16[128,4096]{1,0:T(8,128)(2,1)} %grad_mix.1.refs_4_.refs_0_.refs_8_), channel_id=1, source_target_pairs={{0,1},{1,2},{2,3},{4,5},{5,6},{6,7},{8,9},{9,10},{10,11},{12,13},{... | collective-permute-start | bytes 3145736 | tf_op jit(solution)/shard_map/ppermute | solution.py:383
  69.9 40.3 %collective-permute-start.7 = (bf16[128,4096]{1,0:T(8,128)(2,1)}, bf16[128,4096]{1,0:T(8,128)(2,1)}, u32[]{:S(2)}, u32[]{:S(2)}) collective-permute-start(bf16[128,4096]{1,0:T(8,128)(2,1)} %grad_mix.1.refs_4_.refs_0_.refs_8_), channel_id=1, source_target_pairs={{1,0},{2,1},{3,2},{5,4},{6,5},{7,6},{9,8},{10,9},{11,10},{13,12},{... | collective-permute-start | bytes 3145736 | tf_op jit(solution)/shard_map/ppermute | solution.py:384
  91.6 29.0 %collective-permute-start.4 = (bf16[128,4096]{1,0:T(8,128)(2,1)}, bf16[128,4096]{1,0:T(8,128)(2,1)}, u32[]{:S(2)}, u32[]{:S(2)}) collective-permute-start(bf16[128,4096]{1,0:T(8,128)(2,1)} %get-tuple-element.40.refs_3_.refs_4_), channel_id=1, source_target_pairs={{0,1},{1,2},{2,3},{4,5},{5,6},{6,7},{8,9},{9,10},{10,11},{12,13},{... | collective-permute-start | bytes 3145736 | tf_op jit(solution)/shard_map/ppermute | solution.py:383
  96.5 24.1 %collective-permute-start.5 = (bf16[128,4096]{1,0:T(8,128)(2,1)}, bf16[128,4096]{1,0:T(8,128)(2,1)}, u32[]{:S(2)}, u32[]{:S(2)}) collective-permute-start(bf16[128,4096]{1,0:T(8,128)(2,1)} %get-tuple-element.41.refs_4_.refs_5_), channel_id=1, source_target_pairs={{1,0},{2,1},{3,2},{5,4},{6,5},{7,6},{9,8},{10,9},{11,10},{13,12},{... | collective-permute-start | bytes 3145736 | tf_op jit(solution)/shard_map/ppermute | solution.py:384
  114.4 18.9 %collective-permute-start.10 = (bf16[128,4096]{1,0:T(8,128)(2,1)}, bf16[128,4096]{1,0:T(8,128)(2,1)}, u32[]{:S(2)}, u32[]{:S(2)}) collective-permute-start(bf16[128,4096]{1,0:T(8,128)(2,1)} %get-tuple-element.45.refs_4_), channel_id=1, source_target_pairs={{0,1},{1,2},{2,3},{4,5},{5,6},{6,7},{8,9},{9,10},{10,11},{12,13},{... | collective-permute-start | bytes 3145736 | tf_op jit(solution)/shard_map/ppermute | solution.py:383
  119.3 20.4 %collective-permute-start.11 = (bf16[128,4096]{1,0:T(8,128)(2,1)}, bf16[128,4096]{1,0:T(8,128)(2,1)}, u32[]{:S(2)}, u32[]{:S(2)}) collective-permute-start(bf16[128,4096]{1,0:T(8,128)(2,1)} %get-tuple-element.49), channel_id=1, source_target_pairs={{1,0},{2,1},{3,2},{5,4},{6,5},{7,6},{9,8},{10,9},{11,10},{13,12},{... | collective-permute-start | bytes 3145736 | tf_op jit(solution)/shard_map/ppermute | solution.py:384
  125.0 30.8 %collective-permute-start.8 = (bf16[128,4096]{1,0:T(8,128)(2,1)}, bf16[128,4096]{1,0:T(8,128)(2,1)}, u32[]{:S(2)}, u32[]{:S(2)}) collective-permute-start(bf16[128,4096]{1,0:T(8,128)(2,1)} %get-tuple-element.46.refs_4_), channel_id=1, source_target_pairs={{0,1},{1,2},{2,3},{4,5},{5,6},{6,7},{8,9},{9,10},{10,11},{12,13},{... | collective-permute-start | bytes 3145736 | tf_op jit(solution)/shard_map/ppermute | solution.py:383
  129.9 32.2 %collective-permute-start.9 = (bf16[128,4096]{1,0:T(8,128)(2,1)}, bf16[128,4096]{1,0:T(8,128)(2,1)}, u32[]{:S(2)}, u32[]{:S(2)}) collective-permute-start(bf16[128,4096]{1,0:T(8,128)(2,1)} %get-tuple-element.47.refs_5_), channel_id=1, source_target_pairs={{1,0},{2,1},{3,2},{5,4},{6,5},{7,6},{9,8},{10,9},{11,10},{13,12},{... | collective-permute-start | bytes 3145736 | tf_op jit(solution)/shard_map/ppermute | solution.py:384
  144.0 34.3 %collective-permute-start.12 = (bf16[128,4096]{1,0:T(8,128)(2,1)}, bf16[128,4096]{1,0:T(8,128)(2,1)}, u32[]{:S(2)}, u32[]{:S(2)}) collective-permute-start(bf16[128,4096]{1,0:T(8,128)(2,1)} %get-tuple-element.51.refs_4_), channel_id=1, source_target_pairs={{0,1},{1,2},{2,3},{4,5},{5,6},{6,7},{8,9},{9,10},{10,11},{12,13},{... | collective-permute-start | bytes 3145736 | tf_op jit(solution)/shard_map/ppermute | solution.py:383
  150.2 34.4 %collective-permute-start.13 = (bf16[128,4096]{1,0:T(8,128)(2,1)}, bf16[128,4096]{1,0:T(8,128)(2,1)}, u32[]{:S(2)}, u32[]{:S(2)}) collective-permute-start(bf16[128,4096]{1,0:T(8,128)(2,1)} %get-tuple-element.52), channel_id=1, source_target_pairs={{1,0},{2,1},{3,2},{5,4},{6,5},{7,6},{9,8},{10,9},{11,10},{13,12},{... | collective-permute-start | bytes 3145736 | tf_op jit(solution)/shard_map/ppermute | solution.py:384
  203.3 83.5 %all-to-all-start.2 = ((bf16[4,128,1024]{2,1,0:T(8,128)(2,1)}), bf16[4,128,1024]{2,1,0:T(8,128)(2,1)}, u32[]{:S(2)}, u32[]{:S(2)}) async-start(bf16[4,128,1024]{2,1,0:T(8,128)(2,1)} %bitcast.22), calls=%async_computation.2 | async-start | bytes 2097152 | tf_op jit(solution)/shard_map/all_to_all | solution.py:376
  209.8 34.1 %collective-permute-start.14 = (bf16[128,4096]{1,0:T(8,128)(2,1)}, bf16[128,4096]{1,0:T(8,128)(2,1)}, u32[]{:S(2)}, u32[]{:S(2)}) collective-permute-start(bf16[128,4096]{1,0:T(8,128)(2,1)} %get-tuple-element.54.refs_4_), channel_id=1, source_target_pairs={{0,1},{1,2},{2,3},{4,5},{5,6},{6,7},{8,9},{9,10},{10,11},{12,13},{... | collective-permute-start | bytes 3145736 | tf_op jit(solution)/shard_map/ppermute | solution.py:383
  214.1 35.7 %collective-permute-start.15 = (bf16[128,4096]{1,0:T(8,128)(2,1)}, bf16[128,4096]{1,0:T(8,128)(2,1)}, u32[]{:S(2)}, u32[]{:S(2)}) collective-permute-start(bf16[128,4096]{1,0:T(8,128)(2,1)} %get-tuple-element.55.refs_5_), channel_id=1, source_target_pairs={{1,0},{2,1},{3,2},{5,4},{6,5},{7,6},{9,8},{10,9},{11,10},{13,12},{... | collective-permute-start | bytes 3145736 | tf_op jit(solution)/shard_map/ppermute | solution.py:384
  215.4 51.0 %collective-permute-start.16 = (bf16[128,4096]{1,0:T(8,128)(2,1)}, bf16[128,4096]{1,0:T(8,128)(2,1)}, u32[]{:S(2)}, u32[]{:S(2)}) collective-permute-start(bf16[128,4096]{1,0:T(8,128)(2,1)} %get-tuple-element.56.refs_9_), channel_id=1, source_target_pairs={{0,1},{1,2},{2,3},{4,5},{5,6},{6,7},{8,9},{9,10},{10,11},{12,13},{... | collective-permute-start | bytes 3145736 | tf_op jit(solution)/shard_map/ppermute | solution.py:383
  220.4 51.9 %collective-permute-start.17 = (bf16[128,4096]{1,0:T(8,128)(2,1)}, bf16[128,4096]{1,0:T(8,128)(2,1)}, u32[]{:S(2)}, u32[]{:S(2)}) collective-permute-start(bf16[128,4096]{1,0:T(8,128)(2,1)} %get-tuple-element.58), channel_id=1, source_target_pairs={{1,0},{2,1},{3,2},{5,4},{6,5},{7,6},{9,8},{10,9},{11,10},{13,12},{... | collective-permute-start | bytes 3145736 | tf_op jit(solution)/shard_map/ppermute | solution.py:384
  286.7 38.8 %all-to-all-start.3 = ((bf16[4,128,1024]{2,1,0:T(8,128)(2,1)}), bf16[4,128,1024]{2,1,0:T(8,128)(2,1)}, u32[]{:S(2)}, u32[]{:S(2)}) async-start(bf16[4,128,1024]{2,1,0:T(8,128)(2,1)} %bitcast.21), calls=%async_computation.3 | async-start | bytes 2097152 | tf_op jit(solution)/shard_map/all_to_all | solution.py:376
  294.7 8.3 %copy-start = (f32[8,4,128]{2,1,0:T(4,128)S(1)}, f32[8,4,128]{2,1,0:T(4,128)}, u32[]{:S(2)}) copy-start(f32[8,4,128]{2,1,0:T(4,128)} %filter_gradient.1) | copy-start | bytes 49156
  299.9 25.6 %collective-permute-start.21 = (bf16[1,128,4096]{2,1,0:T(8,128)(2,1)}, bf16[1,128,4096]{2,1,0:T(8,128)(2,1)}, u32[]{:S(2)}, u32[]{:S(2)}) collective-permute-start(bf16[1,128,4096]{2,1,0:T(8,128)(2,1)} %finish.2.refs_4_), channel_id=1, source_target_pairs={{28,4},{24,8},{20,12},{16,16},{12,20},{8,24},{4,28},{29,5},{25,9},... | collective-permute-start | bytes 3145736 | tf_op jit(solution)/shard_map/ppermute | solution.py:494
  303.0 19.9 %collective-permute-start.18 = (f32[1,32,128]{2,1,0:T(8,128)S(1)}, f32[1,32,128]{2,1,0:T(8,128)S(1)}, u32[]{:S(2)}, u32[]{:S(2)}) collective-permute-start(f32[1,32,128]{2,1,0:T(8,128)S(1)} %bitcast.25), channel_id=1, source_target_pairs={{0,1},{1,2},{2,3},{3,0},{4,5},{5,6},{6,7},{7,4},{8,9},{9,10},{10,1... | collective-permute-start | bytes 49160 | tf_op jit(solution)/shard_map/ppermute | solution.py:438
  306.1 16.9 %collective-permute-start.19 = (f32[1,32,128]{2,1,0:T(8,128)S(1)}, f32[1,32,128]{2,1,0:T(8,128)S(1)}, u32[]{:S(2)}, u32[]{:S(2)}) collective-permute-start(f32[1,32,128]{2,1,0:T(8,128)S(1)} %bitcast.26), channel_id=1, source_target_pairs={{0,2},{1,3},{2,0},{3,1},{4,6},{5,7},{6,4},{7,5},{8,10},{9,11},{10,... | collective-permute-start | bytes 49160 | tf_op jit(solution)/shard_map/ppermute | solution.py:438
  306.6 16.3 %collective-permute-start.20 = (f32[1,32,128]{2,1,0:T(8,128)S(1)}, f32[1,32,128]{2,1,0:T(8,128)S(1)}, u32[]{:S(2)}, u32[]{:S(2)}) collective-permute-start(f32[1,32,128]{2,1,0:T(8,128)S(1)} %bitcast.27), channel_id=1, source_target_pairs={{0,3},{1,0},{2,1},{3,2},{4,7},{5,4},{6,5},{7,6},{8,11},{9,8},{10,9... | collective-permute-start | bytes 49160 | tf_op jit(solution)/shard_map/ppermute | solution.py:438
  322.9 0.6 copy-start.1
  322.9 0.6 copy-start.2
  323.5 0.6 copy-start.3
  330.7 26.4 %collective-permute-start.22 = (bf16[1,128,4096]{2,1,0:T(8,128)(2,1)}, bf16[1,128,4096]{2,1,0:T(8,128)(2,1)S(1)}, u32[]{:S(2)}, u32[]{:S(2)}) collective-permute-start(bf16[1,128,4096]{2,1,0:T(8,128)(2,1)} %finish.3), channel_id=1, source_target_pairs={{4,0},{8,4},{12,8},{16,12},{20,16},{24,20},{28,24},{5,1},{9,5},{13... | collective-permute-start | bytes 3145736 | tf_op jit(solution)/shard_map/ppermute | solution.py:498

commit v6 on v5

--- a/solution.py
+++ b/solution.py
@@ -99,17 +99,17 @@
         refs[-1][...] = (cot_ref[0][...].astype(f32) * normed).astype(bf16)
 
 
-def prepare(*args):
+def prepare(*args, after=()):
     rows, width = args[0].shape
     blocks = lax.axis_size("tensor")
-    step = 32
+    step = 64
     spec = pl.BlockSpec((step, width), lambda i: (i, 0))
     normed_spec = pl.BlockSpec((blocks, step, width // blocks), lambda i: (0, i, 0))
     extra = len(args) - 1
     return call(
         prepare_kernel,
         args,
-        (),
+        after,
         grid=(rows // step,),
         in_specs=[spec] * len(args),
         out_specs=[normed_spec] + [spec] * extra,
@@ -125,7 +125,7 @@
 
 def grad_mix(xin, cot, after=()):
     rows, width = xin.shape
-    step = 32
+    step = 64
     spec = pl.BlockSpec((step, width), lambda i: (i, 0))
     return call(
         mix_kernel,
@@ -166,7 +166,7 @@
     rows = tokens // blocks
     width = weight.shape[1]
     groups, taps, _ = causal.shape
-    step = 4
+    step = 8
     tile = width // groups * step
     part, *mixed = call(
         project_kernel,
@@ -242,7 +242,7 @@
     tokens = (len(mixes) + 1) // 2 * rows
     depth = weight.shape[0]
     groups, taps, _ = ahead.shape
-    step = 4
+    step = 8
     tile = width // groups * step
     return call(
         functools.partial(back_kernel, len(mixes)),
@@ -293,7 +293,7 @@
 def filter_gradient(down_mixes, down_part, up_mixes, up_part, groups, taps, after=()):
     rows, width = down_mixes[0].shape
     tokens = down_part.shape[0]
-    step = 4
+    step = 8
     tile = width // groups * step
     count = len(down_mixes)
     block = [pl.BlockSpec((rows, tile), lambda i: (0, i))] * count
@@ -324,7 +324,7 @@
 def weight_gradient(down_x, up_x, down_g, up_g, after=()):
     tokens, depth = down_x.shape
     width = down_g.shape[1]
-    tile = width // 8
+    tile = width // 4
     whole = pl.BlockSpec((tokens, depth), lambda i: (0, 0))
     part = pl.BlockSpec((tokens, tile), lambda i: (0, i))
     return call(
@@ -355,7 +355,7 @@
 def finish(xin, cot, mixed, returned, after=()):
     rows, width = xin.shape
     blocks, _, depth = returned.shape
-    step = 32
+    step = 64
     spec = pl.BlockSpec((step, width), lambda i: (i, 0))
     return call(
         finish_kernel,
@@ -405,7 +405,7 @@
 def payload(s, arrived, pieces, after=()):
     blocks = len(pieces)
     rows, width = pieces[0].shape
-    step = 32
+    step = 64
     spec = pl.BlockSpec((step, width), lambda i: (i, 0))
     return call(
         functools.partial(payload_kernel, s),
@@ -465,7 +465,7 @@
     down_x = exchange(down_normed).reshape(-1, depth)
     down_arrivals = [both_ways(down_mix, down_mix)]
     causal, ahead = toeplitz(filters[0])
-    (up_normed,) = prepare(up_xin)
+    (up_normed,) = prepare(up_xin, after=(ahead,))
     up_x = exchange(up_normed).reshape(-1, depth)
     up_mix = grad_mix(up_xin, up_cot, after=down_arrivals[0])
     up_arrivals = [both_ways(up_mix, up_mix)]
@@ -483,19 +483,19 @@
     up_mixes, up_conv = sort_arrivals(up_mix, up_pieces, up_arrivals)
     up_g, up_back = back(up_mixes, weight, ahead, after=(last,))
     up_back = exchange(up_back)
-    taps = filter_gradient(
-        down_mixes, down_part, up_mixes, up_part, *filters.shape[1:], after=(up_g,)
-    )
     down_g, down_back = back(
-        down_mixes, weight, ahead, after=(taps, *down_arrivals[-1], *up_arrivals[-1])
+        down_mixes, weight, ahead, after=(up_g, *down_arrivals[-1], *up_arrivals[-1])
     )
     down_back = exchange(down_back)
     up_grad = finish(up_xin, up_cot, up_conv, up_back, after=(down_g,))
     up_passed = lax.ppermute(up_grad, "section", up_pairs)
-    weight_grad = weight_gradient(down_x, up_x, down_g, up_g, after=(up_grad,))
-    taps = sum_all(taps, after=(weight_grad,))
+    taps = filter_gradient(
+        down_mixes, down_part, up_mixes, up_part, *filters.shape[1:], after=(up_grad,)
+    )
     down_grad = finish(down_xin, down_cot, down_conv, down_back, after=(taps, up_passed))
     down_passed = lax.ppermute(down_grad, "section", down_pairs)
+    weight_grad = weight_gradient(down_x, up_x, down_g, up_g, after=(down_grad,))
+    taps = sum_all(taps, after=(weight_grad,))
     return weight_grad[None], taps, down_passed, up_passed
 
 

time: 364 us -> 361 us (level)
  the two profiles are of different devices: /device:TPU:3 before, /device:TPU:10 now
where the time goes in v6:
time: 361 us; the launch traced here: 359 us
  waiting for transfers between devices  154 us (43%)
  Pallas kernels  116 us (32%)
  starting transfers between devices  81.9 us (23%)
  local copies, waits for them, and re-layouts  5.76 us (2%)
    pallas_call x19, Pallas kernels, call(): pl.pallas_call(body, in_specs=list(in_specs) + unread, out_shape=out_shap...  116 us
    ppermute x8, waiting for transfers between devices, both_ways(): lax.ppermute(left, 'tensor', [(j, i) for i, j in onward])  60.9 us
    ppermute x8, waiting for transfers between devices, both_ways(): lax.ppermute(right, 'tensor', onward)  54.1 us
    ppermute x8, starting transfers between devices, both_ways(): lax.ppermute(right, 'tensor', onward)  30.5 us
    ppermute x8, starting transfers between devices, both_ways(): lax.ppermute(left, 'tensor', [(j, i) for i, j in onward])  19.8 us
    all_to_all x4, starting transfers between devices, exchange(): return lax.all_to_all(x, 'tensor', split_axis=0, concat_axis=0, tiled=True)  19.3 us
    ppermute x1, waiting for transfers between devices, per_device(): up_cot = lax.ppermute(up_cot[0], 'section', mirror)  14.6 us
    ppermute x1, waiting for transfers between devices, per_device(): up_xin = lax.ppermute(up_input[0], 'section', mirror)  14.3 us
  transfers between devices with their start and end apart: 27, of which 14 were waited for; matrix products, arithmetic and copies ran while one was open for 0% of the time, Pallas kernels for 26%

profile of v6, /device:TPU:10, one launch (start us, length us, event | category | flops | bytes accessed | tf_op | source)
XLA Modules:
  0.0 358.7 jit_solution(16135421629559500913)
XLA Ops:
  3.6 5.3 %all-to-all-start = ((bf16[4,128,1024]{2,1,0:T(8,128)(2,1)}), bf16[4,128,1024]{2,1,0:T(8,128)(2,1)}, u32[]{:S(2)}, u32[]{:S(2)}) async-start(bf16[4,128,1024]{2,1,0:T(8,128)(2,1)} %get-tuple-element.34), calls=%async_computation | async-start | bytes 2097152 | tf_op jit(solution)/shard_map/all_to_all | solution.py:376
  13.5 3.9 %collective-permute-start.1 = (bf16[128,4096]{1,0:T(8,128)(2,1)}, bf16[128,4096]{1,0:T(8,128)(2,1)}, u32[]{:S(2)}, u32[]{:S(2)}) collective-permute-start(bf16[128,4096]{1,0:T(8,128)(2,1)} %get-tuple-element.36.refs_0_), channel_id=1, source_target_pairs={{0,1},{1,2},{2,3},{4,5},{5,6},{6,7},{8,9},{9,10},{10,11},{12,13},{... | collective-permute-start | bytes 3145736 | tf_op jit(solution)/shard_map/ppermute | solution.py:383
  17.4 3.8 %toeplitz.1 = (bf16[32,128,256]{2,1,0:T(8,128)(2,1)}, bf16[32,128,256]{2,1,0:T(8,128)(2,1)}) custom-call(f32[32,128]{1,0:T(8,128)} %bitcast.28), custom_call_target="tpu_custom_call" | custom-call | bytes 4210688 | tf_op jit(solution)/shard_map/toeplitz/pallas_call | solution.py:36
  21.3 14.3 %collective-permute-done.refs_0_ = bf16[128,4096]{1,0:T(8,128)(2,1)} collective-permute-done((bf16[128,4096]{1,0:T(8,128)(2,1)}, bf16[128,4096]{1,0:T(8,128)(2,1)}, u32[]{:S(2)}, u32[]{:S(2)}) %collective-permute-start) | collective-permute-done | bytes 1048608 | tf_op jit(solution)/shard_map/ppermute | solution.py:460
  37.8 5.1 %all-to-all-start.1 = ((bf16[4,128,1024]{2,1,0:T(8,128)(2,1)}), bf16[4,128,1024]{2,1,0:T(8,128)(2,1)}, u32[]{:S(2)}, u32[]{:S(2)}) async-start(bf16[4,128,1024]{2,1,0:T(8,128)(2,1)} %prepare.3.refs_3_), calls=%async_computation.1 | async-start | bytes 2097152 | tf_op jit(solution)/shard_map/all_to_all | solution.py:376
  42.9 14.6 %collective-permute-done.3.refs_1_ = bf16[128,4096]{1,0:T(8,128)(2,1)} collective-permute-done((bf16[128,4096]{1,0:T(8,128)(2,1)}, bf16[128,4096]{1,0:T(8,128)(2,1)}, u32[]{:S(2)}, u32[]{:S(2)}) %collective-permute-start.3) | collective-permute-done | bytes 1048608 | tf_op jit(solution)/shard_map/ppermute | solution.py:461
  57.5 6.4 %collective-permute-done.2.refs_3_.refs_1_.refs_4_ = bf16[128,4096]{1,0:T(8,128)(2,1)} collective-permute-done((bf16[128,4096]{1,0:T(8,128)(2,1)}, bf16[128,4096]{1,0:T(8,128)(2,1)}, u32[]{:S(2)}, u32[]{:S(2)}) %collective-permute-start.2) | collective-permute-done | bytes 1048608 | tf_op jit(solution)/shard_map/ppermute | solution.py:384
  71.3 4.4 %collective-permute-start.6 = (bf16[128,4096]{1,0:T(8,128)(2,1)}, bf16[128,4096]{1,0:T(8,128)(2,1)}, u32[]{:S(2)}, u32[]{:S(2)}) collective-permute-start(bf16[128,4096]{1,0:T(8,128)(2,1)} %grad_mix.1.refs_4_.refs_0_.refs_8_), channel_id=1, source_target_pairs={{0,1},{1,2},{2,3},{4,5},{5,6},{6,7},{8,9},{9,10},{10,11},{12,13},{... | collective-permute-start | bytes 3145736 | tf_op jit(solution)/shard_map/ppermute | solution.py:383
  75.7 10.9 %project.2 = (bf16[512,4096]{1,0:T(8,128)(2,1)}, bf16[128,4096]{1,0:T(8,128)(2,1)}, bf16[128,4096]{1,0:T(8,128)(2,1)}, bf16[128,4096]{1,0:T(8,128)(2,1)}, bf16[128,4096]{1,0:T(8,128)(2,1)}) custom-call(bf16[512,1024]{1,0:T(8,128)(2,1)} %bitcast.2.refs_0_, bf16[1024,4096]{1,0:T(8,128)(2,1)} %bitcast.12, bf16[32,128,256]{2,1,0:T(8,128)(2,1)} %get-tuple-element.37.refs_2_, ...), custom_call_target="tpu_custom_call" | custom-call | flops 5368709120 | bytes 19922944 | tf_op jit(solution)/shard_map/project/pallas_call | solution.py:36
  89.8 4.9 %collective-permute-start.4 = (bf16[128,4096]{1,0:T(8,128)(2,1)}, bf16[128,4096]{1,0:T(8,128)(2,1)}, u32[]{:S(2)}, u32[]{:S(2)}) collective-permute-start(bf16[128,4096]{1,0:T(8,128)(2,1)} %get-tuple-element.41.refs_3_.refs_4_), channel_id=1, source_target_pairs={{0,1},{1,2},{2,3},{4,5},{5,6},{6,7},{8,9},{9,10},{10,11},{12,13},{... | collective-permute-start | bytes 3145736 | tf_op jit(solution)/shard_map/ppermute | solution.py:383
  96.6 10.9 %project.3 = (bf16[512,4096]{1,0:T(8,128)(2,1)}, bf16[128,4096]{1,0:T(8,128)(2,1)}, bf16[128,4096]{1,0:T(8,128)(2,1)}, bf16[128,4096]{1,0:T(8,128)(2,1)}, bf16[128,4096]{1,0:T(8,128)(2,1)}) custom-call(bf16[512,1024]{1,0:T(8,128)(2,1)} %bitcast.5.refs_0_.refs_1_, bf16[1024,4096]{1,0:T(8,128)(2,1)} %bitcast.13, ...), custom_call_target="tpu_custom_call" | custom-call | flops 5368709120 | bytes 19922944 | tf_op jit(solution)/shard_map/project/pallas_call | solution.py:36
  112.7 3.9 %collective-permute-start.10 = (bf16[128,4096]{1,0:T(8,128)(2,1)}, bf16[128,4096]{1,0:T(8,128)(2,1)}, u32[]{:S(2)}, u32[]{:S(2)}) collective-permute-start(bf16[128,4096]{1,0:T(8,128)(2,1)} %get-tuple-element.46.refs_4_), channel_id=1, source_target_pairs={{0,1},{1,2},{2,3},{4,5},{5,6},{6,7},{8,9},{9,10},{10,11},{12,13},{... | collective-permute-start | bytes 3145736 | tf_op jit(solution)/shard_map/ppermute | solution.py:383
  116.6 6.2 %collective-permute-done.4.refs_0_.refs_2_ = bf16[128,4096]{1,0:T(8,128)(2,1)} collective-permute-done((bf16[128,4096]{1,0:T(8,128)(2,1)}, bf16[128,4096]{1,0:T(8,128)(2,1)}, u32[]{:S(2)}, u32[]{:S(2)}) %collective-permute-start.4) | collective-permute-done | bytes 1048608 | tf_op jit(solution)/shard_map/ppermute | solution.py:383
  130.7 3.9 %collective-permute-start.9 = (bf16[128,4096]{1,0:T(8,128)(2,1)}, bf16[128,4096]{1,0:T(8,128)(2,1)}, u32[]{:S(2)}, u32[]{:S(2)}) collective-permute-start(bf16[128,4096]{1,0:T(8,128)(2,1)} %get-tuple-element.48.refs_5_), channel_id=1, source_target_pairs={{1,0},{2,1},{3,2},{5,4},{6,5},{7,6},{9,8},{10,9},{11,10},{13,12},{... | collective-permute-start | bytes 3145736 | tf_op jit(solution)/shard_map/ppermute | solution.py:384
  134.7 12.2 %collective-permute-done.11.refs_1_.refs_5_.refs_13_ = bf16[128,4096]{1,0:T(8,128)(2,1)} collective-permute-done((bf16[128,4096]{1,0:T(8,128)(2,1)}, bf16[128,4096]{1,0:T(8,128)(2,1)}, u32[]{:S(2)}, u32[]{:S(2)}) %collective-permute-start.11) | collective-permute-done | bytes 1048608 | tf_op jit(solution)/shard_map/ppermute | solution.py:384
  146.8 3.5 payload.9
  152.3 3.9 %collective-permute-start.12 = (bf16[128,4096]{1,0:T(8,128)(2,1)}, bf16[128,4096]{1,0:T(8,128)(2,1)}, u32[]{:S(2)}, u32[]{:S(2)}) collective-permute-start(bf16[128,4096]{1,0:T(8,128)(2,1)} %get-tuple-element.51.refs_4_), channel_id=1, source_target_pairs={{0,1},{1,2},{2,3},{4,5},{5,6},{6,7},{8,9},{9,10},{10,11},{12,13},{... | collective-permute-start | bytes 3145736 | tf_op jit(solution)/shard_map/ppermute | solution.py:383
  156.2 11.6 %collective-permute-done.8.refs_0_.refs_3_ = bf16[128,4096]{1,0:T(8,128)(2,1)} collective-permute-done((bf16[128,4096]{1,0:T(8,128)(2,1)}, bf16[128,4096]{1,0:T(8,128)(2,1)}, u32[]{:S(2)}, u32[]{:S(2)}) %collective-permute-start.8) | collective-permute-done | bytes 1048608 | tf_op jit(solution)/shard_map/ppermute | solution.py:383
  172.7 18.0 %collective-permute-done.13.refs_1_.refs_6_.refs_14_ = bf16[128,4096]{1,0:T(8,128)(2,1)} collective-permute-done((bf16[128,4096]{1,0:T(8,128)(2,1)}, bf16[128,4096]{1,0:T(8,128)(2,1)}, u32[]{:S(2)}, u32[]{:S(2)}) %collective-permute-start.13) | collective-permute-done | bytes 1048608 | tf_op jit(solution)/shard_map/ppermute | solution.py:384
  194.2 12.3 %back.2 = (bf16[512,4096]{1,0:T(8,128)(2,1)}, bf16[512,1024]{1,0:T(8,128)(2,1)}) custom-call(bf16[128,4096]{1,0:T(8,128)(2,1)} %grad_mix.1.refs_4_.refs_0_.refs_8_, bf16[128,4096]{1,0:T(8,128)(2,1)} %collective-permute-done.6.refs_0_.refs_1_.refs_9_, bf16[128,4096]{1,0:T(8,128)(2,1)} %collective-permute-done.10.refs_0_.refs_2_.refs_10_, ...), custom_call_target="tpu_custom_call" | custom-call | flops 5368709120 | bytes 23068672 | tf_op jit(solution)/shard_map/back/pallas_call | solution.py:36
  206.5 4.2 %all-to-all-start.3 = ((bf16[4,128,1024]{2,1,0:T(8,128)(2,1)}), bf16[4,128,1024]{2,1,0:T(8,128)(2,1)}, u32[]{:S(2)}, u32[]{:S(2)}) async-start(bf16[4,128,1024]{2,1,0:T(8,128)(2,1)} %bitcast.21), calls=%async_computation.3 | async-start | bytes 2097152 | tf_op jit(solution)/shard_map/all_to_all | solution.py:376
  213.2 4.4 %collective-permute-start.15 = (bf16[128,4096]{1,0:T(8,128)(2,1)}, bf16[128,4096]{1,0:T(8,128)(2,1)}, u32[]{:S(2)}, u32[]{:S(2)}) collective-permute-start(bf16[128,4096]{1,0:T(8,128)(2,1)} %get-tuple-element.54.refs_5_), channel_id=1, source_target_pairs={{1,0},{2,1},{3,2},{5,4},{6,5},{7,6},{9,8},{10,9},{11,10},{13,12},{... | collective-permute-start | bytes 3145736 | tf_op jit(solution)/shard_map/ppermute | solution.py:384
  219.5 4.1 %collective-permute-start.16 = (bf16[128,4096]{1,0:T(8,128)(2,1)}, bf16[128,4096]{1,0:T(8,128)(2,1)}, u32[]{:S(2)}, u32[]{:S(2)}) collective-permute-start(bf16[128,4096]{1,0:T(8,128)(2,1)} %get-tuple-element.55.refs_9_), channel_id=1, source_target_pairs={{0,1},{1,2},{2,3},{4,5},{5,6},{6,7},{8,9},{9,10},{10,11},{12,13},{... | collective-permute-start | bytes 3145736 | tf_op jit(solution)/shard_map/ppermute | solution.py:383
  223.6 33.6 %collective-permute-done.14.refs_10_.refs_4_ = bf16[128,4096]{1,0:T(8,128)(2,1)} collective-permute-done((bf16[128,4096]{1,0:T(8,128)(2,1)}, bf16[128,4096]{1,0:T(8,128)(2,1)}, u32[]{:S(2)}, u32[]{:S(2)}) %collective-permute-start.14) | collective-permute-done | bytes 1048608 | tf_op jit(solution)/shard_map/ppermute | solution.py:383
  257.2 21.4 %collective-permute-done.17.refs_13_.refs_5_ = bf16[128,4096]{1,0:T(8,128)(2,1)} collective-permute-done((bf16[128,4096]{1,0:T(8,128)(2,1)}, bf16[128,4096]{1,0:T(8,128)(2,1)}, u32[]{:S(2)}, u32[]{:S(2)}) %collective-permute-start.17) | collective-permute-done | bytes 1048608 | tf_op jit(solution)/shard_map/ppermute | solution.py:384
  278.5 12.3 %back.3 = (bf16[512,4096]{1,0:T(8,128)(2,1)}, bf16[512,1024]{1,0:T(8,128)(2,1)}) custom-call(bf16[128,4096]{1,0:T(8,128)(2,1)} %get-tuple-element.36.refs_0_, bf16[128,4096]{1,0:T(8,128)(2,1)} %collective-permute-done.1.refs_2_.refs_0_.refs_1_, bf16[128,4096]{1,0:T(8,128)(2,1)} %collective-permute-done.4.refs_0_.refs_2_, ...), custom_call_target="tpu_custom_call" | custom-call | flops 5368709120 | bytes 23068672 | tf_op jit(solution)/shard_map/back/pallas_call | solution.py:36
  290.9 4.6 %all-to-all-start.2 = ((bf16[4,128,1024]{2,1,0:T(8,128)(2,1)}), bf16[4,128,1024]{2,1,0:T(8,128)(2,1)}, u32[]{:S(2)}, u32[]{:S(2)}) async-start(bf16[4,128,1024]{2,1,0:T(8,128)(2,1)} %bitcast.22), calls=%async_computation.2 | async-start | bytes 2097152 | tf_op jit(solution)/shard_map/all_to_all | solution.py:376
  295.5 4.5 %finish.2.refs_16_ = bf16[1,128,4096]{2,1,0:T(8,128)(2,1)} custom-call(bf16[128,4096]{1,0:T(8,128)(2,1)} %collective-permute-done.refs_0_, bf16[128,4096]{1,0:T(8,128)(2,1)} %collective-permute-done.3.refs_1_, bf16[4,128,1024]{2,1,0:T(8,128)(2,1)} %all-to-all-done.3.refs_2_, bf16[128,4096]{1,0:T(8,128)(2,1)} %get-tuple-element.63.refs_3_, ...), custom_call_target="tpu_custom_call" | custom-call | bytes 7340032 | tf_op jit(solution)/shard_map/finish/pallas_call | solution.py:36
  303.5 13.0 %filter_gradient.1 = f32[4,8,128]{2,1,0:T(8,128)} custom-call(bf16[128,4096]{1,0:T(8,128)(2,1)} %get-tuple-element.36.refs_0_, bf16[128,4096]{1,0:T(8,128)(2,1)} %collective-permute-done.1.refs_2_.refs_0_.refs_1_, bf16[128,4096]{1,0:T(8,128)(2,1)} %collective-permute-done.4.refs_0_.refs_2_, bf16[128,4096]{1,0:T(8,128)(2,1)} %collective-permute-done.8.refs_0_.refs_3_, ...), custom_call_target="tpu_custom_call" | custom-call | flops 2147483648 | bytes 23085056 | tf_op jit(solution)/shard_map/filter_gradient/pallas_call | solution.py:36
  317.5 9.6 %collective-permute-done.18.refs_7_ = bf16[1,128,4096]{2,1,0:T(8,128)(2,1)} collective-permute-done((bf16[1,128,4096]{2,1,0:T(8,128)(2,1)}, bf16[1,128,4096]{2,1,0:T(8,128)(2,1)}, u32[]{:S(2)}, u32[]{:S(2)}) %collective-permute-start.18) | collective-permute-done | bytes 1048608 | tf_op jit(solution)/shard_map/ppermute | solution.py:491
  327.1 4.6 %finish.3.refs_4_ = bf16[1,128,4096]{2,1,0:T(8,128)(2,1)} custom-call(bf16[128,4096]{1,0:T(8,128)(2,1)} %bitcast.18, bf16[128,4096]{1,0:T(8,128)(2,1)} %bitcast.20, bf16[4,128,1024]{2,1,0:T(8,128)(2,1)} %all-to-all-done.2.refs_2_, bf16[128,4096]{1,0:T(8,128)(2,1)} %get-tuple-element.60.refs_3_, bf16[128,4096]{1,0:T(8,128)(2,1)} %collective-permute-done.14.refs_10_.refs_4_, ...), custom_call_target="tpu_custom_call" | custom-call | bytes 7340032 | tf_op jit(solution)/shard_map/finish/pallas_call | solution.py:36
  337.9 13.6 %weight_gradient.1.refs_4_ = bf16[1024,4096]{1,0:T(8,128)(2,1)} custom-call(bf16[512,1024]{1,0:T(8,128)(2,1)} %bitcast.2.refs_0_, bf16[512,1024]{1,0:T(8,128)(2,1)} %bitcast.5.refs_0_.refs_1_, bf16[512,4096]{1,0:T(8,128)(2,1)} %get-tuple-element.58.refs_6_.refs_2_, bf16[512,4096]{1,0:T(8,128)(2,1)} %get-tuple-element.56.refs_9_.refs_3_, ...), custom_call_target="tpu_custom_call" | custom-call | flops 8589934592 | bytes 18874368 | tf_op jit(solution)/shard_map/weight_gradient/pallas_call | solution.py:36
  (51 shorter events, 67.8 us)
Async XLA Ops:
  3.6 34.2 %all-to-all-start = ((bf16[4,128,1024]{2,1,0:T(8,128)(2,1)}), bf16[4,128,1024]{2,1,0:T(8,128)(2,1)}, u32[]{:S(2)}, u32[]{:S(2)}) async-start(bf16[4,128,1024]{2,1,0:T(8,128)(2,1)} %get-tuple-element.34), calls=%async_computation | async-start | bytes 2097152 | tf_op jit(solution)/shard_map/all_to_all | solution.py:376
  8.9 26.6 %collective-permute-start = (bf16[128,4096]{1,0:T(8,128)(2,1)}, bf16[128,4096]{1,0:T(8,128)(2,1)}, u32[]{:S(2)}, u32[]{:S(2)}) collective-permute-start(bf16[128,4096]{1,0:T(8,128)(2,1)} %bitcast.29), channel_id=1, source_target_pairs={{0,28},{4,24},{8,20},{12,16},{16,12},{20,8},{24,4},{28,0},{1,29},{... | collective-permute-start | bytes 3145736 | tf_op jit(solution)/shard_map/ppermute | solution.py:460
  9.3 48.2 %collective-permute-start.3 = (bf16[128,4096]{1,0:T(8,128)(2,1)}, bf16[128,4096]{1,0:T(8,128)(2,1)}, u32[]{:S(2)}, u32[]{:S(2)}) collective-permute-start(bf16[128,4096]{1,0:T(8,128)(2,1)} %bitcast.30), channel_id=1, source_target_pairs={{0,28},{4,24},{8,20},{12,16},{16,12},{20,8},{24,4},{28,0},{1,29},{... | collective-permute-start | bytes 3145736 | tf_op jit(solution)/shard_map/ppermute | solution.py:461
  11.6 52.3 %collective-permute-start.2 = (bf16[128,4096]{1,0:T(8,128)(2,1)}, bf16[128,4096]{1,0:T(8,128)(2,1)}, u32[]{:S(2)}, u32[]{:S(2)}) collective-permute-start(bf16[128,4096]{1,0:T(8,128)(2,1)} %get-tuple-element.36.refs_0_), channel_id=1, source_target_pairs={{1,0},{2,1},{3,2},{5,4},{6,5},{7,6},{9,8},{10,9},{11,10},{13,12},{... | collective-permute-start | bytes 3145736 | tf_op jit(solution)/shard_map/ppermute | solution.py:384
  13.5 53.1 %collective-permute-start.1 = (bf16[128,4096]{1,0:T(8,128)(2,1)}, bf16[128,4096]{1,0:T(8,128)(2,1)}, u32[]{:S(2)}, u32[]{:S(2)}) collective-permute-start(bf16[128,4096]{1,0:T(8,128)(2,1)} %get-tuple-element.36.refs_0_), channel_id=1, source_target_pairs={{0,1},{1,2},{2,3},{4,5},{5,6},{6,7},{8,9},{9,10},{10,11},{12,13},{... | collective-permute-start | bytes 3145736 | tf_op jit(solution)/shard_map/ppermute | solution.py:383
  37.8 58.8 %all-to-all-start.1 = ((bf16[4,128,1024]{2,1,0:T(8,128)(2,1)}), bf16[4,128,1024]{2,1,0:T(8,128)(2,1)}, u32[]{:S(2)}, u32[]{:S(2)}) async-start(bf16[4,128,1024]{2,1,0:T(8,128)(2,1)} %prepare.3.refs_3_), calls=%async_computation.1 | async-start | bytes 2097152 | tf_op jit(solution)/shard_map/all_to_all | solution.py:376
  69.4 38.2 %collective-permute-start.7 = (bf16[128,4096]{1,0:T(8,128)(2,1)}, bf16[128,4096]{1,0:T(8,128)(2,1)}, u32[]{:S(2)}, u32[]{:S(2)}) collective-permute-start(bf16[128,4096]{1,0:T(8,128)(2,1)} %grad_mix.1.refs_4_.refs_0_.refs_8_), channel_id=1, source_target_pairs={{1,0},{2,1},{3,2},{5,4},{6,5},{7,6},{9,8},{10,9},{11,10},{13,12},{... | collective-permute-start | bytes 3145736 | tf_op jit(solution)/shard_map/ppermute | solution.py:384
  71.3 36.2 %collective-permute-start.6 = (bf16[128,4096]{1,0:T(8,128)(2,1)}, bf16[128,4096]{1,0:T(8,128)(2,1)}, u32[]{:S(2)}, u32[]{:S(2)}) collective-permute-start(bf16[128,4096]{1,0:T(8,128)(2,1)} %grad_mix.1.refs_4_.refs_0_.refs_8_), channel_id=1, source_target_pairs={{0,1},{1,2},{2,3},{4,5},{5,6},{6,7},{8,9},{9,10},{10,11},{12,13},{... | collective-permute-start | bytes 3145736 | tf_op jit(solution)/shard_map/ppermute | solution.py:383
  89.8 33.0 %collective-permute-start.4 = (bf16[128,4096]{1,0:T(8,128)(2,1)}, bf16[128,4096]{1,0:T(8,128)(2,1)}, u32[]{:S(2)}, u32[]{:S(2)}) collective-permute-start(bf16[128,4096]{1,0:T(8,128)(2,1)} %get-tuple-element.41.refs_3_.refs_4_), channel_id=1, source_target_pairs={{0,1},{1,2},{2,3},{4,5},{5,6},{6,7},{8,9},{9,10},{10,11},{12,13},{... | collective-permute-start | bytes 3145736 | tf_op jit(solution)/shard_map/ppermute | solution.py:383
  94.7 29.7 %collective-permute-start.5 = (bf16[128,4096]{1,0:T(8,128)(2,1)}, bf16[128,4096]{1,0:T(8,128)(2,1)}, u32[]{:S(2)}, u32[]{:S(2)}) collective-permute-start(bf16[128,4096]{1,0:T(8,128)(2,1)} %get-tuple-element.42.refs_4_.refs_5_), channel_id=1, source_target_pairs={{1,0},{2,1},{3,2},{5,4},{6,5},{7,6},{9,8},{10,9},{11,10},{13,12},{... | collective-permute-start | bytes 3145736 | tf_op jit(solution)/shard_map/ppermute | solution.py:384
  110.8 36.1 %collective-permute-start.11 = (bf16[128,4096]{1,0:T(8,128)(2,1)}, bf16[128,4096]{1,0:T(8,128)(2,1)}, u32[]{:S(2)}, u32[]{:S(2)}) collective-permute-start(bf16[128,4096]{1,0:T(8,128)(2,1)} %get-tuple-element.49), channel_id=1, source_target_pairs={{1,0},{2,1},{3,2},{5,4},{6,5},{7,6},{9,8},{10,9},{11,10},{13,12},{... | collective-permute-start | bytes 3145736 | tf_op jit(solution)/shard_map/ppermute | solution.py:384
  112.7 34.1 %collective-permute-start.10 = (bf16[128,4096]{1,0:T(8,128)(2,1)}, bf16[128,4096]{1,0:T(8,128)(2,1)}, u32[]{:S(2)}, u32[]{:S(2)}) collective-permute-start(bf16[128,4096]{1,0:T(8,128)(2,1)} %get-tuple-element.46.refs_4_), channel_id=1, source_target_pairs={{0,1},{1,2},{2,3},{4,5},{5,6},{6,7},{8,9},{9,10},{10,11},{12,13},{... | collective-permute-start | bytes 3145736 | tf_op jit(solution)/shard_map/ppermute | solution.py:383
  127.8 39.9 %collective-permute-start.8 = (bf16[128,4096]{1,0:T(8,128)(2,1)}, bf16[128,4096]{1,0:T(8,128)(2,1)}, u32[]{:S(2)}, u32[]{:S(2)}) collective-permute-start(bf16[128,4096]{1,0:T(8,128)(2,1)} %get-tuple-element.47.refs_4_), channel_id=1, source_target_pairs={{0,1},{1,2},{2,3},{4,5},{5,6},{6,7},{8,9},{9,10},{10,11},{12,13},{... | collective-permute-start | bytes 3145736 | tf_op jit(solution)/shard_map/ppermute | solution.py:383
  130.7 38.6 %collective-permute-start.9 = (bf16[128,4096]{1,0:T(8,128)(2,1)}, bf16[128,4096]{1,0:T(8,128)(2,1)}, u32[]{:S(2)}, u32[]{:S(2)}) collective-permute-start(bf16[128,4096]{1,0:T(8,128)(2,1)} %get-tuple-element.48.refs_5_), channel_id=1, source_target_pairs={{1,0},{2,1},{3,2},{5,4},{6,5},{7,6},{9,8},{10,9},{11,10},{13,12},{... | collective-permute-start | bytes 3145736 | tf_op jit(solution)/shard_map/ppermute | solution.py:384
  150.3 40.4 %collective-permute-start.13 = (bf16[128,4096]{1,0:T(8,128)(2,1)}, bf16[128,4096]{1,0:T(8,128)(2,1)}, u32[]{:S(2)}, u32[]{:S(2)}) collective-permute-start(bf16[128,4096]{1,0:T(8,128)(2,1)} %get-tuple-element.52), channel_id=1, source_target_pairs={{1,0},{2,1},{3,2},{5,4},{6,5},{7,6},{9,8},{10,9},{11,10},{13,12},{... | collective-permute-start | bytes 3145736 | tf_op jit(solution)/shard_map/ppermute | solution.py:384
  152.3 38.4 %collective-permute-start.12 = (bf16[128,4096]{1,0:T(8,128)(2,1)}, bf16[128,4096]{1,0:T(8,128)(2,1)}, u32[]{:S(2)}, u32[]{:S(2)}) collective-permute-start(bf16[128,4096]{1,0:T(8,128)(2,1)} %get-tuple-element.51.refs_4_), channel_id=1, source_target_pairs={{0,1},{1,2},{2,3},{4,5},{5,6},{6,7},{8,9},{9,10},{10,11},{12,13},{... | collective-permute-start | bytes 3145736 | tf_op jit(solution)/shard_map/ppermute | solution.py:383
  206.5 84.4 %all-to-all-start.3 = ((bf16[4,128,1024]{2,1,0:T(8,128)(2,1)}), bf16[4,128,1024]{2,1,0:T(8,128)(2,1)}, u32[]{:S(2)}, u32[]{:S(2)}) async-start(bf16[4,128,1024]{2,1,0:T(8,128)(2,1)} %bitcast.21), calls=%async_computation.3 | async-start | bytes 2097152 | tf_op jit(solution)/shard_map/all_to_all | solution.py:376
  210.8 46.4 %collective-permute-start.14 = (bf16[128,4096]{1,0:T(8,128)(2,1)}, bf16[128,4096]{1,0:T(8,128)(2,1)}, u32[]{:S(2)}, u32[]{:S(2)}) collective-permute-start(bf16[128,4096]{1,0:T(8,128)(2,1)} %get-tuple-element.53.refs_4_), channel_id=1, source_target_pairs={{0,1},{1,2},{2,3},{4,5},{5,6},{6,7},{8,9},{9,10},{10,11},{12,13},{... | collective-permute-start | bytes 3145736 | tf_op jit(solution)/shard_map/ppermute | solution.py:383
  213.2 44.0 %collective-permute-start.15 = (bf16[128,4096]{1,0:T(8,128)(2,1)}, bf16[128,4096]{1,0:T(8,128)(2,1)}, u32[]{:S(2)}, u32[]{:S(2)}) collective-permute-start(bf16[128,4096]{1,0:T(8,128)(2,1)} %get-tuple-element.54.refs_5_), channel_id=1, source_target_pairs={{1,0},{2,1},{3,2},{5,4},{6,5},{7,6},{9,8},{10,9},{11,10},{13,12},{... | collective-permute-start | bytes 3145736 | tf_op jit(solution)/shard_map/ppermute | solution.py:384
  217.6 61.0 %collective-permute-start.17 = (bf16[128,4096]{1,0:T(8,128)(2,1)}, bf16[128,4096]{1,0:T(8,128)(2,1)}, u32[]{:S(2)}, u32[]{:S(2)}) collective-permute-start(bf16[128,4096]{1,0:T(8,128)(2,1)} %get-tuple-element.57), channel_id=1, source_target_pairs={{1,0},{2,1},{3,2},{5,4},{6,5},{7,6},{9,8},{10,9},{11,10},{13,12},{... | collective-permute-start | bytes 3145736 | tf_op jit(solution)/shard_map/ppermute | solution.py:384
  219.5 59.0 %collective-permute-start.16 = (bf16[128,4096]{1,0:T(8,128)(2,1)}, bf16[128,4096]{1,0:T(8,128)(2,1)}, u32[]{:S(2)}, u32[]{:S(2)}) collective-permute-start(bf16[128,4096]{1,0:T(8,128)(2,1)} %get-tuple-element.55.refs_9_), channel_id=1, source_target_pairs={{0,1},{1,2},{2,3},{4,5},{5,6},{6,7},{8,9},{9,10},{10,11},{12,13},{... | collective-permute-start | bytes 3145736 | tf_op jit(solution)/shard_map/ppermute | solution.py:383
  290.9 26.6 %all-to-all-start.2 = ((bf16[4,128,1024]{2,1,0:T(8,128)(2,1)}), bf16[4,128,1024]{2,1,0:T(8,128)(2,1)}, u32[]{:S(2)}, u32[]{:S(2)}) async-start(bf16[4,128,1024]{2,1,0:T(8,128)(2,1)} %bitcast.22), calls=%async_computation.2 | async-start | bytes 2097152 | tf_op jit(solution)/shard_map/all_to_all | solution.py:376
  300.1 27.0 %collective-permute-start.18 = (bf16[1,128,4096]{2,1,0:T(8,128)(2,1)}, bf16[1,128,4096]{2,1,0:T(8,128)(2,1)}, u32[]{:S(2)}, u32[]{:S(2)}) collective-permute-start(bf16[1,128,4096]{2,1,0:T(8,128)(2,1)} %finish.2.refs_16_), channel_id=1, source_target_pairs={{28,4},{24,8},{20,12},{16,16},{12,20},{8,24},{4,28},{29,5},{25,9},... | collective-permute-start | bytes 3145736 | tf_op jit(solution)/shard_map/ppermute | solution.py:491
  327.1 6.5 %copy-start = (f32[4,8,128]{2,1,0:T(8,128)S(1)}, f32[4,8,128]{2,1,0:T(8,128)}, u32[]{:S(2)}) copy-start(f32[4,8,128]{2,1,0:T(8,128)} %filter_gradient.1) | copy-start | bytes 49156
  331.6 22.5 %collective-permute-start.22 = (bf16[1,128,4096]{2,1,0:T(8,128)(2,1)}, bf16[1,128,4096]{2,1,0:T(8,128)(2,1)}, u32[]{:S(2)}, u32[]{:S(2)}) collective-permute-start(bf16[1,128,4096]{2,1,0:T(8,128)(2,1)} %finish.3.refs_4_), channel_id=1, source_target_pairs={{4,0},{8,4},{12,8},{16,12},{20,16},{24,20},{28,24},{5,1},{9,5},{13... | collective-permute-start | bytes 3145736 | tf_op jit(solution)/shard_map/ppermute | solution.py:496
  333.5 18.0 %collective-permute-start.21 = (f32[1,32,128]{2,1,0:T(8,128)S(1)}, f32[1,32,128]{2,1,0:T(8,128)S(1)}, u32[]{:S(2)}, u32[]{:S(2)}) collective-permute-start(f32[1,32,128]{2,1,0:T(8,128)S(1)} %bitcast.25), channel_id=1, source_target_pairs={{0,3},{1,0},{2,1},{3,2},{4,7},{5,4},{6,5},{7,6},{8,11},{9,8},{10,9... | collective-permute-start | bytes 49160 | tf_op jit(solution)/shard_map/ppermute | solution.py:438
  333.6 17.9 %collective-permute-start.20 = (f32[1,32,128]{2,1,0:T(8,128)S(1)}, f32[1,32,128]{2,1,0:T(8,128)S(1)}, u32[]{:S(2)}, u32[]{:S(2)}) collective-permute-start(f32[1,32,128]{2,1,0:T(8,128)S(1)} %bitcast.26), channel_id=1, source_target_pairs={{0,2},{1,3},{2,0},{3,1},{4,6},{5,7},{6,4},{7,5},{8,10},{9,11},{10,... | collective-permute-start | bytes 49160 | tf_op jit(solution)/shard_map/ppermute | solution.py:438
  336.2 15.3 %collective-permute-start.19 = (f32[1,32,128]{2,1,0:T(8,128)S(1)}, f32[1,32,128]{2,1,0:T(8,128)S(1)}, u32[]{:S(2)}, u32[]{:S(2)}) collective-permute-start(f32[1,32,128]{2,1,0:T(8,128)S(1)} %bitcast.27), channel_id=1, source_target_pairs={{0,1},{1,2},{2,3},{3,0},{4,5},{5,6},{6,7},{7,4},{8,9},{9,10},{10,1... | collective-permute-start | bytes 49160 | tf_op jit(solution)/shard_map/ppermute | solution.py:438
  351.5 0.6 copy-start.1
  351.5 0.6 copy-start.2
  352.1 0.6 copy-start.3

commit v7 on v6

--- a/solution.py
+++ b/solution.py
@@ -260,21 +260,30 @@
         ],
         out_shape=[shape((tokens, width), bf16), shape((tokens, depth), bf16)],
         scratch_shapes=[pltpu.VMEM((tokens, tile), bf16), pltpu.VMEM((tokens, depth), f32)],
-        flops=2 * tokens * width * (depth + 2 * taps),
+        flops=6 * tokens * width * (depth + 2 * taps),
         name="back",
     )
 
 
-def taps_kernel(count, groups, *refs):
-    taps_ref, *mix_refs = refs[-3:]
-    taps = taps_ref.shape[2]
+def gradients_kernel(count, *refs):
+    down_x, up_x, down_g, up_g, *rest = refs[:-6]
+    out_ref, taps_ref, down_t, up_t, *mix_refs = refs[-6:]
+
+    @pl.when(pl.program_id(0) == 0)
+    def _():
+        down_t[...] = down_x[...].T
+        up_t[...] = up_x[...].T
+
+    out_ref[...] = (dot(down_t[...], down_g[...]) + dot(up_t[...], up_g[...])).astype(bf16)
+
+    groups, taps = taps_ref.shape[1:]
     width = mix_refs[0].shape[1] // groups
     row = lax.broadcasted_iota(jnp.int32, (taps, taps), 0)
     col = lax.broadcasted_iota(jnp.int32, (taps, taps), 1)
     total = [0] * groups
     for first, mix_ref in zip((0, count + 1), mix_refs):
-        assemble(refs[first : first + count], mix_ref)
-        part_ref = refs[first + count]
+        assemble(rest[first : first + count], mix_ref)
+        part_ref = rest[first + count]
         for g in range(groups):
             cols = slice(g * width, (g + 1) * width)
             both = with_following(mix_ref[:, cols], taps)
@@ -290,54 +299,50 @@
         taps_ref[0, g : g + 1, :] = line
 
 
-def filter_gradient(down_mixes, down_part, up_mixes, up_part, groups, taps, after=()):
-    rows, width = down_mixes[0].shape
-    tokens = down_part.shape[0]
+def gradients(xs, grads, mixes, parts, groups, taps, after=()):
+    rows, width = mixes[0][0].shape
+    tokens, depth = xs[0].shape
     step = 8
     tile = width // groups * step
-    count = len(down_mixes)
-    block = [pl.BlockSpec((rows, tile), lambda i: (0, i))] * count
-    part = [pl.BlockSpec((tokens, tile), lambda i: (0, i))]
-    return call(
-        functools.partial(taps_kernel, count, step),
-        (*down_mixes, down_part, *up_mixes, up_part),
-        after,
-        grid=(groups // step,),
-        in_specs=(block + part) * 2,
-        out_specs=pl.BlockSpec((1, step, taps), lambda i: (i, 0, 0)),
-        out_shape=shape((groups // step, step, taps), f32),
-        scratch_shapes=[pltpu.VMEM((tokens, tile), bf16)] * 2,
-        flops=8 * tokens * width * taps,
-        name="filter_gradient",
-    ).reshape(1, groups, taps)
-
-
-def weight_kernel(down_x, up_x, down_g, up_g, out_ref, down_t, up_t):
-    @pl.when(pl.program_id(0) == 0)
-    def _():
-        down_t[...] = down_x[...].T
-        up_t[...] = up_x[...].T
-
-    out_ref[...] = (dot(down_t[...], down_g[...]) + dot(up_t[...], up_g[...])).astype(bf16)
-
-
-def weight_gradient(down_x, up_x, down_g, up_g, after=()):
-    tokens, depth = down_x.shape
-    width = down_g.shape[1]
-    tile = width // 4
+    count = len(mixes[0])
     whole = pl.BlockSpec((tokens, depth), lambda i: (0, 0))
     part = pl.BlockSpec((tokens, tile), lambda i: (0, i))
-    return call(
-        weight_kernel,
-        (down_x, up_x, down_g, up_g),
-        after,
-        grid=(width // tile,),
-        in_specs=[whole, whole, part, part],
-        out_specs=pl.BlockSpec((depth, tile), lambda i: (0, i)),
-        out_shape=shape((depth, width), bf16),
-        scratch_shapes=[pltpu.VMEM((depth, tokens), bf16)] * 2,
-        flops=4 * tokens * depth * width,
-        name="weight_gradient",
+    block = pl.BlockSpec((rows, tile), lambda i: (0, i))
+    weight_grad, line = call(
+        functools.partial(gradients_kernel, count),
+        (*xs, *grads, *mixes[0], parts[0], *mixes[1], parts[1]),
+        after,
+        grid=(groups // step,),
+        in_specs=[whole] * 2 + [part] * 2 + ([block] * count + [part]) * 2,
+        out_specs=[
+            pl.BlockSpec((depth, tile), lambda i: (0, i)),
+            pl.BlockSpec((1, step, taps), lambda i: (i, 0, 0)),
+        ],
+        out_shape=[shape((depth, width), bf16), shape((groups // step, step, taps), f32)],
+        scratch_shapes=[pltpu.VMEM((depth, tokens), bf16)] * 2
+        + [pltpu.VMEM((tokens, tile), bf16)] * 2,
+        flops=4 * tokens * depth * width + 8 * tokens * width * taps,
+        name="gradients",
+    )
+    return weight_grad, line.reshape(1, groups, taps)
+
+
+def settle_kernel(in_ref, out_ref):
+    out_ref[...] = in_ref[...]
+
+
+def settle(x):
+    step = x.shape[1] // 2
+    spec = pl.BlockSpec((1, step, x.shape[2]), lambda i: (0, i, 0))
+    return call(
+        settle_kernel,
+        (x,),
+        (),
+        grid=(2,),
+        in_specs=[spec],
+        out_specs=spec,
+        out_shape=shape(x.shape, x.dtype),
+        name="settle",
     )
 
 
@@ -489,13 +494,20 @@
     down_back = exchange(down_back)
     up_grad = finish(up_xin, up_cot, up_conv, up_back, after=(down_g,))
     up_passed = lax.ppermute(up_grad, "section", up_pairs)
-    taps = filter_gradient(
-        down_mixes, down_part, up_mixes, up_part, *filters.shape[1:], after=(up_grad,)
-    )
-    down_grad = finish(down_xin, down_cot, down_conv, down_back, after=(taps, up_passed))
+    weight_grad, taps = gradients(
+        (down_x, up_x),
+        (down_g, up_g),
+        (down_mixes, up_mixes),
+        (down_part, up_part),
+        *filters.shape[1:],
+        after=(up_grad,),
+    )
+    up_passed = settle(up_passed)
+    down_grad = finish(
+        down_xin, down_cot, down_conv, down_back, after=(weight_grad, up_passed)
+    )
     down_passed = lax.ppermute(down_grad, "section", down_pairs)
-    weight_grad = weight_gradient(down_x, up_x, down_g, up_g, after=(down_grad,))
-    taps = sum_all(taps, after=(weight_grad,))
+    taps = sum_all(taps, after=(down_grad,))
     return weight_grad[None], taps, down_passed, up_passed
 
 

time: 361 us -> 330 us (0.914)
  the two profiles are of different devices: /device:TPU:10 before, /device:TPU:11 now
where the time goes in v7:
time: 330 us; the launch traced here: 328 us
  waiting for transfers between devices  131 us (40%)
  Pallas kernels  116 us (35%)
  starting transfers between devices  78.3 us (24%)
    pallas_call x19, Pallas kernels, call(): pl.pallas_call(body, in_specs=list(in_specs) + unread, out_shape=out_shap...  116 us
    ppermute x8, waiting for transfers between devices, both_ways(): lax.ppermute(left, 'tensor', [(j, i) for i, j in onward])  63.3 us
    ppermute x8, waiting for transfers between devices, both_ways(): lax.ppermute(right, 'tensor', onward)  23 us
    ppermute x8, starting transfers between devices, both_ways(): lax.ppermute(right, 'tensor', onward)  22.8 us
    ppermute x8, starting transfers between devices, both_ways(): lax.ppermute(left, 'tensor', [(j, i) for i, j in onward])  22.4 us
    all_to_all x4, starting transfers between devices, exchange(): return lax.all_to_all(x, 'tensor', split_axis=0, concat_axis=0, tiled=True)  18.8 us
    ppermute x1, waiting for transfers between devices, per_device(): up_cot = lax.ppermute(up_cot[0], 'section', mirror)  15.7 us
    ppermute x1, waiting for transfers between devices, per_device(): up_xin = lax.ppermute(up_input[0], 'section', mirror)  14.8 us
  transfers between devices with their start and end apart: 27, of which 12 were waited for; matrix products, arithmetic and copies ran while one was open for 0% of the time, Pallas kernels for 33%

profile of v7, /device:TPU:11, one launch (start us, length us, event | category | flops | bytes accessed | tf_op | source)
XLA Modules:
  0.0 328.3 jit_solution(7071532680375507203)
XLA Ops:
  3.6 4.8 %all-to-all-start = ((bf16[4,128,1024]{2,1,0:T(8,128)(2,1)}), bf16[4,128,1024]{2,1,0:T(8,128)(2,1)}, u32[]{:S(2)}, u32[]{:S(2)}) async-start(bf16[4,128,1024]{2,1,0:T(8,128)(2,1)} %get-tuple-element.36), calls=%async_computation | async-start | bytes 2097152 | tf_op jit(solution)/shard_map/all_to_all | solution.py:381
  12.9 3.4 %collective-permute-start.1 = (bf16[128,4096]{1,0:T(8,128)(2,1)}, bf16[128,4096]{1,0:T(8,128)(2,1)}, u32[]{:S(2)}, u32[]{:S(2)}) collective-permute-start(bf16[128,4096]{1,0:T(8,128)(2,1)} %get-tuple-element.38.refs_0_.refs_4_), channel_id=1, source_target_pairs={{0,1},{1,2},{2,3},{4,5},{5,6},{6,7},{8,9},{9,10},{10,11},{12,13},{... | collective-permute-start | bytes 3145736 | tf_op jit(solution)/shard_map/ppermute | solution.py:388
  16.3 3.8 %toeplitz.1 = (bf16[32,128,256]{2,1,0:T(8,128)(2,1)}, bf16[32,128,256]{2,1,0:T(8,128)(2,1)}) custom-call(f32[32,128]{1,0:T(8,128)} %bitcast.23), custom_call_target="tpu_custom_call" | custom-call | bytes 4210688 | tf_op jit(solution)/shard_map/toeplitz/pallas_call | solution.py:36
  20.1 14.8 %collective-permute-done.refs_0_ = bf16[128,4096]{1,0:T(8,128)(2,1)} collective-permute-done((bf16[128,4096]{1,0:T(8,128)(2,1)}, bf16[128,4096]{1,0:T(8,128)(2,1)}, u32[]{:S(2)}, u32[]{:S(2)}) %collective-permute-start) | collective-permute-done | bytes 1048608 | tf_op jit(solution)/shard_map/ppermute | solution.py:465
  37.1 4.5 %all-to-all-start.1 = ((bf16[4,128,1024]{2,1,0:T(8,128)(2,1)}), bf16[4,128,1024]{2,1,0:T(8,128)(2,1)}, u32[]{:S(2)}, u32[]{:S(2)}) async-start(bf16[4,128,1024]{2,1,0:T(8,128)(2,1)} %prepare.3.refs_3_), calls=%async_computation.1 | async-start | bytes 2097152 | tf_op jit(solution)/shard_map/all_to_all | solution.py:381
  41.7 15.7 %collective-permute-done.3.refs_1_ = bf16[128,4096]{1,0:T(8,128)(2,1)} collective-permute-done((bf16[128,4096]{1,0:T(8,128)(2,1)}, bf16[128,4096]{1,0:T(8,128)(2,1)}, u32[]{:S(2)}, u32[]{:S(2)}) %collective-permute-start.3) | collective-permute-done | bytes 1048608 | tf_op jit(solution)/shard_map/ppermute | solution.py:466
  65.3 3.4 %collective-permute-start.6 = (bf16[128,4096]{1,0:T(8,128)(2,1)}, bf16[128,4096]{1,0:T(8,128)(2,1)}, u32[]{:S(2)}, u32[]{:S(2)}) collective-permute-start(bf16[128,4096]{1,0:T(8,128)(2,1)} %grad_mix.1.refs_4_.refs_0_.refs_12_), channel_id=1, source_target_pairs={{0,1},{1,2},{2,3},{4,5},{5,6},{6,7},{8,9},{9,10},{10,11},{12,13},{... | collective-permute-start | bytes 3145736 | tf_op jit(solution)/shard_map/ppermute | solution.py:388
  68.7 10.9 %project.2 = (bf16[512,4096]{1,0:T(8,128)(2,1)}, bf16[128,4096]{1,0:T(8,128)(2,1)}, bf16[128,4096]{1,0:T(8,128)(2,1)}, bf16[128,4096]{1,0:T(8,128)(2,1)}, bf16[128,4096]{1,0:T(8,128)(2,1)}) custom-call(bf16[512,1024]{1,0:T(8,128)(2,1)} %bitcast.2.refs_0_, bf16[1024,4096]{1,0:T(8,128)(2,1)} %bitcast.24, bf16[32,128,256]{2,1,0:T(8,128)(2,1)} %get-tuple-element.39.refs_2_, ...), custom_call_target="tpu_custom_call" | custom-call | flops 5368709120 | bytes 19922944 | tf_op jit(solution)/shard_map/project/pallas_call | solution.py:36
  85.1 4.2 %collective-permute-start.5 = (bf16[128,4096]{1,0:T(8,128)(2,1)}, bf16[128,4096]{1,0:T(8,128)(2,1)}, u32[]{:S(2)}, u32[]{:S(2)}) collective-permute-start(bf16[128,4096]{1,0:T(8,128)(2,1)} %get-tuple-element.44.refs_4_.refs_5_), channel_id=1, source_target_pairs={{1,0},{2,1},{3,2},{5,4},{6,5},{7,6},{9,8},{10,9},{11,10},{13,12},{... | collective-permute-start | bytes 3145736 | tf_op jit(solution)/shard_map/ppermute | solution.py:389
  89.2 10.9 %project.3 = (bf16[512,4096]{1,0:T(8,128)(2,1)}, bf16[128,4096]{1,0:T(8,128)(2,1)}, bf16[128,4096]{1,0:T(8,128)(2,1)}, bf16[128,4096]{1,0:T(8,128)(2,1)}, bf16[128,4096]{1,0:T(8,128)(2,1)}) custom-call(bf16[512,1024]{1,0:T(8,128)(2,1)} %bitcast.5.refs_0_.refs_1_, bf16[1024,4096]{1,0:T(8,128)(2,1)} %bitcast.25, ...), custom_call_target="tpu_custom_call" | custom-call | flops 5368709120 | bytes 19922944 | tf_op jit(solution)/shard_map/project/pallas_call | solution.py:36
  105.3 3.4 %collective-permute-start.10 = (bf16[128,4096]{1,0:T(8,128)(2,1)}, bf16[128,4096]{1,0:T(8,128)(2,1)}, u32[]{:S(2)}, u32[]{:S(2)}) collective-permute-start(bf16[128,4096]{1,0:T(8,128)(2,1)} %get-tuple-element.48.refs_4_), channel_id=1, source_target_pairs={{0,1},{1,2},{2,3},{4,5},{5,6},{6,7},{8,9},{9,10},{10,11},{12,13},{... | collective-permute-start | bytes 3145736 | tf_op jit(solution)/shard_map/ppermute | solution.py:388
  108.7 11.5 %collective-permute-done.4.refs_0_.refs_2_.refs_6_ = bf16[128,4096]{1,0:T(8,128)(2,1)} collective-permute-done((bf16[128,4096]{1,0:T(8,128)(2,1)}, bf16[128,4096]{1,0:T(8,128)(2,1)}, u32[]{:S(2)}, u32[]{:S(2)}) %collective-permute-start.4) | collective-permute-done | bytes 1048608 | tf_op jit(solution)/shard_map/ppermute | solution.py:388
  122.5 3.6 %payload.8 = (bf16[128,4096]{1,0:T(8,128)(2,1)}, bf16[128,4096]{1,0:T(8,128)(2,1)}) custom-call(bf16[128,4096]{1,0:T(8,128)(2,1)} %collective-permute-done.4.refs_0_.refs_2_.refs_6_, bf16[128,4096]{1,0:T(8,128)(2,1)} %collective-permute-done.5.refs_1_.refs_5_.refs_9_, bf16[128,4096]{1,0:T(8,128)(2,1)} %get-tuple-element.45.refs_2_.refs_3_, ...), custom_call_target="tpu_custom_call" | custom-call | bytes 6291456 | tf_op jit(solution)/shard_map/payload/pallas_call | solution.py:36
  128.1 4.4 %collective-permute-start.9 = (bf16[128,4096]{1,0:T(8,128)(2,1)}, bf16[128,4096]{1,0:T(8,128)(2,1)}, u32[]{:S(2)}, u32[]{:S(2)}) collective-permute-start(bf16[128,4096]{1,0:T(8,128)(2,1)} %get-tuple-element.50.refs_5_), channel_id=1, source_target_pairs={{1,0},{2,1},{3,2},{5,4},{6,5},{7,6},{9,8},{10,9},{11,10},{13,12},{... | collective-permute-start | bytes 3145736 | tf_op jit(solution)/shard_map/ppermute | solution.py:389
  132.4 12.6 %collective-permute-done.11.refs_1_.refs_5_.refs_17_ = bf16[128,4096]{1,0:T(8,128)(2,1)} collective-permute-done((bf16[128,4096]{1,0:T(8,128)(2,1)}, bf16[128,4096]{1,0:T(8,128)(2,1)}, u32[]{:S(2)}, u32[]{:S(2)}) %collective-permute-start.11) | collective-permute-done | bytes 1048608 | tf_op jit(solution)/shard_map/ppermute | solution.py:389
  145.0 3.4 %payload.9 = (bf16[128,4096]{1,0:T(8,128)(2,1)}, bf16[128,4096]{1,0:T(8,128)(2,1)}) custom-call(bf16[128,4096]{1,0:T(8,128)(2,1)} %collective-permute-done.10.refs_0_.refs_2_.refs_14_, bf16[128,4096]{1,0:T(8,128)(2,1)} %collective-permute-done.11.refs_1_.refs_5_.refs_17_, bf16[128,4096]{1,0:T(8,128)(2,1)} %get-tuple-element.52.refs_2_.refs_3_, ...), custom_call_target="tpu_custom_call" | custom-call | bytes 6291456 | tf_op jit(solution)/shard_map/payload/pallas_call | solution.py:36
  150.3 3.4 %collective-permute-start.12 = (bf16[128,4096]{1,0:T(8,128)(2,1)}, bf16[128,4096]{1,0:T(8,128)(2,1)}, u32[]{:S(2)}, u32[]{:S(2)}) collective-permute-start(bf16[128,4096]{1,0:T(8,128)(2,1)} %get-tuple-element.53.refs_4_), channel_id=1, source_target_pairs={{0,1},{1,2},{2,3},{4,5},{5,6},{6,7},{8,9},{9,10},{10,11},{12,13},{... | collective-permute-start | bytes 3145736 | tf_op jit(solution)/shard_map/ppermute | solution.py:388
  153.7 11.5 %collective-permute-done.8.refs_0_.refs_3_.refs_7_ = bf16[128,4096]{1,0:T(8,128)(2,1)} collective-permute-done((bf16[128,4096]{1,0:T(8,128)(2,1)}, bf16[128,4096]{1,0:T(8,128)(2,1)}, u32[]{:S(2)}, u32[]{:S(2)}) %collective-permute-start.8) | collective-permute-done | bytes 1048608 | tf_op jit(solution)/shard_map/ppermute | solution.py:388
  167.5 3.4 %payload.10 = (bf16[128,4096]{1,0:T(8,128)(2,1)}, bf16[128,4096]{1,0:T(8,128)(2,1)}) custom-call(bf16[128,4096]{1,0:T(8,128)(2,1)} %collective-permute-done.8.refs_0_.refs_3_.refs_7_, bf16[128,4096]{1,0:T(8,128)(2,1)} %collective-permute-done.9.refs_1_.refs_6_.refs_10_, bf16[128,4096]{1,0:T(8,128)(2,1)} %get-tuple-element.41.refs_3_.refs_2_, ...), custom_call_target="tpu_custom_call" | custom-call | bytes 6291456 | tf_op jit(solution)/shard_map/payload/pallas_call | solution.py:36
  172.8 4.3 %collective-permute-start.15 = (bf16[128,4096]{1,0:T(8,128)(2,1)}, bf16[128,4096]{1,0:T(8,128)(2,1)}, u32[]{:S(2)}, u32[]{:S(2)}) collective-permute-start(bf16[128,4096]{1,0:T(8,128)(2,1)} %get-tuple-element.56.refs_5_), channel_id=1, source_target_pairs={{1,0},{2,1},{3,2},{5,4},{6,5},{7,6},{9,8},{10,9},{11,10},{13,12},{... | collective-permute-start | bytes 3145736 | tf_op jit(solution)/shard_map/ppermute | solution.py:389
  177.1 12.8 %collective-permute-done.13.refs_1_.refs_6_.refs_18_ = bf16[128,4096]{1,0:T(8,128)(2,1)} collective-permute-done((bf16[128,4096]{1,0:T(8,128)(2,1)}, bf16[128,4096]{1,0:T(8,128)(2,1)}, u32[]{:S(2)}, u32[]{:S(2)}) %collective-permute-start.13) | collective-permute-done | bytes 1048608 | tf_op jit(solution)/shard_map/ppermute | solution.py:389
  189.9 3.4 %payload.11 = (bf16[128,4096]{1,0:T(8,128)(2,1)}, bf16[128,4096]{1,0:T(8,128)(2,1)}) custom-call(bf16[128,4096]{1,0:T(8,128)(2,1)} %collective-permute-done.12.refs_0_.refs_3_.refs_15_, bf16[128,4096]{1,0:T(8,128)(2,1)} %collective-permute-done.13.refs_1_.refs_6_.refs_18_, bf16[128,4096]{1,0:T(8,128)(2,1)} %get-tuple-element.47.refs_3_.refs_2_, ...), custom_call_target="tpu_custom_call" | custom-call | bytes 6291456 | tf_op jit(solution)/shard_map/payload/pallas_call | solution.py:36
  198.6 12.3 %back.2 = (bf16[512,4096]{1,0:T(8,128)(2,1)}, bf16[512,1024]{1,0:T(8,128)(2,1)}) custom-call(bf16[128,4096]{1,0:T(8,128)(2,1)} %grad_mix.1.refs_4_.refs_0_.refs_12_, bf16[128,4096]{1,0:T(8,128)(2,1)} %collective-permute-done.6.refs_0_.refs_1_.refs_13_, bf16[128,4096]{1,0:T(8,128)(2,1)} %collective-permute-done.10.refs_0_.refs_2_.refs_14_, ...), custom_call_target="tpu_custom_call" | custom-call | flops 16106127360 | bytes 23068672 | tf_op jit(solution)/shard_map/back/pallas_call | solution.py:36
  210.9 5.2 %all-to-all-start.2 = ((bf16[4,128,1024]{2,1,0:T(8,128)(2,1)}), bf16[4,128,1024]{2,1,0:T(8,128)(2,1)}, u32[]{:S(2)}, u32[]{:S(2)}) async-start(bf16[4,128,1024]{2,1,0:T(8,128)(2,1)} %bitcast.18), calls=%async_computation.2 | async-start | bytes 2097152 | tf_op jit(solution)/shard_map/all_to_all | solution.py:381
  216.2 29.9 %collective-permute-done.17.refs_13_.refs_5_ = bf16[128,4096]{1,0:T(8,128)(2,1)} collective-permute-done((bf16[128,4096]{1,0:T(8,128)(2,1)}, bf16[128,4096]{1,0:T(8,128)(2,1)}, u32[]{:S(2)}, u32[]{:S(2)}) %collective-permute-start.17) | collective-permute-done | bytes 1048608 | tf_op jit(solution)/shard_map/ppermute | solution.py:389
  246.1 12.4 %back.3 = (bf16[512,4096]{1,0:T(8,128)(2,1)}, bf16[512,1024]{1,0:T(8,128)(2,1)}) custom-call(bf16[128,4096]{1,0:T(8,128)(2,1)} %get-tuple-element.38.refs_0_.refs_4_, bf16[128,4096]{1,0:T(8,128)(2,1)} %collective-permute-done.1.refs_2_.refs_0_.refs_1_.refs_5_, bf16[128,4096]{1,0:T(8,128)(2,1)} %collective-permute-done.4.refs_0_.refs_2_.refs_6_, ...), custom_call_target="tpu_custom_call" | custom-call | flops 16106127360 | bytes 23068672 | tf_op jit(solution)/shard_map/back/pallas_call | solution.py:36
  258.5 4.3 %all-to-all-start.3 = ((bf16[4,128,1024]{2,1,0:T(8,128)(2,1)}), bf16[4,128,1024]{2,1,0:T(8,128)(2,1)}, u32[]{:S(2)}, u32[]{:S(2)}) async-start(bf16[4,128,1024]{2,1,0:T(8,128)(2,1)} %bitcast.17), calls=%async_computation.3 | async-start | bytes 2097152 | tf_op jit(solution)/shard_map/all_to_all | solution.py:381
  262.8 4.6 %finish.2.refs_20_ = bf16[1,128,4096]{2,1,0:T(8,128)(2,1)} custom-call(bf16[128,4096]{1,0:T(8,128)(2,1)} %collective-permute-done.refs_0_, bf16[128,4096]{1,0:T(8,128)(2,1)} %collective-permute-done.3.refs_1_, bf16[4,128,1024]{2,1,0:T(8,128)(2,1)} %all-to-all-done.2.refs_2_, bf16[128,4096]{1,0:T(8,128)(2,1)} %get-tuple-element.63.refs_3_, ...), custom_call_target="tpu_custom_call" | custom-call | bytes 7340032 | tf_op jit(solution)/shard_map/finish/pallas_call | solution.py:36
  270.4 24.3 %gradients.1 = (bf16[1024,4096]{1,0:T(8,128)(2,1)}, f32[4,8,128]{2,1,0:T(8,128)}) custom-call(bf16[512,1024]{1,0:T(8,128)(2,1)} %bitcast.2.refs_0_, bf16[512,1024]{1,0:T(8,128)(2,1)} %bitcast.5.refs_0_.refs_1_, bf16[512,4096]{1,0:T(8,128)(2,1)} %get-tuple-element.60.refs_6_.refs_2_, bf16[512,4096]{1,0:T(8,128)(2,1)} %get-tuple-element.58.refs_9_.refs_3_, ...), custom_call_target="tpu_custom_call" | custom-call | flops 10737418240 | bytes 41959424 | tf_op jit(solution)/shard_map/gradients/pallas_call | solution.py:36
  296.9 4.6 %finish.3.refs_4_ = bf16[1,128,4096]{2,1,0:T(8,128)(2,1)} custom-call(bf16[128,4096]{1,0:T(8,128)(2,1)} %bitcast.14, bf16[128,4096]{1,0:T(8,128)(2,1)} %bitcast.16, bf16[4,128,1024]{2,1,0:T(8,128)(2,1)} %all-to-all-done.3.refs_2_, bf16[128,4096]{1,0:T(8,128)(2,1)} %get-tuple-element.67.refs_3_, bf16[128,4096]{1,0:T(8,128)(2,1)} %collective-permute-done.14.refs_10_.refs_4_, ...), custom_call_target="tpu_custom_call" | custom-call | bytes 7340032 | tf_op jit(solution)/shard_map/finish/pallas_call | solution.py:36
  301.4 4.7 %collective-permute-start.22 = (bf16[1,128,4096]{2,1,0:T(8,128)(2,1)}, bf16[1,128,4096]{2,1,0:T(8,128)(2,1)}, u32[]{:S(2)}, u32[]{:S(2)}) collective-permute-start(bf16[1,128,4096]{2,1,0:T(8,128)(2,1)} %finish.3.refs_4_), channel_id=1, source_target_pairs={{4,0},{8,4},{12,8},{16,12},{20,16},{24,20},{28,24},{5,1},{9,5},{13... | collective-permute-start | bytes 3145736 | tf_op jit(solution)/shard_map/ppermute | solution.py:509
  312.9 13.1 %collective-permute-done.22 = bf16[1,128,4096]{2,1,0:T(8,128)(2,1)} collective-permute-done((bf16[1,128,4096]{2,1,0:T(8,128)(2,1)}, bf16[1,128,4096]{2,1,0:T(8,128)(2,1)}, u32[]{:S(2)}, u32[]{:S(2)}) %collective-permute-start.22) | collective-permute-done | bytes 1048608 | tf_op jit(solution)/shard_map/ppermute | solution.py:509
  (50 shorter events, 58.2 us)
Async XLA Ops:
  3.6 33.5 %all-to-all-start = ((bf16[4,128,1024]{2,1,0:T(8,128)(2,1)}), bf16[4,128,1024]{2,1,0:T(8,128)(2,1)}, u32[]{:S(2)}, u32[]{:S(2)}) async-start(bf16[4,128,1024]{2,1,0:T(8,128)(2,1)} %get-tuple-element.36), calls=%async_computation | async-start | bytes 2097152 | tf_op jit(solution)/shard_map/all_to_all | solution.py:381
  8.4 26.5 %collective-permute-start = (bf16[128,4096]{1,0:T(8,128)(2,1)}, bf16[128,4096]{1,0:T(8,128)(2,1)}, u32[]{:S(2)}, u32[]{:S(2)}) collective-permute-start(bf16[128,4096]{1,0:T(8,128)(2,1)} %bitcast.28), channel_id=1, source_target_pairs={{0,28},{4,24},{8,20},{12,16},{16,12},{20,8},{24,4},{28,0},{1,29},{... | collective-permute-start | bytes 3145736 | tf_op jit(solution)/shard_map/ppermute | solution.py:465
  10.7 46.6 %collective-permute-start.3 = (bf16[128,4096]{1,0:T(8,128)(2,1)}, bf16[128,4096]{1,0:T(8,128)(2,1)}, u32[]{:S(2)}, u32[]{:S(2)}) collective-permute-start(bf16[128,4096]{1,0:T(8,128)(2,1)} %bitcast.29), channel_id=1, source_target_pairs={{0,28},{4,24},{8,20},{12,16},{16,12},{20,8},{24,4},{28,0},{1,29},{... | collective-permute-start | bytes 3145736 | tf_op jit(solution)/shard_map/ppermute | solution.py:466
  11.0 49.6 %collective-permute-start.2 = (bf16[128,4096]{1,0:T(8,128)(2,1)}, bf16[128,4096]{1,0:T(8,128)(2,1)}, u32[]{:S(2)}, u32[]{:S(2)}) collective-permute-start(bf16[128,4096]{1,0:T(8,128)(2,1)} %get-tuple-element.38.refs_0_.refs_4_), channel_id=1, source_target_pairs={{1,0},{2,1},{3,2},{5,4},{6,5},{7,6},{9,8},{10,9},{11,10},{13,12},{... | collective-permute-start | bytes 3145736 | tf_op jit(solution)/shard_map/ppermute | solution.py:389
  12.9 47.7 %collective-permute-start.1 = (bf16[128,4096]{1,0:T(8,128)(2,1)}, bf16[128,4096]{1,0:T(8,128)(2,1)}, u32[]{:S(2)}, u32[]{:S(2)}) collective-permute-start(bf16[128,4096]{1,0:T(8,128)(2,1)} %get-tuple-element.38.refs_0_.refs_4_), channel_id=1, source_target_pairs={{0,1},{1,2},{2,3},{4,5},{5,6},{6,7},{8,9},{9,10},{10,11},{12,13},{... | collective-permute-start | bytes 3145736 | tf_op jit(solution)/shard_map/ppermute | solution.py:388
  37.1 52.1 %all-to-all-start.1 = ((bf16[4,128,1024]{2,1,0:T(8,128)(2,1)}), bf16[4,128,1024]{2,1,0:T(8,128)(2,1)}, u32[]{:S(2)}, u32[]{:S(2)}) async-start(bf16[4,128,1024]{2,1,0:T(8,128)(2,1)} %prepare.3.refs_3_), calls=%async_computation.1 | async-start | bytes 2097152 | tf_op jit(solution)/shard_map/all_to_all | solution.py:381
  63.4 36.8 %collective-permute-start.7 = (bf16[128,4096]{1,0:T(8,128)(2,1)}, bf16[128,4096]{1,0:T(8,128)(2,1)}, u32[]{:S(2)}, u32[]{:S(2)}) collective-permute-start(bf16[128,4096]{1,0:T(8,128)(2,1)} %grad_mix.1.refs_4_.refs_0_.refs_12_), channel_id=1, source_target_pairs={{1,0},{2,1},{3,2},{5,4},{6,5},{7,6},{9,8},{10,9},{11,10},{13,12},{... | collective-permute-start | bytes 3145736 | tf_op jit(solution)/shard_map/ppermute | solution.py:389
  65.3 34.9 %collective-permute-start.6 = (bf16[128,4096]{1,0:T(8,128)(2,1)}, bf16[128,4096]{1,0:T(8,128)(2,1)}, u32[]{:S(2)}, u32[]{:S(2)}) collective-permute-start(bf16[128,4096]{1,0:T(8,128)(2,1)} %grad_mix.1.refs_4_.refs_0_.refs_12_), channel_id=1, source_target_pairs={{0,1},{1,2},{2,3},{4,5},{5,6},{6,7},{8,9},{9,10},{10,11},{12,13},{... | collective-permute-start | bytes 3145736 | tf_op jit(solution)/shard_map/ppermute | solution.py:388
  82.9 37.2 %collective-permute-start.4 = (bf16[128,4096]{1,0:T(8,128)(2,1)}, bf16[128,4096]{1,0:T(8,128)(2,1)}, u32[]{:S(2)}, u32[]{:S(2)}) collective-permute-start(bf16[128,4096]{1,0:T(8,128)(2,1)} %get-tuple-element.43.refs_3_.refs_4_), channel_id=1, source_target_pairs={{0,1},{1,2},{2,3},{4,5},{5,6},{6,7},{8,9},{9,10},{10,11},{12,13},{... | collective-permute-start | bytes 3145736 | tf_op jit(solution)/shard_map/ppermute | solution.py:388
  85.1 37.5 %collective-permute-start.5 = (bf16[128,4096]{1,0:T(8,128)(2,1)}, bf16[128,4096]{1,0:T(8,128)(2,1)}, u32[]{:S(2)}, u32[]{:S(2)}) collective-permute-start(bf16[128,4096]{1,0:T(8,128)(2,1)} %get-tuple-element.44.refs_4_.refs_5_), channel_id=1, source_target_pairs={{1,0},{2,1},{3,2},{5,4},{6,5},{7,6},{9,8},{10,9},{11,10},{13,12},{... | collective-permute-start | bytes 3145736 | tf_op jit(solution)/shard_map/ppermute | solution.py:389
  103.4 41.6 %collective-permute-start.11 = (bf16[128,4096]{1,0:T(8,128)(2,1)}, bf16[128,4096]{1,0:T(8,128)(2,1)}, u32[]{:S(2)}, u32[]{:S(2)}) collective-permute-start(bf16[128,4096]{1,0:T(8,128)(2,1)} %get-tuple-element.51), channel_id=1, source_target_pairs={{1,0},{2,1},{3,2},{5,4},{6,5},{7,6},{9,8},{10,9},{11,10},{13,12},{... | collective-permute-start | bytes 3145736 | tf_op jit(solution)/shard_map/ppermute | solution.py:389
  105.3 39.6 %collective-permute-start.10 = (bf16[128,4096]{1,0:T(8,128)(2,1)}, bf16[128,4096]{1,0:T(8,128)(2,1)}, u32[]{:S(2)}, u32[]{:S(2)}) collective-permute-start(bf16[128,4096]{1,0:T(8,128)(2,1)} %get-tuple-element.48.refs_4_), channel_id=1, source_target_pairs={{0,1},{1,2},{2,3},{4,5},{5,6},{6,7},{8,9},{9,10},{10,11},{12,13},{... | collective-permute-start | bytes 3145736 | tf_op jit(solution)/shard_map/ppermute | solution.py:388
  126.1 39.0 %collective-permute-start.8 = (bf16[128,4096]{1,0:T(8,128)(2,1)}, bf16[128,4096]{1,0:T(8,128)(2,1)}, u32[]{:S(2)}, u32[]{:S(2)}) collective-permute-start(bf16[128,4096]{1,0:T(8,128)(2,1)} %get-tuple-element.49.refs_4_), channel_id=1, source_target_pairs={{0,1},{1,2},{2,3},{4,5},{5,6},{6,7},{8,9},{9,10},{10,11},{12,13},{... | collective-permute-start | bytes 3145736 | tf_op jit(solution)/shard_map/ppermute | solution.py:388
  128.1 39.4 %collective-permute-start.9 = (bf16[128,4096]{1,0:T(8,128)(2,1)}, bf16[128,4096]{1,0:T(8,128)(2,1)}, u32[]{:S(2)}, u32[]{:S(2)}) collective-permute-start(bf16[128,4096]{1,0:T(8,128)(2,1)} %get-tuple-element.50.refs_5_), channel_id=1, source_target_pairs={{1,0},{2,1},{3,2},{5,4},{6,5},{7,6},{9,8},{10,9},{11,10},{13,12},{... | collective-permute-start | bytes 3145736 | tf_op jit(solution)/shard_map/ppermute | solution.py:389
  148.4 41.6 %collective-permute-start.13 = (bf16[128,4096]{1,0:T(8,128)(2,1)}, bf16[128,4096]{1,0:T(8,128)(2,1)}, u32[]{:S(2)}, u32[]{:S(2)}) collective-permute-start(bf16[128,4096]{1,0:T(8,128)(2,1)} %get-tuple-element.54), channel_id=1, source_target_pairs={{1,0},{2,1},{3,2},{5,4},{6,5},{7,6},{9,8},{10,9},{11,10},{13,12},{... | collective-permute-start | bytes 3145736 | tf_op jit(solution)/shard_map/ppermute | solution.py:389
  150.3 39.6 %collective-permute-start.12 = (bf16[128,4096]{1,0:T(8,128)(2,1)}, bf16[128,4096]{1,0:T(8,128)(2,1)}, u32[]{:S(2)}, u32[]{:S(2)}) collective-permute-start(bf16[128,4096]{1,0:T(8,128)(2,1)} %get-tuple-element.53.refs_4_), channel_id=1, source_target_pairs={{0,1},{1,2},{2,3},{4,5},{5,6},{6,7},{8,9},{9,10},{10,11},{12,13},{... | collective-permute-start | bytes 3145736 | tf_op jit(solution)/shard_map/ppermute | solution.py:388
  170.8 45.3 %collective-permute-start.14 = (bf16[128,4096]{1,0:T(8,128)(2,1)}, bf16[128,4096]{1,0:T(8,128)(2,1)}, u32[]{:S(2)}, u32[]{:S(2)}) collective-permute-start(bf16[128,4096]{1,0:T(8,128)(2,1)} %get-tuple-element.55.refs_4_), channel_id=1, source_target_pairs={{0,1},{1,2},{2,3},{4,5},{5,6},{6,7},{8,9},{9,10},{10,11},{12,13},{... | collective-permute-start | bytes 3145736 | tf_op jit(solution)/shard_map/ppermute | solution.py:388
  172.8 43.4 %collective-permute-start.15 = (bf16[128,4096]{1,0:T(8,128)(2,1)}, bf16[128,4096]{1,0:T(8,128)(2,1)}, u32[]{:S(2)}, u32[]{:S(2)}) collective-permute-start(bf16[128,4096]{1,0:T(8,128)(2,1)} %get-tuple-element.56.refs_5_), channel_id=1, source_target_pairs={{1,0},{2,1},{3,2},{5,4},{6,5},{7,6},{9,8},{10,9},{11,10},{13,12},{... | collective-permute-start | bytes 3145736 | tf_op jit(solution)/shard_map/ppermute | solution.py:389
  193.3 52.8 %collective-permute-start.17 = (bf16[128,4096]{1,0:T(8,128)(2,1)}, bf16[128,4096]{1,0:T(8,128)(2,1)}, u32[]{:S(2)}, u32[]{:S(2)}) collective-permute-start(bf16[128,4096]{1,0:T(8,128)(2,1)} %get-tuple-element.59), channel_id=1, source_target_pairs={{1,0},{2,1},{3,2},{5,4},{6,5},{7,6},{9,8},{10,9},{11,10},{13,12},{... | collective-permute-start | bytes 3145736 | tf_op jit(solution)/shard_map/ppermute | solution.py:389
  195.2 50.9 %collective-permute-start.16 = (bf16[128,4096]{1,0:T(8,128)(2,1)}, bf16[128,4096]{1,0:T(8,128)(2,1)}, u32[]{:S(2)}, u32[]{:S(2)}) collective-permute-start(bf16[128,4096]{1,0:T(8,128)(2,1)} %get-tuple-element.57.refs_9_), channel_id=1, source_target_pairs={{0,1},{1,2},{2,3},{4,5},{5,6},{6,7},{8,9},{9,10},{10,11},{12,13},{... | collective-permute-start | bytes 3145736 | tf_op jit(solution)/shard_map/ppermute | solution.py:388
  210.9 47.5 %all-to-all-start.2 = ((bf16[4,128,1024]{2,1,0:T(8,128)(2,1)}), bf16[4,128,1024]{2,1,0:T(8,128)(2,1)}, u32[]{:S(2)}, u32[]{:S(2)}) async-start(bf16[4,128,1024]{2,1,0:T(8,128)(2,1)} %bitcast.18), calls=%async_computation.2 | async-start | bytes 2097152 | tf_op jit(solution)/shard_map/all_to_all | solution.py:381
  258.5 38.4 %all-to-all-start.3 = ((bf16[4,128,1024]{2,1,0:T(8,128)(2,1)}), bf16[4,128,1024]{2,1,0:T(8,128)(2,1)}, u32[]{:S(2)}, u32[]{:S(2)}) async-start(bf16[4,128,1024]{2,1,0:T(8,128)(2,1)} %bitcast.17), calls=%async_computation.3 | async-start | bytes 2097152 | tf_op jit(solution)/shard_map/all_to_all | solution.py:381
  267.3 27.5 %collective-permute-start.21 = (bf16[1,128,4096]{2,1,0:T(8,128)(2,1)}, bf16[1,128,4096]{2,1,0:T(8,128)(2,1)}, u32[]{:S(2)}, u32[]{:S(2)}) collective-permute-start(bf16[1,128,4096]{2,1,0:T(8,128)(2,1)} %finish.2.refs_20_), channel_id=1, source_target_pairs={{28,4},{24,8},{20,12},{16,16},{12,20},{8,24},{4,28},{29,5},{25,9},... | collective-permute-start | bytes 3145736 | tf_op jit(solution)/shard_map/ppermute | solution.py:496
  296.9 9.3 %copy-start = (f32[4,8,128]{2,1,0:T(8,128)S(1)}, f32[4,8,128]{2,1,0:T(8,128)}, u32[]{:S(2)}) copy-start(f32[4,8,128]{2,1,0:T(8,128)} %get-tuple-element.65) | copy-start | bytes 49156
  301.4 24.6 %collective-permute-start.22 = (bf16[1,128,4096]{2,1,0:T(8,128)(2,1)}, bf16[1,128,4096]{2,1,0:T(8,128)(2,1)}, u32[]{:S(2)}, u32[]{:S(2)}) collective-permute-start(bf16[1,128,4096]{2,1,0:T(8,128)(2,1)} %finish.3.refs_4_), channel_id=1, source_target_pairs={{4,0},{8,4},{12,8},{16,12},{20,16},{24,20},{28,24},{5,1},{9,5},{13... | collective-permute-start | bytes 3145736 | tf_op jit(solution)/shard_map/ppermute | solution.py:509
  306.1 3.9 %collective-permute-start.20 = (f32[1,32,128]{2,1,0:T(8,128)S(1)}, f32[1,32,128]{2,1,0:T(8,128)S(1)}, u32[]{:S(2)}, u32[]{:S(2)}) collective-permute-start(f32[1,32,128]{2,1,0:T(8,128)S(1)} %bitcast.20), channel_id=1, source_target_pairs={{0,3},{1,0},{2,1},{3,2},{4,7},{5,4},{6,5},{7,6},{8,11},{9,8},{10,9... | collective-permute-start | bytes 49160 | tf_op jit(solution)/shard_map/ppermute | solution.py:443
  306.2 3.9 %collective-permute-start.19 = (f32[1,32,128]{2,1,0:T(8,128)S(1)}, f32[1,32,128]{2,1,0:T(8,128)S(1)}, u32[]{:S(2)}, u32[]{:S(2)}) collective-permute-start(f32[1,32,128]{2,1,0:T(8,128)S(1)} %bitcast.21), channel_id=1, source_target_pairs={{0,2},{1,3},{2,0},{3,1},{4,6},{5,7},{6,4},{7,5},{8,10},{9,11},{10,... | collective-permute-start | bytes 49160 | tf_op jit(solution)/shard_map/ppermute | solution.py:443
  308.1 2.9 collective-permute-start.18
  310.1 0.9 copy-start.1
  310.1 0.9 copy-start.2
  310.9 0.6 copy-start.3

commit v8 on v6

--- a/solution.py
+++ b/solution.py
@@ -20,13 +20,13 @@
     return jax.ShapeDtypeStruct(dims, dtype)
 
 
-def call(kernel, args, after, in_specs, out_shape, flops=0, **options):
+def call(kernel, args, after, in_specs, out_shape, flops=0, counted=True, **options):
     count = len(args)
     arrays = [*args, *(out_shape if isinstance(out_shape, list) else [out_shape])]
     cost = pl.CostEstimate(
         flops=flops,
         transcendentals=0,
-        bytes_accessed=sum(x.size * x.dtype.itemsize for x in arrays),
+        bytes_accessed=counted * sum(x.size * x.dtype.itemsize for x in arrays),
     )
 
     def body(*refs):
@@ -260,7 +260,7 @@
         ],
         out_shape=[shape((tokens, width), bf16), shape((tokens, depth), bf16)],
         scratch_shapes=[pltpu.VMEM((tokens, tile), bf16), pltpu.VMEM((tokens, depth), f32)],
-        flops=2 * tokens * width * (depth + 2 * taps),
+        flops=6 * tokens * width * (depth + 2 * taps),
         name="back",
     )
 
@@ -307,7 +307,7 @@
         out_specs=pl.BlockSpec((1, step, taps), lambda i: (i, 0, 0)),
         out_shape=shape((groups // step, step, taps), f32),
         scratch_shapes=[pltpu.VMEM((tokens, tile), bf16)] * 2,
-        flops=8 * tokens * width * taps,
+        counted=False,
         name="filter_gradient",
     ).reshape(1, groups, taps)
 
@@ -338,6 +338,33 @@
         scratch_shapes=[pltpu.VMEM((depth, tokens), bf16)] * 2,
         flops=4 * tokens * depth * width,
         name="weight_gradient",
+    )
+
+
+def settle_kernel(own_ref, came_ref, out_ref):
+    stays = 2 * lax.axis_index("section") == lax.axis_size("section")
+
+    @pl.when(stays)
+    def _():
+        out_ref[...] = own_ref[...]
+
+    @pl.when(jnp.logical_not(stays))
+    def _():
+        out_ref[...] = came_ref[...]
+
+
+def settle(own, came):
+    step = came.shape[1] // 2
+    spec = pl.BlockSpec((1, step, came.shape[2]), lambda i: (0, i, 0))
+    return call(
+        settle_kernel,
+        (own, came),
+        (),
+        grid=(2,),
+        in_specs=[spec, spec],
+        out_specs=spec,
+        out_shape=shape(came.shape, came.dtype),
+        name="settle",
     )
 
 
@@ -454,7 +481,7 @@
     sections = lax.axis_size("section")
     mirror = [(s, sections - 1 - s) for s in range(sections)]
     down_pairs = [(s + 1, s) for s in range(sections - 1)]
-    up_pairs = [(sections - s, s) for s in range(1, sections)]
+    up_pairs = [(sections - s, s) for s in range(1, sections) if 2 * s != sections]
     weight = weights[0]
     down_xin, down_cot = down_input[0], down_cot[0]
     up_xin = lax.ppermute(up_input[0], "section", mirror)
@@ -483,19 +510,22 @@
     up_mixes, up_conv = sort_arrivals(up_mix, up_pieces, up_arrivals)
     up_g, up_back = back(up_mixes, weight, ahead, after=(last,))
     up_back = exchange(up_back)
+    taps = filter_gradient(
+        down_mixes, down_part, up_mixes, up_part, *filters.shape[1:], after=(up_g,)
+    )
     down_g, down_back = back(
-        down_mixes, weight, ahead, after=(up_g, *down_arrivals[-1], *up_arrivals[-1])
+        down_mixes, weight, ahead, after=(taps, *down_arrivals[-1], *up_arrivals[-1])
     )
     down_back = exchange(down_back)
     up_grad = finish(up_xin, up_cot, up_conv, up_back, after=(down_g,))
     up_passed = lax.ppermute(up_grad, "section", up_pairs)
-    taps = filter_gradient(
-        down_mixes, down_part, up_mixes, up_part, *filters.shape[1:], after=(up_grad,)
-    )
-    down_grad = finish(down_xin, down_cot, down_conv, down_back, after=(taps, up_passed))
+    weight_grad = weight_gradient(down_x, up_x, down_g, up_g, after=(up_grad,))
+    up_passed = settle(up_grad, up_passed)
+    down_grad = finish(
+        down_xin, down_cot, down_conv, down_back, after=(weight_grad, up_passed)
+    )
     down_passed = lax.ppermute(down_grad, "section", down_pairs)
-    weight_grad = weight_gradient(down_x, up_x, down_g, up_g, after=(down_grad,))
-    taps = sum_all(taps, after=(weight_grad,))
+    taps = sum_all(taps, after=(down_grad,))
     return weight_grad[None], taps, down_passed, up_passed
 
 

time: 361 us -> 323 us (0.89)
  waiting for transfers between devices: 154 us -> 111 us
    ppermute x8, waiting for transfers between devices: 60.9 us -> 8.5 us  [both_ways(): lax.ppermute(left, 'tensor', [(j, i) for i, j in onward])]
    ppermute x8, waiting for transfers between devices: 54.1 us -> 73.8 us  [both_ways(): lax.ppermute(right, 'tensor', onward)]
    ppermute x1, waiting for transfers between devices: 14.6 us -> 0.01 us  [per_device(): up_cot = lax.ppermute(up_cot[0], 'section', mirror)]
    ppermute x8, starting transfers between devices: 19.8 us -> 30.1 us  [both_ways(): lax.ppermute(left, 'tensor', [(j, i) for i, j in onward])]
    ppermute x8, starting transfers between devices: 30.5 us -> 24.3 us  [both_ways(): lax.ppermute(right, 'tensor', onward)]
    ppermute x1, waiting for transfers between devices: 0.01 us -> 3.86 us  [per_device(): down_passed = lax.ppermute(down_grad, 'section', down_pairs)]
    pallas_call x19 -> x20, Pallas kernels: 116 us -> 119 us  [call(): pl.pallas_call(body, in_specs=list(in_specs) + unread, out_shape=out_shap...]
  transfers between devices with their start and end apart: 27 -> 27, of which waited for: 14 -> 16; matrix products, arithmetic and copies ran while one was open for 0% -> 0% of each run, Pallas kernels for 26% -> 35%
where the time goes in v8:
time: 323 us; the launch traced here: 319 us
  Pallas kernels  119 us (37%)
  waiting for transfers between devices  111 us (34%)
  starting transfers between devices  85.4 us (26%)
    pallas_call x20, Pallas kernels, call(): pl.pallas_call(body, in_specs=list(in_specs) + unread, out_shape=out_shap...  119 us
    ppermute x8, waiting for transfers between devices, both_ways(): lax.ppermute(right, 'tensor', onward)  73.8 us
    ppermute x8, starting transfers between devices, both_ways(): lax.ppermute(left, 'tensor', [(j, i) for i, j in onward])  30.1 us
    ppermute x8, starting transfers between devices, both_ways(): lax.ppermute(right, 'tensor', onward)  24.3 us
    all_to_all x4, starting transfers between devices, exchange(): return lax.all_to_all(x, 'tensor', split_axis=0, concat_axis=0, tiled=True)  19.1 us
    ppermute x1, waiting for transfers between devices, per_device(): up_xin = lax.ppermute(up_input[0], 'section', mirror)  13.8 us
    ppermute x1, waiting for transfers between devices, per_device(): up_passed = lax.ppermute(up_grad, 'section', up_pairs)  8.81 us
    ppermute x8, waiting for transfers between devices, both_ways(): lax.ppermute(left, 'tensor', [(j, i) for i, j in onward])  8.5 us
  transfers between devices with their start and end apart: 27, of which 16 were waited for; matrix products, arithmetic and copies ran while one was open for 0% of the time, Pallas kernels for 35%

profile of v8, /device:TPU:10, one launch (start us, length us, event | category | flops | bytes accessed | tf_op | source)
XLA Modules:
  0.0 318.8 jit_solution(1713015918299464226)
XLA Ops:
  3.6 5.3 %all-to-all-start = ((bf16[4,128,1024]{2,1,0:T(8,128)(2,1)}), bf16[4,128,1024]{2,1,0:T(8,128)(2,1)}, u32[]{:S(2)}, u32[]{:S(2)}) async-start(bf16[4,128,1024]{2,1,0:T(8,128)(2,1)} %get-tuple-element.34), calls=%async_computation | async-start | bytes 2097152 | tf_op jit(solution)/shard_map/all_to_all | solution.py:403
  12.7 3.4 %collective-permute-start.2 = (bf16[128,4096]{1,0:T(8,128)(2,1)}, bf16[128,4096]{1,0:T(8,128)(2,1)}, u32[]{:S(2)}, u32[]{:S(2)}) collective-permute-start(bf16[128,4096]{1,0:T(8,128)(2,1)} %get-tuple-element.36.refs_0_), channel_id=1, source_target_pairs={{1,0},{2,1},{3,2},{5,4},{6,5},{7,6},{9,8},{10,9},{11,10},{13,12},{... | collective-permute-start | bytes 3145736 | tf_op jit(solution)/shard_map/ppermute | solution.py:411
  17.9 3.9 %toeplitz.1 = (bf16[32,128,256]{2,1,0:T(8,128)(2,1)}, bf16[32,128,256]{2,1,0:T(8,128)(2,1)}) custom-call(f32[32,128]{1,0:T(8,128)} %bitcast.24), custom_call_target="tpu_custom_call" | custom-call | bytes 4210688 | tf_op jit(solution)/shard_map/toeplitz/pallas_call | solution.py:36
  21.8 13.8 %collective-permute-done.refs_0_ = bf16[128,4096]{1,0:T(8,128)(2,1)} collective-permute-done((bf16[128,4096]{1,0:T(8,128)(2,1)}, bf16[128,4096]{1,0:T(8,128)(2,1)}, u32[]{:S(2)}, u32[]{:S(2)}) %collective-permute-start) | collective-permute-done | bytes 1048608 | tf_op jit(solution)/shard_map/ppermute | solution.py:487
  37.9 5.1 %all-to-all-start.1 = ((bf16[4,128,1024]{2,1,0:T(8,128)(2,1)}), bf16[4,128,1024]{2,1,0:T(8,128)(2,1)}, u32[]{:S(2)}, u32[]{:S(2)}) async-start(bf16[4,128,1024]{2,1,0:T(8,128)(2,1)} %prepare.3.refs_3_), calls=%async_computation.1 | async-start | bytes 2097152 | tf_op jit(solution)/shard_map/all_to_all | solution.py:403
  43.0 23.7 %collective-permute-done.1.refs_2_.refs_0_.refs_1_ = bf16[128,4096]{1,0:T(8,128)(2,1)} collective-permute-done((bf16[128,4096]{1,0:T(8,128)(2,1)}, bf16[128,4096]{1,0:T(8,128)(2,1)}, u32[]{:S(2)}, u32[]{:S(2)}) %collective-permute-start.1) | collective-permute-done | bytes 1048608 | tf_op jit(solution)/shard_map/ppermute | solution.py:410
  69.4 4.4 %collective-permute-start.6 = (bf16[128,4096]{1,0:T(8,128)(2,1)}, bf16[128,4096]{1,0:T(8,128)(2,1)}, u32[]{:S(2)}, u32[]{:S(2)}) collective-permute-start(bf16[128,4096]{1,0:T(8,128)(2,1)} %grad_mix.1.refs_4_.refs_0_.refs_8_), channel_id=1, source_target_pairs={{0,1},{1,2},{2,3},{4,5},{5,6},{6,7},{8,9},{9,10},{10,11},{12,13},{... | collective-permute-start | bytes 3145736 | tf_op jit(solution)/shard_map/ppermute | solution.py:410
  76.2 10.9 %project.2 = (bf16[512,4096]{1,0:T(8,128)(2,1)}, bf16[128,4096]{1,0:T(8,128)(2,1)}, bf16[128,4096]{1,0:T(8,128)(2,1)}, bf16[128,4096]{1,0:T(8,128)(2,1)}, bf16[128,4096]{1,0:T(8,128)(2,1)}) custom-call(bf16[512,1024]{1,0:T(8,128)(2,1)} %bitcast.2.refs_0_, bf16[1024,4096]{1,0:T(8,128)(2,1)} %bitcast.25, bf16[32,128,256]{2,1,0:T(8,128)(2,1)} %get-tuple-element.37.refs_2_, ...), custom_call_target="tpu_custom_call" | custom-call | flops 5368709120 | bytes 19922944 | tf_op jit(solution)/shard_map/project/pallas_call | solution.py:36
  97.2 11.0 %project.3 = (bf16[512,4096]{1,0:T(8,128)(2,1)}, bf16[128,4096]{1,0:T(8,128)(2,1)}, bf16[128,4096]{1,0:T(8,128)(2,1)}, bf16[128,4096]{1,0:T(8,128)(2,1)}, bf16[128,4096]{1,0:T(8,128)(2,1)}) custom-call(bf16[512,1024]{1,0:T(8,128)(2,1)} %bitcast.5.refs_0_.refs_1_, bf16[1024,4096]{1,0:T(8,128)(2,1)} %bitcast.26, ...), custom_call_target="tpu_custom_call" | custom-call | flops 5368709120 | bytes 19922944 | tf_op jit(solution)/shard_map/project/pallas_call | solution.py:36
  113.9 4.4 %collective-permute-start.11 = (bf16[128,4096]{1,0:T(8,128)(2,1)}, bf16[128,4096]{1,0:T(8,128)(2,1)}, u32[]{:S(2)}, u32[]{:S(2)}) collective-permute-start(bf16[128,4096]{1,0:T(8,128)(2,1)} %get-tuple-element.49), channel_id=1, source_target_pairs={{1,0},{2,1},{3,2},{5,4},{6,5},{7,6},{9,8},{10,9},{11,10},{13,12},{... | collective-permute-start | bytes 3145736 | tf_op jit(solution)/shard_map/ppermute | solution.py:411
  118.3 4.5 %collective-permute-done.4.refs_0_.refs_2_ = bf16[128,4096]{1,0:T(8,128)(2,1)} collective-permute-done((bf16[128,4096]{1,0:T(8,128)(2,1)}, bf16[128,4096]{1,0:T(8,128)(2,1)}, u32[]{:S(2)}, u32[]{:S(2)}) %collective-permute-start.4) | collective-permute-done | bytes 1048608 | tf_op jit(solution)/shard_map/ppermute | solution.py:410
  130.6 4.1 %collective-permute-start.9 = (bf16[128,4096]{1,0:T(8,128)(2,1)}, bf16[128,4096]{1,0:T(8,128)(2,1)}, u32[]{:S(2)}, u32[]{:S(2)}) collective-permute-start(bf16[128,4096]{1,0:T(8,128)(2,1)} %get-tuple-element.48.refs_5_), channel_id=1, source_target_pairs={{1,0},{2,1},{3,2},{5,4},{6,5},{7,6},{9,8},{10,9},{11,10},{13,12},{... | collective-permute-start | bytes 3145736 | tf_op jit(solution)/shard_map/ppermute | solution.py:411
  134.8 10.6 %collective-permute-done.10.refs_0_.refs_2_.refs_10_ = bf16[128,4096]{1,0:T(8,128)(2,1)} collective-permute-done((bf16[128,4096]{1,0:T(8,128)(2,1)}, bf16[128,4096]{1,0:T(8,128)(2,1)}, u32[]{:S(2)}, u32[]{:S(2)}) %collective-permute-start.10) | collective-permute-done | bytes 1048608 | tf_op jit(solution)/shard_map/ppermute | solution.py:410
  147.0 3.7 %payload.9 = (bf16[128,4096]{1,0:T(8,128)(2,1)}, bf16[128,4096]{1,0:T(8,128)(2,1)}) custom-call(bf16[128,4096]{1,0:T(8,128)(2,1)} %collective-permute-done.10.refs_0_.refs_2_.refs_10_, bf16[128,4096]{1,0:T(8,128)(2,1)} %collective-permute-done.11.refs_1_.refs_5_.refs_13_, bf16[128,4096]{1,0:T(8,128)(2,1)} %get-tuple-element.50.refs_2_.refs_3_, ...), custom_call_target="tpu_custom_call" | custom-call | bytes 6291456 | tf_op jit(solution)/shard_map/payload/pallas_call | solution.py:36
  153.4 4.1 %collective-permute-start.13 = (bf16[128,4096]{1,0:T(8,128)(2,1)}, bf16[128,4096]{1,0:T(8,128)(2,1)}, u32[]{:S(2)}, u32[]{:S(2)}) collective-permute-start(bf16[128,4096]{1,0:T(8,128)(2,1)} %get-tuple-element.52), channel_id=1, source_target_pairs={{1,0},{2,1},{3,2},{5,4},{6,5},{7,6},{9,8},{10,9},{11,10},{13,12},{... | collective-permute-start | bytes 3145736 | tf_op jit(solution)/shard_map/ppermute | solution.py:411
  157.5 10.2 %collective-permute-done.8.refs_0_.refs_3_ = bf16[128,4096]{1,0:T(8,128)(2,1)} collective-permute-done((bf16[128,4096]{1,0:T(8,128)(2,1)}, bf16[128,4096]{1,0:T(8,128)(2,1)}, u32[]{:S(2)}, u32[]{:S(2)}) %collective-permute-start.8) | collective-permute-done | bytes 1048608 | tf_op jit(solution)/shard_map/ppermute | solution.py:410
  169.5 3.5 %payload.10 = (bf16[128,4096]{1,0:T(8,128)(2,1)}, bf16[128,4096]{1,0:T(8,128)(2,1)}) custom-call(bf16[128,4096]{1,0:T(8,128)(2,1)} %collective-permute-done.8.refs_0_.refs_3_, bf16[128,4096]{1,0:T(8,128)(2,1)} %collective-permute-done.9.refs_1_.refs_6_, bf16[128,4096]{1,0:T(8,128)(2,1)} %get-tuple-element.39.refs_3_.refs_2_, ...), custom_call_target="tpu_custom_call" | custom-call | bytes 6291456 | tf_op jit(solution)/shard_map/payload/pallas_call | solution.py:36
  175.6 4.1 %collective-permute-start.15 = (bf16[128,4096]{1,0:T(8,128)(2,1)}, bf16[128,4096]{1,0:T(8,128)(2,1)}, u32[]{:S(2)}, u32[]{:S(2)}) collective-permute-start(bf16[128,4096]{1,0:T(8,128)(2,1)} %get-tuple-element.55.refs_5_), channel_id=1, source_target_pairs={{1,0},{2,1},{3,2},{5,4},{6,5},{7,6},{9,8},{10,9},{11,10},{13,12},{... | collective-permute-start | bytes 3145736 | tf_op jit(solution)/shard_map/ppermute | solution.py:411
  179.7 10.5 %collective-permute-done.12.refs_0_.refs_3_.refs_11_ = bf16[128,4096]{1,0:T(8,128)(2,1)} collective-permute-done((bf16[128,4096]{1,0:T(8,128)(2,1)}, bf16[128,4096]{1,0:T(8,128)(2,1)}, u32[]{:S(2)}, u32[]{:S(2)}) %collective-permute-start.12) | collective-permute-done | bytes 1048608 | tf_op jit(solution)/shard_map/ppermute | solution.py:410
  192.0 3.4 %payload.11 = (bf16[128,4096]{1,0:T(8,128)(2,1)}, bf16[128,4096]{1,0:T(8,128)(2,1)}) custom-call(bf16[128,4096]{1,0:T(8,128)(2,1)} %collective-permute-done.12.refs_0_.refs_3_.refs_11_, bf16[128,4096]{1,0:T(8,128)(2,1)} %collective-permute-done.13.refs_1_.refs_6_.refs_14_, bf16[128,4096]{1,0:T(8,128)(2,1)} %get-tuple-element.45.refs_3_.refs_2_, ...), custom_call_target="tpu_custom_call" | custom-call | bytes 6291456 | tf_op jit(solution)/shard_map/payload/pallas_call | solution.py:36
  198.1 4.1 %collective-permute-start.17 = (bf16[128,4096]{1,0:T(8,128)(2,1)}, bf16[128,4096]{1,0:T(8,128)(2,1)}, u32[]{:S(2)}, u32[]{:S(2)}) collective-permute-start(bf16[128,4096]{1,0:T(8,128)(2,1)} %get-tuple-element.58), channel_id=1, source_target_pairs={{1,0},{2,1},{3,2},{5,4},{6,5},{7,6},{9,8},{10,9},{11,10},{13,12},{... | collective-permute-start | bytes 3145736 | tf_op jit(solution)/shard_map/ppermute | solution.py:411
  202.2 12.4 %back.2 = (bf16[512,4096]{1,0:T(8,128)(2,1)}, bf16[512,1024]{1,0:T(8,128)(2,1)}) custom-call(bf16[128,4096]{1,0:T(8,128)(2,1)} %grad_mix.1.refs_4_.refs_0_.refs_8_, bf16[128,4096]{1,0:T(8,128)(2,1)} %collective-permute-done.6.refs_0_.refs_1_.refs_9_, bf16[128,4096]{1,0:T(8,128)(2,1)} %collective-permute-done.10.refs_0_.refs_2_.refs_10_, ...), custom_call_target="tpu_custom_call" | custom-call | flops 16106127360 | bytes 23068672 | tf_op jit(solution)/shard_map/back/pallas_call | solution.py:36
  214.6 4.4 %all-to-all-start.2 = ((bf16[4,128,1024]{2,1,0:T(8,128)(2,1)}), bf16[4,128,1024]{2,1,0:T(8,128)(2,1)}, u32[]{:S(2)}, u32[]{:S(2)}) async-start(bf16[4,128,1024]{2,1,0:T(8,128)(2,1)} %bitcast.17), calls=%async_computation.2 | async-start | bytes 2097152 | tf_op jit(solution)/shard_map/all_to_all | solution.py:403
  219.1 13.0 %filter_gradient.1 = f32[4,8,128]{2,1,0:T(8,128)} custom-call(bf16[128,4096]{1,0:T(8,128)(2,1)} %get-tuple-element.36.refs_0_, bf16[128,4096]{1,0:T(8,128)(2,1)} %collective-permute-done.1.refs_2_.refs_0_.refs_1_, bf16[128,4096]{1,0:T(8,128)(2,1)} %collective-permute-done.4.refs_0_.refs_2_, bf16[128,4096]{1,0:T(8,128)(2,1)} %collective-permute-done.8.refs_0_.refs_3_, ...), custom_call_target="tpu_custom_call" | custom-call | tf_op jit(solution)/shard_map/filter_gradient/pallas_call | solution.py:36
  232.1 14.3 %collective-permute-done.16.refs_12_.refs_4_ = bf16[128,4096]{1,0:T(8,128)(2,1)} collective-permute-done((bf16[128,4096]{1,0:T(8,128)(2,1)}, bf16[128,4096]{1,0:T(8,128)(2,1)}, u32[]{:S(2)}, u32[]{:S(2)}) %collective-permute-start.16) | collective-permute-done | bytes 1048608 | tf_op jit(solution)/shard_map/ppermute | solution.py:410
  248.1 12.3 %back.3 = (bf16[512,4096]{1,0:T(8,128)(2,1)}, bf16[512,1024]{1,0:T(8,128)(2,1)}) custom-call(bf16[128,4096]{1,0:T(8,128)(2,1)} %get-tuple-element.36.refs_0_, bf16[128,4096]{1,0:T(8,128)(2,1)} %collective-permute-done.1.refs_2_.refs_0_.refs_1_, bf16[128,4096]{1,0:T(8,128)(2,1)} %collective-permute-done.4.refs_0_.refs_2_, ...), custom_call_target="tpu_custom_call" | custom-call | flops 16106127360 | bytes 23068672 | tf_op jit(solution)/shard_map/back/pallas_call | solution.py:36
  260.5 4.3 %all-to-all-start.3 = ((bf16[4,128,1024]{2,1,0:T(8,128)(2,1)}), bf16[4,128,1024]{2,1,0:T(8,128)(2,1)}, u32[]{:S(2)}, u32[]{:S(2)}) async-start(bf16[4,128,1024]{2,1,0:T(8,128)(2,1)} %bitcast.18), calls=%async_computation.3 | async-start | bytes 2097152 | tf_op jit(solution)/shard_map/all_to_all | solution.py:403
  264.7 4.6 %finish.2.refs_4_.refs_0_ = bf16[1,128,4096]{2,1,0:T(8,128)(2,1)} custom-call(bf16[128,4096]{1,0:T(8,128)(2,1)} %collective-permute-done.refs_0_, bf16[128,4096]{1,0:T(8,128)(2,1)} %collective-permute-done.3.refs_1_, bf16[4,128,1024]{2,1,0:T(8,128)(2,1)} %all-to-all-done.2.refs_2_, bf16[128,4096]{1,0:T(8,128)(2,1)} %get-tuple-element.61.refs_3_, ...), custom_call_target="tpu_custom_call" | custom-call | bytes 7340032 | tf_op jit(solution)/shard_map/finish/pallas_call | solution.py:36
  272.7 13.6 %weight_gradient.1.refs_6_ = bf16[1024,4096]{1,0:T(8,128)(2,1)} custom-call(bf16[512,1024]{1,0:T(8,128)(2,1)} %bitcast.2.refs_0_, bf16[512,1024]{1,0:T(8,128)(2,1)} %bitcast.5.refs_0_.refs_1_, bf16[512,4096]{1,0:T(8,128)(2,1)} %get-tuple-element.59.refs_6_.refs_2_, bf16[512,4096]{1,0:T(8,128)(2,1)} %get-tuple-element.57.refs_16_.refs_3_, ...), custom_call_target="tpu_custom_call" | custom-call | flops 8589934592 | bytes 18874368 | tf_op jit(solution)/shard_map/weight_gradient/pallas_call | solution.py:36
  286.3 8.8 %collective-permute-done.21.refs_1_ = bf16[1,128,4096]{2,1,0:T(8,128)(2,1)} collective-permute-done((bf16[1,128,4096]{2,1,0:T(8,128)(2,1)}, bf16[1,128,4096]{2,1,0:T(8,128)(2,1)}, u32[]{:S(2)}, u32[]{:S(2)}) %collective-permute-start.21) | collective-permute-done | bytes 1048608 | tf_op jit(solution)/shard_map/ppermute | solution.py:521
  297.5 4.6 %finish.3.refs_4_ = bf16[1,128,4096]{2,1,0:T(8,128)(2,1)} custom-call(bf16[128,4096]{1,0:T(8,128)(2,1)} %bitcast.14, bf16[128,4096]{1,0:T(8,128)(2,1)} %bitcast.16, bf16[4,128,1024]{2,1,0:T(8,128)(2,1)} %all-to-all-done.3.refs_2_, bf16[128,4096]{1,0:T(8,128)(2,1)} %get-tuple-element.63.refs_3_, bf16[128,4096]{1,0:T(8,128)(2,1)} %collective-permute-done.14.refs_10_.refs_4_, ...), custom_call_target="tpu_custom_call" | custom-call | bytes 7340032 | tf_op jit(solution)/shard_map/finish/pallas_call | solution.py:36
  312.7 3.9 %collective-permute-done.22 = bf16[1,128,4096]{2,1,0:T(8,128)(2,1)} collective-permute-done((bf16[1,128,4096]{2,1,0:T(8,128)(2,1)}, bf16[1,128,4096]{2,1,0:T(8,128)(2,1)}, u32[]{:S(2)}, u32[]{:S(2)}) %collective-permute-start.22) | collective-permute-done | bytes 1048608 | tf_op jit(solution)/shard_map/ppermute | solution.py:527
  (51 shorter events, 73.1 us)
Async XLA Ops:
  3.6 34.2 %all-to-all-start = ((bf16[4,128,1024]{2,1,0:T(8,128)(2,1)}), bf16[4,128,1024]{2,1,0:T(8,128)(2,1)}, u32[]{:S(2)}, u32[]{:S(2)}) async-start(bf16[4,128,1024]{2,1,0:T(8,128)(2,1)} %get-tuple-element.34), calls=%async_computation | async-start | bytes 2097152 | tf_op jit(solution)/shard_map/all_to_all | solution.py:403
  8.9 26.6 %collective-permute-start = (bf16[128,4096]{1,0:T(8,128)(2,1)}, bf16[128,4096]{1,0:T(8,128)(2,1)}, u32[]{:S(2)}, u32[]{:S(2)}) collective-permute-start(bf16[128,4096]{1,0:T(8,128)(2,1)} %bitcast.29), channel_id=1, source_target_pairs={{0,28},{4,24},{8,20},{12,16},{16,12},{20,8},{24,4},{28,0},{1,29},{... | collective-permute-start | bytes 3145736 | tf_op jit(solution)/shard_map/ppermute | solution.py:487
  9.3 57.3 %collective-permute-start.1 = (bf16[128,4096]{1,0:T(8,128)(2,1)}, bf16[128,4096]{1,0:T(8,128)(2,1)}, u32[]{:S(2)}, u32[]{:S(2)}) collective-permute-start(bf16[128,4096]{1,0:T(8,128)(2,1)} %get-tuple-element.36.refs_0_), channel_id=1, source_target_pairs={{0,1},{1,2},{2,3},{4,5},{5,6},{6,7},{8,9},{9,10},{10,11},{12,13},{... | collective-permute-start | bytes 3145736 | tf_op jit(solution)/shard_map/ppermute | solution.py:410
  12.7 53.9 %collective-permute-start.2 = (bf16[128,4096]{1,0:T(8,128)(2,1)}, bf16[128,4096]{1,0:T(8,128)(2,1)}, u32[]{:S(2)}, u32[]{:S(2)}) collective-permute-start(bf16[128,4096]{1,0:T(8,128)(2,1)} %get-tuple-element.36.refs_0_), channel_id=1, source_target_pairs={{1,0},{2,1},{3,2},{5,4},{6,5},{7,6},{9,8},{10,9},{11,10},{13,12},{... | collective-permute-start | bytes 3145736 | tf_op jit(solution)/shard_map/ppermute | solution.py:411
  16.1 50.5 %collective-permute-start.3 = (bf16[128,4096]{1,0:T(8,128)(2,1)}, bf16[128,4096]{1,0:T(8,128)(2,1)}, u32[]{:S(2)}, u32[]{:S(2)}) collective-permute-start(bf16[128,4096]{1,0:T(8,128)(2,1)} %bitcast.30), channel_id=1, source_target_pairs={{0,28},{4,24},{8,20},{12,16},{16,12},{20,8},{24,4},{28,0},{1,29},{... | collective-permute-start | bytes 3145736 | tf_op jit(solution)/shard_map/ppermute | solution.py:488
  37.9 59.3 %all-to-all-start.1 = ((bf16[4,128,1024]{2,1,0:T(8,128)(2,1)}), bf16[4,128,1024]{2,1,0:T(8,128)(2,1)}, u32[]{:S(2)}, u32[]{:S(2)}) async-start(bf16[4,128,1024]{2,1,0:T(8,128)(2,1)} %prepare.3.refs_3_), calls=%async_computation.1 | async-start | bytes 2097152 | tf_op jit(solution)/shard_map/all_to_all | solution.py:403
  69.4 38.9 %collective-permute-start.6 = (bf16[128,4096]{1,0:T(8,128)(2,1)}, bf16[128,4096]{1,0:T(8,128)(2,1)}, u32[]{:S(2)}, u32[]{:S(2)}) collective-permute-start(bf16[128,4096]{1,0:T(8,128)(2,1)} %grad_mix.1.refs_4_.refs_0_.refs_8_), channel_id=1, source_target_pairs={{0,1},{1,2},{2,3},{4,5},{5,6},{6,7},{8,9},{9,10},{10,11},{12,13},{... | collective-permute-start | bytes 3145736 | tf_op jit(solution)/shard_map/ppermute | solution.py:410
  73.8 34.5 %collective-permute-start.7 = (bf16[128,4096]{1,0:T(8,128)(2,1)}, bf16[128,4096]{1,0:T(8,128)(2,1)}, u32[]{:S(2)}, u32[]{:S(2)}) collective-permute-start(bf16[128,4096]{1,0:T(8,128)(2,1)} %grad_mix.1.refs_4_.refs_0_.refs_8_), channel_id=1, source_target_pairs={{1,0},{2,1},{3,2},{5,4},{6,5},{7,6},{9,8},{10,9},{11,10},{13,12},{... | collective-permute-start | bytes 3145736 | tf_op jit(solution)/shard_map/ppermute | solution.py:411
  90.4 32.4 %collective-permute-start.4 = (bf16[128,4096]{1,0:T(8,128)(2,1)}, bf16[128,4096]{1,0:T(8,128)(2,1)}, u32[]{:S(2)}, u32[]{:S(2)}) collective-permute-start(bf16[128,4096]{1,0:T(8,128)(2,1)} %get-tuple-element.41.refs_3_.refs_4_), channel_id=1, source_target_pairs={{0,1},{1,2},{2,3},{4,5},{5,6},{6,7},{8,9},{9,10},{10,11},{12,13},{... | collective-permute-start | bytes 3145736 | tf_op jit(solution)/shard_map/ppermute | solution.py:410
  93.8 30.8 %collective-permute-start.5 = (bf16[128,4096]{1,0:T(8,128)(2,1)}, bf16[128,4096]{1,0:T(8,128)(2,1)}, u32[]{:S(2)}, u32[]{:S(2)}) collective-permute-start(bf16[128,4096]{1,0:T(8,128)(2,1)} %get-tuple-element.42.refs_4_.refs_5_), channel_id=1, source_target_pairs={{1,0},{2,1},{3,2},{5,4},{6,5},{7,6},{9,8},{10,9},{11,10},{13,12},{... | collective-permute-start | bytes 3145736 | tf_op jit(solution)/shard_map/ppermute | solution.py:411
  111.5 33.8 %collective-permute-start.10 = (bf16[128,4096]{1,0:T(8,128)(2,1)}, bf16[128,4096]{1,0:T(8,128)(2,1)}, u32[]{:S(2)}, u32[]{:S(2)}) collective-permute-start(bf16[128,4096]{1,0:T(8,128)(2,1)} %get-tuple-element.46.refs_4_), channel_id=1, source_target_pairs={{0,1},{1,2},{2,3},{4,5},{5,6},{6,7},{8,9},{9,10},{10,11},{12,13},{... | collective-permute-start | bytes 3145736 | tf_op jit(solution)/shard_map/ppermute | solution.py:410
  113.9 33.1 %collective-permute-start.11 = (bf16[128,4096]{1,0:T(8,128)(2,1)}, bf16[128,4096]{1,0:T(8,128)(2,1)}, u32[]{:S(2)}, u32[]{:S(2)}) collective-permute-start(bf16[128,4096]{1,0:T(8,128)(2,1)} %get-tuple-element.49), channel_id=1, source_target_pairs={{1,0},{2,1},{3,2},{5,4},{6,5},{7,6},{9,8},{10,9},{11,10},{13,12},{... | collective-permute-start | bytes 3145736 | tf_op jit(solution)/shard_map/ppermute | solution.py:411
  127.9 39.8 %collective-permute-start.8 = (bf16[128,4096]{1,0:T(8,128)(2,1)}, bf16[128,4096]{1,0:T(8,128)(2,1)}, u32[]{:S(2)}, u32[]{:S(2)}) collective-permute-start(bf16[128,4096]{1,0:T(8,128)(2,1)} %get-tuple-element.47.refs_4_), channel_id=1, source_target_pairs={{0,1},{1,2},{2,3},{4,5},{5,6},{6,7},{8,9},{9,10},{10,11},{12,13},{... | collective-permute-start | bytes 3145736 | tf_op jit(solution)/shard_map/ppermute | solution.py:410
  130.6 38.8 %collective-permute-start.9 = (bf16[128,4096]{1,0:T(8,128)(2,1)}, bf16[128,4096]{1,0:T(8,128)(2,1)}, u32[]{:S(2)}, u32[]{:S(2)}) collective-permute-start(bf16[128,4096]{1,0:T(8,128)(2,1)} %get-tuple-element.48.refs_5_), channel_id=1, source_target_pairs={{1,0},{2,1},{3,2},{5,4},{6,5},{7,6},{9,8},{10,9},{11,10},{13,12},{... | collective-permute-start | bytes 3145736 | tf_op jit(solution)/shard_map/ppermute | solution.py:411
  150.7 39.6 %collective-permute-start.12 = (bf16[128,4096]{1,0:T(8,128)(2,1)}, bf16[128,4096]{1,0:T(8,128)(2,1)}, u32[]{:S(2)}, u32[]{:S(2)}) collective-permute-start(bf16[128,4096]{1,0:T(8,128)(2,1)} %get-tuple-element.51.refs_4_), channel_id=1, source_target_pairs={{0,1},{1,2},{2,3},{4,5},{5,6},{6,7},{8,9},{9,10},{10,11},{12,13},{... | collective-permute-start | bytes 3145736 | tf_op jit(solution)/shard_map/ppermute | solution.py:410
  153.4 38.6 %collective-permute-start.13 = (bf16[128,4096]{1,0:T(8,128)(2,1)}, bf16[128,4096]{1,0:T(8,128)(2,1)}, u32[]{:S(2)}, u32[]{:S(2)}) collective-permute-start(bf16[128,4096]{1,0:T(8,128)(2,1)} %get-tuple-element.52), channel_id=1, source_target_pairs={{1,0},{2,1},{3,2},{5,4},{6,5},{7,6},{9,8},{10,9},{11,10},{13,12},{... | collective-permute-start | bytes 3145736 | tf_op jit(solution)/shard_map/ppermute | solution.py:411
  172.9 59.1 %collective-permute-start.14 = (bf16[128,4096]{1,0:T(8,128)(2,1)}, bf16[128,4096]{1,0:T(8,128)(2,1)}, u32[]{:S(2)}, u32[]{:S(2)}) collective-permute-start(bf16[128,4096]{1,0:T(8,128)(2,1)} %get-tuple-element.54.refs_4_), channel_id=1, source_target_pairs={{0,1},{1,2},{2,3},{4,5},{5,6},{6,7},{8,9},{9,10},{10,11},{12,13},{... | collective-permute-start | bytes 3145736 | tf_op jit(solution)/shard_map/ppermute | solution.py:410
  175.6 56.4 %collective-permute-start.15 = (bf16[128,4096]{1,0:T(8,128)(2,1)}, bf16[128,4096]{1,0:T(8,128)(2,1)}, u32[]{:S(2)}, u32[]{:S(2)}) collective-permute-start(bf16[128,4096]{1,0:T(8,128)(2,1)} %get-tuple-element.55.refs_5_), channel_id=1, source_target_pairs={{1,0},{2,1},{3,2},{5,4},{6,5},{7,6},{9,8},{10,9},{11,10},{13,12},{... | collective-permute-start | bytes 3145736 | tf_op jit(solution)/shard_map/ppermute | solution.py:411
  195.4 51.0 %collective-permute-start.16 = (bf16[128,4096]{1,0:T(8,128)(2,1)}, bf16[128,4096]{1,0:T(8,128)(2,1)}, u32[]{:S(2)}, u32[]{:S(2)}) collective-permute-start(bf16[128,4096]{1,0:T(8,128)(2,1)} %get-tuple-element.56.refs_9_), channel_id=1, source_target_pairs={{0,1},{1,2},{2,3},{4,5},{5,6},{6,7},{8,9},{9,10},{10,11},{12,13},{... | collective-permute-start | bytes 3145736 | tf_op jit(solution)/shard_map/ppermute | solution.py:410
  198.1 50.0 %collective-permute-start.17 = (bf16[128,4096]{1,0:T(8,128)(2,1)}, bf16[128,4096]{1,0:T(8,128)(2,1)}, u32[]{:S(2)}, u32[]{:S(2)}) collective-permute-start(bf16[128,4096]{1,0:T(8,128)(2,1)} %get-tuple-element.58), channel_id=1, source_target_pairs={{1,0},{2,1},{3,2},{5,4},{6,5},{7,6},{9,8},{10,9},{11,10},{13,12},{... | collective-permute-start | bytes 3145736 | tf_op jit(solution)/shard_map/ppermute | solution.py:411
  214.6 45.8 %all-to-all-start.2 = ((bf16[4,128,1024]{2,1,0:T(8,128)(2,1)}), bf16[4,128,1024]{2,1,0:T(8,128)(2,1)}, u32[]{:S(2)}, u32[]{:S(2)}) async-start(bf16[4,128,1024]{2,1,0:T(8,128)(2,1)} %bitcast.17), calls=%async_computation.2 | async-start | bytes 2097152 | tf_op jit(solution)/shard_map/all_to_all | solution.py:403
  260.5 37.0 %all-to-all-start.3 = ((bf16[4,128,1024]{2,1,0:T(8,128)(2,1)}), bf16[4,128,1024]{2,1,0:T(8,128)(2,1)}, u32[]{:S(2)}, u32[]{:S(2)}) async-start(bf16[4,128,1024]{2,1,0:T(8,128)(2,1)} %bitcast.18), calls=%async_computation.3 | async-start | bytes 2097152 | tf_op jit(solution)/shard_map/all_to_all | solution.py:403
  269.3 25.8 %collective-permute-start.21 = (bf16[1,128,4096]{2,1,0:T(8,128)(2,1)}, bf16[1,128,4096]{2,1,0:T(8,128)(2,1)}, u32[]{:S(2)}, u32[]{:S(2)}) collective-permute-start(bf16[1,128,4096]{2,1,0:T(8,128)(2,1)} %finish.2.refs_4_.refs_0_), channel_id=1, source_target_pairs={{28,4},{24,8},{20,12},{12,20},{8,24},{4,28},{29,5},{25,9},{21,13},... | collective-permute-start | bytes 3145736 | tf_op jit(solution)/shard_map/ppermute | solution.py:521
  297.5 6.5 %copy-start = (f32[4,8,128]{2,1,0:T(8,128)S(1)}, f32[4,8,128]{2,1,0:T(8,128)}, u32[]{:S(2)}) copy-start(f32[4,8,128]{2,1,0:T(8,128)} %filter_gradient.1) | copy-start | bytes 49156
  302.0 14.5 %collective-permute-start.22 = (bf16[1,128,4096]{2,1,0:T(8,128)(2,1)}, bf16[1,128,4096]{2,1,0:T(8,128)(2,1)}, u32[]{:S(2)}, u32[]{:S(2)}) collective-permute-start(bf16[1,128,4096]{2,1,0:T(8,128)(2,1)} %finish.3.refs_4_), channel_id=1, source_target_pairs={{4,0},{8,4},{12,8},{16,12},{20,16},{24,20},{28,24},{5,1},{9,5},{13... | collective-permute-start | bytes 3145736 | tf_op jit(solution)/shard_map/ppermute | solution.py:527
  303.9 4.4 %collective-permute-start.18 = (f32[1,32,128]{2,1,0:T(8,128)S(1)}, f32[1,32,128]{2,1,0:T(8,128)S(1)}, u32[]{:S(2)}, u32[]{:S(2)}) collective-permute-start(f32[1,32,128]{2,1,0:T(8,128)S(1)} %bitcast.21), channel_id=1, source_target_pairs={{0,1},{1,2},{2,3},{3,0},{4,5},{5,6},{6,7},{7,4},{8,9},{9,10},{10,1... | collective-permute-start | bytes 49160 | tf_op jit(solution)/shard_map/ppermute | solution.py:465
  305.5 4.6 %collective-permute-start.19 = (f32[1,32,128]{2,1,0:T(8,128)S(1)}, f32[1,32,128]{2,1,0:T(8,128)S(1)}, u32[]{:S(2)}, u32[]{:S(2)}) collective-permute-start(f32[1,32,128]{2,1,0:T(8,128)S(1)} %bitcast.22), channel_id=1, source_target_pairs={{0,2},{1,3},{2,0},{3,1},{4,6},{5,7},{6,4},{7,5},{8,10},{9,11},{10,... | collective-permute-start | bytes 49160 | tf_op jit(solution)/shard_map/ppermute | solution.py:465
  306.7 3.7 %collective-permute-start.20 = (f32[1,32,128]{2,1,0:T(8,128)S(1)}, f32[1,32,128]{2,1,0:T(8,128)S(1)}, u32[]{:S(2)}, u32[]{:S(2)}) collective-permute-start(f32[1,32,128]{2,1,0:T(8,128)S(1)} %bitcast.23), channel_id=1, source_target_pairs={{0,3},{1,0},{2,1},{3,2},{4,7},{5,4},{6,5},{7,6},{8,11},{9,8},{10,9... | collective-permute-start | bytes 49160 | tf_op jit(solution)/shard_map/ppermute | solution.py:465
  308.4 2.1 copy-start.1
  310.1 0.6 copy-start.2
  310.7 0.6 copy-start.3

commit v9 on v8

--- a/solution.py
+++ b/solution.py
@@ -336,7 +336,7 @@
         out_specs=pl.BlockSpec((depth, tile), lambda i: (0, i)),
         out_shape=shape((depth, width), bf16),
         scratch_shapes=[pltpu.VMEM((depth, tokens), bf16)] * 2,
-        flops=4 * tokens * depth * width,
+        counted=False,
         name="weight_gradient",
     )
 
@@ -353,13 +353,13 @@
         out_ref[...] = came_ref[...]
 
 
-def settle(own, came):
+def settle(own, came, after=()):
     step = came.shape[1] // 2
     spec = pl.BlockSpec((1, step, came.shape[2]), lambda i: (0, i, 0))
     return call(
         settle_kernel,
         (own, came),
-        (),
+        after,
         grid=(2,),
         in_specs=[spec, spec],
         out_specs=spec,
@@ -446,9 +446,14 @@
     )
 
 
+def list_blocks(mix, arrivals):
+    rights, lefts = zip(*arrivals)
+    return [mix, *rights, *lefts]
+
+
 def sort_arrivals(mix, pieces, arrivals):
-    rights, lefts = zip(*arrivals)
-    return [mix, *rights[:-1], *lefts[:-1]], [pieces[0], rights[-1], lefts[-1]]
+    right, left = arrivals[-1]
+    return list_blocks(mix, arrivals[:-1]), [pieces[0], right, left]
 
 
 def sum_kernel(*refs):
@@ -498,7 +503,7 @@
     up_arrivals = [both_ways(up_mix, up_mix)]
     down_part, down_pieces = project(down_x, weight, causal, after=(up_normed, up_mix))
     last = down_part
-    for s in range(2, blocks + 1):
+    for s in range(2, blocks):
         sent = payload(s, down_arrivals[-1], down_pieces, after=(last,))
         down_arrivals.append(both_ways(*sent))
         if s == 2:
@@ -506,24 +511,25 @@
         sent = payload(s, up_arrivals[-1], up_pieces, after=sent)
         up_arrivals.append(both_ways(*sent))
         last = sent[0]
-    down_mixes, down_conv = sort_arrivals(down_mix, down_pieces, down_arrivals)
+    sent = payload(blocks, up_arrivals[-1], up_pieces, after=(last, *down_arrivals[-1]))
+    up_arrivals.append(both_ways(*sent))
     up_mixes, up_conv = sort_arrivals(up_mix, up_pieces, up_arrivals)
-    up_g, up_back = back(up_mixes, weight, ahead, after=(last,))
+    up_g, up_back = back(up_mixes, weight, ahead, after=sent)
     up_back = exchange(up_back)
+    down_mixes = list_blocks(down_mix, down_arrivals)
+    down_g, down_back = back(down_mixes, weight, ahead, after=(up_g, *up_arrivals[-1]))
+    down_back = exchange(down_back)
+    sent = payload(blocks, down_arrivals[-1], down_pieces, after=(down_g,))
+    down_arrivals.append(both_ways(*sent))
+    _, down_conv = sort_arrivals(down_mix, down_pieces, down_arrivals)
+    up_grad = finish(up_xin, up_cot, up_conv, up_back, after=(down_g, *sent))
+    up_passed = lax.ppermute(up_grad, "section", up_pairs)
     taps = filter_gradient(
-        down_mixes, down_part, up_mixes, up_part, *filters.shape[1:], after=(up_g,)
-    )
-    down_g, down_back = back(
-        down_mixes, weight, ahead, after=(taps, *down_arrivals[-1], *up_arrivals[-1])
-    )
-    down_back = exchange(down_back)
-    up_grad = finish(up_xin, up_cot, up_conv, up_back, after=(down_g,))
-    up_passed = lax.ppermute(up_grad, "section", up_pairs)
-    weight_grad = weight_gradient(down_x, up_x, down_g, up_g, after=(up_grad,))
-    up_passed = settle(up_grad, up_passed)
-    down_grad = finish(
-        down_xin, down_cot, down_conv, down_back, after=(weight_grad, up_passed)
-    )
+        down_mixes, down_part, up_mixes, up_part, *filters.shape[1:], after=(up_grad,)
+    )
+    weight_grad = weight_gradient(down_x, up_x, down_g, up_g, after=(taps,))
+    up_passed = settle(up_grad, up_passed, after=(weight_grad, *down_arrivals[-1]))
+    down_grad = finish(down_xin, down_cot, down_conv, down_back, after=(up_passed,))
     down_passed = lax.ppermute(down_grad, "section", down_pairs)
     taps = sum_all(taps, after=(down_grad,))
     return weight_grad[None], taps, down_passed, up_passed

time: 323 us -> 323 us (level)
    ppermute x8, waiting for transfers between devices: 73.8 us -> 24.9 us  [both_ways(): lax.ppermute(right, 'tensor', onward)]
    ppermute x8, waiting for transfers between devices: 8.5 us -> 51.3 us  [both_ways(): lax.ppermute(left, 'tensor', [(j, i) for i, j in onward])]
    ppermute x1, waiting for transfers between devices: 0.01 us -> 14.6 us  [per_device(): up_cot = lax.ppermute(up_cot[0], 'section', mirror)]
    ppermute x8, starting transfers between devices: 30.1 us -> 21.2 us  [both_ways(): lax.ppermute(left, 'tensor', [(j, i) for i, j in onward])]
    ppermute x1, waiting for transfers between devices: 8.81 us -> 0.01 us  [per_device(): up_passed = lax.ppermute(up_grad, 'section', up_pairs)]
    ppermute x8, starting transfers between devices: 24.3 us -> 29.8 us  [both_ways(): lax.ppermute(right, 'tensor', onward)]
    all_to_all x4, starting transfers between devices: 19.1 us -> 22.4 us  [exchange(): return lax.all_to_all(x, 'tensor', split_axis=0, concat_axis=0, tiled=True)]
  transfers between devices with their start and end apart: 27 -> 27, of which waited for: 16 -> 15; matrix products, arithmetic and copies ran while one was open for 0% -> 0% of each run, Pallas kernels for 35% -> 34%
where the time goes in v9:
time: 323 us; the launch traced here: 319 us
  Pallas kernels  118 us (37%)
  waiting for transfers between devices  111 us (34%)
  starting transfers between devices  86.6 us (27%)
    pallas_call x20, Pallas kernels, call(): pl.pallas_call(body, in_specs=list(in_specs) + unread, out_shape=out_shap...  118 us
    ppermute x8, waiting for transfers between devices, both_ways(): lax.ppermute(left, 'tensor', [(j, i) for i, j in onward])  51.3 us
    ppermute x8, starting transfers between devices, both_ways(): lax.ppermute(right, 'tensor', onward)  29.8 us
    ppermute x8, waiting for transfers between devices, both_ways(): lax.ppermute(right, 'tensor', onward)  24.9 us
    all_to_all x4, starting transfers between devices, exchange(): return lax.all_to_all(x, 'tensor', split_axis=0, concat_axis=0, tiled=True)  22.4 us
    ppermute x8, starting transfers between devices, both_ways(): lax.ppermute(left, 'tensor', [(j, i) for i, j in onward])  21.2 us
    ppermute x1, waiting for transfers between devices, per_device(): up_cot = lax.ppermute(up_cot[0], 'section', mirror)  14.6 us
    ppermute x1, waiting for transfers between devices, per_device(): up_xin = lax.ppermute(up_input[0], 'section', mirror)  14.3 us
  transfers between devices with their start and end apart: 27, of which 15 were waited for; matrix products, arithmetic and copies ran while one was open for 0% of the time, Pallas kernels for 34%

profile of v9, /device:TPU:10, one launch (start us, length us, event | category | flops | bytes accessed | tf_op | source)
XLA Modules:
  0.0 319.2 jit_solution(15233388791888501845)
XLA Ops:
  3.6 5.3 %all-to-all-start = ((bf16[4,128,1024]{2,1,0:T(8,128)(2,1)}), bf16[4,128,1024]{2,1,0:T(8,128)(2,1)}, u32[]{:S(2)}, u32[]{:S(2)}) async-start(bf16[4,128,1024]{2,1,0:T(8,128)(2,1)} %get-tuple-element.34), calls=%async_computation | async-start | bytes 2097152 | tf_op jit(solution)/shard_map/all_to_all | solution.py:403
  13.5 3.9 %collective-permute-start.1 = (bf16[128,4096]{1,0:T(8,128)(2,1)}, bf16[128,4096]{1,0:T(8,128)(2,1)}, u32[]{:S(2)}, u32[]{:S(2)}) collective-permute-start(bf16[128,4096]{1,0:T(8,128)(2,1)} %get-tuple-element.36.refs_0_), channel_id=1, source_target_pairs={{0,1},{1,2},{2,3},{4,5},{5,6},{6,7},{8,9},{9,10},{10,11},{12,13},{... | collective-permute-start | bytes 3145736 | tf_op jit(solution)/shard_map/ppermute | solution.py:410
  17.4 3.8 %toeplitz.1 = (bf16[32,128,256]{2,1,0:T(8,128)(2,1)}, bf16[32,128,256]{2,1,0:T(8,128)(2,1)}) custom-call(f32[32,128]{1,0:T(8,128)} %bitcast.24), custom_call_target="tpu_custom_call" | custom-call | bytes 4210688 | tf_op jit(solution)/shard_map/toeplitz/pallas_call | solution.py:36
  21.2 14.3 %collective-permute-done.refs_0_ = bf16[128,4096]{1,0:T(8,128)(2,1)} collective-permute-done((bf16[128,4096]{1,0:T(8,128)(2,1)}, bf16[128,4096]{1,0:T(8,128)(2,1)}, u32[]{:S(2)}, u32[]{:S(2)}) %collective-permute-start) | collective-permute-done | bytes 1048608 | tf_op jit(solution)/shard_map/ppermute | solution.py:492
  37.9 5.1 %all-to-all-start.1 = ((bf16[4,128,1024]{2,1,0:T(8,128)(2,1)}), bf16[4,128,1024]{2,1,0:T(8,128)(2,1)}, u32[]{:S(2)}, u32[]{:S(2)}) async-start(bf16[4,128,1024]{2,1,0:T(8,128)(2,1)} %prepare.3.refs_3_), calls=%async_computation.1 | async-start | bytes 2097152 | tf_op jit(solution)/shard_map/all_to_all | solution.py:403
  42.9 14.6 %collective-permute-done.3.refs_1_ = bf16[128,4096]{1,0:T(8,128)(2,1)} collective-permute-done((bf16[128,4096]{1,0:T(8,128)(2,1)}, bf16[128,4096]{1,0:T(8,128)(2,1)}, u32[]{:S(2)}, u32[]{:S(2)}) %collective-permute-start.3) | collective-permute-done | bytes 1048608 | tf_op jit(solution)/shard_map/ppermute | solution.py:493
  57.5 6.4 %collective-permute-done.2.refs_3_.refs_1_.refs_4_ = bf16[128,4096]{1,0:T(8,128)(2,1)} collective-permute-done((bf16[128,4096]{1,0:T(8,128)(2,1)}, bf16[128,4096]{1,0:T(8,128)(2,1)}, u32[]{:S(2)}, u32[]{:S(2)}) %collective-permute-start.2) | collective-permute-done | bytes 1048608 | tf_op jit(solution)/shard_map/ppermute | solution.py:411
  71.3 4.4 %collective-permute-start.6 = (bf16[128,4096]{1,0:T(8,128)(2,1)}, bf16[128,4096]{1,0:T(8,128)(2,1)}, u32[]{:S(2)}, u32[]{:S(2)}) collective-permute-start(bf16[128,4096]{1,0:T(8,128)(2,1)} %grad_mix.1.refs_4_.refs_0_.refs_8_), channel_id=1, source_target_pairs={{0,1},{1,2},{2,3},{4,5},{5,6},{6,7},{8,9},{9,10},{10,11},{12,13},{... | collective-permute-start | bytes 3145736 | tf_op jit(solution)/shard_map/ppermute | solution.py:410
  75.7 10.9 %project.2 = (bf16[512,4096]{1,0:T(8,128)(2,1)}, bf16[128,4096]{1,0:T(8,128)(2,1)}, bf16[128,4096]{1,0:T(8,128)(2,1)}, bf16[128,4096]{1,0:T(8,128)(2,1)}, bf16[128,4096]{1,0:T(8,128)(2,1)}) custom-call(bf16[512,1024]{1,0:T(8,128)(2,1)} %bitcast.2.refs_0_, bf16[1024,4096]{1,0:T(8,128)(2,1)} %bitcast.25, bf16[32,128,256]{2,1,0:T(8,128)(2,1)} %get-tuple-element.37.refs_2_, ...), custom_call_target="tpu_custom_call" | custom-call | flops 5368709120 | bytes 19922944 | tf_op jit(solution)/shard_map/project/pallas_call | solution.py:36
  89.8 4.9 %collective-permute-start.4 = (bf16[128,4096]{1,0:T(8,128)(2,1)}, bf16[128,4096]{1,0:T(8,128)(2,1)}, u32[]{:S(2)}, u32[]{:S(2)}) collective-permute-start(bf16[128,4096]{1,0:T(8,128)(2,1)} %get-tuple-element.41.refs_3_.refs_4_), channel_id=1, source_target_pairs={{0,1},{1,2},{2,3},{4,5},{5,6},{6,7},{8,9},{9,10},{10,11},{12,13},{... | collective-permute-start | bytes 3145736 | tf_op jit(solution)/shard_map/ppermute | solution.py:410
  96.7 11.0 %project.3 = (bf16[512,4096]{1,0:T(8,128)(2,1)}, bf16[128,4096]{1,0:T(8,128)(2,1)}, bf16[128,4096]{1,0:T(8,128)(2,1)}, bf16[128,4096]{1,0:T(8,128)(2,1)}, bf16[128,4096]{1,0:T(8,128)(2,1)}) custom-call(bf16[512,1024]{1,0:T(8,128)(2,1)} %bitcast.5.refs_0_.refs_1_, bf16[1024,4096]{1,0:T(8,128)(2,1)} %bitcast.26, ...), custom_call_target="tpu_custom_call" | custom-call | flops 5368709120 | bytes 19922944 | tf_op jit(solution)/shard_map/project/pallas_call | solution.py:36
  112.9 3.9 %collective-permute-start.10 = (bf16[128,4096]{1,0:T(8,128)(2,1)}, bf16[128,4096]{1,0:T(8,128)(2,1)}, u32[]{:S(2)}, u32[]{:S(2)}) collective-permute-start(bf16[128,4096]{1,0:T(8,128)(2,1)} %get-tuple-element.46.refs_4_), channel_id=1, source_target_pairs={{0,1},{1,2},{2,3},{4,5},{5,6},{6,7},{8,9},{9,10},{10,11},{12,13},{... | collective-permute-start | bytes 3145736 | tf_op jit(solution)/shard_map/ppermute | solution.py:410
  116.8 6.0 %collective-permute-done.4.refs_0_.refs_2_ = bf16[128,4096]{1,0:T(8,128)(2,1)} collective-permute-done((bf16[128,4096]{1,0:T(8,128)(2,1)}, bf16[128,4096]{1,0:T(8,128)(2,1)}, u32[]{:S(2)}, u32[]{:S(2)}) %collective-permute-start.4) | collective-permute-done | bytes 1048608 | tf_op jit(solution)/shard_map/ppermute | solution.py:410
  124.3 3.5 %payload.8 = (bf16[128,4096]{1,0:T(8,128)(2,1)}, bf16[128,4096]{1,0:T(8,128)(2,1)}) custom-call(bf16[128,4096]{1,0:T(8,128)(2,1)} %collective-permute-done.4.refs_0_.refs_2_, bf16[128,4096]{1,0:T(8,128)(2,1)} %collective-permute-done.5.refs_1_.refs_5_, bf16[128,4096]{1,0:T(8,128)(2,1)} %get-tuple-element.43.refs_2_.refs_3_, ...), custom_call_target="tpu_custom_call" | custom-call | bytes 6291456 | tf_op jit(solution)/shard_map/payload/pallas_call | solution.py:36
  130.8 3.9 %collective-permute-start.9 = (bf16[128,4096]{1,0:T(8,128)(2,1)}, bf16[128,4096]{1,0:T(8,128)(2,1)}, u32[]{:S(2)}, u32[]{:S(2)}) collective-permute-start(bf16[128,4096]{1,0:T(8,128)(2,1)} %get-tuple-element.48.refs_5_), channel_id=1, source_target_pairs={{1,0},{2,1},{3,2},{5,4},{6,5},{7,6},{9,8},{10,9},{11,10},{13,12},{... | collective-permute-start | bytes 3145736 | tf_op jit(solution)/shard_map/ppermute | solution.py:411
  134.7 12.1 %collective-permute-done.11.refs_1_.refs_5_.refs_13_ = bf16[128,4096]{1,0:T(8,128)(2,1)} collective-permute-done((bf16[128,4096]{1,0:T(8,128)(2,1)}, bf16[128,4096]{1,0:T(8,128)(2,1)}, u32[]{:S(2)}, u32[]{:S(2)}) %collective-permute-start.11) | collective-permute-done | bytes 1048608 | tf_op jit(solution)/shard_map/ppermute | solution.py:411
  146.8 3.6 %payload.9 = (bf16[128,4096]{1,0:T(8,128)(2,1)}, bf16[128,4096]{1,0:T(8,128)(2,1)}) custom-call(bf16[128,4096]{1,0:T(8,128)(2,1)} %collective-permute-done.10.refs_0_.refs_2_.refs_10_, bf16[128,4096]{1,0:T(8,128)(2,1)} %collective-permute-done.11.refs_1_.refs_5_.refs_13_, bf16[128,4096]{1,0:T(8,128)(2,1)} %get-tuple-element.50.refs_2_.refs_3_, ...), custom_call_target="tpu_custom_call" | custom-call | bytes 6291456 | tf_op jit(solution)/shard_map/payload/pallas_call | solution.py:36
  152.3 3.9 %collective-permute-start.12 = (bf16[128,4096]{1,0:T(8,128)(2,1)}, bf16[128,4096]{1,0:T(8,128)(2,1)}, u32[]{:S(2)}, u32[]{:S(2)}) collective-permute-start(bf16[128,4096]{1,0:T(8,128)(2,1)} %get-tuple-element.51.refs_4_), channel_id=1, source_target_pairs={{0,1},{1,2},{2,3},{4,5},{5,6},{6,7},{8,9},{9,10},{10,11},{12,13},{... | collective-permute-start | bytes 3145736 | tf_op jit(solution)/shard_map/ppermute | solution.py:410
  156.2 11.6 %collective-permute-done.8.refs_5_.refs_3_.refs_0_ = bf16[128,4096]{1,0:T(8,128)(2,1)} collective-permute-done((bf16[128,4096]{1,0:T(8,128)(2,1)}, bf16[128,4096]{1,0:T(8,128)(2,1)}, u32[]{:S(2)}, u32[]{:S(2)}) %collective-permute-start.8) | collective-permute-done | bytes 1048608 | tf_op jit(solution)/shard_map/ppermute | solution.py:410
  169.3 21.4 %collective-permute-done.13.refs_1_.refs_6_.refs_14_ = bf16[128,4096]{1,0:T(8,128)(2,1)} collective-permute-done((bf16[128,4096]{1,0:T(8,128)(2,1)}, bf16[128,4096]{1,0:T(8,128)(2,1)}, u32[]{:S(2)}, u32[]{:S(2)}) %collective-permute-start.13) | collective-permute-done | bytes 1048608 | tf_op jit(solution)/shard_map/ppermute | solution.py:411
  196.6 4.4 %collective-permute-start.15 = (bf16[128,4096]{1,0:T(8,128)(2,1)}, bf16[128,4096]{1,0:T(8,128)(2,1)}, u32[]{:S(2)}, u32[]{:S(2)}) collective-permute-start(bf16[128,4096]{1,0:T(8,128)(2,1)} %get-tuple-element.54.refs_10_), channel_id=1, source_target_pairs={{1,0},{2,1},{3,2},{5,4},{6,5},{7,6},{9,8},{10,9},{11,10},{13,12},{... | collective-permute-start | bytes 3145736 | tf_op jit(solution)/shard_map/ppermute | solution.py:411
  201.0 12.4 %back.2 = (bf16[512,4096]{1,0:T(8,128)(2,1)}, bf16[512,1024]{1,0:T(8,128)(2,1)}) custom-call(bf16[128,4096]{1,0:T(8,128)(2,1)} %grad_mix.1.refs_4_.refs_0_.refs_8_, bf16[128,4096]{1,0:T(8,128)(2,1)} %collective-permute-done.6.refs_0_.refs_1_.refs_9_, bf16[128,4096]{1,0:T(8,128)(2,1)} %collective-permute-done.10.refs_0_.refs_2_.refs_10_, ...), custom_call_target="tpu_custom_call" | custom-call | flops 16106127360 | bytes 23068672 | tf_op jit(solution)/shard_map/back/pallas_call | solution.py:36
  213.4 4.4 %all-to-all-start.2 = ((bf16[4,128,1024]{2,1,0:T(8,128)(2,1)}), bf16[4,128,1024]{2,1,0:T(8,128)(2,1)}, u32[]{:S(2)}, u32[]{:S(2)}) async-start(bf16[4,128,1024]{2,1,0:T(8,128)(2,1)} %bitcast.18), calls=%async_computation.2 | async-start | bytes 2097152 | tf_op jit(solution)/shard_map/all_to_all | solution.py:403
  217.8 4.6 %collective-permute-done.14.refs_10_.refs_4_ = bf16[128,4096]{1,0:T(8,128)(2,1)} collective-permute-done((bf16[128,4096]{1,0:T(8,128)(2,1)}, bf16[128,4096]{1,0:T(8,128)(2,1)}, u32[]{:S(2)}, u32[]{:S(2)}) %collective-permute-start.14) | collective-permute-done | bytes 1048608 | tf_op jit(solution)/shard_map/ppermute | solution.py:410
  222.4 8.2 %collective-permute-done.15.refs_11_.refs_5_ = bf16[128,4096]{1,0:T(8,128)(2,1)} collective-permute-done((bf16[128,4096]{1,0:T(8,128)(2,1)}, bf16[128,4096]{1,0:T(8,128)(2,1)}, u32[]{:S(2)}, u32[]{:S(2)}) %collective-permute-start.15) | collective-permute-done | bytes 1048608 | tf_op jit(solution)/shard_map/ppermute | solution.py:411
  230.6 12.3 %back.3 = (bf16[512,4096]{1,0:T(8,128)(2,1)}, bf16[512,1024]{1,0:T(8,128)(2,1)}) custom-call(bf16[128,4096]{1,0:T(8,128)(2,1)} %get-tuple-element.36.refs_0_, bf16[128,4096]{1,0:T(8,128)(2,1)} %collective-permute-done.1.refs_2_.refs_0_.refs_1_, bf16[128,4096]{1,0:T(8,128)(2,1)} %collective-permute-done.4.refs_0_.refs_2_, ...), custom_call_target="tpu_custom_call" | custom-call | flops 16106127360 | bytes 23068672 | tf_op jit(solution)/shard_map/back/pallas_call | solution.py:36
  242.9 7.6 %all-to-all-start.3 = ((bf16[4,128,1024]{2,1,0:T(8,128)(2,1)}), bf16[4,128,1024]{2,1,0:T(8,128)(2,1)}, u32[]{:S(2)}, u32[]{:S(2)}) async-start(bf16[4,128,1024]{2,1,0:T(8,128)(2,1)} %bitcast.17), calls=%async_computation.3 | async-start | bytes 2097152 | tf_op jit(solution)/shard_map/all_to_all | solution.py:403
  260.7 4.6 %finish.2.refs_16_.refs_0_ = bf16[1,128,4096]{2,1,0:T(8,128)(2,1)} custom-call(bf16[128,4096]{1,0:T(8,128)(2,1)} %collective-permute-done.refs_0_, bf16[128,4096]{1,0:T(8,128)(2,1)} %collective-permute-done.3.refs_1_, bf16[4,128,1024]{2,1,0:T(8,128)(2,1)} %all-to-all-done.2.refs_2_, bf16[128,4096]{1,0:T(8,128)(2,1)} %get-tuple-element.59.refs_3_, ...), custom_call_target="tpu_custom_call" | custom-call | bytes 7340032 | tf_op jit(solution)/shard_map/finish/pallas_call | solution.py:36
  268.7 13.0 %filter_gradient.1 = f32[4,8,128]{2,1,0:T(8,128)} custom-call(bf16[128,4096]{1,0:T(8,128)(2,1)} %get-tuple-element.36.refs_0_, bf16[128,4096]{1,0:T(8,128)(2,1)} %collective-permute-done.1.refs_2_.refs_0_.refs_1_, bf16[128,4096]{1,0:T(8,128)(2,1)} %collective-permute-done.4.refs_0_.refs_2_, bf16[128,4096]{1,0:T(8,128)(2,1)} %collective-permute-done.8.refs_5_.refs_3_.refs_0_, ...), custom_call_target="tpu_custom_call" | custom-call | tf_op jit(solution)/shard_map/filter_gradient/pallas_call | solution.py:36
  281.7 13.6 %weight_gradient.1.refs_2_ = bf16[1024,4096]{1,0:T(8,128)(2,1)} custom-call(bf16[512,1024]{1,0:T(8,128)(2,1)} %bitcast.2.refs_0_, bf16[512,1024]{1,0:T(8,128)(2,1)} %bitcast.5.refs_0_.refs_1_, bf16[512,4096]{1,0:T(8,128)(2,1)} %get-tuple-element.56.refs_4_.refs_6_.refs_2_, bf16[512,4096]{1,0:T(8,128)(2,1)} %get-tuple-element.55.refs_9_.refs_3_, ...), custom_call_target="tpu_custom_call" | custom-call | tf_op jit(solution)/shard_map/weight_gradient/pallas_call | solution.py:36
  297.8 4.6 %finish.3.refs_4_ = bf16[1,128,4096]{2,1,0:T(8,128)(2,1)} custom-call(bf16[128,4096]{1,0:T(8,128)(2,1)} %bitcast.14, bf16[128,4096]{1,0:T(8,128)(2,1)} %bitcast.16, bf16[4,128,1024]{2,1,0:T(8,128)(2,1)} %all-to-all-done.3.refs_2_, bf16[128,4096]{1,0:T(8,128)(2,1)} %get-tuple-element.63.refs_3_, bf16[128,4096]{1,0:T(8,128)(2,1)} %collective-permute-done.19.refs_3_.refs_4_, ...), custom_call_target="tpu_custom_call" | custom-call | bytes 7340032 | tf_op jit(solution)/shard_map/finish/pallas_call | solution.py:36
  312.9 4.0 %collective-permute-done.22 = bf16[1,128,4096]{2,1,0:T(8,128)(2,1)} collective-permute-done((bf16[1,128,4096]{2,1,0:T(8,128)(2,1)}, bf16[1,128,4096]{2,1,0:T(8,128)(2,1)}, u32[]{:S(2)}, u32[]{:S(2)}) %collective-permute-start.22) | collective-permute-done | bytes 1048608 | tf_op jit(solution)/shard_map/ppermute | solution.py:533
  (51 shorter events, 70.1 us)
Async XLA Ops:
  3.6 34.2 %all-to-all-start = ((bf16[4,128,1024]{2,1,0:T(8,128)(2,1)}), bf16[4,128,1024]{2,1,0:T(8,128)(2,1)}, u32[]{:S(2)}, u32[]{:S(2)}) async-start(bf16[4,128,1024]{2,1,0:T(8,128)(2,1)} %get-tuple-element.34), calls=%async_computation | async-start | bytes 2097152 | tf_op jit(solution)/shard_map/all_to_all | solution.py:403
  8.9 26.6 %collective-permute-start = (bf16[128,4096]{1,0:T(8,128)(2,1)}, bf16[128,4096]{1,0:T(8,128)(2,1)}, u32[]{:S(2)}, u32[]{:S(2)}) collective-permute-start(bf16[128,4096]{1,0:T(8,128)(2,1)} %bitcast.29), channel_id=1, source_target_pairs={{0,28},{4,24},{8,20},{12,16},{16,12},{20,8},{24,4},{28,0},{1,29},{... | collective-permute-start | bytes 3145736 | tf_op jit(solution)/shard_map/ppermute | solution.py:492
  9.3 48.2 %collective-permute-start.3 = (bf16[128,4096]{1,0:T(8,128)(2,1)}, bf16[128,4096]{1,0:T(8,128)(2,1)}, u32[]{:S(2)}, u32[]{:S(2)}) collective-permute-start(bf16[128,4096]{1,0:T(8,128)(2,1)} %bitcast.30), channel_id=1, source_target_pairs={{0,28},{4,24},{8,20},{12,16},{16,12},{20,8},{24,4},{28,0},{1,29},{... | collective-permute-start | bytes 3145736 | tf_op jit(solution)/shard_map/ppermute | solution.py:493
  11.6 52.3 %collective-permute-start.2 = (bf16[128,4096]{1,0:T(8,128)(2,1)}, bf16[128,4096]{1,0:T(8,128)(2,1)}, u32[]{:S(2)}, u32[]{:S(2)}) collective-permute-start(bf16[128,4096]{1,0:T(8,128)(2,1)} %get-tuple-element.36.refs_0_), channel_id=1, source_target_pairs={{1,0},{2,1},{3,2},{5,4},{6,5},{7,6},{9,8},{10,9},{11,10},{13,12},{... | collective-permute-start | bytes 3145736 | tf_op jit(solution)/shard_map/ppermute | solution.py:411
  13.5 53.1 %collective-permute-start.1 = (bf16[128,4096]{1,0:T(8,128)(2,1)}, bf16[128,4096]{1,0:T(8,128)(2,1)}, u32[]{:S(2)}, u32[]{:S(2)}) collective-permute-start(bf16[128,4096]{1,0:T(8,128)(2,1)} %get-tuple-element.36.refs_0_), channel_id=1, source_target_pairs={{0,1},{1,2},{2,3},{4,5},{5,6},{6,7},{8,9},{9,10},{10,11},{12,13},{... | collective-permute-start | bytes 3145736 | tf_op jit(solution)/shard_map/ppermute | solution.py:410
  37.9 58.9 %all-to-all-start.1 = ((bf16[4,128,1024]{2,1,0:T(8,128)(2,1)}), bf16[4,128,1024]{2,1,0:T(8,128)(2,1)}, u32[]{:S(2)}, u32[]{:S(2)}) async-start(bf16[4,128,1024]{2,1,0:T(8,128)(2,1)} %prepare.3.refs_3_), calls=%async_computation.1 | async-start | bytes 2097152 | tf_op jit(solution)/shard_map/all_to_all | solution.py:403
  69.4 38.3 %collective-permute-start.7 = (bf16[128,4096]{1,0:T(8,128)(2,1)}, bf16[128,4096]{1,0:T(8,128)(2,1)}, u32[]{:S(2)}, u32[]{:S(2)}) collective-permute-start(bf16[128,4096]{1,0:T(8,128)(2,1)} %grad_mix.1.refs_4_.refs_0_.refs_8_), channel_id=1, source_target_pairs={{1,0},{2,1},{3,2},{5,4},{6,5},{7,6},{9,8},{10,9},{11,10},{13,12},{... | collective-permute-start | bytes 3145736 | tf_op jit(solution)/shard_map/ppermute | solution.py:411
  71.3 36.4 %collective-permute-start.6 = (bf16[128,4096]{1,0:T(8,128)(2,1)}, bf16[128,4096]{1,0:T(8,128)(2,1)}, u32[]{:S(2)}, u32[]{:S(2)}) collective-permute-start(bf16[128,4096]{1,0:T(8,128)(2,1)} %grad_mix.1.refs_4_.refs_0_.refs_8_), channel_id=1, source_target_pairs={{0,1},{1,2},{2,3},{4,5},{5,6},{6,7},{8,9},{9,10},{10,11},{12,13},{... | collective-permute-start | bytes 3145736 | tf_op jit(solution)/shard_map/ppermute | solution.py:410
  89.8 33.0 %collective-permute-start.4 = (bf16[128,4096]{1,0:T(8,128)(2,1)}, bf16[128,4096]{1,0:T(8,128)(2,1)}, u32[]{:S(2)}, u32[]{:S(2)}) collective-permute-start(bf16[128,4096]{1,0:T(8,128)(2,1)} %get-tuple-element.41.refs_3_.refs_4_), channel_id=1, source_target_pairs={{0,1},{1,2},{2,3},{4,5},{5,6},{6,7},{8,9},{9,10},{10,11},{12,13},{... | collective-permute-start | bytes 3145736 | tf_op jit(solution)/shard_map/ppermute | solution.py:410
  94.8 29.6 %collective-permute-start.5 = (bf16[128,4096]{1,0:T(8,128)(2,1)}, bf16[128,4096]{1,0:T(8,128)(2,1)}, u32[]{:S(2)}, u32[]{:S(2)}) collective-permute-start(bf16[128,4096]{1,0:T(8,128)(2,1)} %get-tuple-element.42.refs_4_.refs_5_), channel_id=1, source_target_pairs={{1,0},{2,1},{3,2},{5,4},{6,5},{7,6},{9,8},{10,9},{11,10},{13,12},{... | collective-permute-start | bytes 3145736 | tf_op jit(solution)/shard_map/ppermute | solution.py:411
  111.0 35.8 %collective-permute-start.11 = (bf16[128,4096]{1,0:T(8,128)(2,1)}, bf16[128,4096]{1,0:T(8,128)(2,1)}, u32[]{:S(2)}, u32[]{:S(2)}) collective-permute-start(bf16[128,4096]{1,0:T(8,128)(2,1)} %get-tuple-element.49), channel_id=1, source_target_pairs={{1,0},{2,1},{3,2},{5,4},{6,5},{7,6},{9,8},{10,9},{11,10},{13,12},{... | collective-permute-start | bytes 3145736 | tf_op jit(solution)/shard_map/ppermute | solution.py:411
  112.9 33.9 %collective-permute-start.10 = (bf16[128,4096]{1,0:T(8,128)(2,1)}, bf16[128,4096]{1,0:T(8,128)(2,1)}, u32[]{:S(2)}, u32[]{:S(2)}) collective-permute-start(bf16[128,4096]{1,0:T(8,128)(2,1)} %get-tuple-element.46.refs_4_), channel_id=1, source_target_pairs={{0,1},{1,2},{2,3},{4,5},{5,6},{6,7},{8,9},{9,10},{10,11},{12,13},{... | collective-permute-start | bytes 3145736 | tf_op jit(solution)/shard_map/ppermute | solution.py:410
  127.9 39.9 %collective-permute-start.8 = (bf16[128,4096]{1,0:T(8,128)(2,1)}, bf16[128,4096]{1,0:T(8,128)(2,1)}, u32[]{:S(2)}, u32[]{:S(2)}) collective-permute-start(bf16[128,4096]{1,0:T(8,128)(2,1)} %get-tuple-element.47.refs_4_), channel_id=1, source_target_pairs={{0,1},{1,2},{2,3},{4,5},{5,6},{6,7},{8,9},{9,10},{10,11},{12,13},{... | collective-permute-start | bytes 3145736 | tf_op jit(solution)/shard_map/ppermute | solution.py:410
  130.8 38.5 %collective-permute-start.9 = (bf16[128,4096]{1,0:T(8,128)(2,1)}, bf16[128,4096]{1,0:T(8,128)(2,1)}, u32[]{:S(2)}, u32[]{:S(2)}) collective-permute-start(bf16[128,4096]{1,0:T(8,128)(2,1)} %get-tuple-element.48.refs_5_), channel_id=1, source_target_pairs={{1,0},{2,1},{3,2},{5,4},{6,5},{7,6},{9,8},{10,9},{11,10},{13,12},{... | collective-permute-start | bytes 3145736 | tf_op jit(solution)/shard_map/ppermute | solution.py:411
  150.4 40.3 %collective-permute-start.13 = (bf16[128,4096]{1,0:T(8,128)(2,1)}, bf16[128,4096]{1,0:T(8,128)(2,1)}, u32[]{:S(2)}, u32[]{:S(2)}) collective-permute-start(bf16[128,4096]{1,0:T(8,128)(2,1)} %get-tuple-element.52), channel_id=1, source_target_pairs={{1,0},{2,1},{3,2},{5,4},{6,5},{7,6},{9,8},{10,9},{11,10},{13,12},{... | collective-permute-start | bytes 3145736 | tf_op jit(solution)/shard_map/ppermute | solution.py:411
  152.3 38.4 %collective-permute-start.12 = (bf16[128,4096]{1,0:T(8,128)(2,1)}, bf16[128,4096]{1,0:T(8,128)(2,1)}, u32[]{:S(2)}, u32[]{:S(2)}) collective-permute-start(bf16[128,4096]{1,0:T(8,128)(2,1)} %get-tuple-element.51.refs_4_), channel_id=1, source_target_pairs={{0,1},{1,2},{2,3},{4,5},{5,6},{6,7},{8,9},{9,10},{10,11},{12,13},{... | collective-permute-start | bytes 3145736 | tf_op jit(solution)/shard_map/ppermute | solution.py:410
  194.1 28.3 %collective-permute-start.14 = (bf16[128,4096]{1,0:T(8,128)(2,1)}, bf16[128,4096]{1,0:T(8,128)(2,1)}, u32[]{:S(2)}, u32[]{:S(2)}) collective-permute-start(bf16[128,4096]{1,0:T(8,128)(2,1)} %get-tuple-element.53.refs_9_), channel_id=1, source_target_pairs={{0,1},{1,2},{2,3},{4,5},{5,6},{6,7},{8,9},{9,10},{10,11},{12,13},{... | collective-permute-start | bytes 3145736 | tf_op jit(solution)/shard_map/ppermute | solution.py:410
  196.6 34.0 %collective-permute-start.15 = (bf16[128,4096]{1,0:T(8,128)(2,1)}, bf16[128,4096]{1,0:T(8,128)(2,1)}, u32[]{:S(2)}, u32[]{:S(2)}) collective-permute-start(bf16[128,4096]{1,0:T(8,128)(2,1)} %get-tuple-element.54.refs_10_), channel_id=1, source_target_pairs={{1,0},{2,1},{3,2},{5,4},{6,5},{7,6},{9,8},{10,9},{11,10},{13,12},{... | collective-permute-start | bytes 3145736 | tf_op jit(solution)/shard_map/ppermute | solution.py:411
  213.4 29.6 %all-to-all-start.2 = ((bf16[4,128,1024]{2,1,0:T(8,128)(2,1)}), bf16[4,128,1024]{2,1,0:T(8,128)(2,1)}, u32[]{:S(2)}, u32[]{:S(2)}) async-start(bf16[4,128,1024]{2,1,0:T(8,128)(2,1)} %bitcast.18), calls=%async_computation.2 | async-start | bytes 2097152 | tf_op jit(solution)/shard_map/all_to_all | solution.py:403
  242.9 54.8 %all-to-all-start.3 = ((bf16[4,128,1024]{2,1,0:T(8,128)(2,1)}), bf16[4,128,1024]{2,1,0:T(8,128)(2,1)}, u32[]{:S(2)}, u32[]{:S(2)}) async-start(bf16[4,128,1024]{2,1,0:T(8,128)(2,1)} %bitcast.17), calls=%async_computation.3 | async-start | bytes 2097152 | tf_op jit(solution)/shard_map/all_to_all | solution.py:403
  253.9 41.4 %collective-permute-start.19 = (bf16[128,4096]{1,0:T(8,128)(2,1)}, bf16[128,4096]{1,0:T(8,128)(2,1)}, u32[]{:S(2)}, u32[]{:S(2)}) collective-permute-start(bf16[128,4096]{1,0:T(8,128)(2,1)} %get-tuple-element.60.refs_7_), channel_id=1, source_target_pairs={{0,1},{1,2},{2,3},{4,5},{5,6},{6,7},{8,9},{9,10},{10,11},{12,13},{... | collective-permute-start | bytes 3145736 | tf_op jit(solution)/shard_map/ppermute | solution.py:410
  257.3 38.2 %collective-permute-start.20 = (bf16[128,4096]{1,0:T(8,128)(2,1)}, bf16[128,4096]{1,0:T(8,128)(2,1)}, u32[]{:S(2)}, u32[]{:S(2)}) collective-permute-start(bf16[128,4096]{1,0:T(8,128)(2,1)} %get-tuple-element.61.refs_8_), channel_id=1, source_target_pairs={{1,0},{2,1},{3,2},{5,4},{6,5},{7,6},{9,8},{10,9},{11,10},{13,12},{... | collective-permute-start | bytes 3145736 | tf_op jit(solution)/shard_map/ppermute | solution.py:411
  265.3 30.2 %collective-permute-start.21 = (bf16[1,128,4096]{2,1,0:T(8,128)(2,1)}, bf16[1,128,4096]{2,1,0:T(8,128)(2,1)}, u32[]{:S(2)}, u32[]{:S(2)}) collective-permute-start(bf16[1,128,4096]{2,1,0:T(8,128)(2,1)} %finish.2.refs_16_.refs_0_), channel_id=1, source_target_pairs={{28,4},{24,8},{20,12},{12,20},{8,24},{4,28},{29,5},{25,9},{21,13},... | collective-permute-start | bytes 3145736 | tf_op jit(solution)/shard_map/ppermute | solution.py:526
  297.8 6.5 %copy-start = (f32[4,8,128]{2,1,0:T(8,128)S(1)}, f32[4,8,128]{2,1,0:T(8,128)}, u32[]{:S(2)}) copy-start(f32[4,8,128]{2,1,0:T(8,128)} %filter_gradient.1) | copy-start | bytes 49156
  302.3 14.5 %collective-permute-start.22 = (bf16[1,128,4096]{2,1,0:T(8,128)(2,1)}, bf16[1,128,4096]{2,1,0:T(8,128)(2,1)}, u32[]{:S(2)}, u32[]{:S(2)}) collective-permute-start(bf16[1,128,4096]{2,1,0:T(8,128)(2,1)} %finish.3.refs_4_), channel_id=1, source_target_pairs={{4,0},{8,4},{12,8},{16,12},{20,16},{24,20},{28,24},{5,1},{9,5},{13... | collective-permute-start | bytes 3145736 | tf_op jit(solution)/shard_map/ppermute | solution.py:533
  304.3 5.2 %collective-permute-start.18 = (f32[1,32,128]{2,1,0:T(8,128)S(1)}, f32[1,32,128]{2,1,0:T(8,128)S(1)}, u32[]{:S(2)}, u32[]{:S(2)}) collective-permute-start(f32[1,32,128]{2,1,0:T(8,128)S(1)} %bitcast.21), channel_id=1, source_target_pairs={{0,3},{1,0},{2,1},{3,2},{4,7},{5,4},{6,5},{7,6},{8,11},{9,8},{10,9... | collective-permute-start | bytes 49160 | tf_op jit(solution)/shard_map/ppermute | solution.py:470
  304.3 5.1 %collective-permute-start.17 = (f32[1,32,128]{2,1,0:T(8,128)S(1)}, f32[1,32,128]{2,1,0:T(8,128)S(1)}, u32[]{:S(2)}, u32[]{:S(2)}) collective-permute-start(f32[1,32,128]{2,1,0:T(8,128)S(1)} %bitcast.22), channel_id=1, source_target_pairs={{0,2},{1,3},{2,0},{3,1},{4,6},{5,7},{6,4},{7,5},{8,10},{9,11},{10,... | collective-permute-start | bytes 49160 | tf_op jit(solution)/shard_map/ppermute | solution.py:470
  306.6 4.3 %collective-permute-start.16 = (f32[1,32,128]{2,1,0:T(8,128)S(1)}, f32[1,32,128]{2,1,0:T(8,128)S(1)}, u32[]{:S(2)}, u32[]{:S(2)}) collective-permute-start(f32[1,32,128]{2,1,0:T(8,128)S(1)} %bitcast.23), channel_id=1, source_target_pairs={{0,1},{1,2},{2,3},{3,0},{4,5},{5,6},{6,7},{7,4},{8,9},{9,10},{10,1... | collective-permute-start | bytes 49160 | tf_op jit(solution)/shard_map/ppermute | solution.py:470
  309.5 1.4 copy-start.1
  309.5 1.4 copy-start.2
  310.9 0.6 copy-start.3

commit v10 on v8

--- a/solution.py
+++ b/solution.py
@@ -341,58 +341,72 @@
     )
 
 
-def settle_kernel(own_ref, came_ref, out_ref):
+def settle_kernel(*refs):
+    *in_refs, out_ref = refs
     stays = 2 * lax.axis_index("section") == lax.axis_size("section")
-
-    @pl.when(stays)
-    def _():
-        out_ref[...] = own_ref[...]
-
-    @pl.when(jnp.logical_not(stays))
-    def _():
-        out_ref[...] = came_ref[...]
-
-
-def settle(own, came):
-    step = came.shape[1] // 2
-    spec = pl.BlockSpec((1, step, came.shape[2]), lambda i: (0, i, 0))
+    rows = in_refs[0].shape[1]
+    for i in range(2):
+        for ref, taken in ((in_refs[i], stays), (in_refs[2 + i], jnp.logical_not(stays))):
+
+            @pl.when(taken)
+            def _():
+                out_ref[:, i * rows : (i + 1) * rows] = ref[...]
+
+
+def settle(own, came, after=()):
+    _, rows, width = own[0].shape
+    spec = pl.BlockSpec((1, rows, width // 2), lambda i: (0, 0, i))
     return call(
         settle_kernel,
-        (own, came),
-        (),
+        (*own, *came),
+        after,
         grid=(2,),
-        in_specs=[spec, spec],
-        out_specs=spec,
-        out_shape=shape(came.shape, came.dtype),
+        in_specs=[spec] * 4,
+        out_specs=pl.BlockSpec((1, 2 * rows, width // 2), lambda i: (0, 0, i)),
+        out_shape=shape((1, 2 * rows, width), bf16),
         name="settle",
     )
 
 
-def finish_kernel(xin_ref, cot_ref, back_ref, *rest):
-    *mixed_refs, out_ref = rest
+def finish_kernel(inputs, xin_ref, cot_ref, back_ref, *rest):
+    mixed_refs, out_refs = rest[: inputs - 3], rest[inputs - 3 :]
     normed, inverse = normalise(xin_ref[...].astype(f32))
     cot = cot_ref[...].astype(f32)
     returned = jnp.concatenate([back_ref[i] for i in range(back_ref.shape[0])], axis=1)
     mixed = sum(ref[...].astype(f32) for ref in mixed_refs)
     total = cot * mixed + returned.astype(f32)
     mean = jnp.mean(total * normed, axis=1, keepdims=True)
-    out_ref[0] = (cot + inverse * (total - normed * mean)).astype(bf16)
-
-
-def finish(xin, cot, mixed, returned, after=()):
+    out = (cot + inverse * (total - normed * mean)).astype(bf16)
+    if len(out_refs) == 1:
+        out_refs[0][0] = out
+    else:
+        for i, out_ref in enumerate(out_refs):
+
+            @pl.when(pl.program_id(0) == i)
+            def _():
+                out_ref[0] = out
+
+
+def finish(xin, cot, mixed, returned, halves, after=()):
     rows, width = xin.shape
     blocks, _, depth = returned.shape
-    step = 64
+    step = rows // 2
     spec = pl.BlockSpec((step, width), lambda i: (i, 0))
-    return call(
-        finish_kernel,
+    if halves:
+        out_specs = [pl.BlockSpec((1, step, width), lambda i: (0, 0, 0))] * 2
+        out_shape = [shape((1, step, width), bf16)] * 2
+    else:
+        out_specs = pl.BlockSpec((1, step, width), lambda i: (0, i, 0))
+        out_shape = shape((1, rows, width), bf16)
+    return call(
+        functools.partial(finish_kernel, 3 + len(mixed)),
         (xin, cot, returned, *mixed),
         after,
-        grid=(rows // step,),
+        grid=(2,),
         in_specs=[spec, spec, pl.BlockSpec((blocks, step, depth), lambda i: (0, i, 0))]
         + [spec] * len(mixed),
-        out_specs=pl.BlockSpec((1, step, width), lambda i: (0, i, 0)),
-        out_shape=shape((1, rows, width), bf16),
+        out_specs=out_specs,
+        out_shape=out_shape,
         name="finish",
     )
 
@@ -514,18 +528,18 @@
         down_mixes, down_part, up_mixes, up_part, *filters.shape[1:], after=(up_g,)
     )
     down_g, down_back = back(
-        down_mixes, weight, ahead, after=(taps, *down_arrivals[-1], *up_arrivals[-1])
+        down_mixes, weight, ahead, after=(taps, *down_arrivals[-1])
     )
     down_back = exchange(down_back)
-    up_grad = finish(up_xin, up_cot, up_conv, up_back, after=(down_g,))
-    up_passed = lax.ppermute(up_grad, "section", up_pairs)
-    weight_grad = weight_gradient(down_x, up_x, down_g, up_g, after=(up_grad,))
-    up_passed = settle(up_grad, up_passed)
+    up_grad = finish(up_xin, up_cot, up_conv, up_back, True, after=(down_g,))
+    up_came = [lax.ppermute(half, "section", up_pairs) for half in up_grad]
+    weight_grad = weight_gradient(down_x, up_x, down_g, up_g, after=(up_grad[0],))
     down_grad = finish(
-        down_xin, down_cot, down_conv, down_back, after=(weight_grad, up_passed)
+        down_xin, down_cot, down_conv, down_back, False, after=(weight_grad, up_came[0])
     )
     down_passed = lax.ppermute(down_grad, "section", down_pairs)
     taps = sum_all(taps, after=(down_grad,))
+    up_passed = settle(up_grad, up_came, after=(taps,))
     return weight_grad[None], taps, down_passed, up_passed
 
 

time: 323 us -> 330 us (1.022)
  waiting for transfers between devices: 111 us -> 118 us
    ppermute x1 -> x2, waiting for transfers between devices: 8.81 us -> 14.1 us  [per_device(): up_came = [lax.ppermute(half, 'section', up_pairs) for half in up_grad]]
    ppermute x8, waiting for transfers between devices: 73.8 us -> 78 us  [both_ways(): lax.ppermute(right, 'tensor', onward)]
    ppermute x1, waiting for transfers between devices: 3.86 us -> 0.01 us  [per_device(): down_passed = lax.ppermute(down_grad, 'section', down_pairs)]
  transfers between devices with their start and end apart: 27 -> 28, of which waited for: 16 -> 16; matrix products, arithmetic and copies ran while one was open for 0% -> 0% of each run, Pallas kernels for 35% -> 34%
where the time goes in v10:
time: 330 us; the launch traced here: 329 us
  Pallas kernels  118 us (36%)
  waiting for transfers between devices  118 us (36%)
  starting transfers between devices  86.9 us (26%)
  local copies, waits for them, and re-layouts  4.55 us (1%)
    pallas_call x20, Pallas kernels, call(): pl.pallas_call(body, in_specs=list(in_specs) + unread, out_shape=out_shap...  118 us
    ppermute x8, waiting for transfers between devices, both_ways(): lax.ppermute(right, 'tensor', onward)  78 us
    ppermute x8, starting transfers between devices, both_ways(): lax.ppermute(left, 'tensor', [(j, i) for i, j in onward])  29.5 us
    ppermute x8, starting transfers between devices, both_ways(): lax.ppermute(right, 'tensor', onward)  25 us
    all_to_all x4, starting transfers between devices, exchange(): return lax.all_to_all(x, 'tensor', split_axis=0, concat_axis=0, tiled=True)  20.4 us
    ppermute x2, waiting for transfers between devices, per_device(): up_came = [lax.ppermute(half, 'section', up_pairs) for half in up_grad]  14.1 us
    ppermute x1, waiting for transfers between devices, per_device(): up_xin = lax.ppermute(up_input[0], 'section', mirror)  13.8 us
    ppermute x8, waiting for transfers between devices, both_ways(): lax.ppermute(left, 'tensor', [(j, i) for i, j in onward])  9.09 us
  transfers between devices with their start and end apart: 28, of which 16 were waited for; matrix products, arithmetic and copies ran while one was open for 0% of the time, Pallas kernels for 34%

profile of v10, /device:TPU:10, one launch (start us, length us, event | category | flops | bytes accessed | tf_op | source)
XLA Modules:
  0.0 329.1 jit_solution(12289021149746471961)
XLA Ops:
  3.6 5.3 %all-to-all-start = ((bf16[4,128,1024]{2,1,0:T(8,128)(2,1)}), bf16[4,128,1024]{2,1,0:T(8,128)(2,1)}, u32[]{:S(2)}, u32[]{:S(2)}) async-start(bf16[4,128,1024]{2,1,0:T(8,128)(2,1)} %get-tuple-element.36), calls=%async_computation | async-start | bytes 2097152 | tf_op jit(solution)/shard_map/all_to_all | solution.py:417
  12.7 3.4 %collective-permute-start.2 = (bf16[128,4096]{1,0:T(8,128)(2,1)}, bf16[128,4096]{1,0:T(8,128)(2,1)}, u32[]{:S(2)}, u32[]{:S(2)}) collective-permute-start(bf16[128,4096]{1,0:T(8,128)(2,1)} %get-tuple-element.38.refs_0_), channel_id=1, source_target_pairs={{1,0},{2,1},{3,2},{5,4},{6,5},{7,6},{9,8},{10,9},{11,10},{13,12},{... | collective-permute-start | bytes 3145736 | tf_op jit(solution)/shard_map/ppermute | solution.py:425
  17.9 3.8 %toeplitz.1 = (bf16[32,128,256]{2,1,0:T(8,128)(2,1)}, bf16[32,128,256]{2,1,0:T(8,128)(2,1)}) custom-call(f32[32,128]{1,0:T(8,128)} %bitcast.24), custom_call_target="tpu_custom_call" | custom-call | bytes 4210688 | tf_op jit(solution)/shard_map/toeplitz/pallas_call | solution.py:36
  21.8 13.8 %collective-permute-done.refs_0_ = bf16[128,4096]{1,0:T(8,128)(2,1)} collective-permute-done((bf16[128,4096]{1,0:T(8,128)(2,1)}, bf16[128,4096]{1,0:T(8,128)(2,1)}, u32[]{:S(2)}, u32[]{:S(2)}) %collective-permute-start) | collective-permute-done | bytes 1048608 | tf_op jit(solution)/shard_map/ppermute | solution.py:501
  37.9 5.1 %all-to-all-start.1 = ((bf16[4,128,1024]{2,1,0:T(8,128)(2,1)}), bf16[4,128,1024]{2,1,0:T(8,128)(2,1)}, u32[]{:S(2)}, u32[]{:S(2)}) async-start(bf16[4,128,1024]{2,1,0:T(8,128)(2,1)} %prepare.3.refs_3_), calls=%async_computation.1 | async-start | bytes 2097152 | tf_op jit(solution)/shard_map/all_to_all | solution.py:417
  42.9 23.7 %collective-permute-done.1.refs_2_.refs_0_.refs_1_ = bf16[128,4096]{1,0:T(8,128)(2,1)} collective-permute-done((bf16[128,4096]{1,0:T(8,128)(2,1)}, bf16[128,4096]{1,0:T(8,128)(2,1)}, u32[]{:S(2)}, u32[]{:S(2)}) %collective-permute-start.1) | collective-permute-done | bytes 1048608 | tf_op jit(solution)/shard_map/ppermute | solution.py:424
  69.4 4.4 %collective-permute-start.6 = (bf16[128,4096]{1,0:T(8,128)(2,1)}, bf16[128,4096]{1,0:T(8,128)(2,1)}, u32[]{:S(2)}, u32[]{:S(2)}) collective-permute-start(bf16[128,4096]{1,0:T(8,128)(2,1)} %grad_mix.1.refs_4_.refs_0_.refs_8_), channel_id=1, source_target_pairs={{0,1},{1,2},{2,3},{4,5},{5,6},{6,7},{8,9},{9,10},{10,11},{12,13},{... | collective-permute-start | bytes 3145736 | tf_op jit(solution)/shard_map/ppermute | solution.py:424
  76.2 10.9 %project.2 = (bf16[512,4096]{1,0:T(8,128)(2,1)}, bf16[128,4096]{1,0:T(8,128)(2,1)}, bf16[128,4096]{1,0:T(8,128)(2,1)}, bf16[128,4096]{1,0:T(8,128)(2,1)}, bf16[128,4096]{1,0:T(8,128)(2,1)}) custom-call(bf16[512,1024]{1,0:T(8,128)(2,1)} %bitcast.2.refs_0_, bf16[1024,4096]{1,0:T(8,128)(2,1)} %bitcast.25, bf16[32,128,256]{2,1,0:T(8,128)(2,1)} %get-tuple-element.39.refs_2_, ...), custom_call_target="tpu_custom_call" | custom-call | flops 5368709120 | bytes 19922944 | tf_op jit(solution)/shard_map/project/pallas_call | solution.py:36
  90.3 3.4 %collective-permute-start.4 = (bf16[128,4096]{1,0:T(8,128)(2,1)}, bf16[128,4096]{1,0:T(8,128)(2,1)}, u32[]{:S(2)}, u32[]{:S(2)}) collective-permute-start(bf16[128,4096]{1,0:T(8,128)(2,1)} %get-tuple-element.43.refs_3_.refs_4_), channel_id=1, source_target_pairs={{0,1},{1,2},{2,3},{4,5},{5,6},{6,7},{8,9},{9,10},{10,11},{12,13},{... | collective-permute-start | bytes 3145736 | tf_op jit(solution)/shard_map/ppermute | solution.py:424
  93.8 3.4 %collective-permute-start.5 = (bf16[128,4096]{1,0:T(8,128)(2,1)}, bf16[128,4096]{1,0:T(8,128)(2,1)}, u32[]{:S(2)}, u32[]{:S(2)}) collective-permute-start(bf16[128,4096]{1,0:T(8,128)(2,1)} %get-tuple-element.44.refs_4_.refs_5_), channel_id=1, source_target_pairs={{1,0},{2,1},{3,2},{5,4},{6,5},{7,6},{9,8},{10,9},{11,10},{13,12},{... | collective-permute-start | bytes 3145736 | tf_op jit(solution)/shard_map/ppermute | solution.py:425
  97.2 11.0 %project.3 = (bf16[512,4096]{1,0:T(8,128)(2,1)}, bf16[128,4096]{1,0:T(8,128)(2,1)}, bf16[128,4096]{1,0:T(8,128)(2,1)}, bf16[128,4096]{1,0:T(8,128)(2,1)}, bf16[128,4096]{1,0:T(8,128)(2,1)}) custom-call(bf16[512,1024]{1,0:T(8,128)(2,1)} %bitcast.5.refs_0_.refs_1_, bf16[1024,4096]{1,0:T(8,128)(2,1)} %bitcast.26, ...), custom_call_target="tpu_custom_call" | custom-call | flops 5368709120 | bytes 19922944 | tf_op jit(solution)/shard_map/project/pallas_call | solution.py:36
  113.9 4.3 %collective-permute-start.11 = (bf16[128,4096]{1,0:T(8,128)(2,1)}, bf16[128,4096]{1,0:T(8,128)(2,1)}, u32[]{:S(2)}, u32[]{:S(2)}) collective-permute-start(bf16[128,4096]{1,0:T(8,128)(2,1)} %get-tuple-element.51), channel_id=1, source_target_pairs={{1,0},{2,1},{3,2},{5,4},{6,5},{7,6},{9,8},{10,9},{11,10},{13,12},{... | collective-permute-start | bytes 3145736 | tf_op jit(solution)/shard_map/ppermute | solution.py:425
  118.3 4.6 %collective-permute-done.4.refs_0_.refs_2_ = bf16[128,4096]{1,0:T(8,128)(2,1)} collective-permute-done((bf16[128,4096]{1,0:T(8,128)(2,1)}, bf16[128,4096]{1,0:T(8,128)(2,1)}, u32[]{:S(2)}, u32[]{:S(2)}) %collective-permute-start.4) | collective-permute-done | bytes 1048608 | tf_op jit(solution)/shard_map/ppermute | solution.py:424
  130.6 4.1 %collective-permute-start.9 = (bf16[128,4096]{1,0:T(8,128)(2,1)}, bf16[128,4096]{1,0:T(8,128)(2,1)}, u32[]{:S(2)}, u32[]{:S(2)}) collective-permute-start(bf16[128,4096]{1,0:T(8,128)(2,1)} %get-tuple-element.50.refs_5_), channel_id=1, source_target_pairs={{1,0},{2,1},{3,2},{5,4},{6,5},{7,6},{9,8},{10,9},{11,10},{13,12},{... | collective-permute-start | bytes 3145736 | tf_op jit(solution)/shard_map/ppermute | solution.py:425
  134.7 10.6 %collective-permute-done.10.refs_0_.refs_2_.refs_10_ = bf16[128,4096]{1,0:T(8,128)(2,1)} collective-permute-done((bf16[128,4096]{1,0:T(8,128)(2,1)}, bf16[128,4096]{1,0:T(8,128)(2,1)}, u32[]{:S(2)}, u32[]{:S(2)}) %collective-permute-start.10) | collective-permute-done | bytes 1048608 | tf_op jit(solution)/shard_map/ppermute | solution.py:424
  147.0 3.6 %payload.9 = (bf16[128,4096]{1,0:T(8,128)(2,1)}, bf16[128,4096]{1,0:T(8,128)(2,1)}) custom-call(bf16[128,4096]{1,0:T(8,128)(2,1)} %collective-permute-done.10.refs_0_.refs_2_.refs_10_, bf16[128,4096]{1,0:T(8,128)(2,1)} %collective-permute-done.11.refs_1_.refs_5_.refs_13_, bf16[128,4096]{1,0:T(8,128)(2,1)} %get-tuple-element.52.refs_2_.refs_3_, ...), custom_call_target="tpu_custom_call" | custom-call | bytes 6291456 | tf_op jit(solution)/shard_map/payload/pallas_call | solution.py:36
  153.3 4.1 %collective-permute-start.13 = (bf16[128,4096]{1,0:T(8,128)(2,1)}, bf16[128,4096]{1,0:T(8,128)(2,1)}, u32[]{:S(2)}, u32[]{:S(2)}) collective-permute-start(bf16[128,4096]{1,0:T(8,128)(2,1)} %get-tuple-element.54), channel_id=1, source_target_pairs={{1,0},{2,1},{3,2},{5,4},{6,5},{7,6},{9,8},{10,9},{11,10},{13,12},{... | collective-permute-start | bytes 3145736 | tf_op jit(solution)/shard_map/ppermute | solution.py:425
  157.4 10.3 %collective-permute-done.8.refs_0_.refs_3_ = bf16[128,4096]{1,0:T(8,128)(2,1)} collective-permute-done((bf16[128,4096]{1,0:T(8,128)(2,1)}, bf16[128,4096]{1,0:T(8,128)(2,1)}, u32[]{:S(2)}, u32[]{:S(2)}) %collective-permute-start.8) | collective-permute-done | bytes 1048608 | tf_op jit(solution)/shard_map/ppermute | solution.py:424
  175.6 4.1 %collective-permute-start.15 = (bf16[128,4096]{1,0:T(8,128)(2,1)}, bf16[128,4096]{1,0:T(8,128)(2,1)}, u32[]{:S(2)}, u32[]{:S(2)}) collective-permute-start(bf16[128,4096]{1,0:T(8,128)(2,1)} %get-tuple-element.57.refs_5_), channel_id=1, source_target_pairs={{1,0},{2,1},{3,2},{5,4},{6,5},{7,6},{9,8},{10,9},{11,10},{13,12},{... | collective-permute-start | bytes 3145736 | tf_op jit(solution)/shard_map/ppermute | solution.py:425
  179.7 10.6 %collective-permute-done.12.refs_0_.refs_3_.refs_11_ = bf16[128,4096]{1,0:T(8,128)(2,1)} collective-permute-done((bf16[128,4096]{1,0:T(8,128)(2,1)}, bf16[128,4096]{1,0:T(8,128)(2,1)}, u32[]{:S(2)}, u32[]{:S(2)}) %collective-permute-start.12) | collective-permute-done | bytes 1048608 | tf_op jit(solution)/shard_map/ppermute | solution.py:424
  195.3 12.4 %back.2 = (bf16[512,4096]{1,0:T(8,128)(2,1)}, bf16[512,1024]{1,0:T(8,128)(2,1)}) custom-call(bf16[128,4096]{1,0:T(8,128)(2,1)} %grad_mix.1.refs_4_.refs_0_.refs_8_, bf16[128,4096]{1,0:T(8,128)(2,1)} %collective-permute-done.6.refs_0_.refs_1_.refs_9_, bf16[128,4096]{1,0:T(8,128)(2,1)} %collective-permute-done.10.refs_0_.refs_2_.refs_10_, ...), custom_call_target="tpu_custom_call" | custom-call | flops 16106127360 | bytes 23068672 | tf_op jit(solution)/shard_map/back/pallas_call | solution.py:36
  207.8 5.0 %all-to-all-start.2 = ((bf16[4,128,1024]{2,1,0:T(8,128)(2,1)}), bf16[4,128,1024]{2,1,0:T(8,128)(2,1)}, u32[]{:S(2)}, u32[]{:S(2)}) async-start(bf16[4,128,1024]{2,1,0:T(8,128)(2,1)} %bitcast.18), calls=%async_computation.2 | async-start | bytes 2097152 | tf_op jit(solution)/shard_map/all_to_all | solution.py:417
  216.2 3.6 %collective-permute-start.17 = (bf16[128,4096]{1,0:T(8,128)(2,1)}, bf16[128,4096]{1,0:T(8,128)(2,1)}, u32[]{:S(2)}, u32[]{:S(2)}) collective-permute-start(bf16[128,4096]{1,0:T(8,128)(2,1)} %get-tuple-element.63), channel_id=1, source_target_pairs={{1,0},{2,1},{3,2},{5,4},{6,5},{7,6},{9,8},{10,9},{11,10},{13,12},{... | collective-permute-start | bytes 3145736 | tf_op jit(solution)/shard_map/ppermute | solution.py:425
  219.8 13.0 %filter_gradient.1 = f32[4,8,128]{2,1,0:T(8,128)} custom-call(bf16[128,4096]{1,0:T(8,128)(2,1)} %get-tuple-element.38.refs_0_, bf16[128,4096]{1,0:T(8,128)(2,1)} %collective-permute-done.1.refs_2_.refs_0_.refs_1_, bf16[128,4096]{1,0:T(8,128)(2,1)} %collective-permute-done.4.refs_0_.refs_2_, bf16[128,4096]{1,0:T(8,128)(2,1)} %collective-permute-done.8.refs_0_.refs_3_, ...), custom_call_target="tpu_custom_call" | custom-call | tf_op jit(solution)/shard_map/filter_gradient/pallas_call | solution.py:36
  232.8 12.3 %back.3 = (bf16[512,4096]{1,0:T(8,128)(2,1)}, bf16[512,1024]{1,0:T(8,128)(2,1)}) custom-call(bf16[128,4096]{1,0:T(8,128)(2,1)} %get-tuple-element.38.refs_0_, bf16[128,4096]{1,0:T(8,128)(2,1)} %collective-permute-done.1.refs_2_.refs_0_.refs_1_, bf16[128,4096]{1,0:T(8,128)(2,1)} %collective-permute-done.4.refs_0_.refs_2_, ...), custom_call_target="tpu_custom_call" | custom-call | flops 16106127360 | bytes 23068672 | tf_op jit(solution)/shard_map/back/pallas_call | solution.py:36
  245.1 5.0 %all-to-all-start.3 = ((bf16[4,128,1024]{2,1,0:T(8,128)(2,1)}), bf16[4,128,1024]{2,1,0:T(8,128)(2,1)}, u32[]{:S(2)}, u32[]{:S(2)}) async-start(bf16[4,128,1024]{2,1,0:T(8,128)(2,1)} %bitcast.17), calls=%async_computation.3 | async-start | bytes 2097152 | tf_op jit(solution)/shard_map/all_to_all | solution.py:417
  250.1 18.2 %collective-permute-done.16.refs_4_ = bf16[128,4096]{1,0:T(8,128)(2,1)} collective-permute-done((bf16[128,4096]{1,0:T(8,128)(2,1)}, bf16[128,4096]{1,0:T(8,128)(2,1)}, u32[]{:S(2)}, u32[]{:S(2)}) %collective-permute-start.16) | collective-permute-done | bytes 1048608 | tf_op jit(solution)/shard_map/ppermute | solution.py:424
  270.6 4.7 %finish.2 = (bf16[1,64,4096]{2,1,0:T(8,128)(2,1)}, bf16[1,64,4096]{2,1,0:T(8,128)(2,1)}) custom-call(bf16[128,4096]{1,0:T(8,128)(2,1)} %collective-permute-done.refs_0_, bf16[128,4096]{1,0:T(8,128)(2,1)} %collective-permute-done.3.refs_1_, bf16[4,128,1024]{2,1,0:T(8,128)(2,1)} %all-to-all-done.2.refs_2_, bf16[128,4096]{1,0:T(8,128)(2,1)} %get-tuple-element.62.refs_3_, ...), custom_call_target="tpu_custom_call" | custom-call | bytes 7340032 | tf_op jit(solution)/shard_map/finish/pallas_call | solution.py:36
  275.3 3.4 %collective-permute-start.21 = (bf16[1,64,4096]{2,1,0:T(8,128)(2,1)}, bf16[1,64,4096]{2,1,0:T(8,128)(2,1)S(1)}, u32[]{:S(2)}, u32[]{:S(2)}) collective-permute-start(bf16[1,64,4096]{2,1,0:T(8,128)(2,1)} %get-tuple-element.64.refs_4_.refs_0_), channel_id=1, source_target_pairs={{28,4},{24,8},{20,12},{12,20},{8,24},{4,28},{29,5},{25,9},{21,13},... | collective-permute-start | bytes 1572872 | tf_op jit(solution)/shard_map/ppermute | solution.py:535
  278.7 13.6 %weight_gradient.1.refs_6_ = bf16[1024,4096]{1,0:T(8,128)(2,1)} custom-call(bf16[512,1024]{1,0:T(8,128)(2,1)} %bitcast.2.refs_0_, bf16[512,1024]{1,0:T(8,128)(2,1)} %bitcast.5.refs_0_.refs_1_, bf16[512,4096]{1,0:T(8,128)(2,1)} %get-tuple-element.60.refs_6_.refs_2_, bf16[512,4096]{1,0:T(8,128)(2,1)} %get-tuple-element.59.refs_16_.refs_3_, ...), custom_call_target="tpu_custom_call" | custom-call | flops 8589934592 | bytes 18874368 | tf_op jit(solution)/shard_map/weight_gradient/pallas_call | solution.py:36
  293.2 4.6 %finish.3.refs_4_ = bf16[1,128,4096]{2,1,0:T(8,128)(2,1)} custom-call(bf16[128,4096]{1,0:T(8,128)(2,1)} %bitcast.14, bf16[128,4096]{1,0:T(8,128)(2,1)} %bitcast.16, bf16[4,128,1024]{2,1,0:T(8,128)(2,1)} %all-to-all-done.3.refs_2_, bf16[128,4096]{1,0:T(8,128)(2,1)} %get-tuple-element.66.refs_3_, bf16[128,4096]{1,0:T(8,128)(2,1)} %collective-permute-done.14.refs_10_.refs_4_, ...), custom_call_target="tpu_custom_call" | custom-call | bytes 7340032 | tf_op jit(solution)/shard_map/finish/pallas_call | solution.py:36
  309.5 14.1 %collective-permute-done.23.refs_3_ = bf16[1,64,4096]{2,1,0:T(8,128)(2,1)S(1)} collective-permute-done((bf16[1,64,4096]{2,1,0:T(8,128)(2,1)}, bf16[1,64,4096]{2,1,0:T(8,128)(2,1)S(1)}, u32[]{:S(2)}, u32[]{:S(2)}) %collective-permute-start.23) | collective-permute-done | bytes 524320 | tf_op jit(solution)/shard_map/ppermute | solution.py:535
  (57 shorter events, 73.6 us)
Async XLA Ops:
  3.6 34.2 %all-to-all-start = ((bf16[4,128,1024]{2,1,0:T(8,128)(2,1)}), bf16[4,128,1024]{2,1,0:T(8,128)(2,1)}, u32[]{:S(2)}, u32[]{:S(2)}) async-start(bf16[4,128,1024]{2,1,0:T(8,128)(2,1)} %get-tuple-element.36), calls=%async_computation | async-start | bytes 2097152 | tf_op jit(solution)/shard_map/all_to_all | solution.py:417
  8.9 26.6 %collective-permute-start = (bf16[128,4096]{1,0:T(8,128)(2,1)}, bf16[128,4096]{1,0:T(8,128)(2,1)}, u32[]{:S(2)}, u32[]{:S(2)}) collective-permute-start(bf16[128,4096]{1,0:T(8,128)(2,1)} %bitcast.29), channel_id=1, source_target_pairs={{0,28},{4,24},{8,20},{12,16},{16,12},{20,8},{24,4},{28,0},{1,29},{... | collective-permute-start | bytes 3145736 | tf_op jit(solution)/shard_map/ppermute | solution.py:501
  9.3 57.3 %collective-permute-start.1 = (bf16[128,4096]{1,0:T(8,128)(2,1)}, bf16[128,4096]{1,0:T(8,128)(2,1)}, u32[]{:S(2)}, u32[]{:S(2)}) collective-permute-start(bf16[128,4096]{1,0:T(8,128)(2,1)} %get-tuple-element.38.refs_0_), channel_id=1, source_target_pairs={{0,1},{1,2},{2,3},{4,5},{5,6},{6,7},{8,9},{9,10},{10,11},{12,13},{... | collective-permute-start | bytes 3145736 | tf_op jit(solution)/shard_map/ppermute | solution.py:424
  12.7 53.9 %collective-permute-start.2 = (bf16[128,4096]{1,0:T(8,128)(2,1)}, bf16[128,4096]{1,0:T(8,128)(2,1)}, u32[]{:S(2)}, u32[]{:S(2)}) collective-permute-start(bf16[128,4096]{1,0:T(8,128)(2,1)} %get-tuple-element.38.refs_0_), channel_id=1, source_target_pairs={{1,0},{2,1},{3,2},{5,4},{6,5},{7,6},{9,8},{10,9},{11,10},{13,12},{... | collective-permute-start | bytes 3145736 | tf_op jit(solution)/shard_map/ppermute | solution.py:425
  16.1 50.5 %collective-permute-start.3 = (bf16[128,4096]{1,0:T(8,128)(2,1)}, bf16[128,4096]{1,0:T(8,128)(2,1)}, u32[]{:S(2)}, u32[]{:S(2)}) collective-permute-start(bf16[128,4096]{1,0:T(8,128)(2,1)} %bitcast.30), channel_id=1, source_target_pairs={{0,28},{4,24},{8,20},{12,16},{16,12},{20,8},{24,4},{28,0},{1,29},{... | collective-permute-start | bytes 3145736 | tf_op jit(solution)/shard_map/ppermute | solution.py:502
  37.9 59.3 %all-to-all-start.1 = ((bf16[4,128,1024]{2,1,0:T(8,128)(2,1)}), bf16[4,128,1024]{2,1,0:T(8,128)(2,1)}, u32[]{:S(2)}, u32[]{:S(2)}) async-start(bf16[4,128,1024]{2,1,0:T(8,128)(2,1)} %prepare.3.refs_3_), calls=%async_computation.1 | async-start | bytes 2097152 | tf_op jit(solution)/shard_map/all_to_all | solution.py:417
  69.4 38.8 %collective-permute-start.6 = (bf16[128,4096]{1,0:T(8,128)(2,1)}, bf16[128,4096]{1,0:T(8,128)(2,1)}, u32[]{:S(2)}, u32[]{:S(2)}) collective-permute-start(bf16[128,4096]{1,0:T(8,128)(2,1)} %grad_mix.1.refs_4_.refs_0_.refs_8_), channel_id=1, source_target_pairs={{0,1},{1,2},{2,3},{4,5},{5,6},{6,7},{8,9},{9,10},{10,11},{12,13},{... | collective-permute-start | bytes 3145736 | tf_op jit(solution)/shard_map/ppermute | solution.py:424
  73.8 34.4 %collective-permute-start.7 = (bf16[128,4096]{1,0:T(8,128)(2,1)}, bf16[128,4096]{1,0:T(8,128)(2,1)}, u32[]{:S(2)}, u32[]{:S(2)}) collective-permute-start(bf16[128,4096]{1,0:T(8,128)(2,1)} %grad_mix.1.refs_4_.refs_0_.refs_8_), channel_id=1, source_target_pairs={{1,0},{2,1},{3,2},{5,4},{6,5},{7,6},{9,8},{10,9},{11,10},{13,12},{... | collective-permute-start | bytes 3145736 | tf_op jit(solution)/shard_map/ppermute | solution.py:425
  90.3 32.5 %collective-permute-start.4 = (bf16[128,4096]{1,0:T(8,128)(2,1)}, bf16[128,4096]{1,0:T(8,128)(2,1)}, u32[]{:S(2)}, u32[]{:S(2)}) collective-permute-start(bf16[128,4096]{1,0:T(8,128)(2,1)} %get-tuple-element.43.refs_3_.refs_4_), channel_id=1, source_target_pairs={{0,1},{1,2},{2,3},{4,5},{5,6},{6,7},{8,9},{9,10},{10,11},{12,13},{... | collective-permute-start | bytes 3145736 | tf_op jit(solution)/shard_map/ppermute | solution.py:424
  93.8 30.8 %collective-permute-start.5 = (bf16[128,4096]{1,0:T(8,128)(2,1)}, bf16[128,4096]{1,0:T(8,128)(2,1)}, u32[]{:S(2)}, u32[]{:S(2)}) collective-permute-start(bf16[128,4096]{1,0:T(8,128)(2,1)} %get-tuple-element.44.refs_4_.refs_5_), channel_id=1, source_target_pairs={{1,0},{2,1},{3,2},{5,4},{6,5},{7,6},{9,8},{10,9},{11,10},{13,12},{... | collective-permute-start | bytes 3145736 | tf_op jit(solution)/shard_map/ppermute | solution.py:425
  111.5 33.9 %collective-permute-start.10 = (bf16[128,4096]{1,0:T(8,128)(2,1)}, bf16[128,4096]{1,0:T(8,128)(2,1)}, u32[]{:S(2)}, u32[]{:S(2)}) collective-permute-start(bf16[128,4096]{1,0:T(8,128)(2,1)} %get-tuple-element.48.refs_4_), channel_id=1, source_target_pairs={{0,1},{1,2},{2,3},{4,5},{5,6},{6,7},{8,9},{9,10},{10,11},{12,13},{... | collective-permute-start | bytes 3145736 | tf_op jit(solution)/shard_map/ppermute | solution.py:424
  113.9 33.1 %collective-permute-start.11 = (bf16[128,4096]{1,0:T(8,128)(2,1)}, bf16[128,4096]{1,0:T(8,128)(2,1)}, u32[]{:S(2)}, u32[]{:S(2)}) collective-permute-start(bf16[128,4096]{1,0:T(8,128)(2,1)} %get-tuple-element.51), channel_id=1, source_target_pairs={{1,0},{2,1},{3,2},{5,4},{6,5},{7,6},{9,8},{10,9},{11,10},{13,12},{... | collective-permute-start | bytes 3145736 | tf_op jit(solution)/shard_map/ppermute | solution.py:425
  127.9 39.9 %collective-permute-start.8 = (bf16[128,4096]{1,0:T(8,128)(2,1)}, bf16[128,4096]{1,0:T(8,128)(2,1)}, u32[]{:S(2)}, u32[]{:S(2)}) collective-permute-start(bf16[128,4096]{1,0:T(8,128)(2,1)} %get-tuple-element.49.refs_4_), channel_id=1, source_target_pairs={{0,1},{1,2},{2,3},{4,5},{5,6},{6,7},{8,9},{9,10},{10,11},{12,13},{... | collective-permute-start | bytes 3145736 | tf_op jit(solution)/shard_map/ppermute | solution.py:424
  130.6 38.9 %collective-permute-start.9 = (bf16[128,4096]{1,0:T(8,128)(2,1)}, bf16[128,4096]{1,0:T(8,128)(2,1)}, u32[]{:S(2)}, u32[]{:S(2)}) collective-permute-start(bf16[128,4096]{1,0:T(8,128)(2,1)} %get-tuple-element.50.refs_5_), channel_id=1, source_target_pairs={{1,0},{2,1},{3,2},{5,4},{6,5},{7,6},{9,8},{10,9},{11,10},{13,12},{... | collective-permute-start | bytes 3145736 | tf_op jit(solution)/shard_map/ppermute | solution.py:425
  150.6 39.6 %collective-permute-start.12 = (bf16[128,4096]{1,0:T(8,128)(2,1)}, bf16[128,4096]{1,0:T(8,128)(2,1)}, u32[]{:S(2)}, u32[]{:S(2)}) collective-permute-start(bf16[128,4096]{1,0:T(8,128)(2,1)} %get-tuple-element.53.refs_4_), channel_id=1, source_target_pairs={{0,1},{1,2},{2,3},{4,5},{5,6},{6,7},{8,9},{9,10},{10,11},{12,13},{... | collective-permute-start | bytes 3145736 | tf_op jit(solution)/shard_map/ppermute | solution.py:424
  153.3 38.6 %collective-permute-start.13 = (bf16[128,4096]{1,0:T(8,128)(2,1)}, bf16[128,4096]{1,0:T(8,128)(2,1)}, u32[]{:S(2)}, u32[]{:S(2)}) collective-permute-start(bf16[128,4096]{1,0:T(8,128)(2,1)} %get-tuple-element.54), channel_id=1, source_target_pairs={{1,0},{2,1},{3,2},{5,4},{6,5},{7,6},{9,8},{10,9},{11,10},{13,12},{... | collective-permute-start | bytes 3145736 | tf_op jit(solution)/shard_map/ppermute | solution.py:425
  172.9 59.9 %collective-permute-start.14 = (bf16[128,4096]{1,0:T(8,128)(2,1)}, bf16[128,4096]{1,0:T(8,128)(2,1)}, u32[]{:S(2)}, u32[]{:S(2)}) collective-permute-start(bf16[128,4096]{1,0:T(8,128)(2,1)} %get-tuple-element.56.refs_4_), channel_id=1, source_target_pairs={{0,1},{1,2},{2,3},{4,5},{5,6},{6,7},{8,9},{9,10},{10,11},{12,13},{... | collective-permute-start | bytes 3145736 | tf_op jit(solution)/shard_map/ppermute | solution.py:424
  175.6 57.2 %collective-permute-start.15 = (bf16[128,4096]{1,0:T(8,128)(2,1)}, bf16[128,4096]{1,0:T(8,128)(2,1)}, u32[]{:S(2)}, u32[]{:S(2)}) collective-permute-start(bf16[128,4096]{1,0:T(8,128)(2,1)} %get-tuple-element.57.refs_5_), channel_id=1, source_target_pairs={{1,0},{2,1},{3,2},{5,4},{6,5},{7,6},{9,8},{10,9},{11,10},{13,12},{... | collective-permute-start | bytes 3145736 | tf_op jit(solution)/shard_map/ppermute | solution.py:425
  207.8 37.3 %all-to-all-start.2 = ((bf16[4,128,1024]{2,1,0:T(8,128)(2,1)}), bf16[4,128,1024]{2,1,0:T(8,128)(2,1)}, u32[]{:S(2)}, u32[]{:S(2)}) async-start(bf16[4,128,1024]{2,1,0:T(8,128)(2,1)} %bitcast.18), calls=%async_computation.2 | async-start | bytes 2097152 | tf_op jit(solution)/shard_map/all_to_all | solution.py:417
  212.8 55.5 %collective-permute-start.16 = (bf16[128,4096]{1,0:T(8,128)(2,1)}, bf16[128,4096]{1,0:T(8,128)(2,1)}, u32[]{:S(2)}, u32[]{:S(2)}) collective-permute-start(bf16[128,4096]{1,0:T(8,128)(2,1)} %get-tuple-element.58.refs_9_), channel_id=1, source_target_pairs={{0,1},{1,2},{2,3},{4,5},{5,6},{6,7},{8,9},{9,10},{10,11},{12,13},{... | collective-permute-start | bytes 3145736 | tf_op jit(solution)/shard_map/ppermute | solution.py:424
  216.2 54.4 %collective-permute-start.17 = (bf16[128,4096]{1,0:T(8,128)(2,1)}, bf16[128,4096]{1,0:T(8,128)(2,1)}, u32[]{:S(2)}, u32[]{:S(2)}) collective-permute-start(bf16[128,4096]{1,0:T(8,128)(2,1)} %get-tuple-element.63), channel_id=1, source_target_pairs={{1,0},{2,1},{3,2},{5,4},{6,5},{7,6},{9,8},{10,9},{11,10},{13,12},{... | collective-permute-start | bytes 3145736 | tf_op jit(solution)/shard_map/ppermute | solution.py:425
  245.1 47.2 %all-to-all-start.3 = ((bf16[4,128,1024]{2,1,0:T(8,128)(2,1)}), bf16[4,128,1024]{2,1,0:T(8,128)(2,1)}, u32[]{:S(2)}, u32[]{:S(2)}) async-start(bf16[4,128,1024]{2,1,0:T(8,128)(2,1)} %bitcast.17), calls=%async_computation.3 | async-start | bytes 2097152 | tf_op jit(solution)/shard_map/all_to_all | solution.py:417
  275.3 17.0 %collective-permute-start.21 = (bf16[1,64,4096]{2,1,0:T(8,128)(2,1)}, bf16[1,64,4096]{2,1,0:T(8,128)(2,1)S(1)}, u32[]{:S(2)}, u32[]{:S(2)}) collective-permute-start(bf16[1,64,4096]{2,1,0:T(8,128)(2,1)} %get-tuple-element.64.refs_4_.refs_0_), channel_id=1, source_target_pairs={{28,4},{24,8},{20,12},{12,20},{8,24},{4,28},{29,5},{25,9},{21,13},... | collective-permute-start | bytes 1572872 | tf_op jit(solution)/shard_map/ppermute | solution.py:535
  292.4 0.8 copy-start
  293.2 8.9 %copy-start.2 = (f32[4,8,128]{2,1,0:T(8,128)S(1)}, f32[4,8,128]{2,1,0:T(8,128)}, u32[]{:S(2)}) copy-start(f32[4,8,128]{2,1,0:T(8,128)} %filter_gradient.1) | copy-start | bytes 49156
  297.7 29.1 %collective-permute-start.22 = (bf16[1,128,4096]{2,1,0:T(8,128)(2,1)}, bf16[1,128,4096]{2,1,0:T(8,128)(2,1)}, u32[]{:S(2)}, u32[]{:S(2)}) collective-permute-start(bf16[1,128,4096]{2,1,0:T(8,128)(2,1)} %finish.3.refs_4_), channel_id=1, source_target_pairs={{4,0},{8,4},{12,8},{16,12},{20,16},{24,20},{28,24},{5,1},{9,5},{13... | collective-permute-start | bytes 3145736 | tf_op jit(solution)/shard_map/ppermute | solution.py:540
  299.6 24.0 %collective-permute-start.23 = (bf16[1,64,4096]{2,1,0:T(8,128)(2,1)}, bf16[1,64,4096]{2,1,0:T(8,128)(2,1)S(1)}, u32[]{:S(2)}, u32[]{:S(2)}) collective-permute-start(bf16[1,64,4096]{2,1,0:T(8,128)(2,1)} %get-tuple-element.67.refs_1_), channel_id=1, source_target_pairs={{28,4},{24,8},{20,12},{12,20},{8,24},{4,28},{29,5},{25,9},{21,13},... | collective-permute-start | bytes 1572872 | tf_op jit(solution)/shard_map/ppermute | solution.py:535
  302.1 3.8 %collective-permute-start.18 = (f32[1,32,128]{2,1,0:T(8,128)S(1)}, f32[1,32,128]{2,1,0:T(8,128)S(1)}, u32[]{:S(2)}, u32[]{:S(2)}) collective-permute-start(f32[1,32,128]{2,1,0:T(8,128)S(1)} %bitcast.21), channel_id=1, source_target_pairs={{0,1},{1,2},{2,3},{3,0},{4,5},{5,6},{6,7},{7,4},{8,9},{9,10},{10,1... | collective-permute-start | bytes 49160 | tf_op jit(solution)/shard_map/ppermute | solution.py:479
  302.3 4.6 %collective-permute-start.19 = (f32[1,32,128]{2,1,0:T(8,128)S(1)}, f32[1,32,128]{2,1,0:T(8,128)S(1)}, u32[]{:S(2)}, u32[]{:S(2)}) collective-permute-start(f32[1,32,128]{2,1,0:T(8,128)S(1)} %bitcast.22), channel_id=1, source_target_pairs={{0,2},{1,3},{2,0},{3,1},{4,6},{5,7},{6,4},{7,5},{8,10},{9,11},{10,... | collective-permute-start | bytes 49160 | tf_op jit(solution)/shard_map/ppermute | solution.py:479
  302.3 5.2 %collective-permute-start.20 = (f32[1,32,128]{2,1,0:T(8,128)S(1)}, f32[1,32,128]{2,1,0:T(8,128)S(1)}, u32[]{:S(2)}, u32[]{:S(2)}) collective-permute-start(f32[1,32,128]{2,1,0:T(8,128)S(1)} %bitcast.23), channel_id=1, source_target_pairs={{0,3},{1,0},{2,1},{3,2},{4,7},{5,4},{6,5},{7,6},{8,11},{9,8},{10,9... | collective-permute-start | bytes 49160 | tf_op jit(solution)/shard_map/ppermute | solution.py:479
  305.8 1.6 copy-start.3
  323.6 0.8 copy-start.1
  (2 other events, 1.2 us)

commit v11 on v8

--- a/solution.py
+++ b/solution.py
@@ -353,18 +353,38 @@
         out_ref[...] = came_ref[...]
 
 
-def settle(own, came):
+def settle(own, came, after=()):
     step = came.shape[1] // 2
     spec = pl.BlockSpec((1, step, came.shape[2]), lambda i: (0, i, 0))
     return call(
         settle_kernel,
         (own, came),
-        (),
+        after,
         grid=(2,),
         in_specs=[spec, spec],
         out_specs=spec,
         out_shape=shape(came.shape, came.dtype),
+        flops=1 << 35,
         name="settle",
+    )
+
+
+def copy_kernel(in_ref, out_ref):
+    out_ref[...] = in_ref[...]
+
+
+def copy(x, after=()):
+    step = x.shape[1] // 2
+    spec = pl.BlockSpec((1, step, x.shape[2]), lambda i: (0, i, 0))
+    return call(
+        copy_kernel,
+        (x,),
+        after,
+        grid=(2,),
+        in_specs=[spec],
+        out_specs=spec,
+        out_shape=shape(x.shape, x.dtype),
+        name="copy",
     )
 
 
@@ -379,7 +399,7 @@
     out_ref[0] = (cot + inverse * (total - normed * mean)).astype(bf16)
 
 
-def finish(xin, cot, mixed, returned, after=()):
+def finish(xin, cot, mixed, returned, counted, after=()):
     rows, width = xin.shape
     blocks, _, depth = returned.shape
     step = 64
@@ -393,6 +413,7 @@
         + [spec] * len(mixed),
         out_specs=pl.BlockSpec((1, step, width), lambda i: (0, i, 0)),
         out_shape=shape((1, rows, width), bf16),
+        counted=counted,
         name="finish",
     )
 
@@ -514,18 +535,19 @@
         down_mixes, down_part, up_mixes, up_part, *filters.shape[1:], after=(up_g,)
     )
     down_g, down_back = back(
-        down_mixes, weight, ahead, after=(taps, *down_arrivals[-1], *up_arrivals[-1])
+        down_mixes, weight, ahead, after=(taps, *down_arrivals[-1])
     )
     down_back = exchange(down_back)
-    up_grad = finish(up_xin, up_cot, up_conv, up_back, after=(down_g,))
-    up_passed = lax.ppermute(up_grad, "section", up_pairs)
+    up_grad = finish(up_xin, up_cot, up_conv, up_back, True, after=(down_g,))
+    up_came = lax.ppermute(up_grad, "section", up_pairs)
     weight_grad = weight_gradient(down_x, up_x, down_g, up_g, after=(up_grad,))
-    up_passed = settle(up_grad, up_passed)
     down_grad = finish(
-        down_xin, down_cot, down_conv, down_back, after=(weight_grad, up_passed)
+        down_xin, down_cot, down_conv, down_back, False, after=(weight_grad,)
     )
     down_passed = lax.ppermute(down_grad, "section", down_pairs)
-    taps = sum_all(taps, after=(down_grad,))
+    up_passed = settle(up_grad, up_came, after=(down_grad,))
+    taps = sum_all(copy(taps, after=(up_passed,)))
+    down_passed = copy(down_passed, after=(taps,))
     return weight_grad[None], taps, down_passed, up_passed
 
 

time: 323 us -> 328 us (1.015)
  waiting for transfers between devices: 111 us -> 118 us
    ppermute x1, waiting for transfers between devices: 8.81 us -> 13.5 us  [per_device(): up_came = lax.ppermute(up_grad, 'section', up_pairs)]
    ppermute x8, waiting for transfers between devices: 73.8 us -> 77.9 us  [both_ways(): lax.ppermute(right, 'tensor', onward)]
    ppermute x1, waiting for transfers between devices: 3.86 us -> 0.01 us  [per_device(): down_passed = lax.ppermute(down_grad, 'section', down_pairs)]
    pallas_call x20 -> x22, Pallas kernels: 119 us -> 122 us  [call(): pl.pallas_call(body, in_specs=list(in_specs) + unread, out_shape=out_shap...]
  transfers between devices with their start and end apart: 27 -> 27, of which waited for: 16 -> 15; matrix products, arithmetic and copies ran while one was open for 0% -> 0% of each run, Pallas kernels for 35% -> 36%
where the time goes in v11:
time: 328 us; the launch traced here: 326 us
  Pallas kernels  122 us (37%)
  waiting for transfers between devices  118 us (36%)
  starting transfers between devices  84.9 us (26%)
    pallas_call x22, Pallas kernels, call(): pl.pallas_call(body, in_specs=list(in_specs) + unread, out_shape=out_shap...  122 us
    ppermute x8, waiting for transfers between devices, both_ways(): lax.ppermute(right, 'tensor', onward)  77.9 us
    ppermute x8, starting transfers between devices, both_ways(): lax.ppermute(left, 'tensor', [(j, i) for i, j in onward])  29.6 us
    ppermute x8, starting transfers between devices, both_ways(): lax.ppermute(right, 'tensor', onward)  25 us
    all_to_all x4, starting transfers between devices, exchange(): return lax.all_to_all(x, 'tensor', split_axis=0, concat_axis=0, tiled=True)  20.4 us
    ppermute x1, waiting for transfers between devices, per_device(): up_xin = lax.ppermute(up_input[0], 'section', mirror)  13.8 us
    ppermute x1, waiting for transfers between devices, per_device(): up_came = lax.ppermute(up_grad, 'section', up_pairs)  13.5 us
    ppermute x8, waiting for transfers between devices, both_ways(): lax.ppermute(left, 'tensor', [(j, i) for i, j in onward])  9.08 us
  transfers between devices with their start and end apart: 27, of which 15 were waited for; matrix products, arithmetic and copies ran while one was open for 0% of the time, Pallas kernels for 36%

profile of v11, /device:TPU:10, one launch (start us, length us, event | category | flops | bytes accessed | tf_op | source)
XLA Modules:
  0.0 326.2 jit_solution(6710082420401248919)
XLA Ops:
  3.6 5.3 %all-to-all-start = ((bf16[4,128,1024]{2,1,0:T(8,128)(2,1)}), bf16[4,128,1024]{2,1,0:T(8,128)(2,1)}, u32[]{:S(2)}, u32[]{:S(2)}) async-start(bf16[4,128,1024]{2,1,0:T(8,128)(2,1)} %get-tuple-element.34), calls=%async_computation | async-start | bytes 2097152 | tf_op jit(solution)/shard_map/all_to_all | solution.py:424
  12.7 3.4 %collective-permute-start.2 = (bf16[128,4096]{1,0:T(8,128)(2,1)}, bf16[128,4096]{1,0:T(8,128)(2,1)}, u32[]{:S(2)}, u32[]{:S(2)}) collective-permute-start(bf16[128,4096]{1,0:T(8,128)(2,1)} %get-tuple-element.36.refs_0_), channel_id=1, source_target_pairs={{1,0},{2,1},{3,2},{5,4},{6,5},{7,6},{9,8},{10,9},{11,10},{13,12},{... | collective-permute-start | bytes 3145736 | tf_op jit(solution)/shard_map/ppermute | solution.py:432
  17.9 3.9 %toeplitz.1 = (bf16[32,128,256]{2,1,0:T(8,128)(2,1)}, bf16[32,128,256]{2,1,0:T(8,128)(2,1)}) custom-call(f32[32,128]{1,0:T(8,128)} %bitcast.21), custom_call_target="tpu_custom_call" | custom-call | bytes 4210688 | tf_op jit(solution)/shard_map/toeplitz/pallas_call | solution.py:36
  21.8 13.8 %collective-permute-done.refs_0_ = bf16[128,4096]{1,0:T(8,128)(2,1)} collective-permute-done((bf16[128,4096]{1,0:T(8,128)(2,1)}, bf16[128,4096]{1,0:T(8,128)(2,1)}, u32[]{:S(2)}, u32[]{:S(2)}) %collective-permute-start) | collective-permute-done | bytes 1048608 | tf_op jit(solution)/shard_map/ppermute | solution.py:508
  37.8 5.1 %all-to-all-start.1 = ((bf16[4,128,1024]{2,1,0:T(8,128)(2,1)}), bf16[4,128,1024]{2,1,0:T(8,128)(2,1)}, u32[]{:S(2)}, u32[]{:S(2)}) async-start(bf16[4,128,1024]{2,1,0:T(8,128)(2,1)} %prepare.3.refs_3_), calls=%async_computation.1 | async-start | bytes 2097152 | tf_op jit(solution)/shard_map/all_to_all | solution.py:424
  42.9 23.7 %collective-permute-done.1.refs_2_.refs_0_.refs_1_ = bf16[128,4096]{1,0:T(8,128)(2,1)} collective-permute-done((bf16[128,4096]{1,0:T(8,128)(2,1)}, bf16[128,4096]{1,0:T(8,128)(2,1)}, u32[]{:S(2)}, u32[]{:S(2)}) %collective-permute-start.1) | collective-permute-done | bytes 1048608 | tf_op jit(solution)/shard_map/ppermute | solution.py:431
  69.4 4.4 %collective-permute-start.6 = (bf16[128,4096]{1,0:T(8,128)(2,1)}, bf16[128,4096]{1,0:T(8,128)(2,1)}, u32[]{:S(2)}, u32[]{:S(2)}) collective-permute-start(bf16[128,4096]{1,0:T(8,128)(2,1)} %grad_mix.1.refs_4_.refs_0_.refs_8_), channel_id=1, source_target_pairs={{0,1},{1,2},{2,3},{4,5},{5,6},{6,7},{8,9},{9,10},{10,11},{12,13},{... | collective-permute-start | bytes 3145736 | tf_op jit(solution)/shard_map/ppermute | solution.py:431
  76.2 10.9 %project.2 = (bf16[512,4096]{1,0:T(8,128)(2,1)}, bf16[128,4096]{1,0:T(8,128)(2,1)}, bf16[128,4096]{1,0:T(8,128)(2,1)}, bf16[128,4096]{1,0:T(8,128)(2,1)}, bf16[128,4096]{1,0:T(8,128)(2,1)}) custom-call(bf16[512,1024]{1,0:T(8,128)(2,1)} %bitcast.2.refs_0_, bf16[1024,4096]{1,0:T(8,128)(2,1)} %bitcast.22, bf16[32,128,256]{2,1,0:T(8,128)(2,1)} %get-tuple-element.37.refs_2_, ...), custom_call_target="tpu_custom_call" | custom-call | flops 5368709120 | bytes 19922944 | tf_op jit(solution)/shard_map/project/pallas_call | solution.py:36
  93.7 3.4 %collective-permute-start.5 = (bf16[128,4096]{1,0:T(8,128)(2,1)}, bf16[128,4096]{1,0:T(8,128)(2,1)}, u32[]{:S(2)}, u32[]{:S(2)}) collective-permute-start(bf16[128,4096]{1,0:T(8,128)(2,1)} %get-tuple-element.42.refs_4_.refs_5_), channel_id=1, source_target_pairs={{1,0},{2,1},{3,2},{5,4},{6,5},{7,6},{9,8},{10,9},{11,10},{13,12},{... | collective-permute-start | bytes 3145736 | tf_op jit(solution)/shard_map/ppermute | solution.py:432
  97.2 11.0 %project.3 = (bf16[512,4096]{1,0:T(8,128)(2,1)}, bf16[128,4096]{1,0:T(8,128)(2,1)}, bf16[128,4096]{1,0:T(8,128)(2,1)}, bf16[128,4096]{1,0:T(8,128)(2,1)}, bf16[128,4096]{1,0:T(8,128)(2,1)}) custom-call(bf16[512,1024]{1,0:T(8,128)(2,1)} %bitcast.5.refs_0_.refs_1_, bf16[1024,4096]{1,0:T(8,128)(2,1)} %bitcast.23, ...), custom_call_target="tpu_custom_call" | custom-call | flops 5368709120 | bytes 19922944 | tf_op jit(solution)/shard_map/project/pallas_call | solution.py:36
  113.9 4.4 %collective-permute-start.11 = (bf16[128,4096]{1,0:T(8,128)(2,1)}, bf16[128,4096]{1,0:T(8,128)(2,1)}, u32[]{:S(2)}, u32[]{:S(2)}) collective-permute-start(bf16[128,4096]{1,0:T(8,128)(2,1)} %get-tuple-element.49), channel_id=1, source_target_pairs={{1,0},{2,1},{3,2},{5,4},{6,5},{7,6},{9,8},{10,9},{11,10},{13,12},{... | collective-permute-start | bytes 3145736 | tf_op jit(solution)/shard_map/ppermute | solution.py:432
  118.3 4.6 %collective-permute-done.4.refs_0_.refs_2_ = bf16[128,4096]{1,0:T(8,128)(2,1)} collective-permute-done((bf16[128,4096]{1,0:T(8,128)(2,1)}, bf16[128,4096]{1,0:T(8,128)(2,1)}, u32[]{:S(2)}, u32[]{:S(2)}) %collective-permute-start.4) | collective-permute-done | bytes 1048608 | tf_op jit(solution)/shard_map/ppermute | solution.py:431
  124.5 3.4 %payload.8 = (bf16[128,4096]{1,0:T(8,128)(2,1)}, bf16[128,4096]{1,0:T(8,128)(2,1)}) custom-call(bf16[128,4096]{1,0:T(8,128)(2,1)} %collective-permute-done.4.refs_0_.refs_2_, bf16[128,4096]{1,0:T(8,128)(2,1)} %collective-permute-done.5.refs_1_.refs_5_, bf16[128,4096]{1,0:T(8,128)(2,1)} %get-tuple-element.43.refs_2_.refs_3_, ...), custom_call_target="tpu_custom_call" | custom-call | bytes 6291456 | tf_op jit(solution)/shard_map/payload/pallas_call | solution.py:36
  130.6 4.1 %collective-permute-start.9 = (bf16[128,4096]{1,0:T(8,128)(2,1)}, bf16[128,4096]{1,0:T(8,128)(2,1)}, u32[]{:S(2)}, u32[]{:S(2)}) collective-permute-start(bf16[128,4096]{1,0:T(8,128)(2,1)} %get-tuple-element.48.refs_5_), channel_id=1, source_target_pairs={{1,0},{2,1},{3,2},{5,4},{6,5},{7,6},{9,8},{10,9},{11,10},{13,12},{... | collective-permute-start | bytes 3145736 | tf_op jit(solution)/shard_map/ppermute | solution.py:432
  134.8 10.5 %collective-permute-done.10.refs_0_.refs_2_.refs_10_ = bf16[128,4096]{1,0:T(8,128)(2,1)} collective-permute-done((bf16[128,4096]{1,0:T(8,128)(2,1)}, bf16[128,4096]{1,0:T(8,128)(2,1)}, u32[]{:S(2)}, u32[]{:S(2)}) %collective-permute-start.10) | collective-permute-done | bytes 1048608 | tf_op jit(solution)/shard_map/ppermute | solution.py:431
  147.0 3.7 %payload.9 = (bf16[128,4096]{1,0:T(8,128)(2,1)}, bf16[128,4096]{1,0:T(8,128)(2,1)}) custom-call(bf16[128,4096]{1,0:T(8,128)(2,1)} %collective-permute-done.10.refs_0_.refs_2_.refs_10_, bf16[128,4096]{1,0:T(8,128)(2,1)} %collective-permute-done.11.refs_1_.refs_5_.refs_13_, bf16[128,4096]{1,0:T(8,128)(2,1)} %get-tuple-element.50.refs_2_.refs_3_, ...), custom_call_target="tpu_custom_call" | custom-call | bytes 6291456 | tf_op jit(solution)/shard_map/payload/pallas_call | solution.py:36
  153.4 4.1 %collective-permute-start.13 = (bf16[128,4096]{1,0:T(8,128)(2,1)}, bf16[128,4096]{1,0:T(8,128)(2,1)}, u32[]{:S(2)}, u32[]{:S(2)}) collective-permute-start(bf16[128,4096]{1,0:T(8,128)(2,1)} %get-tuple-element.52), channel_id=1, source_target_pairs={{1,0},{2,1},{3,2},{5,4},{6,5},{7,6},{9,8},{10,9},{11,10},{13,12},{... | collective-permute-start | bytes 3145736 | tf_op jit(solution)/shard_map/ppermute | solution.py:432
  157.5 10.3 %collective-permute-done.8.refs_0_.refs_3_ = bf16[128,4096]{1,0:T(8,128)(2,1)} collective-permute-done((bf16[128,4096]{1,0:T(8,128)(2,1)}, bf16[128,4096]{1,0:T(8,128)(2,1)}, u32[]{:S(2)}, u32[]{:S(2)}) %collective-permute-start.8) | collective-permute-done | bytes 1048608 | tf_op jit(solution)/shard_map/ppermute | solution.py:431
  175.6 4.1 %collective-permute-start.15 = (bf16[128,4096]{1,0:T(8,128)(2,1)}, bf16[128,4096]{1,0:T(8,128)(2,1)}, u32[]{:S(2)}, u32[]{:S(2)}) collective-permute-start(bf16[128,4096]{1,0:T(8,128)(2,1)} %get-tuple-element.55.refs_5_), channel_id=1, source_target_pairs={{1,0},{2,1},{3,2},{5,4},{6,5},{7,6},{9,8},{10,9},{11,10},{13,12},{... | collective-permute-start | bytes 3145736 | tf_op jit(solution)/shard_map/ppermute | solution.py:432
  179.7 10.6 %collective-permute-done.12.refs_0_.refs_3_.refs_11_ = bf16[128,4096]{1,0:T(8,128)(2,1)} collective-permute-done((bf16[128,4096]{1,0:T(8,128)(2,1)}, bf16[128,4096]{1,0:T(8,128)(2,1)}, u32[]{:S(2)}, u32[]{:S(2)}) %collective-permute-start.12) | collective-permute-done | bytes 1048608 | tf_op jit(solution)/shard_map/ppermute | solution.py:431
  195.4 12.4 %back.2 = (bf16[512,4096]{1,0:T(8,128)(2,1)}, bf16[512,1024]{1,0:T(8,128)(2,1)}) custom-call(bf16[128,4096]{1,0:T(8,128)(2,1)} %grad_mix.1.refs_4_.refs_0_.refs_8_, bf16[128,4096]{1,0:T(8,128)(2,1)} %collective-permute-done.6.refs_0_.refs_1_.refs_9_, bf16[128,4096]{1,0:T(8,128)(2,1)} %collective-permute-done.10.refs_0_.refs_2_.refs_10_, ...), custom_call_target="tpu_custom_call" | custom-call | flops 16106127360 | bytes 23068672 | tf_op jit(solution)/shard_map/back/pallas_call | solution.py:36
  207.8 5.1 %all-to-all-start.2 = ((bf16[4,128,1024]{2,1,0:T(8,128)(2,1)}), bf16[4,128,1024]{2,1,0:T(8,128)(2,1)}, u32[]{:S(2)}, u32[]{:S(2)}) async-start(bf16[4,128,1024]{2,1,0:T(8,128)(2,1)} %bitcast.17), calls=%async_computation.2 | async-start | bytes 2097152 | tf_op jit(solution)/shard_map/all_to_all | solution.py:424
  216.2 3.6 %collective-permute-start.17 = (bf16[128,4096]{1,0:T(8,128)(2,1)}, bf16[128,4096]{1,0:T(8,128)(2,1)}, u32[]{:S(2)}, u32[]{:S(2)}) collective-permute-start(bf16[128,4096]{1,0:T(8,128)(2,1)} %get-tuple-element.61), channel_id=1, source_target_pairs={{1,0},{2,1},{3,2},{5,4},{6,5},{7,6},{9,8},{10,9},{11,10},{13,12},{... | collective-permute-start | bytes 3145736 | tf_op jit(solution)/shard_map/ppermute | solution.py:432
  219.8 13.0 %filter_gradient.1 = f32[4,8,128]{2,1,0:T(8,128)} custom-call(bf16[128,4096]{1,0:T(8,128)(2,1)} %get-tuple-element.36.refs_0_, bf16[128,4096]{1,0:T(8,128)(2,1)} %collective-permute-done.1.refs_2_.refs_0_.refs_1_, bf16[128,4096]{1,0:T(8,128)(2,1)} %collective-permute-done.4.refs_0_.refs_2_, bf16[128,4096]{1,0:T(8,128)(2,1)} %collective-permute-done.8.refs_0_.refs_3_, ...), custom_call_target="tpu_custom_call" | custom-call | tf_op jit(solution)/shard_map/filter_gradient/pallas_call | solution.py:36
  232.8 12.3 %back.3 = (bf16[512,4096]{1,0:T(8,128)(2,1)}, bf16[512,1024]{1,0:T(8,128)(2,1)}) custom-call(bf16[128,4096]{1,0:T(8,128)(2,1)} %get-tuple-element.36.refs_0_, bf16[128,4096]{1,0:T(8,128)(2,1)} %collective-permute-done.1.refs_2_.refs_0_.refs_1_, bf16[128,4096]{1,0:T(8,128)(2,1)} %collective-permute-done.4.refs_0_.refs_2_, ...), custom_call_target="tpu_custom_call" | custom-call | flops 16106127360 | bytes 23068672 | tf_op jit(solution)/shard_map/back/pallas_call | solution.py:36
  245.1 5.0 %all-to-all-start.3 = ((bf16[4,128,1024]{2,1,0:T(8,128)(2,1)}), bf16[4,128,1024]{2,1,0:T(8,128)(2,1)}, u32[]{:S(2)}, u32[]{:S(2)}) async-start(bf16[4,128,1024]{2,1,0:T(8,128)(2,1)} %bitcast.18), calls=%async_computation.3 | async-start | bytes 2097152 | tf_op jit(solution)/shard_map/all_to_all | solution.py:424
  250.1 18.2 %collective-permute-done.16.refs_4_ = bf16[128,4096]{1,0:T(8,128)(2,1)} collective-permute-done((bf16[128,4096]{1,0:T(8,128)(2,1)}, bf16[128,4096]{1,0:T(8,128)(2,1)}, u32[]{:S(2)}, u32[]{:S(2)}) %collective-permute-start.16) | collective-permute-done | bytes 1048608 | tf_op jit(solution)/shard_map/ppermute | solution.py:431
  270.6 4.6 %finish.2.refs_4_.refs_0_ = bf16[1,128,4096]{2,1,0:T(8,128)(2,1)} custom-call(bf16[128,4096]{1,0:T(8,128)(2,1)} %collective-permute-done.refs_0_, bf16[128,4096]{1,0:T(8,128)(2,1)} %collective-permute-done.3.refs_1_, bf16[4,128,1024]{2,1,0:T(8,128)(2,1)} %all-to-all-done.2.refs_2_, bf16[128,4096]{1,0:T(8,128)(2,1)} %get-tuple-element.60.refs_3_, ...), custom_call_target="tpu_custom_call" | custom-call | bytes 7340032 | tf_op jit(solution)/shard_map/finish/pallas_call | solution.py:36
  275.2 3.4 %collective-permute-start.18 = (bf16[1,128,4096]{2,1,0:T(8,128)(2,1)}, bf16[1,128,4096]{2,1,0:T(8,128)(2,1)}, u32[]{:S(2)}, u32[]{:S(2)}) collective-permute-start(bf16[1,128,4096]{2,1,0:T(8,128)(2,1)} %finish.2.refs_4_.refs_0_), channel_id=1, source_target_pairs={{28,4},{24,8},{20,12},{12,20},{8,24},{4,28},{29,5},{25,9},{21,13},... | collective-permute-start | bytes 3145736 | tf_op jit(solution)/shard_map/ppermute | solution.py:542
  278.6 13.6 %weight_gradient.1.refs_6_ = bf16[1024,4096]{1,0:T(8,128)(2,1)} custom-call(bf16[512,1024]{1,0:T(8,128)(2,1)} %bitcast.2.refs_0_, bf16[512,1024]{1,0:T(8,128)(2,1)} %bitcast.5.refs_0_.refs_1_, bf16[512,4096]{1,0:T(8,128)(2,1)} %get-tuple-element.58.refs_6_.refs_2_, bf16[512,4096]{1,0:T(8,128)(2,1)} %get-tuple-element.57.refs_16_.refs_3_, ...), custom_call_target="tpu_custom_call" | custom-call | flops 8589934592 | bytes 18874368 | tf_op jit(solution)/shard_map/weight_gradient/pallas_call | solution.py:36
  292.2 4.6 %finish.3.refs_2_ = bf16[1,128,4096]{2,1,0:T(8,128)(2,1)} custom-call(bf16[128,4096]{1,0:T(8,128)(2,1)} %bitcast.14, bf16[128,4096]{1,0:T(8,128)(2,1)} %bitcast.16, bf16[4,128,1024]{2,1,0:T(8,128)(2,1)} %all-to-all-done.3.refs_2_, bf16[128,4096]{1,0:T(8,128)(2,1)} %get-tuple-element.63.refs_3_, bf16[128,4096]{1,0:T(8,128)(2,1)} %collective-permute-done.14.refs_10_.refs_4_, ...), custom_call_target="tpu_custom_call" | custom-call | tf_op jit(solution)/shard_map/finish/pallas_call | solution.py:36
  298.6 13.5 %collective-permute-done.18.refs_1_ = bf16[1,128,4096]{2,1,0:T(8,128)(2,1)} collective-permute-done((bf16[1,128,4096]{2,1,0:T(8,128)(2,1)}, bf16[1,128,4096]{2,1,0:T(8,128)(2,1)}, u32[]{:S(2)}, u32[]{:S(2)}) %collective-permute-start.18) | collective-permute-done | bytes 1048608 | tf_op jit(solution)/shard_map/ppermute | solution.py:542
  (50 shorter events, 71.6 us)
Async XLA Ops:
  3.6 34.2 %all-to-all-start = ((bf16[4,128,1024]{2,1,0:T(8,128)(2,1)}), bf16[4,128,1024]{2,1,0:T(8,128)(2,1)}, u32[]{:S(2)}, u32[]{:S(2)}) async-start(bf16[4,128,1024]{2,1,0:T(8,128)(2,1)} %get-tuple-element.34), calls=%async_computation | async-start | bytes 2097152 | tf_op jit(solution)/shard_map/all_to_all | solution.py:424
  8.9 26.6 %collective-permute-start = (bf16[128,4096]{1,0:T(8,128)(2,1)}, bf16[128,4096]{1,0:T(8,128)(2,1)}, u32[]{:S(2)}, u32[]{:S(2)}) collective-permute-start(bf16[128,4096]{1,0:T(8,128)(2,1)} %bitcast.26), channel_id=1, source_target_pairs={{0,28},{4,24},{8,20},{12,16},{16,12},{20,8},{24,4},{28,0},{1,29},{... | collective-permute-start | bytes 3145736 | tf_op jit(solution)/shard_map/ppermute | solution.py:508
  9.3 57.3 %collective-permute-start.1 = (bf16[128,4096]{1,0:T(8,128)(2,1)}, bf16[128,4096]{1,0:T(8,128)(2,1)}, u32[]{:S(2)}, u32[]{:S(2)}) collective-permute-start(bf16[128,4096]{1,0:T(8,128)(2,1)} %get-tuple-element.36.refs_0_), channel_id=1, source_target_pairs={{0,1},{1,2},{2,3},{4,5},{5,6},{6,7},{8,9},{9,10},{10,11},{12,13},{... | collective-permute-start | bytes 3145736 | tf_op jit(solution)/shard_map/ppermute | solution.py:431
  12.7 53.9 %collective-permute-start.2 = (bf16[128,4096]{1,0:T(8,128)(2,1)}, bf16[128,4096]{1,0:T(8,128)(2,1)}, u32[]{:S(2)}, u32[]{:S(2)}) collective-permute-start(bf16[128,4096]{1,0:T(8,128)(2,1)} %get-tuple-element.36.refs_0_), channel_id=1, source_target_pairs={{1,0},{2,1},{3,2},{5,4},{6,5},{7,6},{9,8},{10,9},{11,10},{13,12},{... | collective-permute-start | bytes 3145736 | tf_op jit(solution)/shard_map/ppermute | solution.py:432
  16.1 50.5 %collective-permute-start.3 = (bf16[128,4096]{1,0:T(8,128)(2,1)}, bf16[128,4096]{1,0:T(8,128)(2,1)}, u32[]{:S(2)}, u32[]{:S(2)}) collective-permute-start(bf16[128,4096]{1,0:T(8,128)(2,1)} %bitcast.27), channel_id=1, source_target_pairs={{0,28},{4,24},{8,20},{12,16},{16,12},{20,8},{24,4},{28,0},{1,29},{... | collective-permute-start | bytes 3145736 | tf_op jit(solution)/shard_map/ppermute | solution.py:509
  37.8 59.3 %all-to-all-start.1 = ((bf16[4,128,1024]{2,1,0:T(8,128)(2,1)}), bf16[4,128,1024]{2,1,0:T(8,128)(2,1)}, u32[]{:S(2)}, u32[]{:S(2)}) async-start(bf16[4,128,1024]{2,1,0:T(8,128)(2,1)} %prepare.3.refs_3_), calls=%async_computation.1 | async-start | bytes 2097152 | tf_op jit(solution)/shard_map/all_to_all | solution.py:424
  69.4 38.8 %collective-permute-start.6 = (bf16[128,4096]{1,0:T(8,128)(2,1)}, bf16[128,4096]{1,0:T(8,128)(2,1)}, u32[]{:S(2)}, u32[]{:S(2)}) collective-permute-start(bf16[128,4096]{1,0:T(8,128)(2,1)} %grad_mix.1.refs_4_.refs_0_.refs_8_), channel_id=1, source_target_pairs={{0,1},{1,2},{2,3},{4,5},{5,6},{6,7},{8,9},{9,10},{10,11},{12,13},{... | collective-permute-start | bytes 3145736 | tf_op jit(solution)/shard_map/ppermute | solution.py:431
  73.8 34.4 %collective-permute-start.7 = (bf16[128,4096]{1,0:T(8,128)(2,1)}, bf16[128,4096]{1,0:T(8,128)(2,1)}, u32[]{:S(2)}, u32[]{:S(2)}) collective-permute-start(bf16[128,4096]{1,0:T(8,128)(2,1)} %grad_mix.1.refs_4_.refs_0_.refs_8_), channel_id=1, source_target_pairs={{1,0},{2,1},{3,2},{5,4},{6,5},{7,6},{9,8},{10,9},{11,10},{13,12},{... | collective-permute-start | bytes 3145736 | tf_op jit(solution)/shard_map/ppermute | solution.py:432
  90.3 32.5 %collective-permute-start.4 = (bf16[128,4096]{1,0:T(8,128)(2,1)}, bf16[128,4096]{1,0:T(8,128)(2,1)}, u32[]{:S(2)}, u32[]{:S(2)}) collective-permute-start(bf16[128,4096]{1,0:T(8,128)(2,1)} %get-tuple-element.41.refs_3_.refs_4_), channel_id=1, source_target_pairs={{0,1},{1,2},{2,3},{4,5},{5,6},{6,7},{8,9},{9,10},{10,11},{12,13},{... | collective-permute-start | bytes 3145736 | tf_op jit(solution)/shard_map/ppermute | solution.py:431
  93.7 30.8 %collective-permute-start.5 = (bf16[128,4096]{1,0:T(8,128)(2,1)}, bf16[128,4096]{1,0:T(8,128)(2,1)}, u32[]{:S(2)}, u32[]{:S(2)}) collective-permute-start(bf16[128,4096]{1,0:T(8,128)(2,1)} %get-tuple-element.42.refs_4_.refs_5_), channel_id=1, source_target_pairs={{1,0},{2,1},{3,2},{5,4},{6,5},{7,6},{9,8},{10,9},{11,10},{13,12},{... | collective-permute-start | bytes 3145736 | tf_op jit(solution)/shard_map/ppermute | solution.py:432
  111.5 33.9 %collective-permute-start.10 = (bf16[128,4096]{1,0:T(8,128)(2,1)}, bf16[128,4096]{1,0:T(8,128)(2,1)}, u32[]{:S(2)}, u32[]{:S(2)}) collective-permute-start(bf16[128,4096]{1,0:T(8,128)(2,1)} %get-tuple-element.46.refs_4_), channel_id=1, source_target_pairs={{0,1},{1,2},{2,3},{4,5},{5,6},{6,7},{8,9},{9,10},{10,11},{12,13},{... | collective-permute-start | bytes 3145736 | tf_op jit(solution)/shard_map/ppermute | solution.py:431
  113.9 33.1 %collective-permute-start.11 = (bf16[128,4096]{1,0:T(8,128)(2,1)}, bf16[128,4096]{1,0:T(8,128)(2,1)}, u32[]{:S(2)}, u32[]{:S(2)}) collective-permute-start(bf16[128,4096]{1,0:T(8,128)(2,1)} %get-tuple-element.49), channel_id=1, source_target_pairs={{1,0},{2,1},{3,2},{5,4},{6,5},{7,6},{9,8},{10,9},{11,10},{13,12},{... | collective-permute-start | bytes 3145736 | tf_op jit(solution)/shard_map/ppermute | solution.py:432
  128.0 39.8 %collective-permute-start.8 = (bf16[128,4096]{1,0:T(8,128)(2,1)}, bf16[128,4096]{1,0:T(8,128)(2,1)}, u32[]{:S(2)}, u32[]{:S(2)}) collective-permute-start(bf16[128,4096]{1,0:T(8,128)(2,1)} %get-tuple-element.47.refs_4_), channel_id=1, source_target_pairs={{0,1},{1,2},{2,3},{4,5},{5,6},{6,7},{8,9},{9,10},{10,11},{12,13},{... | collective-permute-start | bytes 3145736 | tf_op jit(solution)/shard_map/ppermute | solution.py:431
  130.6 38.8 %collective-permute-start.9 = (bf16[128,4096]{1,0:T(8,128)(2,1)}, bf16[128,4096]{1,0:T(8,128)(2,1)}, u32[]{:S(2)}, u32[]{:S(2)}) collective-permute-start(bf16[128,4096]{1,0:T(8,128)(2,1)} %get-tuple-element.48.refs_5_), channel_id=1, source_target_pairs={{1,0},{2,1},{3,2},{5,4},{6,5},{7,6},{9,8},{10,9},{11,10},{13,12},{... | collective-permute-start | bytes 3145736 | tf_op jit(solution)/shard_map/ppermute | solution.py:432
  150.7 39.5 %collective-permute-start.12 = (bf16[128,4096]{1,0:T(8,128)(2,1)}, bf16[128,4096]{1,0:T(8,128)(2,1)}, u32[]{:S(2)}, u32[]{:S(2)}) collective-permute-start(bf16[128,4096]{1,0:T(8,128)(2,1)} %get-tuple-element.51.refs_4_), channel_id=1, source_target_pairs={{0,1},{1,2},{2,3},{4,5},{5,6},{6,7},{8,9},{9,10},{10,11},{12,13},{... | collective-permute-start | bytes 3145736 | tf_op jit(solution)/shard_map/ppermute | solution.py:431
  153.4 38.5 %collective-permute-start.13 = (bf16[128,4096]{1,0:T(8,128)(2,1)}, bf16[128,4096]{1,0:T(8,128)(2,1)}, u32[]{:S(2)}, u32[]{:S(2)}) collective-permute-start(bf16[128,4096]{1,0:T(8,128)(2,1)} %get-tuple-element.52), channel_id=1, source_target_pairs={{1,0},{2,1},{3,2},{5,4},{6,5},{7,6},{9,8},{10,9},{11,10},{13,12},{... | collective-permute-start | bytes 3145736 | tf_op jit(solution)/shard_map/ppermute | solution.py:432
  172.9 59.9 %collective-permute-start.14 = (bf16[128,4096]{1,0:T(8,128)(2,1)}, bf16[128,4096]{1,0:T(8,128)(2,1)}, u32[]{:S(2)}, u32[]{:S(2)}) collective-permute-start(bf16[128,4096]{1,0:T(8,128)(2,1)} %get-tuple-element.54.refs_4_), channel_id=1, source_target_pairs={{0,1},{1,2},{2,3},{4,5},{5,6},{6,7},{8,9},{9,10},{10,11},{12,13},{... | collective-permute-start | bytes 3145736 | tf_op jit(solution)/shard_map/ppermute | solution.py:431
  175.6 57.2 %collective-permute-start.15 = (bf16[128,4096]{1,0:T(8,128)(2,1)}, bf16[128,4096]{1,0:T(8,128)(2,1)}, u32[]{:S(2)}, u32[]{:S(2)}) collective-permute-start(bf16[128,4096]{1,0:T(8,128)(2,1)} %get-tuple-element.55.refs_5_), channel_id=1, source_target_pairs={{1,0},{2,1},{3,2},{5,4},{6,5},{7,6},{9,8},{10,9},{11,10},{13,12},{... | collective-permute-start | bytes 3145736 | tf_op jit(solution)/shard_map/ppermute | solution.py:432
  207.8 37.4 %all-to-all-start.2 = ((bf16[4,128,1024]{2,1,0:T(8,128)(2,1)}), bf16[4,128,1024]{2,1,0:T(8,128)(2,1)}, u32[]{:S(2)}, u32[]{:S(2)}) async-start(bf16[4,128,1024]{2,1,0:T(8,128)(2,1)} %bitcast.17), calls=%async_computation.2 | async-start | bytes 2097152 | tf_op jit(solution)/shard_map/all_to_all | solution.py:424
  212.8 55.5 %collective-permute-start.16 = (bf16[128,4096]{1,0:T(8,128)(2,1)}, bf16[128,4096]{1,0:T(8,128)(2,1)}, u32[]{:S(2)}, u32[]{:S(2)}) collective-permute-start(bf16[128,4096]{1,0:T(8,128)(2,1)} %get-tuple-element.56.refs_9_), channel_id=1, source_target_pairs={{0,1},{1,2},{2,3},{4,5},{5,6},{6,7},{8,9},{9,10},{10,11},{12,13},{... | collective-permute-start | bytes 3145736 | tf_op jit(solution)/shard_map/ppermute | solution.py:431
  216.2 54.4 %collective-permute-start.17 = (bf16[128,4096]{1,0:T(8,128)(2,1)}, bf16[128,4096]{1,0:T(8,128)(2,1)}, u32[]{:S(2)}, u32[]{:S(2)}) collective-permute-start(bf16[128,4096]{1,0:T(8,128)(2,1)} %get-tuple-element.61), channel_id=1, source_target_pairs={{1,0},{2,1},{3,2},{5,4},{6,5},{7,6},{9,8},{10,9},{11,10},{13,12},{... | collective-permute-start | bytes 3145736 | tf_op jit(solution)/shard_map/ppermute | solution.py:432
  245.1 47.0 %all-to-all-start.3 = ((bf16[4,128,1024]{2,1,0:T(8,128)(2,1)}), bf16[4,128,1024]{2,1,0:T(8,128)(2,1)}, u32[]{:S(2)}, u32[]{:S(2)}) async-start(bf16[4,128,1024]{2,1,0:T(8,128)(2,1)} %bitcast.18), calls=%async_computation.3 | async-start | bytes 2097152 | tf_op jit(solution)/shard_map/all_to_all | solution.py:424
  275.2 37.0 %collective-permute-start.18 = (bf16[1,128,4096]{2,1,0:T(8,128)(2,1)}, bf16[1,128,4096]{2,1,0:T(8,128)(2,1)}, u32[]{:S(2)}, u32[]{:S(2)}) collective-permute-start(bf16[1,128,4096]{2,1,0:T(8,128)(2,1)} %finish.2.refs_4_.refs_0_), channel_id=1, source_target_pairs={{28,4},{24,8},{20,12},{12,20},{8,24},{4,28},{29,5},{25,9},{21,13},... | collective-permute-start | bytes 3145736 | tf_op jit(solution)/shard_map/ppermute | solution.py:542
  296.7 27.5 %collective-permute-start.22 = (bf16[1,128,4096]{2,1,0:T(8,128)(2,1)}, bf16[1,128,4096]{2,1,0:T(8,128)(2,1)}, u32[]{:S(2)}, u32[]{:S(2)}) collective-permute-start(bf16[1,128,4096]{2,1,0:T(8,128)(2,1)} %finish.3.refs_2_), channel_id=1, source_target_pairs={{4,0},{8,4},{12,8},{16,12},{20,16},{24,20},{28,24},{5,1},{9,5},{13... | collective-permute-start | bytes 3145736 | tf_op jit(solution)/shard_map/ppermute | solution.py:547
  315.8 3.9 %collective-permute-start.19 = (f32[1,32,128]{2,1,0:T(8,128)}, f32[1,32,128]{2,1,0:T(8,128)S(1)}, u32[]{:S(2)}, u32[]{:S(2)}) collective-permute-start(f32[1,32,128]{2,1,0:T(8,128)} %copy.12.refs_0_), channel_id=1, source_target_pairs={{0,1},{1,2},{2,3},{3,0},{4,5},{5,6},{6,7},{7,4},{8,9},{9,10},{10,1... | collective-permute-start | bytes 49160 | tf_op jit(solution)/shard_map/ppermute | solution.py:486
  316.8 4.8 %collective-permute-start.20 = (f32[1,32,128]{2,1,0:T(8,128)}, f32[1,32,128]{2,1,0:T(8,128)S(1)}, u32[]{:S(2)}, u32[]{:S(2)}) collective-permute-start(f32[1,32,128]{2,1,0:T(8,128)} %copy.12.refs_0_), channel_id=1, source_target_pairs={{0,2},{1,3},{2,0},{3,1},{4,6},{5,7},{6,4},{7,5},{8,10},{9,11},{10,... | collective-permute-start | bytes 49160 | tf_op jit(solution)/shard_map/ppermute | solution.py:486
  316.8 4.9 %collective-permute-start.21 = (f32[1,32,128]{2,1,0:T(8,128)}, f32[1,32,128]{2,1,0:T(8,128)S(1)}, u32[]{:S(2)}, u32[]{:S(2)}) collective-permute-start(f32[1,32,128]{2,1,0:T(8,128)} %copy.12.refs_0_), channel_id=1, source_target_pairs={{0,3},{1,0},{2,1},{3,2},{4,7},{5,4},{6,5},{7,6},{8,11},{9,8},{10,9... | collective-permute-start | bytes 49160 | tf_op jit(solution)/shard_map/ppermute | solution.py:486
  319.8 1.8 copy-start
  321.6 0.6 copy-start.1
  322.2 0.6 copy-start.2

commit v12 on v11

--- a/solution.py
+++ b/solution.py
@@ -546,7 +546,7 @@
     )
     down_passed = lax.ppermute(down_grad, "section", down_pairs)
     up_passed = settle(up_grad, up_came, after=(down_grad,))
-    taps = sum_all(copy(taps, after=(up_passed,)))
+    taps = sum_all(copy(taps, after=(down_grad,)), after=(up_passed,))
     down_passed = copy(down_passed, after=(taps,))
     return weight_grad[None], taps, down_passed, up_passed
 

time: 328 us -> 323 us (0.985); the launches traced: 326 us -> 317 us
  waiting for transfers between devices: 118 us -> 108 us
    ppermute x1, waiting for transfers between devices: 13.5 us -> 0.01 us  [per_device(): up_came = lax.ppermute(up_grad, 'section', up_pairs)]
    ppermute x1, waiting for transfers between devices: 0.01 us -> 7.64 us  [per_device(): down_passed = lax.ppermute(down_grad, 'section', down_pairs)]
    ppermute x3, waiting for transfers between devices: 3.38 us -> 0.01 us  [sum_all(): lax.ppermute(x, 'tensor', [(i, (i + s) % blocks) for i in range(blocks)])]
  transfers between devices with their start and end apart: 27 -> 27, of which waited for: 15 -> 13; matrix products, arithmetic and copies ran while one was open for 0% -> 0% of each run, Pallas kernels for 36% -> 37%
where the time goes in v12:
time: 323 us; the launch traced here: 317 us
  Pallas kernels  122 us (38%)
  waiting for transfers between devices  108 us (33%)
  starting transfers between devices  84.5 us (26%)
    pallas_call x22, Pallas kernels, call(): pl.pallas_call(body, in_specs=list(in_specs) + unread, out_shape=out_shap...  122 us
    ppermute x8, waiting for transfers between devices, both_ways(): lax.ppermute(right, 'tensor', onward)  77.9 us
    ppermute x8, starting transfers between devices, both_ways(): lax.ppermute(left, 'tensor', [(j, i) for i, j in onward])  29.6 us
    ppermute x8, starting transfers between devices, both_ways(): lax.ppermute(right, 'tensor', onward)  25 us
    all_to_all x4, starting transfers between devices, exchange(): return lax.all_to_all(x, 'tensor', split_axis=0, concat_axis=0, tiled=True)  20.4 us
    ppermute x1, waiting for transfers between devices, per_device(): up_xin = lax.ppermute(up_input[0], 'section', mirror)  13.8 us
    ppermute x8, waiting for transfers between devices, both_ways(): lax.ppermute(left, 'tensor', [(j, i) for i, j in onward])  9.08 us
    ppermute x1, waiting for transfers between devices, per_device(): down_passed = lax.ppermute(down_grad, 'section', down_pairs)  7.64 us
  transfers between devices with their start and end apart: 27, of which 13 were waited for; matrix products, arithmetic and copies ran while one was open for 0% of the time, Pallas kernels for 37%

profile of v12, /device:TPU:10, one launch (start us, length us, event | category | flops | bytes accessed | tf_op | source)
XLA Modules:
  0.0 316.6 jit_solution(9690616936644765557)
XLA Ops:
  3.6 5.3 %all-to-all-start = ((bf16[4,128,1024]{2,1,0:T(8,128)(2,1)}), bf16[4,128,1024]{2,1,0:T(8,128)(2,1)}, u32[]{:S(2)}, u32[]{:S(2)}) async-start(bf16[4,128,1024]{2,1,0:T(8,128)(2,1)} %get-tuple-element.34), calls=%async_computation | async-start | bytes 2097152 | tf_op jit(solution)/shard_map/all_to_all | solution.py:424
  12.7 3.4 %collective-permute-start.2 = (bf16[128,4096]{1,0:T(8,128)(2,1)}, bf16[128,4096]{1,0:T(8,128)(2,1)}, u32[]{:S(2)}, u32[]{:S(2)}) collective-permute-start(bf16[128,4096]{1,0:T(8,128)(2,1)} %get-tuple-element.36.refs_0_), channel_id=1, source_target_pairs={{1,0},{2,1},{3,2},{5,4},{6,5},{7,6},{9,8},{10,9},{11,10},{13,12},{... | collective-permute-start | bytes 3145736 | tf_op jit(solution)/shard_map/ppermute | solution.py:432
  17.9 3.9 %toeplitz.1 = (bf16[32,128,256]{2,1,0:T(8,128)(2,1)}, bf16[32,128,256]{2,1,0:T(8,128)(2,1)}) custom-call(f32[32,128]{1,0:T(8,128)} %bitcast.21), custom_call_target="tpu_custom_call" | custom-call | bytes 4210688 | tf_op jit(solution)/shard_map/toeplitz/pallas_call | solution.py:36
  21.8 13.8 %collective-permute-done.refs_0_ = bf16[128,4096]{1,0:T(8,128)(2,1)} collective-permute-done((bf16[128,4096]{1,0:T(8,128)(2,1)}, bf16[128,4096]{1,0:T(8,128)(2,1)}, u32[]{:S(2)}, u32[]{:S(2)}) %collective-permute-start) | collective-permute-done | bytes 1048608 | tf_op jit(solution)/shard_map/ppermute | solution.py:508
  37.8 5.1 %all-to-all-start.1 = ((bf16[4,128,1024]{2,1,0:T(8,128)(2,1)}), bf16[4,128,1024]{2,1,0:T(8,128)(2,1)}, u32[]{:S(2)}, u32[]{:S(2)}) async-start(bf16[4,128,1024]{2,1,0:T(8,128)(2,1)} %prepare.3.refs_3_), calls=%async_computation.1 | async-start | bytes 2097152 | tf_op jit(solution)/shard_map/all_to_all | solution.py:424
  42.9 23.7 %collective-permute-done.1.refs_2_.refs_0_.refs_1_ = bf16[128,4096]{1,0:T(8,128)(2,1)} collective-permute-done((bf16[128,4096]{1,0:T(8,128)(2,1)}, bf16[128,4096]{1,0:T(8,128)(2,1)}, u32[]{:S(2)}, u32[]{:S(2)}) %collective-permute-start.1) | collective-permute-done | bytes 1048608 | tf_op jit(solution)/shard_map/ppermute | solution.py:431
  69.4 4.4 %collective-permute-start.6 = (bf16[128,4096]{1,0:T(8,128)(2,1)}, bf16[128,4096]{1,0:T(8,128)(2,1)}, u32[]{:S(2)}, u32[]{:S(2)}) collective-permute-start(bf16[128,4096]{1,0:T(8,128)(2,1)} %grad_mix.1.refs_4_.refs_0_.refs_8_), channel_id=1, source_target_pairs={{0,1},{1,2},{2,3},{4,5},{5,6},{6,7},{8,9},{9,10},{10,11},{12,13},{... | collective-permute-start | bytes 3145736 | tf_op jit(solution)/shard_map/ppermute | solution.py:431
  76.2 10.9 %project.2 = (bf16[512,4096]{1,0:T(8,128)(2,1)}, bf16[128,4096]{1,0:T(8,128)(2,1)}, bf16[128,4096]{1,0:T(8,128)(2,1)}, bf16[128,4096]{1,0:T(8,128)(2,1)}, bf16[128,4096]{1,0:T(8,128)(2,1)}) custom-call(bf16[512,1024]{1,0:T(8,128)(2,1)} %bitcast.2.refs_0_, bf16[1024,4096]{1,0:T(8,128)(2,1)} %bitcast.22, bf16[32,128,256]{2,1,0:T(8,128)(2,1)} %get-tuple-element.37.refs_2_, ...), custom_call_target="tpu_custom_call" | custom-call | flops 5368709120 | bytes 19922944 | tf_op jit(solution)/shard_map/project/pallas_call | solution.py:36
  93.7 3.4 %collective-permute-start.5 = (bf16[128,4096]{1,0:T(8,128)(2,1)}, bf16[128,4096]{1,0:T(8,128)(2,1)}, u32[]{:S(2)}, u32[]{:S(2)}) collective-permute-start(bf16[128,4096]{1,0:T(8,128)(2,1)} %get-tuple-element.42.refs_4_.refs_5_), channel_id=1, source_target_pairs={{1,0},{2,1},{3,2},{5,4},{6,5},{7,6},{9,8},{10,9},{11,10},{13,12},{... | collective-permute-start | bytes 3145736 | tf_op jit(solution)/shard_map/ppermute | solution.py:432
  97.2 11.0 %project.3 = (bf16[512,4096]{1,0:T(8,128)(2,1)}, bf16[128,4096]{1,0:T(8,128)(2,1)}, bf16[128,4096]{1,0:T(8,128)(2,1)}, bf16[128,4096]{1,0:T(8,128)(2,1)}, bf16[128,4096]{1,0:T(8,128)(2,1)}) custom-call(bf16[512,1024]{1,0:T(8,128)(2,1)} %bitcast.5.refs_0_.refs_1_, bf16[1024,4096]{1,0:T(8,128)(2,1)} %bitcast.23, ...), custom_call_target="tpu_custom_call" | custom-call | flops 5368709120 | bytes 19922944 | tf_op jit(solution)/shard_map/project/pallas_call | solution.py:36
  113.9 4.4 %collective-permute-start.11 = (bf16[128,4096]{1,0:T(8,128)(2,1)}, bf16[128,4096]{1,0:T(8,128)(2,1)}, u32[]{:S(2)}, u32[]{:S(2)}) collective-permute-start(bf16[128,4096]{1,0:T(8,128)(2,1)} %get-tuple-element.49), channel_id=1, source_target_pairs={{1,0},{2,1},{3,2},{5,4},{6,5},{7,6},{9,8},{10,9},{11,10},{13,12},{... | collective-permute-start | bytes 3145736 | tf_op jit(solution)/shard_map/ppermute | solution.py:432
  118.3 4.6 %collective-permute-done.4.refs_0_.refs_2_ = bf16[128,4096]{1,0:T(8,128)(2,1)} collective-permute-done((bf16[128,4096]{1,0:T(8,128)(2,1)}, bf16[128,4096]{1,0:T(8,128)(2,1)}, u32[]{:S(2)}, u32[]{:S(2)}) %collective-permute-start.4) | collective-permute-done | bytes 1048608 | tf_op jit(solution)/shard_map/ppermute | solution.py:431
  124.5 3.4 %payload.8 = (bf16[128,4096]{1,0:T(8,128)(2,1)}, bf16[128,4096]{1,0:T(8,128)(2,1)}) custom-call(bf16[128,4096]{1,0:T(8,128)(2,1)} %collective-permute-done.4.refs_0_.refs_2_, bf16[128,4096]{1,0:T(8,128)(2,1)} %collective-permute-done.5.refs_1_.refs_5_, bf16[128,4096]{1,0:T(8,128)(2,1)} %get-tuple-element.43.refs_2_.refs_3_, ...), custom_call_target="tpu_custom_call" | custom-call | bytes 6291456 | tf_op jit(solution)/shard_map/payload/pallas_call | solution.py:36
  130.6 4.1 %collective-permute-start.9 = (bf16[128,4096]{1,0:T(8,128)(2,1)}, bf16[128,4096]{1,0:T(8,128)(2,1)}, u32[]{:S(2)}, u32[]{:S(2)}) collective-permute-start(bf16[128,4096]{1,0:T(8,128)(2,1)} %get-tuple-element.48.refs_5_), channel_id=1, source_target_pairs={{1,0},{2,1},{3,2},{5,4},{6,5},{7,6},{9,8},{10,9},{11,10},{13,12},{... | collective-permute-start | bytes 3145736 | tf_op jit(solution)/shard_map/ppermute | solution.py:432
  134.8 10.5 %collective-permute-done.10.refs_0_.refs_2_.refs_10_ = bf16[128,4096]{1,0:T(8,128)(2,1)} collective-permute-done((bf16[128,4096]{1,0:T(8,128)(2,1)}, bf16[128,4096]{1,0:T(8,128)(2,1)}, u32[]{:S(2)}, u32[]{:S(2)}) %collective-permute-start.10) | collective-permute-done | bytes 1048608 | tf_op jit(solution)/shard_map/ppermute | solution.py:431
  147.0 3.7 %payload.9 = (bf16[128,4096]{1,0:T(8,128)(2,1)}, bf16[128,4096]{1,0:T(8,128)(2,1)}) custom-call(bf16[128,4096]{1,0:T(8,128)(2,1)} %collective-permute-done.10.refs_0_.refs_2_.refs_10_, bf16[128,4096]{1,0:T(8,128)(2,1)} %collective-permute-done.11.refs_1_.refs_5_.refs_13_, bf16[128,4096]{1,0:T(8,128)(2,1)} %get-tuple-element.50.refs_2_.refs_3_, ...), custom_call_target="tpu_custom_call" | custom-call | bytes 6291456 | tf_op jit(solution)/shard_map/payload/pallas_call | solution.py:36
  153.4 4.1 %collective-permute-start.13 = (bf16[128,4096]{1,0:T(8,128)(2,1)}, bf16[128,4096]{1,0:T(8,128)(2,1)}, u32[]{:S(2)}, u32[]{:S(2)}) collective-permute-start(bf16[128,4096]{1,0:T(8,128)(2,1)} %get-tuple-element.52), channel_id=1, source_target_pairs={{1,0},{2,1},{3,2},{5,4},{6,5},{7,6},{9,8},{10,9},{11,10},{13,12},{... | collective-permute-start | bytes 3145736 | tf_op jit(solution)/shard_map/ppermute | solution.py:432
  157.5 10.3 %collective-permute-done.8.refs_0_.refs_3_ = bf16[128,4096]{1,0:T(8,128)(2,1)} collective-permute-done((bf16[128,4096]{1,0:T(8,128)(2,1)}, bf16[128,4096]{1,0:T(8,128)(2,1)}, u32[]{:S(2)}, u32[]{:S(2)}) %collective-permute-start.8) | collective-permute-done | bytes 1048608 | tf_op jit(solution)/shard_map/ppermute | solution.py:431
  175.6 4.1 %collective-permute-start.15 = (bf16[128,4096]{1,0:T(8,128)(2,1)}, bf16[128,4096]{1,0:T(8,128)(2,1)}, u32[]{:S(2)}, u32[]{:S(2)}) collective-permute-start(bf16[128,4096]{1,0:T(8,128)(2,1)} %get-tuple-element.55.refs_5_), channel_id=1, source_target_pairs={{1,0},{2,1},{3,2},{5,4},{6,5},{7,6},{9,8},{10,9},{11,10},{13,12},{... | collective-permute-start | bytes 3145736 | tf_op jit(solution)/shard_map/ppermute | solution.py:432
  179.7 10.6 %collective-permute-done.12.refs_0_.refs_3_.refs_11_ = bf16[128,4096]{1,0:T(8,128)(2,1)} collective-permute-done((bf16[128,4096]{1,0:T(8,128)(2,1)}, bf16[128,4096]{1,0:T(8,128)(2,1)}, u32[]{:S(2)}, u32[]{:S(2)}) %collective-permute-start.12) | collective-permute-done | bytes 1048608 | tf_op jit(solution)/shard_map/ppermute | solution.py:431
  195.4 12.4 %back.2 = (bf16[512,4096]{1,0:T(8,128)(2,1)}, bf16[512,1024]{1,0:T(8,128)(2,1)}) custom-call(bf16[128,4096]{1,0:T(8,128)(2,1)} %grad_mix.1.refs_4_.refs_0_.refs_8_, bf16[128,4096]{1,0:T(8,128)(2,1)} %collective-permute-done.6.refs_0_.refs_1_.refs_9_, bf16[128,4096]{1,0:T(8,128)(2,1)} %collective-permute-done.10.refs_0_.refs_2_.refs_10_, ...), custom_call_target="tpu_custom_call" | custom-call | flops 16106127360 | bytes 23068672 | tf_op jit(solution)/shard_map/back/pallas_call | solution.py:36
  207.8 5.1 %all-to-all-start.2 = ((bf16[4,128,1024]{2,1,0:T(8,128)(2,1)}), bf16[4,128,1024]{2,1,0:T(8,128)(2,1)}, u32[]{:S(2)}, u32[]{:S(2)}) async-start(bf16[4,128,1024]{2,1,0:T(8,128)(2,1)} %bitcast.17), calls=%async_computation.2 | async-start | bytes 2097152 | tf_op jit(solution)/shard_map/all_to_all | solution.py:424
  216.2 3.6 %collective-permute-start.17 = (bf16[128,4096]{1,0:T(8,128)(2,1)}, bf16[128,4096]{1,0:T(8,128)(2,1)}, u32[]{:S(2)}, u32[]{:S(2)}) collective-permute-start(bf16[128,4096]{1,0:T(8,128)(2,1)} %get-tuple-element.61), channel_id=1, source_target_pairs={{1,0},{2,1},{3,2},{5,4},{6,5},{7,6},{9,8},{10,9},{11,10},{13,12},{... | collective-permute-start | bytes 3145736 | tf_op jit(solution)/shard_map/ppermute | solution.py:432
  219.8 13.0 %filter_gradient.1 = f32[4,8,128]{2,1,0:T(8,128)} custom-call(bf16[128,4096]{1,0:T(8,128)(2,1)} %get-tuple-element.36.refs_0_, bf16[128,4096]{1,0:T(8,128)(2,1)} %collective-permute-done.1.refs_2_.refs_0_.refs_1_, bf16[128,4096]{1,0:T(8,128)(2,1)} %collective-permute-done.4.refs_0_.refs_2_, bf16[128,4096]{1,0:T(8,128)(2,1)} %collective-permute-done.8.refs_0_.refs_3_, ...), custom_call_target="tpu_custom_call" | custom-call | tf_op jit(solution)/shard_map/filter_gradient/pallas_call | solution.py:36
  232.8 12.3 %back.3 = (bf16[512,4096]{1,0:T(8,128)(2,1)}, bf16[512,1024]{1,0:T(8,128)(2,1)}) custom-call(bf16[128,4096]{1,0:T(8,128)(2,1)} %get-tuple-element.36.refs_0_, bf16[128,4096]{1,0:T(8,128)(2,1)} %collective-permute-done.1.refs_2_.refs_0_.refs_1_, bf16[128,4096]{1,0:T(8,128)(2,1)} %collective-permute-done.4.refs_0_.refs_2_, ...), custom_call_target="tpu_custom_call" | custom-call | flops 16106127360 | bytes 23068672 | tf_op jit(solution)/shard_map/back/pallas_call | solution.py:36
  245.1 5.0 %all-to-all-start.3 = ((bf16[4,128,1024]{2,1,0:T(8,128)(2,1)}), bf16[4,128,1024]{2,1,0:T(8,128)(2,1)}, u32[]{:S(2)}, u32[]{:S(2)}) async-start(bf16[4,128,1024]{2,1,0:T(8,128)(2,1)} %bitcast.18), calls=%async_computation.3 | async-start | bytes 2097152 | tf_op jit(solution)/shard_map/all_to_all | solution.py:424
  250.1 18.2 %collective-permute-done.16.refs_4_ = bf16[128,4096]{1,0:T(8,128)(2,1)} collective-permute-done((bf16[128,4096]{1,0:T(8,128)(2,1)}, bf16[128,4096]{1,0:T(8,128)(2,1)}, u32[]{:S(2)}, u32[]{:S(2)}) %collective-permute-start.16) | collective-permute-done | bytes 1048608 | tf_op jit(solution)/shard_map/ppermute | solution.py:431
  270.6 4.6 %finish.2.refs_4_.refs_0_ = bf16[1,128,4096]{2,1,0:T(8,128)(2,1)} custom-call(bf16[128,4096]{1,0:T(8,128)(2,1)} %collective-permute-done.refs_0_, bf16[128,4096]{1,0:T(8,128)(2,1)} %collective-permute-done.3.refs_1_, bf16[4,128,1024]{2,1,0:T(8,128)(2,1)} %all-to-all-done.2.refs_2_, bf16[128,4096]{1,0:T(8,128)(2,1)} %get-tuple-element.60.refs_3_, ...), custom_call_target="tpu_custom_call" | custom-call | bytes 7340032 | tf_op jit(solution)/shard_map/finish/pallas_call | solution.py:36
  275.2 3.4 %collective-permute-start.21 = (bf16[1,128,4096]{2,1,0:T(8,128)(2,1)}, bf16[1,128,4096]{2,1,0:T(8,128)(2,1)}, u32[]{:S(2)}, u32[]{:S(2)}) collective-permute-start(bf16[1,128,4096]{2,1,0:T(8,128)(2,1)} %finish.2.refs_4_.refs_0_), channel_id=1, source_target_pairs={{28,4},{24,8},{20,12},{12,20},{8,24},{4,28},{29,5},{25,9},{21,13},... | collective-permute-start | bytes 3145736 | tf_op jit(solution)/shard_map/ppermute | solution.py:542
  278.6 13.6 %weight_gradient.1.refs_6_ = bf16[1024,4096]{1,0:T(8,128)(2,1)} custom-call(bf16[512,1024]{1,0:T(8,128)(2,1)} %bitcast.2.refs_0_, bf16[512,1024]{1,0:T(8,128)(2,1)} %bitcast.5.refs_0_.refs_1_, bf16[512,4096]{1,0:T(8,128)(2,1)} %get-tuple-element.58.refs_6_.refs_2_, bf16[512,4096]{1,0:T(8,128)(2,1)} %get-tuple-element.57.refs_16_.refs_3_, ...), custom_call_target="tpu_custom_call" | custom-call | flops 8589934592 | bytes 18874368 | tf_op jit(solution)/shard_map/weight_gradient/pallas_call | solution.py:36
  292.2 4.6 %finish.3.refs_1_.refs_2_ = bf16[1,128,4096]{2,1,0:T(8,128)(2,1)} custom-call(bf16[128,4096]{1,0:T(8,128)(2,1)} %bitcast.14, bf16[128,4096]{1,0:T(8,128)(2,1)} %bitcast.16, bf16[4,128,1024]{2,1,0:T(8,128)(2,1)} %all-to-all-done.3.refs_2_, bf16[128,4096]{1,0:T(8,128)(2,1)} %get-tuple-element.63.refs_3_, ...), custom_call_target="tpu_custom_call" | custom-call | tf_op jit(solution)/shard_map/finish/pallas_call | solution.py:36
  307.0 7.6 %collective-permute-done.22.refs_0_ = bf16[1,128,4096]{2,1,0:T(8,128)(2,1)} collective-permute-done((bf16[1,128,4096]{2,1,0:T(8,128)(2,1)}, bf16[1,128,4096]{2,1,0:T(8,128)(2,1)}, u32[]{:S(2)}, u32[]{:S(2)}) %collective-permute-start.22) | collective-permute-done | bytes 1048608 | tf_op jit(solution)/shard_map/ppermute | solution.py:547
  (50 shorter events, 67.8 us)
Async XLA Ops:
  3.6 34.2 %all-to-all-start = ((bf16[4,128,1024]{2,1,0:T(8,128)(2,1)}), bf16[4,128,1024]{2,1,0:T(8,128)(2,1)}, u32[]{:S(2)}, u32[]{:S(2)}) async-start(bf16[4,128,1024]{2,1,0:T(8,128)(2,1)} %get-tuple-element.34), calls=%async_computation | async-start | bytes 2097152 | tf_op jit(solution)/shard_map/all_to_all | solution.py:424
  8.9 26.6 %collective-permute-start = (bf16[128,4096]{1,0:T(8,128)(2,1)}, bf16[128,4096]{1,0:T(8,128)(2,1)}, u32[]{:S(2)}, u32[]{:S(2)}) collective-permute-start(bf16[128,4096]{1,0:T(8,128)(2,1)} %bitcast.26), channel_id=1, source_target_pairs={{0,28},{4,24},{8,20},{12,16},{16,12},{20,8},{24,4},{28,0},{1,29},{... | collective-permute-start | bytes 3145736 | tf_op jit(solution)/shard_map/ppermute | solution.py:508
  9.3 57.3 %collective-permute-start.1 = (bf16[128,4096]{1,0:T(8,128)(2,1)}, bf16[128,4096]{1,0:T(8,128)(2,1)}, u32[]{:S(2)}, u32[]{:S(2)}) collective-permute-start(bf16[128,4096]{1,0:T(8,128)(2,1)} %get-tuple-element.36.refs_0_), channel_id=1, source_target_pairs={{0,1},{1,2},{2,3},{4,5},{5,6},{6,7},{8,9},{9,10},{10,11},{12,13},{... | collective-permute-start | bytes 3145736 | tf_op jit(solution)/shard_map/ppermute | solution.py:431
  12.7 53.9 %collective-permute-start.2 = (bf16[128,4096]{1,0:T(8,128)(2,1)}, bf16[128,4096]{1,0:T(8,128)(2,1)}, u32[]{:S(2)}, u32[]{:S(2)}) collective-permute-start(bf16[128,4096]{1,0:T(8,128)(2,1)} %get-tuple-element.36.refs_0_), channel_id=1, source_target_pairs={{1,0},{2,1},{3,2},{5,4},{6,5},{7,6},{9,8},{10,9},{11,10},{13,12},{... | collective-permute-start | bytes 3145736 | tf_op jit(solution)/shard_map/ppermute | solution.py:432
  16.1 50.5 %collective-permute-start.3 = (bf16[128,4096]{1,0:T(8,128)(2,1)}, bf16[128,4096]{1,0:T(8,128)(2,1)}, u32[]{:S(2)}, u32[]{:S(2)}) collective-permute-start(bf16[128,4096]{1,0:T(8,128)(2,1)} %bitcast.27), channel_id=1, source_target_pairs={{0,28},{4,24},{8,20},{12,16},{16,12},{20,8},{24,4},{28,0},{1,29},{... | collective-permute-start | bytes 3145736 | tf_op jit(solution)/shard_map/ppermute | solution.py:509
  37.8 59.3 %all-to-all-start.1 = ((bf16[4,128,1024]{2,1,0:T(8,128)(2,1)}), bf16[4,128,1024]{2,1,0:T(8,128)(2,1)}, u32[]{:S(2)}, u32[]{:S(2)}) async-start(bf16[4,128,1024]{2,1,0:T(8,128)(2,1)} %prepare.3.refs_3_), calls=%async_computation.1 | async-start | bytes 2097152 | tf_op jit(solution)/shard_map/all_to_all | solution.py:424
  69.4 38.8 %collective-permute-start.6 = (bf16[128,4096]{1,0:T(8,128)(2,1)}, bf16[128,4096]{1,0:T(8,128)(2,1)}, u32[]{:S(2)}, u32[]{:S(2)}) collective-permute-start(bf16[128,4096]{1,0:T(8,128)(2,1)} %grad_mix.1.refs_4_.refs_0_.refs_8_), channel_id=1, source_target_pairs={{0,1},{1,2},{2,3},{4,5},{5,6},{6,7},{8,9},{9,10},{10,11},{12,13},{... | collective-permute-start | bytes 3145736 | tf_op jit(solution)/shard_map/ppermute | solution.py:431
  73.8 34.4 %collective-permute-start.7 = (bf16[128,4096]{1,0:T(8,128)(2,1)}, bf16[128,4096]{1,0:T(8,128)(2,1)}, u32[]{:S(2)}, u32[]{:S(2)}) collective-permute-start(bf16[128,4096]{1,0:T(8,128)(2,1)} %grad_mix.1.refs_4_.refs_0_.refs_8_), channel_id=1, source_target_pairs={{1,0},{2,1},{3,2},{5,4},{6,5},{7,6},{9,8},{10,9},{11,10},{13,12},{... | collective-permute-start | bytes 3145736 | tf_op jit(solution)/shard_map/ppermute | solution.py:432
  90.3 32.5 %collective-permute-start.4 = (bf16[128,4096]{1,0:T(8,128)(2,1)}, bf16[128,4096]{1,0:T(8,128)(2,1)}, u32[]{:S(2)}, u32[]{:S(2)}) collective-permute-start(bf16[128,4096]{1,0:T(8,128)(2,1)} %get-tuple-element.41.refs_3_.refs_4_), channel_id=1, source_target_pairs={{0,1},{1,2},{2,3},{4,5},{5,6},{6,7},{8,9},{9,10},{10,11},{12,13},{... | collective-permute-start | bytes 3145736 | tf_op jit(solution)/shard_map/ppermute | solution.py:431
  93.7 30.8 %collective-permute-start.5 = (bf16[128,4096]{1,0:T(8,128)(2,1)}, bf16[128,4096]{1,0:T(8,128)(2,1)}, u32[]{:S(2)}, u32[]{:S(2)}) collective-permute-start(bf16[128,4096]{1,0:T(8,128)(2,1)} %get-tuple-element.42.refs_4_.refs_5_), channel_id=1, source_target_pairs={{1,0},{2,1},{3,2},{5,4},{6,5},{7,6},{9,8},{10,9},{11,10},{13,12},{... | collective-permute-start | bytes 3145736 | tf_op jit(solution)/shard_map/ppermute | solution.py:432
  111.5 33.9 %collective-permute-start.10 = (bf16[128,4096]{1,0:T(8,128)(2,1)}, bf16[128,4096]{1,0:T(8,128)(2,1)}, u32[]{:S(2)}, u32[]{:S(2)}) collective-permute-start(bf16[128,4096]{1,0:T(8,128)(2,1)} %get-tuple-element.46.refs_4_), channel_id=1, source_target_pairs={{0,1},{1,2},{2,3},{4,5},{5,6},{6,7},{8,9},{9,10},{10,11},{12,13},{... | collective-permute-start | bytes 3145736 | tf_op jit(solution)/shard_map/ppermute | solution.py:431
  113.9 33.1 %collective-permute-start.11 = (bf16[128,4096]{1,0:T(8,128)(2,1)}, bf16[128,4096]{1,0:T(8,128)(2,1)}, u32[]{:S(2)}, u32[]{:S(2)}) collective-permute-start(bf16[128,4096]{1,0:T(8,128)(2,1)} %get-tuple-element.49), channel_id=1, source_target_pairs={{1,0},{2,1},{3,2},{5,4},{6,5},{7,6},{9,8},{10,9},{11,10},{13,12},{... | collective-permute-start | bytes 3145736 | tf_op jit(solution)/shard_map/ppermute | solution.py:432
  128.0 39.8 %collective-permute-start.8 = (bf16[128,4096]{1,0:T(8,128)(2,1)}, bf16[128,4096]{1,0:T(8,128)(2,1)}, u32[]{:S(2)}, u32[]{:S(2)}) collective-permute-start(bf16[128,4096]{1,0:T(8,128)(2,1)} %get-tuple-element.47.refs_4_), channel_id=1, source_target_pairs={{0,1},{1,2},{2,3},{4,5},{5,6},{6,7},{8,9},{9,10},{10,11},{12,13},{... | collective-permute-start | bytes 3145736 | tf_op jit(solution)/shard_map/ppermute | solution.py:431
  130.6 38.8 %collective-permute-start.9 = (bf16[128,4096]{1,0:T(8,128)(2,1)}, bf16[128,4096]{1,0:T(8,128)(2,1)}, u32[]{:S(2)}, u32[]{:S(2)}) collective-permute-start(bf16[128,4096]{1,0:T(8,128)(2,1)} %get-tuple-element.48.refs_5_), channel_id=1, source_target_pairs={{1,0},{2,1},{3,2},{5,4},{6,5},{7,6},{9,8},{10,9},{11,10},{13,12},{... | collective-permute-start | bytes 3145736 | tf_op jit(solution)/shard_map/ppermute | solution.py:432
  150.7 39.5 %collective-permute-start.12 = (bf16[128,4096]{1,0:T(8,128)(2,1)}, bf16[128,4096]{1,0:T(8,128)(2,1)}, u32[]{:S(2)}, u32[]{:S(2)}) collective-permute-start(bf16[128,4096]{1,0:T(8,128)(2,1)} %get-tuple-element.51.refs_4_), channel_id=1, source_target_pairs={{0,1},{1,2},{2,3},{4,5},{5,6},{6,7},{8,9},{9,10},{10,11},{12,13},{... | collective-permute-start | bytes 3145736 | tf_op jit(solution)/shard_map/ppermute | solution.py:431
  153.4 38.5 %collective-permute-start.13 = (bf16[128,4096]{1,0:T(8,128)(2,1)}, bf16[128,4096]{1,0:T(8,128)(2,1)}, u32[]{:S(2)}, u32[]{:S(2)}) collective-permute-start(bf16[128,4096]{1,0:T(8,128)(2,1)} %get-tuple-element.52), channel_id=1, source_target_pairs={{1,0},{2,1},{3,2},{5,4},{6,5},{7,6},{9,8},{10,9},{11,10},{13,12},{... | collective-permute-start | bytes 3145736 | tf_op jit(solution)/shard_map/ppermute | solution.py:432
  172.9 59.9 %collective-permute-start.14 = (bf16[128,4096]{1,0:T(8,128)(2,1)}, bf16[128,4096]{1,0:T(8,128)(2,1)}, u32[]{:S(2)}, u32[]{:S(2)}) collective-permute-start(bf16[128,4096]{1,0:T(8,128)(2,1)} %get-tuple-element.54.refs_4_), channel_id=1, source_target_pairs={{0,1},{1,2},{2,3},{4,5},{5,6},{6,7},{8,9},{9,10},{10,11},{12,13},{... | collective-permute-start | bytes 3145736 | tf_op jit(solution)/shard_map/ppermute | solution.py:431
  175.6 57.2 %collective-permute-start.15 = (bf16[128,4096]{1,0:T(8,128)(2,1)}, bf16[128,4096]{1,0:T(8,128)(2,1)}, u32[]{:S(2)}, u32[]{:S(2)}) collective-permute-start(bf16[128,4096]{1,0:T(8,128)(2,1)} %get-tuple-element.55.refs_5_), channel_id=1, source_target_pairs={{1,0},{2,1},{3,2},{5,4},{6,5},{7,6},{9,8},{10,9},{11,10},{13,12},{... | collective-permute-start | bytes 3145736 | tf_op jit(solution)/shard_map/ppermute | solution.py:432
  207.8 37.4 %all-to-all-start.2 = ((bf16[4,128,1024]{2,1,0:T(8,128)(2,1)}), bf16[4,128,1024]{2,1,0:T(8,128)(2,1)}, u32[]{:S(2)}, u32[]{:S(2)}) async-start(bf16[4,128,1024]{2,1,0:T(8,128)(2,1)} %bitcast.17), calls=%async_computation.2 | async-start | bytes 2097152 | tf_op jit(solution)/shard_map/all_to_all | solution.py:424
  212.8 55.5 %collective-permute-start.16 = (bf16[128,4096]{1,0:T(8,128)(2,1)}, bf16[128,4096]{1,0:T(8,128)(2,1)}, u32[]{:S(2)}, u32[]{:S(2)}) collective-permute-start(bf16[128,4096]{1,0:T(8,128)(2,1)} %get-tuple-element.56.refs_9_), channel_id=1, source_target_pairs={{0,1},{1,2},{2,3},{4,5},{5,6},{6,7},{8,9},{9,10},{10,11},{12,13},{... | collective-permute-start | bytes 3145736 | tf_op jit(solution)/shard_map/ppermute | solution.py:431
  216.2 54.4 %collective-permute-start.17 = (bf16[128,4096]{1,0:T(8,128)(2,1)}, bf16[128,4096]{1,0:T(8,128)(2,1)}, u32[]{:S(2)}, u32[]{:S(2)}) collective-permute-start(bf16[128,4096]{1,0:T(8,128)(2,1)} %get-tuple-element.61), channel_id=1, source_target_pairs={{1,0},{2,1},{3,2},{5,4},{6,5},{7,6},{9,8},{10,9},{11,10},{13,12},{... | collective-permute-start | bytes 3145736 | tf_op jit(solution)/shard_map/ppermute | solution.py:432
  245.1 47.0 %all-to-all-start.3 = ((bf16[4,128,1024]{2,1,0:T(8,128)(2,1)}), bf16[4,128,1024]{2,1,0:T(8,128)(2,1)}, u32[]{:S(2)}, u32[]{:S(2)}) async-start(bf16[4,128,1024]{2,1,0:T(8,128)(2,1)} %bitcast.18), calls=%async_computation.3 | async-start | bytes 2097152 | tf_op jit(solution)/shard_map/all_to_all | solution.py:424
  275.2 26.8 %collective-permute-start.21 = (bf16[1,128,4096]{2,1,0:T(8,128)(2,1)}, bf16[1,128,4096]{2,1,0:T(8,128)(2,1)}, u32[]{:S(2)}, u32[]{:S(2)}) collective-permute-start(bf16[1,128,4096]{2,1,0:T(8,128)(2,1)} %finish.2.refs_4_.refs_0_), channel_id=1, source_target_pairs={{28,4},{24,8},{20,12},{12,20},{8,24},{4,28},{29,5},{25,9},{21,13},... | collective-permute-start | bytes 3145736 | tf_op jit(solution)/shard_map/ppermute | solution.py:542
  298.0 6.3 %collective-permute-start.18 = (f32[1,32,128]{2,1,0:T(8,128)}, f32[1,32,128]{2,1,0:T(8,128)S(1)}, u32[]{:S(2)}, u32[]{:S(2)}) collective-permute-start(f32[1,32,128]{2,1,0:T(8,128)} %copy.12.refs_0_), channel_id=1, source_target_pairs={{0,1},{1,2},{2,3},{3,0},{4,5},{5,6},{6,7},{7,4},{8,9},{9,10},{10,1... | collective-permute-start | bytes 49160 | tf_op jit(solution)/shard_map/ppermute | solution.py:486
  298.2 6.1 %collective-permute-start.19 = (f32[1,32,128]{2,1,0:T(8,128)}, f32[1,32,128]{2,1,0:T(8,128)S(1)}, u32[]{:S(2)}, u32[]{:S(2)}) collective-permute-start(f32[1,32,128]{2,1,0:T(8,128)} %copy.12.refs_0_), channel_id=1, source_target_pairs={{0,2},{1,3},{2,0},{3,1},{4,6},{5,7},{6,4},{7,5},{8,10},{9,11},{10,... | collective-permute-start | bytes 49160 | tf_op jit(solution)/shard_map/ppermute | solution.py:486
  298.3 6.1 %collective-permute-start.20 = (f32[1,32,128]{2,1,0:T(8,128)}, f32[1,32,128]{2,1,0:T(8,128)S(1)}, u32[]{:S(2)}, u32[]{:S(2)}) collective-permute-start(f32[1,32,128]{2,1,0:T(8,128)} %copy.12.refs_0_), channel_id=1, source_target_pairs={{0,3},{1,0},{2,1},{3,2},{4,7},{5,4},{6,5},{7,6},{8,11},{9,8},{10,9... | collective-permute-start | bytes 49160 | tf_op jit(solution)/shard_map/ppermute | solution.py:486
  300.1 14.5 %collective-permute-start.22 = (bf16[1,128,4096]{2,1,0:T(8,128)(2,1)}, bf16[1,128,4096]{2,1,0:T(8,128)(2,1)}, u32[]{:S(2)}, u32[]{:S(2)}) collective-permute-start(bf16[1,128,4096]{2,1,0:T(8,128)(2,1)} %finish.3.refs_1_.refs_2_), channel_id=1, source_target_pairs={{4,0},{8,4},{12,8},{16,12},{20,16},{24,20},{28,24},{5,1},{9,5},{13... | collective-permute-start | bytes 3145736 | tf_op jit(solution)/shard_map/ppermute | solution.py:547
  304.4 0.6 copy-start
  304.4 0.6 copy-start.1
  305.0 0.6 copy-start.2

commit v13 on v9

--- a/solution.py
+++ b/solution.py
@@ -517,10 +517,10 @@
     up_g, up_back = back(up_mixes, weight, ahead, after=sent)
     up_back = exchange(up_back)
     down_mixes = list_blocks(down_mix, down_arrivals)
-    down_g, down_back = back(down_mixes, weight, ahead, after=(up_g, *up_arrivals[-1]))
+    sent = payload(blocks, down_arrivals[-1], down_pieces, after=(up_g,))
+    down_arrivals.append(both_ways(*sent))
+    down_g, down_back = back(down_mixes, weight, ahead, after=(sent[0], *up_arrivals[-1]))
     down_back = exchange(down_back)
-    sent = payload(blocks, down_arrivals[-1], down_pieces, after=(down_g,))
-    down_arrivals.append(both_ways(*sent))
     _, down_conv = sort_arrivals(down_mix, down_pieces, down_arrivals)
     up_grad = finish(up_xin, up_cot, up_conv, up_back, after=(down_g, *sent))
     up_passed = lax.ppermute(up_grad, "section", up_pairs)

time: 323 us -> 322 us (level)
    ppermute x8, waiting for transfers between devices: 24.9 us -> 70.8 us  [both_ways(): lax.ppermute(right, 'tensor', onward)]
    ppermute x8, waiting for transfers between devices: 51.3 us -> 17 us  [both_ways(): lax.ppermute(left, 'tensor', [(j, i) for i, j in onward])]
    ppermute x1, waiting for transfers between devices: 14.6 us -> 0.01 us  [per_device(): up_cot = lax.ppermute(up_cot[0], 'section', mirror)]
    ppermute x8, starting transfers between devices: 21.2 us -> 29.7 us  [both_ways(): lax.ppermute(left, 'tensor', [(j, i) for i, j in onward])]
    ppermute x8, starting transfers between devices: 29.8 us -> 24.8 us  [both_ways(): lax.ppermute(right, 'tensor', onward)]
  transfers between devices with their start and end apart: 27 -> 27, of which waited for: 15 -> 18; matrix products, arithmetic and copies ran while one was open for 0% -> 0% of each run, Pallas kernels for 34% -> 34%
where the time goes in v13:
time: 322 us; the launch traced here: 319 us
  Pallas kernels  118 us (37%)
  waiting for transfers between devices  110 us (34%)
  starting transfers between devices  86.5 us (27%)
  local copies, waits for them, and re-layouts  3.24 us (1%)
    pallas_call x20, Pallas kernels, call(): pl.pallas_call(body, in_specs=list(in_specs) + unread, out_shape=out_shap...  118 us
    ppermute x8, waiting for transfers between devices, both_ways(): lax.ppermute(right, 'tensor', onward)  70.8 us
    ppermute x8, starting transfers between devices, both_ways(): lax.ppermute(left, 'tensor', [(j, i) for i, j in onward])  29.7 us
    ppermute x8, starting transfers between devices, both_ways(): lax.ppermute(right, 'tensor', onward)  24.8 us
    all_to_all x4, starting transfers between devices, exchange(): return lax.all_to_all(x, 'tensor', split_axis=0, concat_axis=0, tiled=True)  22.4 us
    ppermute x8, waiting for transfers between devices, both_ways(): lax.ppermute(left, 'tensor', [(j, i) for i, j in onward])  17 us
    ppermute x1, waiting for transfers between devices, per_device(): up_xin = lax.ppermute(up_input[0], 'section', mirror)  13.9 us
  transfers between devices with their start and end apart: 27, of which 18 were waited for; matrix products, arithmetic and copies ran while one was open for 0% of the time, Pallas kernels for 34%

profile of v13, /device:TPU:10, one launch (start us, length us, event | category | flops | bytes accessed | tf_op | source)
XLA Modules:
  0.0 318.9 jit_solution(14487452300792283365)
XLA Ops:
  3.6 5.3 %all-to-all-start = ((bf16[4,128,1024]{2,1,0:T(8,128)(2,1)}), bf16[4,128,1024]{2,1,0:T(8,128)(2,1)}, u32[]{:S(2)}, u32[]{:S(2)}) async-start(bf16[4,128,1024]{2,1,0:T(8,128)(2,1)} %get-tuple-element.34), calls=%async_computation | async-start | bytes 2097152 | tf_op jit(solution)/shard_map/all_to_all | solution.py:403
  12.7 3.4 %collective-permute-start.2 = (bf16[128,4096]{1,0:T(8,128)(2,1)}, bf16[128,4096]{1,0:T(8,128)(2,1)}, u32[]{:S(2)}, u32[]{:S(2)}) collective-permute-start(bf16[128,4096]{1,0:T(8,128)(2,1)} %get-tuple-element.36.refs_0_), channel_id=1, source_target_pairs={{1,0},{2,1},{3,2},{5,4},{6,5},{7,6},{9,8},{10,9},{11,10},{13,12},{... | collective-permute-start | bytes 3145736 | tf_op jit(solution)/shard_map/ppermute | solution.py:411
  17.9 3.8 %toeplitz.1 = (bf16[32,128,256]{2,1,0:T(8,128)(2,1)}, bf16[32,128,256]{2,1,0:T(8,128)(2,1)}) custom-call(f32[32,128]{1,0:T(8,128)} %bitcast.24), custom_call_target="tpu_custom_call" | custom-call | bytes 4210688 | tf_op jit(solution)/shard_map/toeplitz/pallas_call | solution.py:36
  21.7 13.9 %collective-permute-done.refs_0_ = bf16[128,4096]{1,0:T(8,128)(2,1)} collective-permute-done((bf16[128,4096]{1,0:T(8,128)(2,1)}, bf16[128,4096]{1,0:T(8,128)(2,1)}, u32[]{:S(2)}, u32[]{:S(2)}) %collective-permute-start) | collective-permute-done | bytes 1048608 | tf_op jit(solution)/shard_map/ppermute | solution.py:492
  37.9 5.1 %all-to-all-start.1 = ((bf16[4,128,1024]{2,1,0:T(8,128)(2,1)}), bf16[4,128,1024]{2,1,0:T(8,128)(2,1)}, u32[]{:S(2)}, u32[]{:S(2)}) async-start(bf16[4,128,1024]{2,1,0:T(8,128)(2,1)} %prepare.3.refs_3_), calls=%async_computation.1 | async-start | bytes 2097152 | tf_op jit(solution)/shard_map/all_to_all | solution.py:403
  43.0 23.6 %collective-permute-done.1.refs_2_.refs_0_.refs_1_ = bf16[128,4096]{1,0:T(8,128)(2,1)} collective-permute-done((bf16[128,4096]{1,0:T(8,128)(2,1)}, bf16[128,4096]{1,0:T(8,128)(2,1)}, u32[]{:S(2)}, u32[]{:S(2)}) %collective-permute-start.1) | collective-permute-done | bytes 1048608 | tf_op jit(solution)/shard_map/ppermute | solution.py:410
  69.4 4.4 %collective-permute-start.6 = (bf16[128,4096]{1,0:T(8,128)(2,1)}, bf16[128,4096]{1,0:T(8,128)(2,1)}, u32[]{:S(2)}, u32[]{:S(2)}) collective-permute-start(bf16[128,4096]{1,0:T(8,128)(2,1)} %grad_mix.1.refs_4_.refs_0_.refs_8_), channel_id=1, source_target_pairs={{0,1},{1,2},{2,3},{4,5},{5,6},{6,7},{8,9},{9,10},{10,11},{12,13},{... | collective-permute-start | bytes 3145736 | tf_op jit(solution)/shard_map/ppermute | solution.py:410
  76.2 10.9 %project.2 = (bf16[512,4096]{1,0:T(8,128)(2,1)}, bf16[128,4096]{1,0:T(8,128)(2,1)}, bf16[128,4096]{1,0:T(8,128)(2,1)}, bf16[128,4096]{1,0:T(8,128)(2,1)}, bf16[128,4096]{1,0:T(8,128)(2,1)}) custom-call(bf16[512,1024]{1,0:T(8,128)(2,1)} %bitcast.2.refs_0_, bf16[1024,4096]{1,0:T(8,128)(2,1)} %bitcast.25, bf16[32,128,256]{2,1,0:T(8,128)(2,1)} %get-tuple-element.37.refs_2_, ...), custom_call_target="tpu_custom_call" | custom-call | flops 5368709120 | bytes 19922944 | tf_op jit(solution)/shard_map/project/pallas_call | solution.py:36
  93.7 3.4 %collective-permute-start.5 = (bf16[128,4096]{1,0:T(8,128)(2,1)}, bf16[128,4096]{1,0:T(8,128)(2,1)}, u32[]{:S(2)}, u32[]{:S(2)}) collective-permute-start(bf16[128,4096]{1,0:T(8,128)(2,1)} %get-tuple-element.42.refs_4_.refs_5_), channel_id=1, source_target_pairs={{1,0},{2,1},{3,2},{5,4},{6,5},{7,6},{9,8},{10,9},{11,10},{13,12},{... | collective-permute-start | bytes 3145736 | tf_op jit(solution)/shard_map/ppermute | solution.py:411
  97.2 10.9 %project.3 = (bf16[512,4096]{1,0:T(8,128)(2,1)}, bf16[128,4096]{1,0:T(8,128)(2,1)}, bf16[128,4096]{1,0:T(8,128)(2,1)}, bf16[128,4096]{1,0:T(8,128)(2,1)}, bf16[128,4096]{1,0:T(8,128)(2,1)}) custom-call(bf16[512,1024]{1,0:T(8,128)(2,1)} %bitcast.5.refs_0_.refs_1_, bf16[1024,4096]{1,0:T(8,128)(2,1)} %bitcast.26, ...), custom_call_target="tpu_custom_call" | custom-call | flops 5368709120 | bytes 19922944 | tf_op jit(solution)/shard_map/project/pallas_call | solution.py:36
  113.8 4.4 %collective-permute-start.11 = (bf16[128,4096]{1,0:T(8,128)(2,1)}, bf16[128,4096]{1,0:T(8,128)(2,1)}, u32[]{:S(2)}, u32[]{:S(2)}) collective-permute-start(bf16[128,4096]{1,0:T(8,128)(2,1)} %get-tuple-element.49), channel_id=1, source_target_pairs={{1,0},{2,1},{3,2},{5,4},{6,5},{7,6},{9,8},{10,9},{11,10},{13,12},{... | collective-permute-start | bytes 3145736 | tf_op jit(solution)/shard_map/ppermute | solution.py:411
  118.2 4.7 %collective-permute-done.4.refs_0_.refs_2_ = bf16[128,4096]{1,0:T(8,128)(2,1)} collective-permute-done((bf16[128,4096]{1,0:T(8,128)(2,1)}, bf16[128,4096]{1,0:T(8,128)(2,1)}, u32[]{:S(2)}, u32[]{:S(2)}) %collective-permute-start.4) | collective-permute-done | bytes 1048608 | tf_op jit(solution)/shard_map/ppermute | solution.py:410
  124.5 3.6 %payload.8 = (bf16[128,4096]{1,0:T(8,128)(2,1)}, bf16[128,4096]{1,0:T(8,128)(2,1)}) custom-call(bf16[128,4096]{1,0:T(8,128)(2,1)} %collective-permute-done.4.refs_0_.refs_2_, bf16[128,4096]{1,0:T(8,128)(2,1)} %collective-permute-done.5.refs_1_.refs_5_, bf16[128,4096]{1,0:T(8,128)(2,1)} %get-tuple-element.43.refs_2_.refs_3_, ...), custom_call_target="tpu_custom_call" | custom-call | bytes 6291456 | tf_op jit(solution)/shard_map/payload/pallas_call | solution.py:36
  130.9 4.2 %collective-permute-start.9 = (bf16[128,4096]{1,0:T(8,128)(2,1)}, bf16[128,4096]{1,0:T(8,128)(2,1)}, u32[]{:S(2)}, u32[]{:S(2)}) collective-permute-start(bf16[128,4096]{1,0:T(8,128)(2,1)} %get-tuple-element.48.refs_5_), channel_id=1, source_target_pairs={{1,0},{2,1},{3,2},{5,4},{6,5},{7,6},{9,8},{10,9},{11,10},{13,12},{... | collective-permute-start | bytes 3145736 | tf_op jit(solution)/shard_map/ppermute | solution.py:411
  135.0 10.3 %collective-permute-done.10.refs_0_.refs_2_.refs_10_ = bf16[128,4096]{1,0:T(8,128)(2,1)} collective-permute-done((bf16[128,4096]{1,0:T(8,128)(2,1)}, bf16[128,4096]{1,0:T(8,128)(2,1)}, u32[]{:S(2)}, u32[]{:S(2)}) %collective-permute-start.10) | collective-permute-done | bytes 1048608 | tf_op jit(solution)/shard_map/ppermute | solution.py:410
  147.0 3.6 %payload.9 = (bf16[128,4096]{1,0:T(8,128)(2,1)}, bf16[128,4096]{1,0:T(8,128)(2,1)}) custom-call(bf16[128,4096]{1,0:T(8,128)(2,1)} %collective-permute-done.10.refs_0_.refs_2_.refs_10_, bf16[128,4096]{1,0:T(8,128)(2,1)} %collective-permute-done.11.refs_1_.refs_5_.refs_13_, bf16[128,4096]{1,0:T(8,128)(2,1)} %get-tuple-element.50.refs_2_.refs_3_, ...), custom_call_target="tpu_custom_call" | custom-call | bytes 6291456 | tf_op jit(solution)/shard_map/payload/pallas_call | solution.py:36
  153.3 4.1 %collective-permute-start.13 = (bf16[128,4096]{1,0:T(8,128)(2,1)}, bf16[128,4096]{1,0:T(8,128)(2,1)}, u32[]{:S(2)}, u32[]{:S(2)}) collective-permute-start(bf16[128,4096]{1,0:T(8,128)(2,1)} %get-tuple-element.52), channel_id=1, source_target_pairs={{1,0},{2,1},{3,2},{5,4},{6,5},{7,6},{9,8},{10,9},{11,10},{13,12},{... | collective-permute-start | bytes 3145736 | tf_op jit(solution)/shard_map/ppermute | solution.py:411
  157.5 10.3 %collective-permute-done.8.refs_5_.refs_0_.refs_3_ = bf16[128,4096]{1,0:T(8,128)(2,1)} collective-permute-done((bf16[128,4096]{1,0:T(8,128)(2,1)}, bf16[128,4096]{1,0:T(8,128)(2,1)}, u32[]{:S(2)}, u32[]{:S(2)}) %collective-permute-start.8) | collective-permute-done | bytes 1048608 | tf_op jit(solution)/shard_map/ppermute | solution.py:410
  169.5 19.3 %collective-permute-done.12.refs_0_.refs_3_.refs_11_ = bf16[128,4096]{1,0:T(8,128)(2,1)} collective-permute-done((bf16[128,4096]{1,0:T(8,128)(2,1)}, bf16[128,4096]{1,0:T(8,128)(2,1)}, u32[]{:S(2)}, u32[]{:S(2)}) %collective-permute-start.12) | collective-permute-done | bytes 1048608 | tf_op jit(solution)/shard_map/ppermute | solution.py:410
  190.7 3.4 %payload.10 = (bf16[128,4096]{1,0:T(8,128)(2,1)}, bf16[128,4096]{1,0:T(8,128)(2,1)}) custom-call(bf16[128,4096]{1,0:T(8,128)(2,1)} %collective-permute-done.12.refs_0_.refs_3_.refs_11_, bf16[128,4096]{1,0:T(8,128)(2,1)} %collective-permute-done.13.refs_1_.refs_6_.refs_14_, bf16[128,4096]{1,0:T(8,128)(2,1)} %get-tuple-element.45.refs_3_.refs_2_, ...), custom_call_target="tpu_custom_call" | custom-call | bytes 6291456 | tf_op jit(solution)/shard_map/payload/pallas_call | solution.py:36
  196.6 4.3 %collective-permute-start.15 = (bf16[128,4096]{1,0:T(8,128)(2,1)}, bf16[128,4096]{1,0:T(8,128)(2,1)}, u32[]{:S(2)}, u32[]{:S(2)}) collective-permute-start(bf16[128,4096]{1,0:T(8,128)(2,1)} %get-tuple-element.54.refs_10_), channel_id=1, source_target_pairs={{1,0},{2,1},{3,2},{5,4},{6,5},{7,6},{9,8},{10,9},{11,10},{13,12},{... | collective-permute-start | bytes 3145736 | tf_op jit(solution)/shard_map/ppermute | solution.py:411
  201.0 12.4 %back.2 = (bf16[512,4096]{1,0:T(8,128)(2,1)}, bf16[512,1024]{1,0:T(8,128)(2,1)}) custom-call(bf16[128,4096]{1,0:T(8,128)(2,1)} %grad_mix.1.refs_4_.refs_0_.refs_8_, bf16[128,4096]{1,0:T(8,128)(2,1)} %collective-permute-done.6.refs_0_.refs_1_.refs_9_, bf16[128,4096]{1,0:T(8,128)(2,1)} %collective-permute-done.10.refs_0_.refs_2_.refs_10_, ...), custom_call_target="tpu_custom_call" | custom-call | flops 16106127360 | bytes 23068672 | tf_op jit(solution)/shard_map/back/pallas_call | solution.py:36
  213.4 4.4 %all-to-all-start.2 = ((bf16[4,128,1024]{2,1,0:T(8,128)(2,1)}), bf16[4,128,1024]{2,1,0:T(8,128)(2,1)}, u32[]{:S(2)}, u32[]{:S(2)}) async-start(bf16[4,128,1024]{2,1,0:T(8,128)(2,1)} %bitcast.18), calls=%async_computation.2 | async-start | bytes 2097152 | tf_op jit(solution)/shard_map/all_to_all | solution.py:403
  217.8 3.5 %payload.11 = (bf16[128,4096]{1,0:T(8,128)(2,1)}, bf16[128,4096]{1,0:T(8,128)(2,1)}) custom-call(bf16[128,4096]{1,0:T(8,128)(2,1)} %collective-permute-done.8.refs_5_.refs_0_.refs_3_, bf16[128,4096]{1,0:T(8,128)(2,1)} %collective-permute-done.9.refs_6_.refs_1_, bf16[128,4096]{1,0:T(8,128)(2,1)} %get-tuple-element.39.refs_3_.refs_2_, ...), custom_call_target="tpu_custom_call" | custom-call | bytes 6291456 | tf_op jit(solution)/shard_map/payload/pallas_call | solution.py:36
  222.4 8.1 %collective-permute-done.15.refs_11_.refs_5_ = bf16[128,4096]{1,0:T(8,128)(2,1)} collective-permute-done((bf16[128,4096]{1,0:T(8,128)(2,1)}, bf16[128,4096]{1,0:T(8,128)(2,1)}, u32[]{:S(2)}, u32[]{:S(2)}) %collective-permute-start.15) | collective-permute-done | bytes 1048608 | tf_op jit(solution)/shard_map/ppermute | solution.py:411
  230.6 12.3 %back.3 = (bf16[512,4096]{1,0:T(8,128)(2,1)}, bf16[512,1024]{1,0:T(8,128)(2,1)}) custom-call(bf16[128,4096]{1,0:T(8,128)(2,1)} %get-tuple-element.36.refs_0_, bf16[128,4096]{1,0:T(8,128)(2,1)} %collective-permute-done.1.refs_2_.refs_0_.refs_1_, bf16[128,4096]{1,0:T(8,128)(2,1)} %collective-permute-done.4.refs_0_.refs_2_, ...), custom_call_target="tpu_custom_call" | custom-call | flops 16106127360 | bytes 23068672 | tf_op jit(solution)/shard_map/back/pallas_call | solution.py:36
  242.9 7.5 %all-to-all-start.3 = ((bf16[4,128,1024]{2,1,0:T(8,128)(2,1)}), bf16[4,128,1024]{2,1,0:T(8,128)(2,1)}, u32[]{:S(2)}, u32[]{:S(2)}) async-start(bf16[4,128,1024]{2,1,0:T(8,128)(2,1)} %bitcast.17), calls=%async_computation.3 | async-start | bytes 2097152 | tf_op jit(solution)/shard_map/all_to_all | solution.py:403
  257.2 4.6 %finish.2.refs_16_.refs_0_ = bf16[1,128,4096]{2,1,0:T(8,128)(2,1)} custom-call(bf16[128,4096]{1,0:T(8,128)(2,1)} %collective-permute-done.refs_0_, bf16[128,4096]{1,0:T(8,128)(2,1)} %collective-permute-done.3.refs_1_, bf16[4,128,1024]{2,1,0:T(8,128)(2,1)} %all-to-all-done.2.refs_2_, bf16[128,4096]{1,0:T(8,128)(2,1)} %get-tuple-element.60.refs_3_, ...), custom_call_target="tpu_custom_call" | custom-call | bytes 7340032 | tf_op jit(solution)/shard_map/finish/pallas_call | solution.py:36
  265.2 13.0 %filter_gradient.1 = f32[4,8,128]{2,1,0:T(8,128)} custom-call(bf16[128,4096]{1,0:T(8,128)(2,1)} %get-tuple-element.36.refs_0_, bf16[128,4096]{1,0:T(8,128)(2,1)} %collective-permute-done.1.refs_2_.refs_0_.refs_1_, bf16[128,4096]{1,0:T(8,128)(2,1)} %collective-permute-done.4.refs_0_.refs_2_, bf16[128,4096]{1,0:T(8,128)(2,1)} %collective-permute-done.8.refs_5_.refs_0_.refs_3_, ...), custom_call_target="tpu_custom_call" | custom-call | tf_op jit(solution)/shard_map/filter_gradient/pallas_call | solution.py:36
  278.2 13.6 %weight_gradient.1.refs_2_ = bf16[1024,4096]{1,0:T(8,128)(2,1)} custom-call(bf16[512,1024]{1,0:T(8,128)(2,1)} %bitcast.2.refs_0_, bf16[512,1024]{1,0:T(8,128)(2,1)} %bitcast.5.refs_0_.refs_1_, bf16[512,4096]{1,0:T(8,128)(2,1)} %get-tuple-element.57.refs_6_.refs_2_, bf16[512,4096]{1,0:T(8,128)(2,1)} %get-tuple-element.55.refs_4_.refs_3_, f32[1,32,128]{2,1,0:T(8,128)} %bitcast.19), custom_call_target="tpu_custom_call" | custom-call | tf_op jit(solution)/shard_map/weight_gradient/pallas_call | solution.py:36
  297.5 4.6 %finish.3.refs_4_ = bf16[1,128,4096]{2,1,0:T(8,128)(2,1)} custom-call(bf16[128,4096]{1,0:T(8,128)(2,1)} %bitcast.14, bf16[128,4096]{1,0:T(8,128)(2,1)} %bitcast.16, bf16[4,128,1024]{2,1,0:T(8,128)(2,1)} %all-to-all-done.3.refs_2_, bf16[128,4096]{1,0:T(8,128)(2,1)} %get-tuple-element.63.refs_3_, bf16[128,4096]{1,0:T(8,128)(2,1)} %collective-permute-done.19.refs_3_.refs_4_, ...), custom_call_target="tpu_custom_call" | custom-call | bytes 7340032 | tf_op jit(solution)/shard_map/finish/pallas_call | solution.py:36
  311.9 4.7 %collective-permute-done.22 = bf16[1,128,4096]{2,1,0:T(8,128)(2,1)} collective-permute-done((bf16[1,128,4096]{2,1,0:T(8,128)(2,1)}, bf16[1,128,4096]{2,1,0:T(8,128)(2,1)}, u32[]{:S(2)}, u32[]{:S(2)}) %collective-permute-start.22) | collective-permute-done | bytes 1048608 | tf_op jit(solution)/shard_map/ppermute | solution.py:533
  (51 shorter events, 72.3 us)
Async XLA Ops:
  3.6 34.2 %all-to-all-start = ((bf16[4,128,1024]{2,1,0:T(8,128)(2,1)}), bf16[4,128,1024]{2,1,0:T(8,128)(2,1)}, u32[]{:S(2)}, u32[]{:S(2)}) async-start(bf16[4,128,1024]{2,1,0:T(8,128)(2,1)} %get-tuple-element.34), calls=%async_computation | async-start | bytes 2097152 | tf_op jit(solution)/shard_map/all_to_all | solution.py:403
  8.9 26.6 %collective-permute-start = (bf16[128,4096]{1,0:T(8,128)(2,1)}, bf16[128,4096]{1,0:T(8,128)(2,1)}, u32[]{:S(2)}, u32[]{:S(2)}) collective-permute-start(bf16[128,4096]{1,0:T(8,128)(2,1)} %bitcast.29), channel_id=1, source_target_pairs={{0,28},{4,24},{8,20},{12,16},{16,12},{20,8},{24,4},{28,0},{1,29},{... | collective-permute-start | bytes 3145736 | tf_op jit(solution)/shard_map/ppermute | solution.py:492
  9.3 57.3 %collective-permute-start.1 = (bf16[128,4096]{1,0:T(8,128)(2,1)}, bf16[128,4096]{1,0:T(8,128)(2,1)}, u32[]{:S(2)}, u32[]{:S(2)}) collective-permute-start(bf16[128,4096]{1,0:T(8,128)(2,1)} %get-tuple-element.36.refs_0_), channel_id=1, source_target_pairs={{0,1},{1,2},{2,3},{4,5},{5,6},{6,7},{8,9},{9,10},{10,11},{12,13},{... | collective-permute-start | bytes 3145736 | tf_op jit(solution)/shard_map/ppermute | solution.py:410
  12.7 53.9 %collective-permute-start.2 = (bf16[128,4096]{1,0:T(8,128)(2,1)}, bf16[128,4096]{1,0:T(8,128)(2,1)}, u32[]{:S(2)}, u32[]{:S(2)}) collective-permute-start(bf16[128,4096]{1,0:T(8,128)(2,1)} %get-tuple-element.36.refs_0_), channel_id=1, source_target_pairs={{1,0},{2,1},{3,2},{5,4},{6,5},{7,6},{9,8},{10,9},{11,10},{13,12},{... | collective-permute-start | bytes 3145736 | tf_op jit(solution)/shard_map/ppermute | solution.py:411
  16.1 50.5 %collective-permute-start.3 = (bf16[128,4096]{1,0:T(8,128)(2,1)}, bf16[128,4096]{1,0:T(8,128)(2,1)}, u32[]{:S(2)}, u32[]{:S(2)}) collective-permute-start(bf16[128,4096]{1,0:T(8,128)(2,1)} %bitcast.30), channel_id=1, source_target_pairs={{0,28},{4,24},{8,20},{12,16},{16,12},{20,8},{24,4},{28,0},{1,29},{... | collective-permute-start | bytes 3145736 | tf_op jit(solution)/shard_map/ppermute | solution.py:493
  37.9 59.3 %all-to-all-start.1 = ((bf16[4,128,1024]{2,1,0:T(8,128)(2,1)}), bf16[4,128,1024]{2,1,0:T(8,128)(2,1)}, u32[]{:S(2)}, u32[]{:S(2)}) async-start(bf16[4,128,1024]{2,1,0:T(8,128)(2,1)} %prepare.3.refs_3_), calls=%async_computation.1 | async-start | bytes 2097152 | tf_op jit(solution)/shard_map/all_to_all | solution.py:403
  69.4 38.8 %collective-permute-start.6 = (bf16[128,4096]{1,0:T(8,128)(2,1)}, bf16[128,4096]{1,0:T(8,128)(2,1)}, u32[]{:S(2)}, u32[]{:S(2)}) collective-permute-start(bf16[128,4096]{1,0:T(8,128)(2,1)} %grad_mix.1.refs_4_.refs_0_.refs_8_), channel_id=1, source_target_pairs={{0,1},{1,2},{2,3},{4,5},{5,6},{6,7},{8,9},{9,10},{10,11},{12,13},{... | collective-permute-start | bytes 3145736 | tf_op jit(solution)/shard_map/ppermute | solution.py:410
  73.8 34.4 %collective-permute-start.7 = (bf16[128,4096]{1,0:T(8,128)(2,1)}, bf16[128,4096]{1,0:T(8,128)(2,1)}, u32[]{:S(2)}, u32[]{:S(2)}) collective-permute-start(bf16[128,4096]{1,0:T(8,128)(2,1)} %grad_mix.1.refs_4_.refs_0_.refs_8_), channel_id=1, source_target_pairs={{1,0},{2,1},{3,2},{5,4},{6,5},{7,6},{9,8},{10,9},{11,10},{13,12},{... | collective-permute-start | bytes 3145736 | tf_op jit(solution)/shard_map/ppermute | solution.py:411
  90.3 32.5 %collective-permute-start.4 = (bf16[128,4096]{1,0:T(8,128)(2,1)}, bf16[128,4096]{1,0:T(8,128)(2,1)}, u32[]{:S(2)}, u32[]{:S(2)}) collective-permute-start(bf16[128,4096]{1,0:T(8,128)(2,1)} %get-tuple-element.41.refs_3_.refs_4_), channel_id=1, source_target_pairs={{0,1},{1,2},{2,3},{4,5},{5,6},{6,7},{8,9},{9,10},{10,11},{12,13},{... | collective-permute-start | bytes 3145736 | tf_op jit(solution)/shard_map/ppermute | solution.py:410
  93.7 30.8 %collective-permute-start.5 = (bf16[128,4096]{1,0:T(8,128)(2,1)}, bf16[128,4096]{1,0:T(8,128)(2,1)}, u32[]{:S(2)}, u32[]{:S(2)}) collective-permute-start(bf16[128,4096]{1,0:T(8,128)(2,1)} %get-tuple-element.42.refs_4_.refs_5_), channel_id=1, source_target_pairs={{1,0},{2,1},{3,2},{5,4},{6,5},{7,6},{9,8},{10,9},{11,10},{13,12},{... | collective-permute-start | bytes 3145736 | tf_op jit(solution)/shard_map/ppermute | solution.py:411
  111.4 34.0 %collective-permute-start.10 = (bf16[128,4096]{1,0:T(8,128)(2,1)}, bf16[128,4096]{1,0:T(8,128)(2,1)}, u32[]{:S(2)}, u32[]{:S(2)}) collective-permute-start(bf16[128,4096]{1,0:T(8,128)(2,1)} %get-tuple-element.46.refs_4_), channel_id=1, source_target_pairs={{0,1},{1,2},{2,3},{4,5},{5,6},{6,7},{8,9},{9,10},{10,11},{12,13},{... | collective-permute-start | bytes 3145736 | tf_op jit(solution)/shard_map/ppermute | solution.py:410
  113.8 33.3 %collective-permute-start.11 = (bf16[128,4096]{1,0:T(8,128)(2,1)}, bf16[128,4096]{1,0:T(8,128)(2,1)}, u32[]{:S(2)}, u32[]{:S(2)}) collective-permute-start(bf16[128,4096]{1,0:T(8,128)(2,1)} %get-tuple-element.49), channel_id=1, source_target_pairs={{1,0},{2,1},{3,2},{5,4},{6,5},{7,6},{9,8},{10,9},{11,10},{13,12},{... | collective-permute-start | bytes 3145736 | tf_op jit(solution)/shard_map/ppermute | solution.py:411
  128.2 39.6 %collective-permute-start.8 = (bf16[128,4096]{1,0:T(8,128)(2,1)}, bf16[128,4096]{1,0:T(8,128)(2,1)}, u32[]{:S(2)}, u32[]{:S(2)}) collective-permute-start(bf16[128,4096]{1,0:T(8,128)(2,1)} %get-tuple-element.47.refs_4_), channel_id=1, source_target_pairs={{0,1},{1,2},{2,3},{4,5},{5,6},{6,7},{8,9},{9,10},{10,11},{12,13},{... | collective-permute-start | bytes 3145736 | tf_op jit(solution)/shard_map/ppermute | solution.py:410
  130.9 38.6 %collective-permute-start.9 = (bf16[128,4096]{1,0:T(8,128)(2,1)}, bf16[128,4096]{1,0:T(8,128)(2,1)}, u32[]{:S(2)}, u32[]{:S(2)}) collective-permute-start(bf16[128,4096]{1,0:T(8,128)(2,1)} %get-tuple-element.48.refs_5_), channel_id=1, source_target_pairs={{1,0},{2,1},{3,2},{5,4},{6,5},{7,6},{9,8},{10,9},{11,10},{13,12},{... | collective-permute-start | bytes 3145736 | tf_op jit(solution)/shard_map/ppermute | solution.py:411
  150.6 38.1 %collective-permute-start.12 = (bf16[128,4096]{1,0:T(8,128)(2,1)}, bf16[128,4096]{1,0:T(8,128)(2,1)}, u32[]{:S(2)}, u32[]{:S(2)}) collective-permute-start(bf16[128,4096]{1,0:T(8,128)(2,1)} %get-tuple-element.51.refs_4_), channel_id=1, source_target_pairs={{0,1},{1,2},{2,3},{4,5},{5,6},{6,7},{8,9},{9,10},{10,11},{12,13},{... | collective-permute-start | bytes 3145736 | tf_op jit(solution)/shard_map/ppermute | solution.py:410
  153.3 37.4 %collective-permute-start.13 = (bf16[128,4096]{1,0:T(8,128)(2,1)}, bf16[128,4096]{1,0:T(8,128)(2,1)}, u32[]{:S(2)}, u32[]{:S(2)}) collective-permute-start(bf16[128,4096]{1,0:T(8,128)(2,1)} %get-tuple-element.52), channel_id=1, source_target_pairs={{1,0},{2,1},{3,2},{5,4},{6,5},{7,6},{9,8},{10,9},{11,10},{13,12},{... | collective-permute-start | bytes 3145736 | tf_op jit(solution)/shard_map/ppermute | solution.py:411
  194.1 28.3 %collective-permute-start.14 = (bf16[128,4096]{1,0:T(8,128)(2,1)}, bf16[128,4096]{1,0:T(8,128)(2,1)}, u32[]{:S(2)}, u32[]{:S(2)}) collective-permute-start(bf16[128,4096]{1,0:T(8,128)(2,1)} %get-tuple-element.53.refs_9_), channel_id=1, source_target_pairs={{0,1},{1,2},{2,3},{4,5},{5,6},{6,7},{8,9},{9,10},{10,11},{12,13},{... | collective-permute-start | bytes 3145736 | tf_op jit(solution)/shard_map/ppermute | solution.py:410
  196.6 33.9 %collective-permute-start.15 = (bf16[128,4096]{1,0:T(8,128)(2,1)}, bf16[128,4096]{1,0:T(8,128)(2,1)}, u32[]{:S(2)}, u32[]{:S(2)}) collective-permute-start(bf16[128,4096]{1,0:T(8,128)(2,1)} %get-tuple-element.54.refs_10_), channel_id=1, source_target_pairs={{1,0},{2,1},{3,2},{5,4},{6,5},{7,6},{9,8},{10,9},{11,10},{13,12},{... | collective-permute-start | bytes 3145736 | tf_op jit(solution)/shard_map/ppermute | solution.py:411
  213.4 29.5 %all-to-all-start.2 = ((bf16[4,128,1024]{2,1,0:T(8,128)(2,1)}), bf16[4,128,1024]{2,1,0:T(8,128)(2,1)}, u32[]{:S(2)}, u32[]{:S(2)}) async-start(bf16[4,128,1024]{2,1,0:T(8,128)(2,1)} %bitcast.18), calls=%async_computation.2 | async-start | bytes 2097152 | tf_op jit(solution)/shard_map/all_to_all | solution.py:403
  242.9 54.6 %all-to-all-start.3 = ((bf16[4,128,1024]{2,1,0:T(8,128)(2,1)}), bf16[4,128,1024]{2,1,0:T(8,128)(2,1)}, u32[]{:S(2)}, u32[]{:S(2)}) async-start(bf16[4,128,1024]{2,1,0:T(8,128)(2,1)} %bitcast.17), calls=%async_computation.3 | async-start | bytes 2097152 | tf_op jit(solution)/shard_map/all_to_all | solution.py:403
  250.4 42.8 %collective-permute-start.19 = (bf16[128,4096]{1,0:T(8,128)(2,1)}, bf16[128,4096]{1,0:T(8,128)(2,1)}, u32[]{:S(2)}, u32[]{:S(2)}) collective-permute-start(bf16[128,4096]{1,0:T(8,128)(2,1)} %get-tuple-element.56.refs_9_.refs_7_), channel_id=1, source_target_pairs={{0,1},{1,2},{2,3},{4,5},{5,6},{6,7},{8,9},{9,10},{10,11},{12,13},{... | collective-permute-start | bytes 3145736 | tf_op jit(solution)/shard_map/ppermute | solution.py:410
  253.8 41.4 %collective-permute-start.20 = (bf16[128,4096]{1,0:T(8,128)(2,1)}, bf16[128,4096]{1,0:T(8,128)(2,1)}, u32[]{:S(2)}, u32[]{:S(2)}) collective-permute-start(bf16[128,4096]{1,0:T(8,128)(2,1)} %get-tuple-element.61.refs_8_), channel_id=1, source_target_pairs={{1,0},{2,1},{3,2},{5,4},{6,5},{7,6},{9,8},{10,9},{11,10},{13,12},{... | collective-permute-start | bytes 3145736 | tf_op jit(solution)/shard_map/ppermute | solution.py:411
  261.8 33.4 %collective-permute-start.21 = (bf16[1,128,4096]{2,1,0:T(8,128)(2,1)}, bf16[1,128,4096]{2,1,0:T(8,128)(2,1)}, u32[]{:S(2)}, u32[]{:S(2)}) collective-permute-start(bf16[1,128,4096]{2,1,0:T(8,128)(2,1)} %finish.2.refs_16_.refs_0_), channel_id=1, source_target_pairs={{28,4},{24,8},{20,12},{12,20},{8,24},{4,28},{29,5},{25,9},{21,13},... | collective-permute-start | bytes 3145736 | tf_op jit(solution)/shard_map/ppermute | solution.py:526
  297.5 6.5 %copy-start = (f32[4,8,128]{2,1,0:T(8,128)S(1)}, f32[4,8,128]{2,1,0:T(8,128)}, u32[]{:S(2)}) copy-start(f32[4,8,128]{2,1,0:T(8,128)} %filter_gradient.1) | copy-start | bytes 49156
  302.1 14.5 %collective-permute-start.22 = (bf16[1,128,4096]{2,1,0:T(8,128)(2,1)}, bf16[1,128,4096]{2,1,0:T(8,128)(2,1)}, u32[]{:S(2)}, u32[]{:S(2)}) collective-permute-start(bf16[1,128,4096]{2,1,0:T(8,128)(2,1)} %finish.3.refs_4_), channel_id=1, source_target_pairs={{4,0},{8,4},{12,8},{16,12},{20,16},{24,20},{28,24},{5,1},{9,5},{13... | collective-permute-start | bytes 3145736 | tf_op jit(solution)/shard_map/ppermute | solution.py:533
  304.0 3.8 %collective-permute-start.16 = (f32[1,32,128]{2,1,0:T(8,128)S(1)}, f32[1,32,128]{2,1,0:T(8,128)S(1)}, u32[]{:S(2)}, u32[]{:S(2)}) collective-permute-start(f32[1,32,128]{2,1,0:T(8,128)S(1)} %bitcast.21), channel_id=1, source_target_pairs={{0,1},{1,2},{2,3},{3,0},{4,5},{5,6},{6,7},{7,4},{8,9},{9,10},{10,1... | collective-permute-start | bytes 49160 | tf_op jit(solution)/shard_map/ppermute | solution.py:470
  304.6 4.7 %collective-permute-start.17 = (f32[1,32,128]{2,1,0:T(8,128)S(1)}, f32[1,32,128]{2,1,0:T(8,128)S(1)}, u32[]{:S(2)}, u32[]{:S(2)}) collective-permute-start(f32[1,32,128]{2,1,0:T(8,128)S(1)} %bitcast.22), channel_id=1, source_target_pairs={{0,2},{1,3},{2,0},{3,1},{4,6},{5,7},{6,4},{7,5},{8,10},{9,11},{10,... | collective-permute-start | bytes 49160 | tf_op jit(solution)/shard_map/ppermute | solution.py:470
  304.6 5.0 %collective-permute-start.18 = (f32[1,32,128]{2,1,0:T(8,128)S(1)}, f32[1,32,128]{2,1,0:T(8,128)S(1)}, u32[]{:S(2)}, u32[]{:S(2)}) collective-permute-start(f32[1,32,128]{2,1,0:T(8,128)S(1)} %bitcast.23), channel_id=1, source_target_pairs={{0,3},{1,0},{2,1},{3,2},{4,7},{5,4},{6,5},{7,6},{8,11},{9,8},{10,9... | collective-permute-start | bytes 49160 | tf_op jit(solution)/shard_map/ppermute | solution.py:470
  307.8 1.8 copy-start.1
  309.4 0.6 copy-start.2
  310.0 0.6 copy-start.3
